TPU v7x, 32 devices: a whole 2x2x4 slice. The times are simulated.
32 devices in a mesh: row: 8 (over z, x), col: 4 (over y, core).
Axes of the slice: x: 2, y: 2, z: 4, core: 2. Of those that a mesh axis runs over, the one named last changes fastest.
Arguments:
- node_feats: bfloat16 [8192, 256], P(('row', 'col')), may hold values from -6 to 6
- dest_grad: bfloat16 [4, 2048, 256], P('col', 'row'), may hold values from -6 to 6
- bases: bfloat16 [30, 256, 256], replicated, may hold values from -0.375 to 0.375
- coefs: bfloat16 [2000, 30], replicated, may hold values from -1 to 1
- src_ids: int32 [8, 4, 1024], P('row', 'col'), may hold values from 0 to 1023
- dst_ids: int32 [8, 4, 1024], P('row', 'col'), may hold values from 0 to 2047
- rel_ids: int32 [8, 4, 1024], P('row', 'col'), may hold values from 0 to 1999
- edge_norm: float32 [8, 4, 1024], P('row', 'col'), may hold values from 0.1 to 1
- block_fill: int32 [8, 4, 8], P('row', 'col'), may hold values from 0 to 128, as said below
Outputs:
- node_grad: bfloat16 [8192, 256], P(('row', 'col'))
- basis_grad: float32 [7680, 256], P(('row', 'col'))
- coef_grad: float32 [2000, 30], replicated
Inputs may be any that keep to these rules, and one draw needn't show every extreme that they name: `block_fill`: the first block of every device is full, and blocks after a device's last live block are empty.
All inputs are finite; a program needn't handle non-finite values.
Results may differ from a plain program's by a relative error of at most 0.0049.
Values may be sent and summed in bfloat16 or wider, within the bound.
No kernel may reach another device: no remote copies, remote signals or barrier semaphores. Data moves between devices by JAX's collectives and lax.ppermute only.
A program may use at most 64 MiB of HBM per device.

v0:
```python
import jax
import jax.numpy as jnp
from jax import lax
from jax.sharding import PartitionSpec as P

EDGE_BLOCK = 128


def on_device(
    node_feats, dest_grad, bases, coefs, src_ids, dst_ids, rel_ids, edge_norm, block_fill
):
    col_count = lax.axis_size("col")
    source_rows = lax.all_gather(node_feats, "col", axis=0, tiled=True)
    target_rows = lax.all_gather(dest_grad[0], "row", axis=0, tiled=True)
    sources = src_ids.reshape(-1)
    targets = dst_ids.reshape(-1)
    relations = rel_ids.reshape(-1)
    fills = block_fill.reshape(-1)
    block_total = fills.shape[0]
    position = lax.broadcasted_iota(jnp.int32, (block_total, EDGE_BLOCK), 1)
    live_mask = (position < fills[:, None]).reshape(-1).astype(jnp.float32)
    weights = edge_norm.reshape(-1) * live_mask
    edge_total = sources.shape[0]
    edge_grad = (weights[:, None] * target_rows[targets].astype(jnp.float32)).astype(jnp.bfloat16)
    edge_rows = source_rows[sources]
    edge_coefs = coefs[relations]
    basis_count = bases.shape[0]
    width = bases.shape[1]
    vertex_count = source_rows.shape[0]
    relation_count = coefs.shape[0]
    block_span = 512
    node_part = jnp.zeros((vertex_count, width), jnp.float32)
    coef_part = jnp.zeros((relation_count, basis_count), jnp.float32)
    for offset in range(0, edge_total, block_span):
        grad_block = edge_grad[offset : offset + block_span]
        rows_block = edge_rows[offset : offset + block_span]
        coef_block = edge_coefs[offset : offset + block_span].astype(jnp.float32)
        backed = lax.dot_general(
            grad_block, bases, (((1,), (2,)), ((), ())), preferred_element_type=jnp.float32
        )
        per_edge = jnp.sum(coef_block[:, :, None] * backed, axis=1)
        inner = jnp.sum(backed * rows_block[:, None, :].astype(jnp.float32), axis=2)
        node_part = node_part + jax.ops.segment_sum(
            per_edge, sources[offset : offset + block_span], num_segments=vertex_count
        )
        coef_part = coef_part + jax.ops.segment_sum(
            inner, relations[offset : offset + block_span], num_segments=relation_count
        )
    node_grad = lax.psum_scatter(node_part, "col", scatter_dimension=0, tiled=True).astype(
        jnp.bfloat16
    )
    basis_rows = (edge_coefs[:, :, None] * edge_rows[:, None, :]).reshape(
        edge_total, basis_count * width
    )
    basis_grad = lax.psum_scatter(
        lax.dot_general(
            basis_rows, edge_grad, (((0,), (0,)), ((), ())), preferred_element_type=jnp.float32
        ),
        ("row", "col"),
        scatter_dimension=0,
        tiled=True,
    )
    coef_grad = lax.psum(coef_part, ("row", "col"))
    return (node_grad, basis_grad / col_count, coef_grad / col_count)


def solution(mesh):
    in_specs = (
        P(("row", "col"), None),
        P("col", "row", None),
        P(),
        P(),
        P("row", "col", None),
        P("row", "col", None),
        P("row", "col", None),
        P("row", "col", None),
        P("row", "col", None),
    )
    out_specs = (P(("row", "col"), None), P(("row", "col"), None), P())
    return jax.shard_map(
        on_device, mesh=mesh, in_specs=in_specs, out_specs=out_specs, check_vma=False
    )
```

profile of v0, /device:TPU:0, one launch (start us, length us, event | category | flops | bytes accessed | tf_op | source)
XLA Modules:
  0.0 365.7 jit_solution(9166976303174811536)
XLA Ops:
  7.2 0.0 all-gather.3.cloned.1.call-start
  7.2 0.7 all-gather.3.cloned.1.call-update
  7.9 0.0 all-reduce.2.cloned.1.call-start
  7.9 8.9 %all_gather.7 = bf16[1024,256]{1,0:T(8,128)(2,1)S(1)} all-gather(bf16[256,256]{1,0:T(8,128)(2,1)} %param.9), channel_id=1, replica_groups=mesh['row'=8,'col'=4] {'col'}, dimensions={0}, use_global_device_ids=true | all-gather | bytes 655360 | tf_op jit(solution)/shard_map/all_gather | solution.py:13
  16.8 0.7 compare_select_fusion
  17.5 3.9 %gather_fusion.2 = bf16[1024,256]{1,0:T(8,128)(2,1)S(1)} fusion(bf16[1024,256]{1,0:T(8,128)(2,1)S(1)} %all_gather.7, s32[1024]{0:T(1024)S(1)} %broadcast_clamp_fusion), kind=kCustom, calls=%fused_computation.2 | custom fusion | bytes 1052672 | tf_op jit(solution)/shard_map/gather | solution.py:25
  21.5 0.2 copy.42
  21.7 0.1 slice_convert_fusion
  21.7 0.2 copy.43
  22.0 1.2 copy.36
  23.2 0.7 compare_select_fusion.2
  23.9 3.2 gather_fusion
  27.1 0.2 copy.37
  27.2 0.2 copy.44
  27.5 0.7 slice_bitcast_fusion.5
  28.2 0.7 compare_select_fusion.1
  28.9 0.8 fusion.9
  29.6 23.4 %all-gather.3.cloned.1.call-done = bf16[1,2048,256]{2,1,0:T(8,128)(2,1)} async-done(((bf16[1,256,256]{2,1,0:T(8,128)(2,1)}), bf16[1,2048,256]{2,1,0:T(8,128)(2,1)}) %all-gather.3.cloned.1.call-update) | async-done | bytes 1048592 | tf_op jit(solution)/shard_map/all_gather | solution.py:14
  53.0 4.8 %gather_fusion.1 = bf16[1024,256]{1,0:T(8,128)(2,1)S(1)} fusion(bf16[2048,256]{1,0:T(8,128)(2,1)} %bitcast.38, s32[1024]{0:T(1024)S(1)} %broadcast_clamp_fusion.1), kind=kCustom, calls=%fused_computation.1 | custom fusion | bytes 1052672 | tf_op jit(solution)/shard_map/gather | solution.py:24
  57.9 0.2 multiply_convert_fusion
  58.1 0.0 copy-start.1
  58.1 5.5 %multiply_reduce_fusion.1 = (f32[512,30]{0,1:T(8,128)S(1)}, f32[512,256]{0,1:T(8,128)S(1)}) fusion(f32[512,256]{0,1:T(8,128)S(1)} %copy.43, f32[512,30]{0,1:T(8,128)S(1)} %get-tuple-element.19, bf16[30,256,256]{2,1,0:T(8,128)(2,1)} %param.11, bf16[1024,256]{1,0:T(8,128)(2,1)S(1)} %multiply_convert_fusion), kind=kOutput, calls=%fused_computation.7 | convolution fusion | flops 2028848128 | bytes 5369856 | tf_op jit(solution)/shard_map/dot_general | solution.py:38
  63.6 0.0 copy-done.1
  63.6 0.0 copy-start
  63.6 3.4 multiply_reduce_fusion
  67.0 0.2 copy.45
  67.3 7.0 %scatter_custom_fusion.2 = f32[2000,30]{1,0:T(8,128)} fusion(s32[1024]{0:T(1024)S(1)} %bitcast.44, f32[1024,30]{1,0:T(8,128)S(1)} %copy.45, f32[]{:T(128)} %constant.6.clone.1), kind=kCustom, calls=%fused_computation.17 | custom fusion | flops 30720 | bytes 240004 | tf_op jit(solution)/shard_map/add | solution.py:46
  74.3 0.0 all-reduce.2.cloned.1.call-update
  74.3 0.0 reduce-scatter.3.cloned.1.call-start
  74.4 0.0 copy-done
  74.4 0.2 copy.38
  74.6 1.0 copy.40
  75.6 3.7 %scatter_custom_fusion = f32[1024,256]{1,0:T(8,128)S(1)} fusion(s32[512]{0:T(512)S(1)} %bitcast.46, f32[512,256]{1,0:T(8,128)S(1)} %copy.38, f32[]{:T(128)} %constant.6.clone.1), kind=kCustom, calls=%fused_computation.14 | custom fusion | flops 131072 | bytes 1048580 | tf_op jit(solution)/shard_map/scatter-add | solution.py:43
  79.3 4.0 %scatter_custom_fusion.1 = f32[1024,256]{1,0:T(8,128)S(1)} fusion(s32[512]{0:T(512)S(1)} %bitcast.45, f32[512,256]{1,0:T(8,128)} %copy.40, f32[]{:T(128)} %constant.6.clone.1), kind=kCustom, calls=%fused_computation.12 | custom fusion | flops 131072 | bytes 1049088 | tf_op jit(solution)/shard_map/scatter-add | solution.py:43
  83.4 1.2 add.66
  84.6 0.0 reduce-scatter.3.cloned.1.call-update
  84.6 0.0 reduce-scatter.5.cloned.1.call-start
  84.7 4.1 %broadcast_multiply_fusion = bf16[1024,30,256]{0,2,1:T(8,128)(2,1)S(1)} fusion(bf16[1024,256]{0,1:T(8,128)(2,1)S(1)} %copy.42, bf16[1024,30]{0,1:T(8,128)(2,1)S(1)} %copy.37), kind=kLoop, calls=%fused_computation.10 | loop fusion | flops 7864320 | bytes 16314368 | tf_op jit(solution)/shard_map/mul | solution.py:52
  88.8 6.7 %fusion.11 = f32[7680,256]{1,0:T(8,128)} fusion(bf16[1024,7680]{0,1:T(8,128)(2,1)S(1)} %bitcast.39, bf16[1024,256]{1,0:T(8,128)(2,1)S(1)} %multiply_convert_fusion), kind=kOutput, calls=%fused_computation.42 | convolution fusion | flops 4026531840 | bytes 24117248 | tf_op jit(solution)/shard_map/dot_general | solution.py:56
  95.5 0.0 reduce-scatter.5.cloned.1.call-update
  95.5 107.2 %all-reduce.2.cloned.1.call-done = f32[2000,30]{1,0:T(8,128)} async-done(((f32[2000,30]{1,0:T(8,128)}), f32[2000,30]{1,0:T(8,128)}) %all-reduce.2.cloned.1.call-update) | async-done | bytes 240016 | tf_op jit(solution)/shard_map/psum | solution.py:63
  202.7 1.3 broadcast_multiply_fusion.1
  204.0 1.0 copy.46
  205.1 24.5 %reduce-scatter.3.cloned.1.call-done = f32[256,256]{1,0:T(8,128)} async-done(((f32[1024,256]{1,0:T(8,128)}), f32[256,256]{1,0:T(8,128)}) %reduce-scatter.3.cloned.1.call-update) | async-done | bytes 262160 | tf_op jit(solution)/shard_map/reduce_scatter | solution.py:49
  229.5 1.6 convert_element_type.28
  231.2 126.3 %reduce-scatter.5.cloned.1.call-done = f32[240,256]{1,0:T(8,128)} async-done(((f32[7680,256]{1,0:T(8,128)}), f32[240,256]{1,0:T(8,128)}) %reduce-scatter.5.cloned.1.call-update) | async-done | bytes 245776 | tf_op jit(solution)/shard_map/reduce_scatter | solution.py:55
  357.5 1.7 broadcast_multiply_fusion.2
  (7 shorter events, 0.1 us)
Async XLA Ops:
  7.2 45.9 %all-gather.3.cloned.1.call-start = ((), (), s32[]{:S(2)}) async-start(), calls=%async_computation.5 | async-start | bytes 1179648 | tf_op jit(solution)/shard_map/all_gather | solution.py:14
  7.9 194.8 %all-reduce.2.cloned.1.call-start = ((), (), s32[]{:S(2)}) async-start(), calls=%async_computation.4 | async-start | bytes 2048000 | tf_op jit(solution)/shard_map/psum | solution.py:63
  58.1 5.5 %copy-start.1 = (bf16[30,256,256]{2,1,0:T(8,128)(2,1)S(1)}, bf16[30,256,256]{2,1,0:T(8,128)(2,1)}, u32[]{:S(2)}) copy-start(bf16[30,256,256]{2,1,0:T(8,128)(2,1)} %param.11) | copy-start | bytes 11796484
  63.6 10.8 %copy-start = (s32[1,1,1024]{2,1,0:T(1,128)S(1)}, s32[1,1,1024]{2,1,0:T(1,128)}, u32[]{:S(2)}) copy-start(s32[1,1,1024]{2,1,0:T(1,128)} %param.13) | copy-start | bytes 12292
  74.3 155.2 %reduce-scatter.3.cloned.1.call-start = ((), (), s32[]{:S(2)}) async-start(), calls=%async_computation.2 | async-start | bytes 1310720 | tf_op jit(solution)/shard_map/reduce_scatter | solution.py:49
  84.6 272.9 %reduce-scatter.5.cloned.1.call-start = ((), (), s32[]{:S(2)}) async-start(), calls=%async_computation.3 | async-start | bytes 8110080 | tf_op jit(solution)/shard_map/reduce_scatter | solution.py:55
Sparse Core Ops, SparseCore 0:
  10.1 42.8 all-gather.2
  74.4 128.2 all-reduce.1
  205.4 24.0 reduce-scatter.2
  235.1 122.3 reduce-scatter.4
where the time goes:
time: 366 us
  waiting for transfers between devices  282 us (77%)
  other arithmetic  27.9 us (8%)
  local copies, waits for them, and re-layouts  17.1 us (5%)
  matrix products  15.6 us (4%)
  between operations  13.9 us (4%)
  blocking collectives  8.86 us (2%)
    reduce_scatter x1, waiting for transfers between devices, on_device(): lax.psum_scatter(lax.dot_general(basis_rows, edge_grad, (((0,), (0,)), ((...  126 us
    psum x1, waiting for transfers between devices, on_device(): coef_grad = lax.psum(coef_part, ('row', 'col'))  107 us
    reduce_scatter x1, waiting for transfers between devices, on_device(): lax.psum_scatter(node_part, 'col', scatter_dimension=0, tiled=True)  24.5 us
    all_gather x1, waiting for transfers between devices, on_device(): target_rows = lax.all_gather(dest_grad[0], 'row', axis=0, tiled=True)  23.4 us
    dot_general x2, matrix products, on_device(): lax.dot_general(grad_block, bases, (((1,), (2,)), ((), ())), preferred_el...  8.9 us
    all_gather x1, blocking collectives, on_device(): source_rows = lax.all_gather(node_feats, 'col', axis=0, tiled=True)  8.86 us
    scatter-add x2, other arithmetic, on_device(): jax.ops.segment_sum(per_edge, sources[offset:offset + block_span], num_se...  7.79 us
  transfers between devices with their start and end apart: 4, of which 4 were waited for; matrix products, arithmetic and copies ran while one was open for 10% of the time, Pallas kernels for 0%

commit v1 on v0

v1 whole, which is shorter than its diff:
```python
import functools
import jax
import jax.numpy as jnp
from jax import lax
from jax.experimental import pallas as pl
from jax.experimental.pallas import tpu as pltpu
from jax.sharding import PartitionSpec as P

EDGE_BLOCK = 128
TILE = 16
LANES = 128
PAIR = 2
F32 = jnp.float32
BF16 = jnp.bfloat16
I32 = jnp.int32
VMEM_LIMIT = 56 * 1024 * 1024


def round_up(value, unit):
    return (value + unit - 1) // unit * unit


def split_index(ids, size):
    if size & (size - 1) == 0:
        shift = size.bit_length() - 1
        return ids >> shift, ids & (size - 1)
    return ids // size, ids % size


def wrap(difference, size):
    return jnp.where(difference < 0, difference + size, difference)


def one_hot(ids, depth):
    rows = lax.broadcasted_iota(I32, (depth, ids.shape[1]), 0)
    return jnp.where(rows == ids, 1.0, 0.0).astype(BF16)


def eye(width):
    first = lax.broadcasted_iota(I32, (width, width), 0)
    second = lax.broadcasted_iota(I32, (width, width), 1)
    return jnp.where(first == second, 1.0, 0.0).astype(BF16)


def dot(left, right):
    return lax.dot_general(left, right, (((1,), (0,)), ((), ())), preferred_element_type=F32)


def dot_t(left, right):
    return lax.dot_general(left, right, (((1,), (1,)), ((), ())), preferred_element_type=F32)


def tree_sum(values):
    if len(values) == 1:
        return values[0]
    return tree_sum(values[0::2]) + tree_sum(values[1::2])


def vmem():
    return pl.BlockSpec(memory_space=pltpu.VMEM)


def smem():
    return pl.BlockSpec(memory_space=pltpu.SMEM)


def call(body, out_shape, n_in, scratch, flops, name):
    many = isinstance(out_shape, (tuple, list))
    moved = 1 << 22
    return pl.pallas_call(
        body,
        out_shape=out_shape,
        in_specs=[smem()] + [vmem()] * n_in,
        out_specs=[vmem()] * len(out_shape) if many else vmem(),
        scratch_shapes=scratch,
        compiler_params=pltpu.CompilerParams(vmem_limit_bytes=VMEM_LIMIT),
        cost_estimate=pl.CostEstimate(flops=flops, bytes_accessed=moved, transcendentals=0),
        name=name,
    )


def source_kernel(
    sizes, place, meta, meta_core, feats, feats_core, coefs, xt_ref, ct_ref, table
):
    cols, shard, span, heads, padded = sizes
    count = cols // PAIR
    y, core = place[2], place[3]
    width = feats.shape[-1]
    edges = meta.shape[-1]
    unit = eye(width)
    for far, block in enumerate((feats, feats_core)):
        for sy in range(count):
            for xr in range(PAIR):
                at = (far * count + sy) * shard
                table[xr, :, at : at + shard] = dot_t(unit, block[sy, xr]).astype(BF16)
    for far, source in enumerate((meta, meta_core)):

        def step(index, carry, far=far, source=source):
            xr = index // (edges // span)
            at = pl.multiple_of(index % (edges // span) * span, span)
            ids = source[xr, 0:1, pl.ds(at, span)].astype(I32)
            owner, local = split_index(ids, shard)
            owner_y, owner_core = split_index(owner, PAIR)
            slot = (owner_core ^ core) * count + wrap(y - owner_y, count)
            rows = dot(table[xr], one_hot(slot * shard + local, cols * shard))
            xt_ref[far * PAIR + xr, :, pl.ds(at, span)] = rows.astype(BF16)
            relation = source[xr, 2:3, pl.ds(at, span)].astype(I32)
            high, low = split_index(relation, LANES)
            parts = dot(coefs[...], one_hot(low, LANES))
            total = jnp.zeros((padded, span), F32)
            for head in range(heads):
                total = total + jnp.where(
                    high == head, parts[head * padded : (head + 1) * padded], 0.0
                )
            ct_ref[far * PAIR + xr, :, pl.ds(at, span)] = total
            return carry

        lax.fori_loop(0, PAIR * (edges // span), step, 0)


def grad_kernel(sizes, place, meta, *refs):
    rows_total, shard, span = sizes
    count = rows_total // PAIR
    blocks = refs[:rows_total]
    gt_ref, table = refs[rows_total:]
    a, x = place[0], place[1]
    width = blocks[0].shape[-1]
    edges = meta.shape[-1]
    unit = eye(width)
    for at, block in enumerate(blocks):
        table[:, at * shard : (at + 1) * shard] = dot_t(unit, block[...]).astype(BF16)

    def step(index, carry):
        xr = index // (edges // span)
        at = pl.multiple_of(index % (edges // span) * span, span)
        ids = meta[xr, 1:2, pl.ds(at, span)].astype(I32)
        owner, local = split_index(ids, shard)
        owner_a, owner_x = split_index(owner, PAIR)
        slot = (owner_x ^ x) * count + wrap(a - owner_a, count)
        rows = dot(table[...], one_hot(slot * shard + local, rows_total * shard))
        weight = meta[xr, 3:4, pl.ds(at, span)]
        gt_ref[:, pl.ds(pl.multiple_of(index * span, span), span)] = (rows * weight).astype(BF16)
        return carry

    lax.fori_loop(0, PAIR * (edges // span), step, 0)


def forward_kernel(
    sizes, place, meta, gt_ref, xt_ref, ct_ref, bases_ref, out_ref, total, inner, wide, coef_sum
):
    cols, shard, span, heads, padded = sizes
    count = cols // PAIR
    y, core = place[2], place[3]
    edges = meta.shape[-1]
    width = bases_ref.shape[-1]
    group = bases_ref.shape[0]
    step = pl.program_id(0)

    @pl.when(step == 0)
    def _():
        total[...] = jnp.zeros_like(total)
        inner[...] = jnp.zeros_like(inner)

    def chunk(index, carry):
        at = pl.ds(pl.multiple_of(index * span, span), span)
        grads = gt_ref[:, at]
        rows = xt_ref[0, :, at].astype(F32)
        sums = total[:, at]
        for t in range(group):
            base = step * group + t
            backed = dot(bases_ref[t], grads)
            sums = sums + ct_ref[0, pl.ds(base, 1), at] * backed
            inner[pl.ds(base, 1), at] = jnp.sum(backed * rows, axis=0, keepdims=True)
        total[:, at] = sums
        return carry

    lax.fori_loop(0, edges // span, chunk, 0)

    @pl.when(step == pl.num_programs(0) - 1)
    def _():
        ids = meta[0, 0:1, :].astype(I32)
        owner, local = split_index(ids, shard)
        owner_y, owner_core = split_index(owner, PAIR)
        slot = (owner_core ^ core) * count + wrap(owner_y - y, count)
        place_of = slot * shard + local
        values = total[...].astype(BF16)
        for at in range(cols):
            hot = one_hot(place_of - at * shard, shard)
            out_ref[at, 0:shard, :] = dot_t(hot, values).astype(BF16)
        high, low = split_index(meta[0, 2:3, :].astype(I32), LANES)
        for head in range(heads):
            wide[head * padded : (head + 1) * padded, :] = jnp.where(
                high == head, inner[...], 0.0
            ).astype(BF16)
        coef_sum[...] = dot_t(wide[...], one_hot(low, LANES))
        share = heads * padded // cols
        half = share // 2
        for far in range(PAIR):
            for sy in range(count):
                target = (y + sy) % count * PAIR + (core ^ far)
                for side in range(2):
                    rows = coef_sum[pl.ds(pl.multiple_of(target * share + side * half, 8), half), :]
                    out_ref[
                        far * count + sy,
                        shard : shard + half,
                        side * LANES : (side + 1) * LANES,
                    ] = rows.astype(BF16)


def basis_kernel(sizes, place, gt_ref, gt_core, xt_ref, ct_ref, *refs):
    rows_total, cols, block, groups, basis_count, span = sizes
    a_count, y_count = rows_total // PAIR, cols // PAIR
    a, x, y, core = place[0], place[1], place[2], place[3]
    outs = refs[: 1 + (y_count - 1) * a_count]
    acc, left, tiles = refs[len(outs) :]
    width, edges = xt_ref.shape[1], xt_ref.shape[2]
    tiles_wide = width // TILE
    cover = groups * TILE
    steps = edges // span
    acc[...] = jnp.zeros_like(acc)
    for far, grads in enumerate((gt_ref, gt_core)):

        def step(index, carry, far=far, grads=grads):
            part = far * PAIR + index // steps
            at = pl.ds(pl.multiple_of(index % steps * span, span), span)
            for b in range(basis_count):
                row = ct_ref[part, b : b + 1, at]
                tiles[b] = jnp.broadcast_to(row, (TILE, span)).astype(BF16)
            for sy in range(y_count):
                for sz in range(a_count):
                    owner = ((a + sz) % a_count * PAIR + x) * cols + (y + sy) % y_count * PAIR + core
                    first = owner * block // TILE
                    for q in range(groups):
                        tile = jnp.minimum(first + q, basis_count * tiles_wide - 1)
                        lower = pl.multiple_of(tile % tiles_wide * TILE, TILE)
                        to = ((sy * a_count + sz) * groups + q) * TILE
                        left[to : to + TILE, :] = (
                            tiles[tile // tiles_wide] * xt_ref[part, pl.ds(lower, TILE), at]
                        )
            here = pl.ds(pl.multiple_of(index * span, span), span)
            acc[...] += dot_t(left[...], grads[:, here])
            return carry

        lax.fori_loop(0, PAIR * steps, step, 0)
    for sz in range(a_count):
        outs[0][sz] = acc[sz * cover : (sz + 1) * cover, :]
    for sy in range(1, y_count):
        for sz in range(a_count):
            at = (sy * a_count + sz) * cover
            outs[1 + (sy - 1) * a_count + sz][...] = acc[at : at + cover, :].astype(BF16)


def coef_kernel(sizes, place, *refs):
    cols, heads, padded, divisor = sizes
    count = cols // PAIR
    parts, (out_ref, whole) = refs[:cols], refs[cols:]
    y, core = place[2], place[3]
    share = heads * padded // cols
    half = share // 2
    for far in range(PAIR):
        for sy in range(count):
            target = wrap(y - sy, count) * PAIR + (core ^ far)
            for side in range(2):
                whole[pl.ds(pl.multiple_of(target * share + side * half, 8), half), :] = (
                    parts[far * count + sy][:, side * LANES : (side + 1) * LANES]
                )
    total, width = out_ref.shape
    for head in range(heads):
        piece = whole[head * padded : (head + 1) * padded, :].T
        live = min(LANES, total - head * LANES)
        out_ref[head * LANES : head * LANES + live, :] = piece[:live, :width] / divisor


def on_device(
    node_feats, dest_grad, bases, coefs, src_ids, dst_ids, rel_ids, edge_norm, block_fill
):
    rows_total = lax.axis_size("row")
    cols = lax.axis_size("col")
    a_count, y_count = rows_total // PAIR, cols // PAIR
    shard, width = node_feats.shape
    basis_count = bases.shape[0]
    relation_count = coefs.shape[0]
    edges = src_ids.size
    padded = round_up(basis_count, TILE)
    heads = round_up(relation_count, LANES) // LANES
    while heads * padded % (cols * 2 * TILE):
        heads += 1
    span = 256
    i = lax.axis_index("row")
    j = lax.axis_index("col")
    place = jnp.stack([i // PAIR, i % PAIR, j // PAIR, j % PAIR]).astype(I32)

    def flip_x(value):
        return lax.ppermute(value, "row", [(r, r ^ 1) for r in range(rows_total)])

    def flip_core(value):
        return lax.ppermute(value, "col", [(c, c ^ 1) for c in range(cols)])

    def turn_z(value, by):
        return lax.ppermute(
            value, "row", [(r, (r + by * PAIR) % rows_total) for r in range(rows_total)]
        )

    def turn_y(value, by):
        return lax.ppermute(value, "col", [(c, (c + by * PAIR) % cols) for c in range(cols)])

    own_dest = dest_grad[0]
    dest = [own_dest] + [turn_z(own_dest, s) for s in range(1, a_count)]
    dest = dest + [flip_x(value) for value in dest]

    fills = block_fill.reshape(-1)
    position = lax.broadcasted_iota(I32, (fills.shape[0], EDGE_BLOCK), 1)
    live = (position < fills[:, None]).reshape(-1).astype(F32)
    weights = edge_norm.reshape(-1) * live
    meta = jnp.stack(
        [
            src_ids.reshape(-1).astype(F32),
            dst_ids.reshape(-1).astype(F32),
            rel_ids.reshape(-1).astype(F32),
            weights,
        ]
    )
    meta = jnp.stack([meta, flip_x(meta)])
    meta_core = flip_core(meta)

    feats = jnp.stack([node_feats, flip_x(node_feats)])
    feats = jnp.stack([feats] + [turn_y(feats, s) for s in range(1, y_count)])
    feats_core = flip_core(feats)

    table = jnp.pad(coefs, ((0, heads * LANES - relation_count), (0, padded - basis_count)))
    table = table.reshape(heads, LANES, padded).transpose(0, 2, 1).reshape(heads * padded, LANES)

    xt, ct = call(
        functools.partial(source_kernel, (cols, shard, span, heads, padded)),
        (
            jax.ShapeDtypeStruct((2 * PAIR, width, edges), BF16),
            jax.ShapeDtypeStruct((2 * PAIR, padded, edges), F32),
        ),
        5,
        [pltpu.VMEM((PAIR, width, cols * shard), BF16)],
        2 * 4 * edges * cols * shard * width,
        "source_rows",
    )(place, meta, meta_core, feats, feats_core, table)

    dest_shard = own_dest.shape[0]
    gt = call(
        functools.partial(grad_kernel, (rows_total, dest_shard, span)),
        jax.ShapeDtypeStruct((width, PAIR * edges), BF16),
        1 + rows_total,
        [pltpu.VMEM((width, rows_total * dest_shard), BF16)],
        2 * 2 * edges * rows_total * dest_shard * width,
        "edge_grads",
    )(place, meta, *dest)
    gt_core = flip_core(gt)

    group = max(g for g in range(1, 6) if basis_count % g == 0)
    share_rows = heads * padded // cols // 2
    packed = pl.pallas_call(
        functools.partial(forward_kernel, (cols, shard, span, heads, padded)),
        grid=(basis_count // group,),
        in_specs=[
            smem(),
            pl.BlockSpec(meta.shape, lambda s: (0, 0, 0)),
            pl.BlockSpec((width, edges), lambda s: (0, 0)),
            pl.BlockSpec((1, width, edges), lambda s: (0, 0, 0)),
            pl.BlockSpec((1, padded, edges), lambda s: (0, 0, 0)),
            pl.BlockSpec((group, width, width), lambda s: (s, 0, 0)),
        ],
        out_specs=pl.BlockSpec((cols, shard + share_rows, width), lambda s: (0, 0, 0)),
        out_shape=jax.ShapeDtypeStruct((cols, shard + share_rows, width), BF16),
        scratch_shapes=[
            pltpu.VMEM((width, edges), F32),
            pltpu.VMEM((padded, edges), F32),
            pltpu.VMEM((heads * padded, edges), BF16),
            pltpu.VMEM((heads * padded, LANES), F32),
        ],
        compiler_params=pltpu.CompilerParams(vmem_limit_bytes=VMEM_LIMIT),
        cost_estimate=pl.CostEstimate(
            flops=2 * edges * width * width * basis_count,
            bytes_accessed=bases.size * 2,
            transcendentals=0,
        ),
        name="backed_sums",
    )(place, meta, gt, xt, ct, bases)

    block = basis_count * width // (rows_total * cols)
    cover = block if block % TILE == 0 else round_up(block, TILE) + TILE
    pieces = call(
        functools.partial(
            basis_kernel, (rows_total, cols, block, cover // TILE, basis_count, 2 * span)
        ),
        [jax.ShapeDtypeStruct((a_count, cover, width), F32)]
        + [jax.ShapeDtypeStruct((cover, width), BF16)] * ((y_count - 1) * a_count),
        4,
        [
            pltpu.VMEM((y_count * a_count * cover, width), F32),
            pltpu.VMEM((y_count * a_count * cover, 2 * span), BF16),
            pltpu.VMEM((padded, TILE, 2 * span), BF16),
        ],
        2 * 4 * edges * y_count * a_count * cover * width,
        "basis_terms",
    )(place, gt, gt_core, xt, ct)
    kept, sent = pieces[0], pieces[1:]

    got = {}
    order = list(range(1, a_count)) + [0]
    for sz in order:
        for sy in range(1, y_count):
            got[sz, sy] = turn_y(sent[(sy - 1) * a_count + sz], sy)
    basis_sum = None
    arrived = []
    for sz in order:
        value = kept[sz]
        for sy in range(1, y_count):
            value = value + got[sz, sy].astype(F32)
        if sz:
            arrived.append(turn_z(value.astype(BF16), sz))
        else:
            basis_sum = value
    for value in arrived:
        basis_sum = basis_sum + value.astype(F32)
    if cover != block:
        owner = i * cols + j
        basis_sum = lax.dynamic_slice_in_dim(basis_sum, owner * block % TILE, block, axis=0)
    basis_grad = basis_sum / cols

    joined = packed[0].astype(F32)
    for far in range(PAIR):
        for sy in range(y_count):
            if far or sy:
                target = [
                    (c, ((c // PAIR + sy) % y_count) * PAIR + (c % PAIR ^ far)) for c in range(cols)
                ]
                joined = joined + lax.ppermute(packed[far * y_count + sy], "col", target).astype(
                    F32
                )
    node_grad = joined[:shard].astype(BF16)
    coef_part = joined[shard:]
    low = coef_part.astype(BF16)
    low = (low.astype(F32) + flip_x(low).astype(F32)).astype(BF16)
    coef_part = tree_sum([low.astype(F32)] + [turn_z(low, s).astype(F32) for s in range(1, a_count)])
    shares = []
    for far in range(PAIR):
        for sy in range(y_count):
            target = [
                (c, ((c // PAIR + sy) % y_count) * PAIR + (c % PAIR ^ far)) for c in range(cols)
            ]
            shares.append(lax.ppermute(coef_part, "col", target) if far or sy else coef_part)
    coef_grad = call(
        functools.partial(coef_kernel, (cols, heads, padded, cols)),
        jax.ShapeDtypeStruct((relation_count, basis_count), F32),
        cols,
        [pltpu.VMEM((heads * padded, LANES), F32)],
        1 << 20,
        "coef_rows",
    )(place, *shares)
    return (node_grad, basis_grad, coef_grad)


def solution(mesh):
    in_specs = (
        P(("row", "col"), None),
        P("col", "row", None),
        P(),
        P(),
        P("row", "col", None),
        P("row", "col", None),
        P("row", "col", None),
        P("row", "col", None),
        P("row", "col", None),
    )
    out_specs = (P(("row", "col"), None), P(("row", "col"), None), P())
    return jax.shard_map(
        on_device, mesh=mesh, in_specs=in_specs, out_specs=out_specs, check_vma=False
    )
```

time: 366 us -> 128 us (0.35)
  waiting for transfers between devices: 282 us -> 31.3 us
  Pallas kernels: 0 us -> 42.7 us
  starting transfers between devices: 0.16 us -> 34.8 us
  other arithmetic: 27.9 us -> 8.49 us
  matrix products: 15.6 us -> 0 us
  between operations: 13.9 us -> 0.85 us
  blocking collectives: 8.86 us -> 0 us
  local copies, waits for them, and re-layouts: 17.1 us -> 8.82 us
    reduce_scatter x2 -> x0, waiting for transfers between devices: 151 us -> none  [the longest x1 126 us: on_device(): lax.psum_scatter(lax.dot_general(basis_rows, edge_grad, (((0,), (0,)), ((...]
    psum x1 -> x0, waiting for transfers between devices: 107 us -> none  [on_device(): coef_grad = lax.psum(coef_part, ('row', 'col'))]
    pallas_call x0 -> x5, Pallas kernels: none -> 42.7 us  [the longest x1 12.8 us: on_device(): pl.pallas_call(functools.partial(forward_kernel, (cols, shard, span, head...]
    ppermute x0 -> x30, starting transfers between devices: none -> 34.8 us  [the longest x9 14.9 us: turn_z(): lax.ppermute(value, 'row', [(r, (r + by * PAIR) % rows_total) for r in ra...]
    ppermute x0 -> x30, waiting for transfers between devices: none -> 31.3 us  [the longest x7 13.7 us: flip_x(): return lax.ppermute(value, 'row', [(r, r ^ 1) for r in range(rows_total)])]
    all_gather x1 -> x0, waiting for transfers between devices: 23.4 us -> none  [on_device(): target_rows = lax.all_gather(dest_grad[0], 'row', axis=0, tiled=True)]
    dot_general x3 -> x0, matrix products: 15.6 us -> none  [the longest x2 8.9 us: on_device(): lax.dot_general(grad_block, bases, (((1,), (2,)), ((), ())), preferred_el...]
    gather x5 -> x0, local copies, waits for them, and re-layouts: 12.3 us -> none  [the longest x1 4.82 us: on_device(): target_rows[targets].astype(jnp.float32)]
  transfers between devices with their start and end apart: 4 -> 30, of which waited for: 4 -> 13; matrix products, arithmetic and copies ran while one was open for 10% -> 10% of each run, Pallas kernels for 0% -> 34%
where the time goes in v1:
time: 128 us; the launch traced here: 127 us
  Pallas kernels  42.7 us (33%)
  starting transfers between devices  34.8 us (27%)
  waiting for transfers between devices  31.3 us (24%)
  local copies, waits for them, and re-layouts  8.82 us (7%)
  other arithmetic  8.49 us (7%)
    ppermute x9, starting transfers between devices, turn_z(): lax.ppermute(value, 'row', [(r, (r + by * PAIR) % rows_total) for r in ra...  14.9 us
    ppermute x7, waiting for transfers between devices, flip_x(): return lax.ppermute(value, 'row', [(r, r ^ 1) for r in range(rows_total)])  13.7 us
    pallas_call x1, Pallas kernels, on_device(): pl.pallas_call(functools.partial(forward_kernel, (cols, shard, span, head...  12.8 us
    pallas_call x1, Pallas kernels, on_device(): call(functools.partial(basis_kernel, (rows_total, cols, block, cover // T...  11.6 us
    pallas_call x1, Pallas kernels, on_device(): call(functools.partial(source_kernel, (cols, shard, span, heads, padded))...  9.58 us
    ppermute x7, starting transfers between devices, flip_x(): return lax.ppermute(value, 'row', [(r, r ^ 1) for r in range(rows_total)])  8.68 us
    ppermute x5, waiting for transfers between devices, turn_y(): lax.ppermute(value, 'col', [(c, (c + by * PAIR) % cols) for c in range(co...  8.05 us
    ppermute x3, waiting for transfers between devices, on_device(): lax.ppermute(packed[far * y_count + sy], 'col', target).astype(F32)  7.51 us
  transfers between devices with their start and end apart: 30, of which 13 were waited for; matrix products, arithmetic and copies ran while one was open for 10% of the time, Pallas kernels for 34%

profile of v1, /device:TPU:0, one launch (start us, length us, event | category | flops | bytes accessed | tf_op | source)
XLA Modules:
  0.0 127.0 jit_solution(401401130168029660)
XLA Ops:
  0.6 5.1 %collective-permute-start.3 = (bf16[256,256]{1,0:T(8,128)(2,1)}, bf16[256,256]{1,0:T(8,128)(2,1)S(1)}, u32[]{:S(2)}, u32[]{:S(2)}) collective-permute-start(bf16[256,256]{1,0:T(8,128)(2,1)} %bitcast.73), channel_id=1, source_target_pairs={{0,24},{4,28},{8,0},{12,4},{16,8},{20,12},{24,16},{28,20},{1,25},{... | collective-permute-start | bytes 393224 | tf_op jit(solution)/shard_map/ppermute | solution.py:300
  5.7 1.0 collective-permute-start.1
  6.7 1.5 %collective-permute-start.9 = (bf16[256,256]{1,0:T(8,128)(2,1)}, bf16[256,256]{1,0:T(8,128)(2,1)S(1)}, u32[]{:S(2)}, u32[]{:S(2)}) collective-permute-start(bf16[256,256]{1,0:T(8,128)(2,1)} %param.9), channel_id=1, source_target_pairs={{0,4},{4,0},{8,12},{12,8},{16,20},{20,16},{24,28},{28,24},{1,5},{5... | collective-permute-start | bytes 393224 | tf_op jit(solution)/shard_map/ppermute | solution.py:294
  8.2 0.7 fusion.10
  9.0 0.7 convert_bitcast_fusion
  9.7 0.7 bitcast_select_fusion
  10.4 1.6 %collective-permute-done.9 = bf16[256,256]{1,0:T(8,128)(2,1)S(1)} collective-permute-done((bf16[256,256]{1,0:T(8,128)(2,1)}, bf16[256,256]{1,0:T(8,128)(2,1)S(1)}, u32[]{:S(2)}, u32[]{:S(2)}) %collective-permute-start.9) | collective-permute-done | bytes 131104 | tf_op jit(solution)/shard_map/ppermute | solution.py:294
  11.9 0.9 fusion.12
  12.9 1.6 %collective-permute-start.10 = (bf16[2,256,256]{2,1,0:T(8,128)(2,1)S(1)}, bf16[2,256,256]{2,1,0:T(8,128)(2,1)S(1)}, u32[]{:S(2)}, u32[]{:S(2)}) collective-permute-start(bf16[2,256,256]{2,1,0:T(8,128)(2,1)S(1)} %get-tuple-element.27), channel_id=1, source_target_pairs={{0,2},{1,3},{2,0},{3,1},{4,6},{5,7},{6,4},{7,5},{8,10},{9,11},{10,... | collective-permute-start | bytes 786440 | tf_op jit(solution)/shard_map/ppermute | solution.py:305
  14.5 0.7 convert_bitcast_fusion.2
  15.2 1.6 %collective-permute-start = (f32[4,1024]{1,0:T(4,128)S(1)}, f32[4,1024]{1,0:T(4,128)S(1)}, u32[]{:S(2)}, u32[]{:S(2)}) collective-permute-start(f32[4,1024]{1,0:T(4,128)S(1)} %get-tuple-element.29), channel_id=1, source_target_pairs={{0,4},{4,0},{8,12},{12,8},{16,20},{20,16},{24,28},{28,24},{1,5},{5... | collective-permute-start | bytes 49160 | tf_op jit(solution)/shard_map/ppermute | solution.py:294
  16.7 2.6 %collective-permute-done.10 = bf16[2,256,256]{2,1,0:T(8,128)(2,1)S(1)} collective-permute-done((bf16[2,256,256]{2,1,0:T(8,128)(2,1)S(1)}, bf16[2,256,256]{2,1,0:T(8,128)(2,1)S(1)}, u32[]{:S(2)}, u32[]{:S(2)}) %collective-permute-start.10) | collective-permute-done | bytes 262176 | tf_op jit(solution)/shard_map/ppermute | solution.py:305
  19.4 1.7 %copy_bitcast_fusion = bf16[16,128,32]{1,2,0:T(8,128)(2,1)} fusion(bf16[2000,30]{0,1:T(8,128)(2,1)} %param.12), kind=kLoop, calls=%fused_computation.21 | loop fusion | bytes 251072 | tf_op jit(solution)/shard_map/reshape | solution.py:331
  21.2 1.5 %collective-permute-start.4 = (bf16[256,256]{1,0:T(8,128)(2,1)}, bf16[256,256]{1,0:T(8,128)(2,1)S(1)}, u32[]{:S(2)}, u32[]{:S(2)}) collective-permute-start(bf16[256,256]{1,0:T(8,128)(2,1)} %bitcast.76), channel_id=1, source_target_pairs={{0,4},{4,0},{8,12},{12,8},{16,20},{20,16},{24,28},{28,24},{1,5},{5... | collective-permute-start | bytes 393224 | tf_op jit(solution)/shard_map/ppermute | solution.py:294
  23.2 1.5 %collective-permute-start.6 = (bf16[256,256]{1,0:T(8,128)(2,1)S(1)}, bf16[256,256]{1,0:T(8,128)(2,1)S(1)}, u32[]{:S(2)}, u32[]{:S(2)}) collective-permute-start(bf16[256,256]{1,0:T(8,128)(2,1)S(1)} %collective-permute-done.2.refs_2_), channel_id=1, source_target_pairs={{0,4},{4,0},{8,12},{12,8},{16,20},{20,16},{24,28},{28,24},{1,5},{5... | collective-permute-start | bytes 393224 | tf_op jit(solution)/shard_map/ppermute | solution.py:294
  25.9 1.8 %collective-permute-done.4.refs_4_ = bf16[256,256]{1,0:T(8,128)(2,1)S(1)} collective-permute-done((bf16[256,256]{1,0:T(8,128)(2,1)}, bf16[256,256]{1,0:T(8,128)(2,1)S(1)}, u32[]{:S(2)}, u32[]{:S(2)}) %collective-permute-start.4) | collective-permute-done | bytes 131104 | tf_op jit(solution)/shard_map/ppermute | solution.py:294
  27.7 2.8 %collective-permute-done.7.refs_7_ = bf16[256,256]{1,0:T(8,128)(2,1)S(1)} collective-permute-done((bf16[256,256]{1,0:T(8,128)(2,1)S(1)}, bf16[256,256]{1,0:T(8,128)(2,1)S(1)}, u32[]{:S(2)}, u32[]{:S(2)}) %collective-permute-start.7) | collective-permute-done | bytes 131104 | tf_op jit(solution)/shard_map/ppermute | solution.py:294
  30.5 2.8 %collective-permute-done.6.refs_6_ = bf16[256,256]{1,0:T(8,128)(2,1)S(1)} collective-permute-done((bf16[256,256]{1,0:T(8,128)(2,1)S(1)}, bf16[256,256]{1,0:T(8,128)(2,1)S(1)}, u32[]{:S(2)}, u32[]{:S(2)}) %collective-permute-start.6) | collective-permute-done | bytes 131104 | tf_op jit(solution)/shard_map/ppermute | solution.py:294
  33.3 2.3 %collective-permute-done.5.refs_5_ = bf16[256,256]{1,0:T(8,128)(2,1)S(1)} collective-permute-done((bf16[256,256]{1,0:T(8,128)(2,1)S(1)}, bf16[256,256]{1,0:T(8,128)(2,1)S(1)}, u32[]{:S(2)}, u32[]{:S(2)}) %collective-permute-start.5) | collective-permute-done | bytes 131104 | tf_op jit(solution)/shard_map/ppermute | solution.py:294
  36.3 6.5 %edge_grads.1.gt_ref = bf16[256,2048]{1,0:T(8,128)(2,1)} custom-call(s32[4]{0:T(128)} %pad_add_fusion.place, f32[2,4,1024]{2,1,0:T(4,128)} %copy-done.5, bf16[256,256]{1,0:T(8,128)(2,1)} %bitcast.77, bf16[256,256]{1,0:T(8,128)(2,1)} %copy-done.10, bf16[256,256]{1,0:T(8,128)(2,1)} %copy-done.9, bf16[256,256]{1,0:T(8,128)(2,1)} %copy-done.8, ...), custom_call_target="tpu_custom_call" | custom-call | flops 2147483648 | bytes 4194304 | tf_op jit(solution)/shard_map/edge_grads/pallas_call | solution.py:346
  43.6 9.6 %source_rows.1 = (bf16[4,256,1024]{2,1,0:T(8,128)(2,1)}, f32[4,32,1024]{2,1,0:T(8,128)}) custom-call(s32[4]{0:T(128)} %pad_add_fusion.place, f32[2,4,1024]{2,1,0:T(4,128)} %copy-done.5, f32[2,4,1024]{2,1,0:T(4,128)} %copy-done.15, bf16[2,2,256,256]{3,2,1,0:T(8,128)(2,1)} %copy-done, bf16[2,2,256,256]{3,2,1,0:T(8,128)(2,1)} %copy-done.7, ...), custom_call_target="tpu_custom_call" | custom-call | flops 2147483648 | bytes 4194304 | tf_op jit(solution)/shard_map/source_rows/pallas_call | solution.py:333
  53.2 12.8 %backed_sums.1 = bf16[4,320,256]{2,1,0:T(8,128)(2,1)} custom-call(s32[4]{0:T(128)} %pad_add_fusion.place, f32[2,4,1024]{2,1,0:T(4,128)} %copy-done.5, bf16[256,2048]{1,0:T(8,128)(2,1)} %edge_grads.1.gt_ref, bf16[4,256,1024]{2,1,0:T(8,128)(2,1)} %get-tuple-element.10.xt_ref, f32[4,32,1024]{2,1,0:T(8,128)} %get-tuple-element.11.ct_ref, ...), custom_call_target="tpu_custom_call" | custom-call | flops 4026531840 | bytes 3932160 | tf_op jit(solution)/shard_map/backed_sums/pallas_call | solution.py:358
  66.0 1.1 slice_bitcast_fusion.2
  67.1 1.6 %collective-permute-start.12 = (bf16[320,256]{1,0:T(8,128)(2,1)S(1)}, bf16[320,256]{1,0:T(8,128)(2,1)S(1)}, u32[]{:S(2)}, u32[]{:S(2)}) collective-permute-start(bf16[320,256]{1,0:T(8,128)(2,1)S(1)} %get-tuple-element.23), channel_id=1, source_target_pairs={{0,2},{1,3},{2,0},{3,1},{4,6},{5,7},{6,4},{7,5},{8,10},{9,11},{10,... | collective-permute-start | bytes 491528 | tf_op jit(solution)/shard_map/ppermute | solution.py:434
  69.3 4.9 %collective-permute-done.12 = bf16[320,256]{1,0:T(8,128)(2,1)S(1)} collective-permute-done((bf16[320,256]{1,0:T(8,128)(2,1)S(1)}, bf16[320,256]{1,0:T(8,128)(2,1)S(1)}, u32[]{:S(2)}, u32[]{:S(2)}) %collective-permute-start.12) | collective-permute-done | bytes 163872 | tf_op jit(solution)/shard_map/ppermute | solution.py:434
  74.2 2.6 %collective-permute-done.14 = bf16[320,256]{1,0:T(8,128)(2,1)S(1)} collective-permute-done((bf16[320,256]{1,0:T(8,128)(2,1)S(1)}, bf16[320,256]{1,0:T(8,128)(2,1)S(1)}, u32[]{:S(2)}, u32[]{:S(2)}) %collective-permute-start.14) | collective-permute-done | bytes 163872 | tf_op jit(solution)/shard_map/ppermute | solution.py:434
  76.8 1.0 fusion.2
  77.8 1.6 %collective-permute-start.23 = (bf16[64,256]{1,0:T(8,128)(2,1)S(1)}, bf16[64,256]{1,0:T(8,128)(2,1)S(1)}, u32[]{:S(2)}, u32[]{:S(2)}) collective-permute-start(bf16[64,256]{1,0:T(8,128)(2,1)S(1)} %slice.47), channel_id=1, source_target_pairs={{0,4},{4,0},{8,12},{12,8},{16,20},{20,16},{24,28},{28,24},{1,5},{5... | collective-permute-start | bytes 98312 | tf_op jit(solution)/shard_map/ppermute | solution.py:294
  79.4 2.4 %collective-permute-done.23 = bf16[64,256]{1,0:T(8,128)(2,1)S(1)} collective-permute-done((bf16[64,256]{1,0:T(8,128)(2,1)S(1)}, bf16[64,256]{1,0:T(8,128)(2,1)S(1)}, u32[]{:S(2)}, u32[]{:S(2)}) %collective-permute-start.23) | collective-permute-done | bytes 32800 | tf_op jit(solution)/shard_map/ppermute | solution.py:294
  81.8 3.1 %collective-permute-start.26 = (bf16[64,256]{1,0:T(8,128)(2,1)S(1)}, bf16[64,256]{1,0:T(8,128)(2,1)S(1)}, u32[]{:S(2)}, u32[]{:S(2)}) collective-permute-start(bf16[64,256]{1,0:T(8,128)(2,1)S(1)} %add_convert_fusion), channel_id=1, source_target_pairs={{0,24},{4,28},{8,0},{12,4},{16,8},{20,12},{24,16},{28,20},{1,25},{... | collective-permute-start | bytes 98312 | tf_op jit(solution)/shard_map/ppermute | solution.py:300
  85.0 0.9 collective-permute-start.24
  85.8 1.0 copy-done.6
  86.8 11.6 %basis_terms.1 = (f32[4,240,256]{2,1,0:T(8,128)}, bf16[240,256]{1,0:T(8,128)(2,1)}, bf16[240,256]{1,0:T(8,128)(2,1)}, bf16[240,256]{1,0:T(8,128)(2,1)}, bf16[240,256]{1,0:T(8,128)(2,1)}) custom-call(s32[4]{0:T(128)} %pad_add_fusion.place, bf16[256,2048]{1,0:T(8,128)(2,1)} %edge_grads.1.gt_ref, bf16[256,2048]{1,0:T(8,128)(2,1)} %copy-done.6, ...), custom_call_target="tpu_custom_call" | custom-call | flops 4026531840 | bytes 4194304 | tf_op jit(solution)/shard_map/basis_terms/pallas_call | solution.py:388
  98.4 1.5 %collective-permute-start.17 = (bf16[240,256]{1,0:T(8,128)(2,1)}, bf16[240,256]{1,0:T(8,128)(2,1)S(1)}, u32[]{:S(2)}, u32[]{:S(2)}) collective-permute-start(bf16[240,256]{1,0:T(8,128)(2,1)} %get-tuple-element.14), channel_id=1, source_target_pairs={{0,2},{1,3},{2,0},{3,1},{4,6},{5,7},{6,4},{7,5},{8,10},{9,11},{10,... | collective-permute-start | bytes 368648 | tf_op jit(solution)/shard_map/ppermute | solution.py:305
  100.4 1.5 %collective-permute-start.21 = (bf16[240,256]{1,0:T(8,128)(2,1)}, bf16[240,256]{1,0:T(8,128)(2,1)S(1)}, u32[]{:S(2)}, u32[]{:S(2)}) collective-permute-start(bf16[240,256]{1,0:T(8,128)(2,1)} %get-tuple-element.16), channel_id=1, source_target_pairs={{0,2},{1,3},{2,0},{3,1},{4,6},{5,7},{6,4},{7,5},{8,10},{9,11},{10,... | collective-permute-start | bytes 368648 | tf_op jit(solution)/shard_map/ppermute | solution.py:305
  102.7 2.2 %collective-permute-done.17 = bf16[240,256]{1,0:T(8,128)(2,1)S(1)} collective-permute-done((bf16[240,256]{1,0:T(8,128)(2,1)}, bf16[240,256]{1,0:T(8,128)(2,1)S(1)}, u32[]{:S(2)}, u32[]{:S(2)}) %collective-permute-start.17) | collective-permute-done | bytes 122912 | tf_op jit(solution)/shard_map/ppermute | solution.py:305
  104.9 1.5 %collective-permute-start.16 = (bf16[240,256]{1,0:T(8,128)(2,1)}, bf16[240,256]{1,0:T(8,128)(2,1)S(1)}, u32[]{:S(2)}, u32[]{:S(2)}) collective-permute-start(bf16[240,256]{1,0:T(8,128)(2,1)} %get-tuple-element.13), channel_id=1, source_target_pairs={{0,2},{1,3},{2,0},{3,1},{4,6},{5,7},{6,4},{7,5},{8,10},{9,11},{10,... | collective-permute-start | bytes 368648 | tf_op jit(solution)/shard_map/ppermute | solution.py:305
  106.4 1.1 collective-permute-done.19
  107.5 2.2 %collective-permute-done.21 = bf16[240,256]{1,0:T(8,128)(2,1)S(1)} collective-permute-done((bf16[240,256]{1,0:T(8,128)(2,1)}, bf16[240,256]{1,0:T(8,128)(2,1)S(1)}, u32[]{:S(2)}, u32[]{:S(2)}) %collective-permute-start.21) | collective-permute-done | bytes 122912 | tf_op jit(solution)/shard_map/ppermute | solution.py:305
  109.7 1.3 %fusion.5 = (bf16[240,256]{1,0:T(8,128)(2,1)S(1)}, bf16[240,256]{1,0:T(8,128)(2,1)S(1)}, bf16[240,256]{1,0:T(8,128)(2,1)S(1)}) fusion(bf16[240,256]{1,0:T(8,128)(2,1)S(1)} %collective-permute-done.17, f32[4,240,256]{2,1,0:T(8,128)} %get-tuple-element.12, bf16[240,256]{1,0:T(8,128)(2,1)S(1)} %collective-permute-done.21, ...), kind=kLoop, calls=%fused_computation.11 | loop fusion | flops 552960 | bytes 1474560 | tf_op jit(solution)/shard_map/convert_element_type | solution.py:417
  110.9 3.3 %collective-permute-start.18 = (bf16[240,256]{1,0:T(8,128)(2,1)S(1)}, bf16[240,256]{1,0:T(8,128)(2,1)S(1)}, u32[]{:S(2)}, u32[]{:S(2)}) collective-permute-start(bf16[240,256]{1,0:T(8,128)(2,1)S(1)} %get-tuple-element.20), channel_id=1, source_target_pairs={{0,8},{4,12},{8,16},{12,20},{16,24},{20,28},{24,0},{28,4},{1,9},{5... | collective-permute-start | bytes 368648 | tf_op jit(solution)/shard_map/ppermute | solution.py:300
  114.8 0.9 collective-permute-start.20
  115.8 1.5 %collective-permute-start.27 = (f32[64,256]{1,0:T(8,128)S(1)}, f32[64,256]{1,0:T(8,128)S(1)}, u32[]{:S(2)}, u32[]{:S(2)}) collective-permute-start(f32[64,256]{1,0:T(8,128)S(1)} %add_add_fusion.refs_0_), channel_id=1, source_target_pairs={{0,2},{1,3},{2,0},{3,1},{4,6},{5,7},{6,4},{7,5},{8,10},{9,11},{10,... | collective-permute-start | bytes 196616 | tf_op jit(solution)/shard_map/ppermute | solution.py:448
  117.3 0.7 slice.46
  118.0 2.1 %collective-permute-done.27.refs_1_ = f32[64,256]{1,0:T(8,128)S(1)} collective-permute-done((f32[64,256]{1,0:T(8,128)S(1)}, f32[64,256]{1,0:T(8,128)S(1)}, u32[]{:S(2)}, u32[]{:S(2)}) %collective-permute-start.27) | collective-permute-done | bytes 65568 | tf_op jit(solution)/shard_map/ppermute | solution.py:448
  120.7 2.3 %coef_rows.1 = f32[2000,30]{1,0:T(8,128)} custom-call(s32[4]{0:T(128)} %pad_add_fusion.place, f32[64,256]{1,0:T(8,128)} %copy-done.1, f32[64,256]{1,0:T(8,128)} %copy-done.4, f32[64,256]{1,0:T(8,128)} %copy-done.3, f32[64,256]{1,0:T(8,128)} %copy-done.2), custom_call_target="tpu_custom_call" | custom-call | flops 1048576 | bytes 4194304 | tf_op jit(solution)/shard_map/coef_rows/pallas_call | solution.py:449
  123.0 2.2 %copy.13 = f32[2000,30]{0,1:T(8,128)} copy(f32[2000,30]{1,0:T(8,128)} %coef_rows.1) | data formatting | bytes 480000
  125.2 1.7 %fusion.9 = f32[240,256]{1,0:T(8,128)} fusion(bf16[240,256]{1,0:T(8,128)(2,1)S(1)} %collective-permute-done.22, bf16[240,256]{1,0:T(8,128)(2,1)S(1)} %collective-permute-done.20, bf16[240,256]{1,0:T(8,128)(2,1)S(1)} %collective-permute-done.18, bf16[240,256]{1,0:T(8,128)(2,1)S(1)} %collective-permute-done.16, f32[4,240,256]{2,1,0:T(8,128)} %get-tuple-element.12), kind=kLoop, calls=%fused_computation.16 | loop fusion | flops 552960 | bytes 983040 | tf_op jit(solution)/shard_map/div | solution.py:425
  (68 shorter events, 6.4 us)
Async XLA Ops:
  0.6 22.0 %collective-permute-start.3 = (bf16[256,256]{1,0:T(8,128)(2,1)}, bf16[256,256]{1,0:T(8,128)(2,1)S(1)}, u32[]{:S(2)}, u32[]{:S(2)}) collective-permute-start(bf16[256,256]{1,0:T(8,128)(2,1)} %bitcast.73), channel_id=1, source_target_pairs={{0,24},{4,28},{8,0},{12,4},{16,8},{20,12},{24,16},{28,20},{1,25},{... | collective-permute-start | bytes 393224 | tf_op jit(solution)/shard_map/ppermute | solution.py:300
  5.7 17.5 %collective-permute-start.2 = (bf16[256,256]{1,0:T(8,128)(2,1)}, bf16[256,256]{1,0:T(8,128)(2,1)S(1)}, u32[]{:S(2)}, u32[]{:S(2)}) collective-permute-start(bf16[256,256]{1,0:T(8,128)(2,1)} %bitcast.74), channel_id=1, source_target_pairs={{0,16},{4,20},{8,24},{12,28},{16,0},{20,4},{24,8},{28,12},{1,17},{... | collective-permute-start | bytes 393224 | tf_op jit(solution)/shard_map/ppermute | solution.py:300
  5.7 19.0 %collective-permute-start.1 = (bf16[256,256]{1,0:T(8,128)(2,1)}, bf16[256,256]{1,0:T(8,128)(2,1)S(1)}, u32[]{:S(2)}, u32[]{:S(2)}) collective-permute-start(bf16[256,256]{1,0:T(8,128)(2,1)} %bitcast.75), channel_id=1, source_target_pairs={{0,8},{4,12},{8,16},{12,20},{16,24},{20,28},{24,0},{28,4},{1,9},{5... | collective-permute-start | bytes 393224 | tf_op jit(solution)/shard_map/ppermute | solution.py:300
  6.7 5.2 %collective-permute-start.9 = (bf16[256,256]{1,0:T(8,128)(2,1)}, bf16[256,256]{1,0:T(8,128)(2,1)S(1)}, u32[]{:S(2)}, u32[]{:S(2)}) collective-permute-start(bf16[256,256]{1,0:T(8,128)(2,1)} %param.9), channel_id=1, source_target_pairs={{0,4},{4,0},{8,12},{12,8},{16,20},{20,16},{24,28},{28,24},{1,5},{5... | collective-permute-start | bytes 393224 | tf_op jit(solution)/shard_map/ppermute | solution.py:294
  12.9 6.4 %collective-permute-start.10 = (bf16[2,256,256]{2,1,0:T(8,128)(2,1)S(1)}, bf16[2,256,256]{2,1,0:T(8,128)(2,1)S(1)}, u32[]{:S(2)}, u32[]{:S(2)}) collective-permute-start(bf16[2,256,256]{2,1,0:T(8,128)(2,1)S(1)} %get-tuple-element.27), channel_id=1, source_target_pairs={{0,2},{1,3},{2,0},{3,1},{4,6},{5,7},{6,4},{7,5},{8,10},{9,11},{10,... | collective-permute-start | bytes 786440 | tf_op jit(solution)/shard_map/ppermute | solution.py:305
  15.2 6.0 %collective-permute-start = (f32[4,1024]{1,0:T(4,128)S(1)}, f32[4,1024]{1,0:T(4,128)S(1)}, u32[]{:S(2)}, u32[]{:S(2)}) collective-permute-start(f32[4,1024]{1,0:T(4,128)S(1)} %get-tuple-element.29), channel_id=1, source_target_pairs={{0,4},{4,0},{8,12},{12,8},{16,20},{20,16},{24,28},{28,24},{1,5},{5... | collective-permute-start | bytes 49160 | tf_op jit(solution)/shard_map/ppermute | solution.py:294
  19.4 23.4 %copy-start = (bf16[2,2,256,256]{3,2,1,0:T(8,128)(2,1)}, bf16[2,2,256,256]{3,2,1,0:T(8,128)(2,1)S(1)}, u32[]{:S(2)}) copy-start(bf16[2,2,256,256]{3,2,1,0:T(8,128)(2,1)S(1)} %pad_maximum_fusion.feats) | copy-start | bytes 1572868
  19.4 23.4 %collective-permute-start.11 = (bf16[2,2,256,256]{3,2,1,0:T(8,128)(2,1)S(1)}, bf16[2,2,256,256]{3,2,1,0:T(8,128)(2,1)S(1)}, u32[]{:S(2)}, u32[]{:S(2)}) collective-permute-start(bf16[2,2,256,256]{3,2,1,0:T(8,128)(2,1)S(1)} %pad_maximum_fusion.feats), channel_id=1, source_target_pairs={{0,1},{1,0},{2,3},{3,2},{4,5},{5,4},{6,7},{7,6},{8,9},{9,8},{10,11... | collective-permute-start | bytes 1572872 | tf_op jit(solution)/shard_map/ppermute | solution.py:297
  21.2 6.5 %collective-permute-start.4 = (bf16[256,256]{1,0:T(8,128)(2,1)}, bf16[256,256]{1,0:T(8,128)(2,1)S(1)}, u32[]{:S(2)}, u32[]{:S(2)}) collective-permute-start(bf16[256,256]{1,0:T(8,128)(2,1)} %bitcast.76), channel_id=1, source_target_pairs={{0,4},{4,0},{8,12},{12,8},{16,20},{20,16},{24,28},{28,24},{1,5},{5... | collective-permute-start | bytes 393224 | tf_op jit(solution)/shard_map/ppermute | solution.py:294
  22.7 12.9 %copy-start.8 = (bf16[256,256]{1,0:T(8,128)(2,1)}, bf16[256,256]{1,0:T(8,128)(2,1)S(1)}, u32[]{:S(2)}) copy-start(bf16[256,256]{1,0:T(8,128)(2,1)S(1)} %collective-permute-done.3.refs_3_) | copy-start | bytes 393220
  22.7 7.8 %collective-permute-start.7 = (bf16[256,256]{1,0:T(8,128)(2,1)S(1)}, bf16[256,256]{1,0:T(8,128)(2,1)S(1)}, u32[]{:S(2)}, u32[]{:S(2)}) collective-permute-start(bf16[256,256]{1,0:T(8,128)(2,1)S(1)} %collective-permute-done.3.refs_3_), channel_id=1, source_target_pairs={{0,4},{4,0},{8,12},{12,8},{16,20},{20,16},{24,28},{28,24},{1,5},{5... | collective-permute-start | bytes 393224 | tf_op jit(solution)/shard_map/ppermute | solution.py:294
  23.2 12.4 %copy-start.9 = (bf16[256,256]{1,0:T(8,128)(2,1)}, bf16[256,256]{1,0:T(8,128)(2,1)S(1)}, u32[]{:S(2)}) copy-start(bf16[256,256]{1,0:T(8,128)(2,1)S(1)} %collective-permute-done.2.refs_2_) | copy-start | bytes 393220
  23.2 10.1 %collective-permute-start.6 = (bf16[256,256]{1,0:T(8,128)(2,1)S(1)}, bf16[256,256]{1,0:T(8,128)(2,1)S(1)}, u32[]{:S(2)}, u32[]{:S(2)}) collective-permute-start(bf16[256,256]{1,0:T(8,128)(2,1)S(1)} %collective-permute-done.2.refs_2_), channel_id=1, source_target_pairs={{0,4},{4,0},{8,12},{12,8},{16,20},{20,16},{24,28},{28,24},{1,5},{5... | collective-permute-start | bytes 393224 | tf_op jit(solution)/shard_map/ppermute | solution.py:294
  24.7 10.9 %copy-start.10 = (bf16[256,256]{1,0:T(8,128)(2,1)}, bf16[256,256]{1,0:T(8,128)(2,1)S(1)}, u32[]{:S(2)}) copy-start(bf16[256,256]{1,0:T(8,128)(2,1)S(1)} %collective-permute-done.1.refs_1_) | copy-start | bytes 393220
  24.7 10.9 %collective-permute-start.5 = (bf16[256,256]{1,0:T(8,128)(2,1)S(1)}, bf16[256,256]{1,0:T(8,128)(2,1)S(1)}, u32[]{:S(2)}, u32[]{:S(2)}) collective-permute-start(bf16[256,256]{1,0:T(8,128)(2,1)S(1)} %collective-permute-done.1.refs_1_), channel_id=1, source_target_pairs={{0,4},{4,0},{8,12},{12,8},{16,20},{20,16},{24,28},{28,24},{1,5},{5... | collective-permute-start | bytes 393224 | tf_op jit(solution)/shard_map/ppermute | solution.py:294
  25.9 9.7 %copy-start.5 = (f32[2,4,1024]{2,1,0:T(4,128)}, f32[2,4,1024]{2,1,0:T(4,128)S(1)}, u32[]{:S(2)}) copy-start(f32[2,4,1024]{2,1,0:T(4,128)S(1)} %pad_maximum_fusion.2.meta) | copy-start | bytes 98308
  27.7 7.9 %copy-start.11 = (bf16[256,256]{1,0:T(8,128)(2,1)}, bf16[256,256]{1,0:T(8,128)(2,1)S(1)}, u32[]{:S(2)}) copy-start(bf16[256,256]{1,0:T(8,128)(2,1)S(1)} %collective-permute-done.4.refs_4_) | copy-start | bytes 393220
  27.7 15.0 %collective-permute-start.8 = (f32[2,4,1024]{2,1,0:T(4,128)S(1)}, f32[2,4,1024]{2,1,0:T(4,128)S(1)}, u32[]{:S(2)}, u32[]{:S(2)}) collective-permute-start(f32[2,4,1024]{2,1,0:T(4,128)S(1)} %pad_maximum_fusion.2.meta), channel_id=1, source_target_pairs={{0,1},{1,0},{2,3},{3,2},{4,5},{5,4},{6,7},{7,6},{8,9},{9,8},{10,11... | collective-permute-start | bytes 98312 | tf_op jit(solution)/shard_map/ppermute | solution.py:297
  30.5 5.1 %copy-start.12 = (bf16[256,256]{1,0:T(8,128)(2,1)}, bf16[256,256]{1,0:T(8,128)(2,1)S(1)}, u32[]{:S(2)}) copy-start(bf16[256,256]{1,0:T(8,128)(2,1)S(1)} %collective-permute-done.7.refs_7_) | copy-start | bytes 393220
  33.3 2.3 %copy-start.13 = (bf16[256,256]{1,0:T(8,128)(2,1)}, bf16[256,256]{1,0:T(8,128)(2,1)S(1)}, u32[]{:S(2)}) copy-start(bf16[256,256]{1,0:T(8,128)(2,1)S(1)} %collective-permute-done.6.refs_6_) | copy-start | bytes 393220
  35.6 0.7 copy-start.14
  42.8 43.1 %collective-permute-start.15 = (bf16[256,2048]{1,0:T(8,128)(2,1)}, bf16[256,2048]{1,0:T(8,128)(2,1)S(1)}, u32[]{:S(2)}, u32[]{:S(2)}) collective-permute-start(bf16[256,2048]{1,0:T(8,128)(2,1)} %edge_grads.1.gt_ref), channel_id=1, source_target_pairs={{0,1},{1,0},{2,3},{3,2},{4,5},{5,4},{6,7},{7,6},{8,9},{9,8},{10,11... | collective-permute-start | bytes 3145736 | tf_op jit(solution)/shard_map/ppermute | solution.py:297
  42.8 0.6 copy-start.15
  42.8 0.8 copy-start.7
  67.1 7.1 %collective-permute-start.12 = (bf16[320,256]{1,0:T(8,128)(2,1)S(1)}, bf16[320,256]{1,0:T(8,128)(2,1)S(1)}, u32[]{:S(2)}, u32[]{:S(2)}) collective-permute-start(bf16[320,256]{1,0:T(8,128)(2,1)S(1)} %get-tuple-element.23), channel_id=1, source_target_pairs={{0,2},{1,3},{2,0},{3,1},{4,6},{5,7},{6,4},{7,5},{8,10},{9,11},{10,... | collective-permute-start | bytes 491528 | tf_op jit(solution)/shard_map/ppermute | solution.py:434
  68.7 8.1 %collective-permute-start.14 = (bf16[320,256]{1,0:T(8,128)(2,1)S(1)}, bf16[320,256]{1,0:T(8,128)(2,1)S(1)}, u32[]{:S(2)}, u32[]{:S(2)}) collective-permute-start(bf16[320,256]{1,0:T(8,128)(2,1)S(1)} %get-tuple-element.24), channel_id=1, source_target_pairs={{0,3},{1,2},{2,1},{3,0},{4,7},{5,6},{6,5},{7,4},{8,11},{9,10},{10,... | collective-permute-start | bytes 491528 | tf_op jit(solution)/shard_map/ppermute | solution.py:434
  69.0 7.8 %collective-permute-start.13 = (bf16[320,256]{1,0:T(8,128)(2,1)S(1)}, bf16[320,256]{1,0:T(8,128)(2,1)S(1)}, u32[]{:S(2)}, u32[]{:S(2)}) collective-permute-start(bf16[320,256]{1,0:T(8,128)(2,1)S(1)} %get-tuple-element.25), channel_id=1, source_target_pairs={{0,1},{1,0},{2,3},{3,2},{4,5},{5,4},{6,7},{7,6},{8,9},{9,8},{10,11... | collective-permute-start | bytes 491528 | tf_op jit(solution)/shard_map/ppermute | solution.py:434
  77.8 4.0 %collective-permute-start.23 = (bf16[64,256]{1,0:T(8,128)(2,1)S(1)}, bf16[64,256]{1,0:T(8,128)(2,1)S(1)}, u32[]{:S(2)}, u32[]{:S(2)}) collective-permute-start(bf16[64,256]{1,0:T(8,128)(2,1)S(1)} %slice.47), channel_id=1, source_target_pairs={{0,4},{4,0},{8,12},{12,8},{16,20},{20,16},{24,28},{28,24},{1,5},{5... | collective-permute-start | bytes 98312 | tf_op jit(solution)/shard_map/ppermute | solution.py:294
  81.8 18.6 %collective-permute-start.26 = (bf16[64,256]{1,0:T(8,128)(2,1)S(1)}, bf16[64,256]{1,0:T(8,128)(2,1)S(1)}, u32[]{:S(2)}, u32[]{:S(2)}) collective-permute-start(bf16[64,256]{1,0:T(8,128)(2,1)S(1)} %add_convert_fusion), channel_id=1, source_target_pairs={{0,24},{4,28},{8,0},{12,4},{16,8},{20,12},{24,16},{28,20},{1,25},{... | collective-permute-start | bytes 98312 | tf_op jit(solution)/shard_map/ppermute | solution.py:300
  85.0 17.0 %collective-permute-start.25 = (bf16[64,256]{1,0:T(8,128)(2,1)S(1)}, bf16[64,256]{1,0:T(8,128)(2,1)S(1)}, u32[]{:S(2)}, u32[]{:S(2)}) collective-permute-start(bf16[64,256]{1,0:T(8,128)(2,1)S(1)} %add_convert_fusion), channel_id=1, source_target_pairs={{0,8},{4,12},{8,16},{12,20},{16,24},{20,28},{24,0},{28,4},{1,9},{5... | collective-permute-start | bytes 98312 | tf_op jit(solution)/shard_map/ppermute | solution.py:300
  85.0 17.0 %collective-permute-start.24 = (bf16[64,256]{1,0:T(8,128)(2,1)S(1)}, bf16[64,256]{1,0:T(8,128)(2,1)S(1)}, u32[]{:S(2)}, u32[]{:S(2)}) collective-permute-start(bf16[64,256]{1,0:T(8,128)(2,1)S(1)} %add_convert_fusion), channel_id=1, source_target_pairs={{0,16},{4,20},{8,24},{12,28},{16,0},{20,4},{24,8},{28,12},{1,17},{... | collective-permute-start | bytes 98312 | tf_op jit(solution)/shard_map/ppermute | solution.py:300
  85.8 1.0 copy-start.6
  98.4 6.5 %collective-permute-start.17 = (bf16[240,256]{1,0:T(8,128)(2,1)}, bf16[240,256]{1,0:T(8,128)(2,1)S(1)}, u32[]{:S(2)}, u32[]{:S(2)}) collective-permute-start(bf16[240,256]{1,0:T(8,128)(2,1)} %get-tuple-element.14), channel_id=1, source_target_pairs={{0,2},{1,3},{2,0},{3,1},{4,6},{5,7},{6,4},{7,5},{8,10},{9,11},{10,... | collective-permute-start | bytes 368648 | tf_op jit(solution)/shard_map/ppermute | solution.py:305
  99.9 7.6 %collective-permute-start.19 = (bf16[240,256]{1,0:T(8,128)(2,1)}, bf16[240,256]{1,0:T(8,128)(2,1)S(1)}, u32[]{:S(2)}, u32[]{:S(2)}) collective-permute-start(bf16[240,256]{1,0:T(8,128)(2,1)} %get-tuple-element.15), channel_id=1, source_target_pairs={{0,2},{1,3},{2,0},{3,1},{4,6},{5,7},{6,4},{7,5},{8,10},{9,11},{10,... | collective-permute-start | bytes 368648 | tf_op jit(solution)/shard_map/ppermute | solution.py:305
  100.4 9.2 %collective-permute-start.21 = (bf16[240,256]{1,0:T(8,128)(2,1)}, bf16[240,256]{1,0:T(8,128)(2,1)S(1)}, u32[]{:S(2)}, u32[]{:S(2)}) collective-permute-start(bf16[240,256]{1,0:T(8,128)(2,1)} %get-tuple-element.16), channel_id=1, source_target_pairs={{0,2},{1,3},{2,0},{3,1},{4,6},{5,7},{6,4},{7,5},{8,10},{9,11},{10,... | collective-permute-start | bytes 368648 | tf_op jit(solution)/shard_map/ppermute | solution.py:305
  102.0 18.1 %copy-start.1 = (f32[64,256]{1,0:T(8,128)}, f32[64,256]{1,0:T(8,128)S(1)}, u32[]{:S(2)}) copy-start(f32[64,256]{1,0:T(8,128)S(1)} %add_add_fusion.refs_0_) | copy-start | bytes 196612
  102.0 12.8 %collective-permute-start.29 = (f32[64,256]{1,0:T(8,128)S(1)}, f32[64,256]{1,0:T(8,128)S(1)}, u32[]{:S(2)}, u32[]{:S(2)}) collective-permute-start(f32[64,256]{1,0:T(8,128)S(1)} %add_add_fusion.refs_0_), channel_id=1, source_target_pairs={{0,3},{1,2},{2,1},{3,0},{4,7},{5,6},{6,5},{7,4},{8,11},{9,10},{10,... | collective-permute-start | bytes 196616 | tf_op jit(solution)/shard_map/ppermute | solution.py:448
  102.1 13.7 %collective-permute-start.28 = (f32[64,256]{1,0:T(8,128)S(1)}, f32[64,256]{1,0:T(8,128)S(1)}, u32[]{:S(2)}, u32[]{:S(2)}) collective-permute-start(f32[64,256]{1,0:T(8,128)S(1)} %add_add_fusion.refs_0_), channel_id=1, source_target_pairs={{0,1},{1,0},{2,3},{3,2},{4,5},{5,4},{6,7},{7,6},{8,9},{9,8},{10,11... | collective-permute-start | bytes 196616 | tf_op jit(solution)/shard_map/ppermute | solution.py:448
  104.9 20.4 %collective-permute-start.16 = (bf16[240,256]{1,0:T(8,128)(2,1)}, bf16[240,256]{1,0:T(8,128)(2,1)S(1)}, u32[]{:S(2)}, u32[]{:S(2)}) collective-permute-start(bf16[240,256]{1,0:T(8,128)(2,1)} %get-tuple-element.13), channel_id=1, source_target_pairs={{0,2},{1,3},{2,0},{3,1},{4,6},{5,7},{6,4},{7,5},{8,10},{9,11},{10,... | collective-permute-start | bytes 368648 | tf_op jit(solution)/shard_map/ppermute | solution.py:305
  110.9 14.3 %collective-permute-start.18 = (bf16[240,256]{1,0:T(8,128)(2,1)S(1)}, bf16[240,256]{1,0:T(8,128)(2,1)S(1)}, u32[]{:S(2)}, u32[]{:S(2)}) collective-permute-start(bf16[240,256]{1,0:T(8,128)(2,1)S(1)} %get-tuple-element.20), channel_id=1, source_target_pairs={{0,8},{4,12},{8,16},{12,20},{16,24},{20,28},{24,0},{28,4},{1,9},{5... | collective-permute-start | bytes 368648 | tf_op jit(solution)/shard_map/ppermute | solution.py:300
  114.2 11.0 %collective-permute-start.22 = (bf16[240,256]{1,0:T(8,128)(2,1)S(1)}, bf16[240,256]{1,0:T(8,128)(2,1)S(1)}, u32[]{:S(2)}, u32[]{:S(2)}) collective-permute-start(bf16[240,256]{1,0:T(8,128)(2,1)S(1)} %get-tuple-element.21), channel_id=1, source_target_pairs={{0,24},{4,28},{8,0},{12,4},{16,8},{20,12},{24,16},{28,20},{1,25},{... | collective-permute-start | bytes 368648 | tf_op jit(solution)/shard_map/ppermute | solution.py:300
  114.8 5.2 %copy-start.2 = (f32[64,256]{1,0:T(8,128)}, f32[64,256]{1,0:T(8,128)S(1)}, u32[]{:S(2)}) copy-start(f32[64,256]{1,0:T(8,128)S(1)} %collective-permute-done.29.refs_3_) | copy-start | bytes 196612
  114.8 10.4 %collective-permute-start.20 = (bf16[240,256]{1,0:T(8,128)(2,1)S(1)}, bf16[240,256]{1,0:T(8,128)(2,1)S(1)}, u32[]{:S(2)}, u32[]{:S(2)}) collective-permute-start(bf16[240,256]{1,0:T(8,128)(2,1)S(1)} %get-tuple-element.22), channel_id=1, source_target_pairs={{0,16},{4,20},{8,24},{12,28},{16,0},{20,4},{24,8},{28,12},{1,17},{... | collective-permute-start | bytes 368648 | tf_op jit(solution)/shard_map/ppermute | solution.py:300
  115.8 4.3 %copy-start.3 = (f32[64,256]{1,0:T(8,128)}, f32[64,256]{1,0:T(8,128)S(1)}, u32[]{:S(2)}) copy-start(f32[64,256]{1,0:T(8,128)S(1)} %collective-permute-done.28.refs_2_) | copy-start | bytes 196612
  115.8 4.3 %collective-permute-start.27 = (f32[64,256]{1,0:T(8,128)S(1)}, f32[64,256]{1,0:T(8,128)S(1)}, u32[]{:S(2)}, u32[]{:S(2)}) collective-permute-start(f32[64,256]{1,0:T(8,128)S(1)} %add_add_fusion.refs_0_), channel_id=1, source_target_pairs={{0,2},{1,3},{2,0},{3,1},{4,6},{5,7},{6,4},{7,5},{8,10},{9,11},{10,... | collective-permute-start | bytes 196616 | tf_op jit(solution)/shard_map/ppermute | solution.py:448
  120.0 0.6 copy-start.4

commit v2 on v1

--- a/solution.py
+++ b/solution.py
@@ -32,8 +32,18 @@
 
 
 def one_hot(ids, depth):
+    if depth <= 256:
+        rows = lax.broadcasted_iota(I32, (depth, ids.shape[1]), 0).astype(F32).astype(BF16)
+        one, zero = jnp.ones((), BF16), jnp.zeros((), BF16)
+        return jnp.where(rows == ids.astype(F32).astype(BF16), one, zero)
     rows = lax.broadcasted_iota(I32, (depth, ids.shape[1]), 0)
     return jnp.where(rows == ids, 1.0, 0.0).astype(BF16)
+
+
+def slot_hot(slot, local, slots, depth):
+    return jnp.concatenate(
+        [one_hot(jnp.where(slot == at, local, -1), depth) for at in range(slots)], axis=0
+    )
 
 
 def eye(width):
@@ -64,13 +74,13 @@
     return pl.BlockSpec(memory_space=pltpu.SMEM)
 
 
-def call(body, out_shape, n_in, scratch, flops, name):
+def call(body, out_shape, n_in, scratch, flops, name, unread=0):
     many = isinstance(out_shape, (tuple, list))
     moved = 1 << 22
     return pl.pallas_call(
         body,
         out_shape=out_shape,
-        in_specs=[smem()] + [vmem()] * n_in,
+        in_specs=[smem()] + [vmem()] * n_in + [pl.BlockSpec(memory_space=pl.ANY)] * unread,
         out_specs=[vmem()] * len(out_shape) if many else vmem(),
         scratch_shapes=scratch,
         compiler_params=pltpu.CompilerParams(vmem_limit_bytes=VMEM_LIMIT),
@@ -79,20 +89,39 @@
     )
 
 
-def source_kernel(
-    sizes, place, meta, meta_core, feats, feats_core, coefs, xt_ref, ct_ref, table
-):
-    cols, shard, span, heads, padded = sizes
+def prepare_kernel(fills, src, dst, rel, norm, out_ref):
+    blocks = fills.shape[-1]
+    out_ref[0:1, :] = src[0].astype(F32)
+    out_ref[1:2, :] = dst[0].astype(F32)
+    out_ref[2:3, :] = rel[0].astype(F32)
+    lane = lax.broadcasted_iota(I32, (1, EDGE_BLOCK), 1)
+    for at in range(blocks):
+        here = slice(at * EDGE_BLOCK, (at + 1) * EDGE_BLOCK)
+        live = jnp.where(lane < fills[0, 0, at], 1.0, 0.0)
+        out_ref[3:4, here] = norm[0, :, here] * live
+
+
+def source_kernel(sizes, place, meta, meta_core, feats, feats_core, coefs_t, *refs):
+    cols, shard, span, heads, padded, extra = sizes
+    xt_ref, ct_ref, table, coefs = refs[extra:]
     count = cols // PAIR
     y, core = place[2], place[3]
     width = feats.shape[-1]
     edges = meta.shape[-1]
+    basis_count, relation_count = coefs_t.shape
     unit = eye(width)
     for far, block in enumerate((feats, feats_core)):
         for sy in range(count):
             for xr in range(PAIR):
                 at = (far * count + sy) * shard
                 table[xr, :, at : at + shard] = dot_t(unit, block[sy, xr]).astype(BF16)
+    coefs[...] = jnp.zeros_like(coefs)
+    for head in range(heads):
+        live = min(LANES, relation_count - head * LANES)
+        if live > 0:
+            coefs[head * padded : head * padded + basis_count, 0:live] = coefs_t[
+                :, head * LANES : head * LANES + live
+            ]
     for far, source in enumerate((meta, meta_core)):
 
         def step(index, carry, far=far, source=source):
@@ -102,7 +131,7 @@
             owner, local = split_index(ids, shard)
             owner_y, owner_core = split_index(owner, PAIR)
             slot = (owner_core ^ core) * count + wrap(y - owner_y, count)
-            rows = dot(table[xr], one_hot(slot * shard + local, cols * shard))
+            rows = dot(table[xr], slot_hot(slot, local, cols, shard))
             xt_ref[far * PAIR + xr, :, pl.ds(at, span)] = rows.astype(BF16)
             relation = source[xr, 2:3, pl.ds(at, span)].astype(I32)
             high, low = split_index(relation, LANES)
@@ -115,14 +144,14 @@
             ct_ref[far * PAIR + xr, :, pl.ds(at, span)] = total
             return carry
 
-        lax.fori_loop(0, PAIR * (edges // span), step, 0)
+        lax.fori_loop(0, PAIR * (edges // span), step, 0, unroll=2)
 
 
 def grad_kernel(sizes, place, meta, *refs):
     rows_total, shard, span = sizes
     count = rows_total // PAIR
     blocks = refs[:rows_total]
-    gt_ref, table = refs[rows_total:]
+    gt_ref, table = refs[rows_total + 1 :]
     a, x = place[0], place[1]
     width = blocks[0].shape[-1]
     edges = meta.shape[-1]
@@ -137,18 +166,20 @@
         owner, local = split_index(ids, shard)
         owner_a, owner_x = split_index(owner, PAIR)
         slot = (owner_x ^ x) * count + wrap(a - owner_a, count)
-        rows = dot(table[...], one_hot(slot * shard + local, rows_total * shard))
+        rows = dot(table[...], slot_hot(slot, local, rows_total, shard))
         weight = meta[xr, 3:4, pl.ds(at, span)]
         gt_ref[:, pl.ds(pl.multiple_of(index * span, span), span)] = (rows * weight).astype(BF16)
         return carry
 
-    lax.fori_loop(0, PAIR * (edges // span), step, 0)
+    lax.fori_loop(0, PAIR * (edges // span), step, 0, unroll=2)
 
 
 def forward_kernel(
-    sizes, place, meta, gt_ref, xt_ref, ct_ref, bases_ref, out_ref, total, inner, wide, coef_sum
+    sizes, place, meta, gt_ref, xt_ref, ct_ref, bases_ref, *refs
 ):
     cols, shard, span, heads, padded = sizes
+    outs = refs[:cols]
+    total, inner, wide, coef_sum = refs[cols:]
     count = cols // PAIR
     y, core = place[2], place[3]
     edges = meta.shape[-1]
@@ -161,20 +192,18 @@
         total[...] = jnp.zeros_like(total)
         inner[...] = jnp.zeros_like(inner)
 
-    def chunk(index, carry):
-        at = pl.ds(pl.multiple_of(index * span, span), span)
-        grads = gt_ref[:, at]
+    stacked = bases_ref[...].reshape(group * width, width)
+    for index in range(edges // span):
+        at = slice(index * span, (index + 1) * span)
+        backed = dot(stacked, gt_ref[:, at])
         rows = xt_ref[0, :, at].astype(F32)
         sums = total[:, at]
         for t in range(group):
             base = step * group + t
-            backed = dot(bases_ref[t], grads)
-            sums = sums + ct_ref[0, pl.ds(base, 1), at] * backed
-            inner[pl.ds(base, 1), at] = jnp.sum(backed * rows, axis=0, keepdims=True)
+            mine = backed[t * width : (t + 1) * width]
+            sums = sums + ct_ref[0, pl.ds(base, 1), at] * mine
+            inner[pl.ds(base, 1), at] = jnp.sum(mine * rows, axis=0, keepdims=True)
         total[:, at] = sums
-        return carry
-
-    lax.fori_loop(0, edges // span, chunk, 0)
 
     @pl.when(step == pl.num_programs(0) - 1)
     def _():
@@ -182,11 +211,10 @@
         owner, local = split_index(ids, shard)
         owner_y, owner_core = split_index(owner, PAIR)
         slot = (owner_core ^ core) * count + wrap(owner_y - y, count)
-        place_of = slot * shard + local
         values = total[...].astype(BF16)
         for at in range(cols):
-            hot = one_hot(place_of - at * shard, shard)
-            out_ref[at, 0:shard, :] = dot_t(hot, values).astype(BF16)
+            hot = one_hot(jnp.where(slot == at, local, -1), shard)
+            outs[at][0:shard, :] = dot_t(hot, values).astype(BF16)
         high, low = split_index(meta[0, 2:3, :].astype(I32), LANES)
         for head in range(heads):
             wide[head * padded : (head + 1) * padded, :] = jnp.where(
@@ -200,54 +228,57 @@
                 target = (y + sy) % count * PAIR + (core ^ far)
                 for side in range(2):
                     rows = coef_sum[pl.ds(pl.multiple_of(target * share + side * half, 8), half), :]
-                    out_ref[
-                        far * count + sy,
-                        shard : shard + half,
-                        side * LANES : (side + 1) * LANES,
+                    outs[far * count + sy][
+                        shard : shard + half, side * LANES : (side + 1) * LANES
                     ] = rows.astype(BF16)
 
 
 def basis_kernel(sizes, place, gt_ref, gt_core, xt_ref, ct_ref, *refs):
-    rows_total, cols, block, groups, basis_count, span = sizes
+    rows_total, cols, block, groups, basis_count, span, turns = sizes
     a_count, y_count = rows_total // PAIR, cols // PAIR
     a, x, y, core = place[0], place[1], place[2], place[3]
-    outs = refs[: 1 + (y_count - 1) * a_count]
-    acc, left, tiles = refs[len(outs) :]
+    outs = refs[: y_count * len(turns)]
+    acc, left_even, left_odd, tiles = refs[len(outs) :]
     width, edges = xt_ref.shape[1], xt_ref.shape[2]
     tiles_wide = width // TILE
     cover = groups * TILE
+    spread = tiles.shape[0] // len(outs)
     steps = edges // span
-    acc[...] = jnp.zeros_like(acc)
-    for far, grads in enumerate((gt_ref, gt_core)):
-
-        def step(index, carry, far=far, grads=grads):
-            part = far * PAIR + index // steps
-            at = pl.ds(pl.multiple_of(index % steps * span, span), span)
-            for b in range(basis_count):
-                row = ct_ref[part, b : b + 1, at]
-                tiles[b] = jnp.broadcast_to(row, (TILE, span)).astype(BF16)
-            for sy in range(y_count):
-                for sz in range(a_count):
-                    owner = ((a + sz) % a_count * PAIR + x) * cols + (y + sy) % y_count * PAIR + core
-                    first = owner * block // TILE
-                    for q in range(groups):
-                        tile = jnp.minimum(first + q, basis_count * tiles_wide - 1)
-                        lower = pl.multiple_of(tile % tiles_wide * TILE, TILE)
-                        to = ((sy * a_count + sz) * groups + q) * TILE
-                        left[to : to + TILE, :] = (
-                            tiles[tile // tiles_wide] * xt_ref[part, pl.ds(lower, TILE), at]
-                        )
-            here = pl.ds(pl.multiple_of(index * span, span), span)
-            acc[...] += dot_t(left[...], grads[:, here])
-            return carry
-
-        lax.fori_loop(0, PAIR * steps, step, 0)
-    for sz in range(a_count):
-        outs[0][sz] = acc[sz * cover : (sz + 1) * cover, :]
-    for sy in range(1, y_count):
-        for sz in range(a_count):
-            at = (sy * a_count + sz) * cover
-            outs[1 + (sy - 1) * a_count + sz][...] = acc[at : at + cover, :].astype(BF16)
+    firsts = []
+    for sz in turns:
+        for sy in range(y_count):
+            owner = ((a + sz) % a_count * PAIR + x) * cols + (y + sy) % y_count * PAIR + core
+            firsts.append(owner * block // TILE)
+
+    def build(part, at, left):
+        for order, first in enumerate(firsts):
+            base = first // tiles_wide
+            for extra in range(spread):
+                row = ct_ref[part, pl.ds(jnp.minimum(base + extra, basis_count - 1), 1), at]
+                tiles[order * spread + extra] = jnp.broadcast_to(row, (TILE, span)).astype(BF16)
+            for q in range(groups):
+                tile = jnp.minimum(first + q, basis_count * tiles_wide - 1)
+                lower = pl.multiple_of(tile % tiles_wide * TILE, TILE)
+                to = (order * groups + q) * TILE
+                left[to : to + TILE, :] = (
+                    tiles[order * spread + tile // tiles_wide - base]
+                    * xt_ref[part, pl.ds(lower, TILE), at]
+                )
+
+    for index in range(2 * PAIR * steps):
+        part = index // steps
+        at = slice(index % steps * span, (index % steps + 1) * span)
+        left = left_even if index % 2 == 0 else left_odd
+        build(part, at, left)
+        grads = gt_ref if part < PAIR else gt_core
+        here = index % (PAIR * steps) * span
+        term = dot_t(left[...], grads[:, here : here + span])
+        if index:
+            acc[...] += term
+        else:
+            acc[...] = term
+    for order, out in enumerate(outs):
+        out[...] = acc[order * cover : (order + 1) * cover, :].astype(out.dtype)
 
 
 def coef_kernel(sizes, place, *refs):
@@ -264,11 +295,13 @@
                 whole[pl.ds(pl.multiple_of(target * share + side * half, 8), half), :] = (
                     parts[far * count + sy][:, side * LANES : (side + 1) * LANES]
                 )
-    total, width = out_ref.shape
+    width, total = out_ref.shape
     for head in range(heads):
-        piece = whole[head * padded : (head + 1) * padded, :].T
         live = min(LANES, total - head * LANES)
-        out_ref[head * LANES : head * LANES + live, :] = piece[:live, :width] / divisor
+        if live > 0:
+            out_ref[:, head * LANES : head * LANES + live] = (
+                whole[head * padded : head * padded + width, 0:live] / divisor
+            )
 
 
 def on_device(
@@ -306,41 +339,40 @@
 
     own_dest = dest_grad[0]
     dest = [own_dest] + [turn_z(own_dest, s) for s in range(1, a_count)]
-    dest = dest + [flip_x(value) for value in dest]
-
-    fills = block_fill.reshape(-1)
-    position = lax.broadcasted_iota(I32, (fills.shape[0], EDGE_BLOCK), 1)
-    live = (position < fills[:, None]).reshape(-1).astype(F32)
-    weights = edge_norm.reshape(-1) * live
-    meta = jnp.stack(
-        [
-            src_ids.reshape(-1).astype(F32),
-            dst_ids.reshape(-1).astype(F32),
-            rel_ids.reshape(-1).astype(F32),
-            weights,
-        ]
-    )
+    across = [flip_x(own_dest)]
+    near = flip_x(node_feats)
+
+    meta = pl.pallas_call(
+        prepare_kernel,
+        out_shape=jax.ShapeDtypeStruct((4, edges), F32),
+        in_specs=[smem()] + [vmem()] * 4,
+        out_specs=vmem(),
+        name="edge_table",
+    )(block_fill, src_ids, dst_ids, rel_ids, edge_norm)
     meta = jnp.stack([meta, flip_x(meta)])
     meta_core = flip_core(meta)
 
-    feats = jnp.stack([node_feats, flip_x(node_feats)])
+    feats = jnp.stack([node_feats, near])
+    feats, across[0] = lax.optimization_barrier((feats, across[0]))
     feats = jnp.stack([feats] + [turn_y(feats, s) for s in range(1, y_count)])
+    across += [flip_x(value) for value in dest[1:]]
     feats_core = flip_core(feats)
 
-    table = jnp.pad(coefs, ((0, heads * LANES - relation_count), (0, padded - basis_count)))
-    table = table.reshape(heads, LANES, padded).transpose(0, 2, 1).reshape(heads * padded, LANES)
-
     xt, ct = call(
-        functools.partial(source_kernel, (cols, shard, span, heads, padded)),
+        functools.partial(source_kernel, (cols, shard, span, heads, padded, a_count)),
         (
             jax.ShapeDtypeStruct((2 * PAIR, width, edges), BF16),
             jax.ShapeDtypeStruct((2 * PAIR, padded, edges), F32),
         ),
         5,
-        [pltpu.VMEM((PAIR, width, cols * shard), BF16)],
+        [
+            pltpu.VMEM((PAIR, width, cols * shard), BF16),
+            pltpu.VMEM((heads * padded, LANES), BF16),
+        ],
         2 * 4 * edges * cols * shard * width,
         "source_rows",
-    )(place, meta, meta_core, feats, feats_core, table)
+        a_count,
+    )(place, meta, meta_core, feats, feats_core, coefs.T, *dest)
 
     dest_shard = own_dest.shape[0]
     gt = call(
@@ -350,7 +382,8 @@
         [pltpu.VMEM((width, rows_total * dest_shard), BF16)],
         2 * 2 * edges * rows_total * dest_shard * width,
         "edge_grads",
-    )(place, meta, *dest)
+        1,
+    )(place, meta, *dest, *across, xt)
     gt_core = flip_core(gt)
 
     group = max(g for g in range(1, 6) if basis_count % g == 0)
@@ -366,8 +399,8 @@
             pl.BlockSpec((1, padded, edges), lambda s: (0, 0, 0)),
             pl.BlockSpec((group, width, width), lambda s: (s, 0, 0)),
         ],
-        out_specs=pl.BlockSpec((cols, shard + share_rows, width), lambda s: (0, 0, 0)),
-        out_shape=jax.ShapeDtypeStruct((cols, shard + share_rows, width), BF16),
+        out_specs=[pl.BlockSpec((shard + share_rows, width), lambda s: (0, 0))] * cols,
+        out_shape=[jax.ShapeDtypeStruct((shard + share_rows, width), BF16)] * cols,
         scratch_shapes=[
             pltpu.VMEM((width, edges), F32),
             pltpu.VMEM((padded, edges), F32),
@@ -385,40 +418,47 @@
 
     block = basis_count * width // (rows_total * cols)
     cover = block if block % TILE == 0 else round_up(block, TILE) + TILE
-    pieces = call(
-        functools.partial(
-            basis_kernel, (rows_total, cols, block, cover // TILE, basis_count, 2 * span)
-        ),
-        [jax.ShapeDtypeStruct((a_count, cover, width), F32)]
-        + [jax.ShapeDtypeStruct((cover, width), BF16)] * ((y_count - 1) * a_count),
-        4,
-        [
-            pltpu.VMEM((y_count * a_count * cover, width), F32),
-            pltpu.VMEM((y_count * a_count * cover, 2 * span), BF16),
-            pltpu.VMEM((padded, TILE, 2 * span), BF16),
-        ],
-        2 * 4 * edges * y_count * a_count * cover * width,
-        "basis_terms",
-    )(place, gt, gt_core, xt, ct)
-    kept, sent = pieces[0], pieces[1:]
-
-    got = {}
-    order = list(range(1, a_count)) + [0]
-    for sz in order:
-        for sy in range(1, y_count):
-            got[sz, sy] = turn_y(sent[(sy - 1) * a_count + sz], sy)
-    basis_sum = None
-    arrived = []
-    for sz in order:
-        value = kept[sz]
-        for sy in range(1, y_count):
-            value = value + got[sz, sy].astype(F32)
-        if sz:
-            arrived.append(turn_z(value.astype(BF16), sz))
-        else:
-            basis_sum = value
-    for value in arrived:
-        basis_sum = basis_sum + value.astype(F32)
+
+    def basis_blocks(turns):
+        count = len(turns) * y_count
+        return call(
+            functools.partial(
+                basis_kernel,
+                (rows_total, cols, block, cover // TILE, basis_count, 2 * span, turns),
+            ),
+            [
+                jax.ShapeDtypeStruct((cover, width), BF16 if sy else F32)
+                for _ in turns
+                for sy in range(y_count)
+            ],
+            4,
+            [
+                pltpu.VMEM((count * cover, width), F32),
+                pltpu.VMEM((count * cover, 2 * span), BF16),
+                pltpu.VMEM((count * cover, 2 * span), BF16),
+                pltpu.VMEM((count * (round_up(cover, width) // width + 1), TILE, 2 * span), BF16),
+            ],
+            2 * 4 * edges * count * cover * width,
+            "basis_terms",
+        )(place, gt, gt_core, xt, ct)
+
+    def over_y(turns):
+        blocks = basis_blocks(turns)
+        for order, sz in enumerate(turns):
+            mine = blocks[order * y_count : (order + 1) * y_count]
+            value = mine[0]
+            for sy in range(1, y_count):
+                value = value + turn_y(mine[sy], sy).astype(F32)
+            sums[sz] = value
+
+    sums = {}
+    order = tuple(range(1, a_count)) + (0,)
+    half = a_count // 2
+    over_y(order[:half])
+    over_y(order[half:])
+    basis_sum = sums[0]
+    for sz in range(1, a_count):
+        basis_sum = basis_sum + turn_z(sums[sz].astype(BF16), sz).astype(F32)
     if cover != block:
         owner = i * cols + j
         basis_sum = lax.dynamic_slice_in_dim(basis_sum, owner * block % TILE, block, axis=0)
@@ -448,13 +488,13 @@
             shares.append(lax.ppermute(coef_part, "col", target) if far or sy else coef_part)
     coef_grad = call(
         functools.partial(coef_kernel, (cols, heads, padded, cols)),
-        jax.ShapeDtypeStruct((relation_count, basis_count), F32),
+        jax.ShapeDtypeStruct((basis_count, relation_count), F32),
         cols,
         [pltpu.VMEM((heads * padded, LANES), F32)],
         1 << 20,
         "coef_rows",
     )(place, *shares)
-    return (node_grad, basis_grad, coef_grad)
+    return (node_grad, basis_grad, coef_grad.T)
 
 
 def solution(mesh):

time: 128 us -> 120 us (0.938)
  waiting for transfers between devices: 31.3 us -> 38.4 us
  local copies, waits for them, and re-layouts: 8.82 us -> 3.76 us
  Pallas kernels: 42.7 us -> 38.3 us
  starting transfers between devices: 34.8 us -> 31.7 us
  other arithmetic: 8.49 us -> 6.16 us
    ppermute x9, waiting for transfers between devices: 0.02 us -> 8.77 us  [turn_z(): lax.ppermute(value, 'row', [(r, (r + by * PAIR) % rows_total) for r in ra...]
    ppermute x7, waiting for transfers between devices: 13.7 us -> 8.88 us  [flip_x(): return lax.ppermute(value, 'row', [(r, r ^ 1) for r in range(rows_total)])]
    pallas_call x1, Pallas kernels: 12.8 us -> 9.7 us  [on_device(): pl.pallas_call(functools.partial(forward_kernel, (cols, shard, span, head...]
    unnamed x33 -> x36, local copies, waits for them, and re-layouts: 5.33 us -> 3.09 us
    ppermute x5, waiting for transfers between devices: 8.05 us -> 9.95 us  [turn_y(): lax.ppermute(value, 'col', [(c, (c + by * PAIR) % cols) for c in range(co...]
    reshape x1 -> x0, local copies, waits for them, and re-layouts: 1.71 us -> none  [on_device(): table.reshape(heads, LANES, padded).transpose(0, 2, 1)]
    convert_element_type x3, other arithmetic: 2.67 us -> 1.02 us  [on_device(): basis_sum = basis_sum + turn_z(sums[sz].astype(BF16), sz).astype(F32)]
    pallas_call x2 -> x4, Pallas kernels: 21.2 us -> 21.2 us  [the longest x2 11.8 us: basis_blocks(): call(functools.partial(basis_kernel, (rows_total, cols, block, cover // T...]
  transfers between devices with their start and end apart: 30 -> 30, of which waited for: 13 -> 12; matrix products, arithmetic and copies ran while one was open for 10% -> 4% of each run, Pallas kernels for 34% -> 27%
where the time goes in v2:
time: 120 us; the launch traced here: 119 us
  waiting for transfers between devices  38.4 us (32%)
  Pallas kernels  38.3 us (32%)
  starting transfers between devices  31.7 us (26%)
  other arithmetic  6.16 us (5%)
  local copies, waits for them, and re-layouts  3.76 us (3%)
    ppermute x9, starting transfers between devices, turn_z(): lax.ppermute(value, 'row', [(r, (r + by * PAIR) % rows_total) for r in ra...  14.2 us
    pallas_call x2, Pallas kernels, basis_blocks(): call(functools.partial(basis_kernel, (rows_total, cols, block, cover // T...  11.8 us
    ppermute x5, waiting for transfers between devices, turn_y(): lax.ppermute(value, 'col', [(c, (c + by * PAIR) % cols) for c in range(co...  9.95 us
    pallas_call x1, Pallas kernels, on_device(): pl.pallas_call(functools.partial(forward_kernel, (cols, shard, span, head...  9.7 us
    ppermute x7, waiting for transfers between devices, flip_x(): return lax.ppermute(value, 'row', [(r, r ^ 1) for r in range(rows_total)])  8.88 us
    ppermute x9, waiting for transfers between devices, turn_z(): lax.ppermute(value, 'row', [(r, (r + by * PAIR) % rows_total) for r in ra...  8.77 us
    pallas_call x1, Pallas kernels, on_device(): call(functools.partial(source_kernel, (cols, shard, span, heads, padded,...  7.87 us
    ppermute x3, waiting for transfers between devices, on_device(): lax.ppermute(packed[far * y_count + sy], 'col', target).astype(F32)  7.79 us
  transfers between devices with their start and end apart: 30, of which 12 were waited for; matrix products, arithmetic and copies ran while one was open for 4% of the time, Pallas kernels for 27%

profile of v2, /device:TPU:0, one launch (start us, length us, event | category | flops | bytes accessed | tf_op | source)
XLA Modules:
  0.0 119.2 jit_solution(3392155496989335339)
XLA Ops:
  0.6 3.0 %collective-permute-start.4 = (bf16[256,256]{1,0:T(8,128)(2,1)}, bf16[256,256]{1,0:T(8,128)(2,1)S(1)}, u32[]{:S(2)}, u32[]{:S(2)}) collective-permute-start(bf16[256,256]{1,0:T(8,128)(2,1)} %param.9), channel_id=1, source_target_pairs={{0,4},{4,0},{8,12},{12,8},{16,20},{20,16},{24,28},{28,24},{1,5},{5... | collective-permute-start | bytes 393224 | tf_op jit(solution)/shard_map/ppermute | solution.py:327
  3.7 4.5 %collective-permute-done.4 = bf16[256,256]{1,0:T(8,128)(2,1)S(1)} collective-permute-done((bf16[256,256]{1,0:T(8,128)(2,1)}, bf16[256,256]{1,0:T(8,128)(2,1)S(1)}, u32[]{:S(2)}, u32[]{:S(2)}) %collective-permute-start.4) | collective-permute-done | bytes 131104 | tf_op jit(solution)/shard_map/ppermute | solution.py:327
  8.2 0.9 pad_maximum_fusion.1
  9.1 1.0 collective-permute-done.5.refs_4_
  10.2 1.8 %collective-permute-start.10 = (bf16[2,256,256]{2,1,0:T(8,128)(2,1)S(1)}, bf16[2,256,256]{2,1,0:T(8,128)(2,1)S(1)}, u32[]{:S(2)}, u32[]{:S(2)}) collective-permute-start(bf16[2,256,256]{2,1,0:T(8,128)(2,1)S(1)} %pad_maximum_fusion.1), channel_id=1, source_target_pairs={{0,2},{1,3},{2,0},{3,1},{4,6},{5,7},{6,4},{7,5},{8,10},{9,11},{10,... | collective-permute-start | bytes 786440 | tf_op jit(solution)/shard_map/ppermute | solution.py:338
  11.9 5.7 %collective-permute-done.10 = bf16[2,256,256]{2,1,0:T(8,128)(2,1)S(1)} collective-permute-done((bf16[2,256,256]{2,1,0:T(8,128)(2,1)S(1)}, bf16[2,256,256]{2,1,0:T(8,128)(2,1)S(1)}, u32[]{:S(2)}, u32[]{:S(2)}) %collective-permute-start.10) | collective-permute-done | bytes 262176 | tf_op jit(solution)/shard_map/ppermute | solution.py:338
  17.8 1.5 %edge_table.1 = f32[4,1024]{1,0:T(4,128)} custom-call(s32[1,1,8]{2,1,0:T(1,128)} %fills.1, s32[1,1,1024]{2,1,0:T(1,128)} %src.1, s32[1,1,1024]{2,1,0:T(1,128)} %dst.1, s32[1,1,1024]{2,1,0:T(1,128)} %rel.1, f32[1,1,1024]{2,1,0:T(1,128)} %norm.1), custom_call_target="tpu_custom_call" | custom-call | tf_op jit(solution)/shard_map/edge_table/pallas_call | solution.py:345
  19.3 1.4 %collective-permute-start = (f32[4,1024]{1,0:T(4,128)}, f32[4,1024]{1,0:T(4,128)S(1)}, u32[]{:S(2)}, u32[]{:S(2)}) collective-permute-start(f32[4,1024]{1,0:T(4,128)} %edge_table.1), channel_id=1, source_target_pairs={{0,4},{4,0},{8,12},{12,8},{16,20},{20,16},{24,28},{28,24},{1,5},{5... | collective-permute-start | bytes 49160 | tf_op jit(solution)/shard_map/ppermute | solution.py:327
  20.7 1.6 %collective-permute-start.1 = (bf16[256,256]{1,0:T(8,128)(2,1)}, bf16[256,256]{1,0:T(8,128)(2,1)S(1)}, u32[]{:S(2)}, u32[]{:S(2)}) collective-permute-start(bf16[256,256]{1,0:T(8,128)(2,1)} %bitcast.22), channel_id=1, source_target_pairs={{0,8},{4,12},{8,16},{12,20},{16,24},{20,28},{24,0},{28,4},{1,9},{5... | collective-permute-start | bytes 393224 | tf_op jit(solution)/shard_map/ppermute | solution.py:333
  22.3 2.6 %collective-permute-start.2 = (bf16[256,256]{1,0:T(8,128)(2,1)}, bf16[256,256]{1,0:T(8,128)(2,1)S(1)}, u32[]{:S(2)}, u32[]{:S(2)}) collective-permute-start(bf16[256,256]{1,0:T(8,128)(2,1)} %bitcast.23), channel_id=1, source_target_pairs={{0,16},{4,20},{8,24},{12,28},{16,0},{20,4},{24,8},{28,12},{1,17},{... | collective-permute-start | bytes 393224 | tf_op jit(solution)/shard_map/ppermute | solution.py:333
  24.8 1.3 %collective-permute-start.3 = (bf16[256,256]{1,0:T(8,128)(2,1)}, bf16[256,256]{1,0:T(8,128)(2,1)S(1)}, u32[]{:S(2)}, u32[]{:S(2)}) collective-permute-start(bf16[256,256]{1,0:T(8,128)(2,1)} %bitcast.24), channel_id=1, source_target_pairs={{0,24},{4,28},{8,0},{12,4},{16,8},{20,12},{24,16},{28,20},{1,25},{... | collective-permute-start | bytes 393224 | tf_op jit(solution)/shard_map/ppermute | solution.py:333
  26.2 0.7 pad_maximum_fusion.2.meta
  27.0 0.7 pad_add_fusion.place
  27.7 1.4 %collective-permute-done.1.refs_1_ = bf16[256,256]{1,0:T(8,128)(2,1)S(1)} collective-permute-done((bf16[256,256]{1,0:T(8,128)(2,1)}, bf16[256,256]{1,0:T(8,128)(2,1)S(1)}, u32[]{:S(2)}, u32[]{:S(2)}) %collective-permute-start.1) | collective-permute-done | bytes 131104 | tf_op jit(solution)/shard_map/ppermute | solution.py:333
  29.1 0.6 collective-permute-start.6
  29.7 4.3 %collective-permute-done.2.refs_2_ = bf16[256,256]{1,0:T(8,128)(2,1)S(1)} collective-permute-done((bf16[256,256]{1,0:T(8,128)(2,1)}, bf16[256,256]{1,0:T(8,128)(2,1)S(1)}, u32[]{:S(2)}, u32[]{:S(2)}) %collective-permute-start.2) | collective-permute-done | bytes 131104 | tf_op jit(solution)/shard_map/ppermute | solution.py:333
  34.0 0.5 collective-permute-start.7
  34.6 1.5 %collective-permute-start.8 = (bf16[256,256]{1,0:T(8,128)(2,1)S(1)}, bf16[256,256]{1,0:T(8,128)(2,1)S(1)}, u32[]{:S(2)}, u32[]{:S(2)}) collective-permute-start(bf16[256,256]{1,0:T(8,128)(2,1)S(1)} %collective-permute-done.3.refs_3_), channel_id=1, source_target_pairs={{0,4},{4,0},{8,12},{12,8},{16,20},{20,16},{24,28},{28,24},{1,5},{5... | collective-permute-start | bytes 393224 | tf_op jit(solution)/shard_map/ppermute | solution.py:327
  36.1 0.5 copy-done.17
  36.9 7.9 %source_rows.1 = (bf16[4,256,1024]{2,1,0:T(8,128)(2,1)}, f32[4,32,1024]{2,1,0:T(8,128)}) custom-call(s32[4]{0:T(128)} %pad_add_fusion.place, f32[2,4,1024]{2,1,0:T(4,128)} %copy-done.7, f32[2,4,1024]{2,1,0:T(4,128)} %copy-done.17, bf16[2,2,256,256]{3,2,1,0:T(8,128)(2,1)} %copy-done, bf16[2,2,256,256]{3,2,1,0:T(8,128)(2,1)} %copy-done.9, ...), custom_call_target="tpu_custom_call" | custom-call | flops 2147483648 | bytes 4194304 | tf_op jit(solution)/shard_map/source_rows/pallas_call | solution.py:361
  44.8 0.6 copy-done.14
  45.5 5.7 %edge_grads.1.gt_ref = bf16[256,2048]{1,0:T(8,128)(2,1)} custom-call(s32[4]{0:T(128)} %pad_add_fusion.place, f32[2,4,1024]{2,1,0:T(4,128)} %copy-done.7, bf16[256,256]{1,0:T(8,128)(2,1)} %bitcast.26, bf16[256,256]{1,0:T(8,128)(2,1)} %copy-done.11, bf16[256,256]{1,0:T(8,128)(2,1)} %copy-done.12, bf16[256,256]{1,0:T(8,128)(2,1)} %copy-done.13, ...), custom_call_target="tpu_custom_call" | custom-call | flops 2147483648 | bytes 4194304 | tf_op jit(solution)/shard_map/edge_grads/pallas_call | solution.py:378
  51.2 9.7 %backed_sums.1 = (bf16[320,256]{1,0:T(8,128)(2,1)}, bf16[320,256]{1,0:T(8,128)(2,1)}, bf16[320,256]{1,0:T(8,128)(2,1)}, bf16[320,256]{1,0:T(8,128)(2,1)}) custom-call(s32[4]{0:T(128)} %pad_add_fusion.place, f32[2,4,1024]{2,1,0:T(4,128)} %copy-done.7, bf16[256,2048]{1,0:T(8,128)(2,1)} %edge_grads.1.gt_ref, ...), custom_call_target="tpu_custom_call" | custom-call | flops 4026531840 | bytes 3932160 | tf_op jit(solution)/shard_map/backed_sums/pallas_call | solution.py:391
  60.9 1.5 %collective-permute-start.12 = (bf16[320,256]{1,0:T(8,128)(2,1)}, bf16[320,256]{1,0:T(8,128)(2,1)S(1)}, u32[]{:S(2)}, u32[]{:S(2)}) collective-permute-start(bf16[320,256]{1,0:T(8,128)(2,1)} %get-tuple-element.24), channel_id=1, source_target_pairs={{0,2},{1,3},{2,0},{3,1},{4,6},{5,7},{6,4},{7,5},{8,10},{9,11},{10,... | collective-permute-start | bytes 491528 | tf_op jit(solution)/shard_map/ppermute | solution.py:474
  63.1 5.1 %collective-permute-done.12 = bf16[320,256]{1,0:T(8,128)(2,1)S(1)} collective-permute-done((bf16[320,256]{1,0:T(8,128)(2,1)}, bf16[320,256]{1,0:T(8,128)(2,1)S(1)}, u32[]{:S(2)}, u32[]{:S(2)}) %collective-permute-start.12) | collective-permute-done | bytes 163872 | tf_op jit(solution)/shard_map/ppermute | solution.py:474
  68.1 2.7 %collective-permute-done.14 = bf16[320,256]{1,0:T(8,128)(2,1)S(1)} collective-permute-done((bf16[320,256]{1,0:T(8,128)(2,1)}, bf16[320,256]{1,0:T(8,128)(2,1)S(1)}, u32[]{:S(2)}, u32[]{:S(2)}) %collective-permute-start.14) | collective-permute-done | bytes 163872 | tf_op jit(solution)/shard_map/ppermute | solution.py:474
  70.9 1.0 add_convert_fusion
  71.9 0.6 collective-permute-start.23
  72.5 3.4 %collective-permute-done.23 = bf16[64,256]{1,0:T(8,128)(2,1)S(1)} collective-permute-done((bf16[64,256]{1,0:T(8,128)(2,1)S(1)}, bf16[64,256]{1,0:T(8,128)(2,1)S(1)}, u32[]{:S(2)}, u32[]{:S(2)}) %collective-permute-start.23) | collective-permute-done | bytes 32800 | tf_op jit(solution)/shard_map/ppermute | solution.py:327
  75.9 2.0 %collective-permute-start.24 = (bf16[64,256]{1,0:T(8,128)(2,1)S(1)}, bf16[64,256]{1,0:T(8,128)(2,1)S(1)}, u32[]{:S(2)}, u32[]{:S(2)}) collective-permute-start(bf16[64,256]{1,0:T(8,128)(2,1)S(1)} %add_convert_fusion.4), channel_id=1, source_target_pairs={{0,16},{4,20},{8,24},{12,28},{16,0},{20,4},{24,8},{28,12},{1,17},{... | collective-permute-start | bytes 98312 | tf_op jit(solution)/shard_map/ppermute | solution.py:333
  77.9 2.9 %collective-permute-start.25 = (bf16[64,256]{1,0:T(8,128)(2,1)S(1)}, bf16[64,256]{1,0:T(8,128)(2,1)S(1)}, u32[]{:S(2)}, u32[]{:S(2)}) collective-permute-start(bf16[64,256]{1,0:T(8,128)(2,1)S(1)} %add_convert_fusion.4), channel_id=1, source_target_pairs={{0,8},{4,12},{8,16},{12,20},{16,24},{20,28},{24,0},{28,4},{1,9},{5... | collective-permute-start | bytes 98312 | tf_op jit(solution)/shard_map/ppermute | solution.py:333
  80.9 0.9 collective-permute-start.26
  81.7 1.9 %collective-permute-done.25 = bf16[64,256]{1,0:T(8,128)(2,1)S(1)} collective-permute-done((bf16[64,256]{1,0:T(8,128)(2,1)S(1)}, bf16[64,256]{1,0:T(8,128)(2,1)S(1)}, u32[]{:S(2)}, u32[]{:S(2)}) %collective-permute-start.25) | collective-permute-done | bytes 32800 | tf_op jit(solution)/shard_map/ppermute | solution.py:333
  83.6 1.1 collective-permute-done.26
  84.8 1.6 %collective-permute-start.27 = (f32[64,256]{1,0:T(8,128)S(1)}, f32[64,256]{1,0:T(8,128)S(1)}, u32[]{:S(2)}, u32[]{:S(2)}) collective-permute-start(f32[64,256]{1,0:T(8,128)S(1)} %add_add_fusion.refs_0_), channel_id=1, source_target_pairs={{0,2},{1,3},{2,0},{3,1},{4,6},{5,7},{6,4},{7,5},{8,10},{9,11},{10,... | collective-permute-start | bytes 196616 | tf_op jit(solution)/shard_map/ppermute | solution.py:488
  86.4 1.0 copy-done.8
  87.4 5.9 %basis_terms.3 = (f32[240,256]{1,0:T(8,128)}, bf16[240,256]{1,0:T(8,128)(2,1)}, f32[240,256]{1,0:T(8,128)}, bf16[240,256]{1,0:T(8,128)(2,1)}) custom-call(s32[4]{0:T(128)} %pad_add_fusion.place, bf16[256,2048]{1,0:T(8,128)(2,1)} %edge_grads.1.gt_ref, bf16[256,2048]{1,0:T(8,128)(2,1)} %copy-done.8, bf16[4,256,1024]{2,1,0:T(8,128)(2,1)} %get-tuple-element.21.refs_8_.xt_ref, ...), custom_call_target="tpu_custom_call" | custom-call | flops 2013265920 | bytes 4194304 | tf_op jit(solution)/shard_map/basis_terms/pallas_call | solution.py:424
  93.8 1.5 %collective-permute-start.19 = (bf16[240,256]{1,0:T(8,128)(2,1)}, bf16[240,256]{1,0:T(8,128)(2,1)S(1)}, u32[]{:S(2)}, u32[]{:S(2)}) collective-permute-start(bf16[240,256]{1,0:T(8,128)(2,1)} %get-tuple-element.32), channel_id=1, source_target_pairs={{0,2},{1,3},{2,0},{3,1},{4,6},{5,7},{6,4},{7,5},{8,10},{9,11},{10,... | collective-permute-start | bytes 368648 | tf_op jit(solution)/shard_map/ppermute | solution.py:338
  95.3 5.9 %basis_terms.2 = (f32[240,256]{1,0:T(8,128)}, bf16[240,256]{1,0:T(8,128)(2,1)}, f32[240,256]{1,0:T(8,128)}, bf16[240,256]{1,0:T(8,128)(2,1)}) custom-call(s32[4]{0:T(128)} %pad_add_fusion.place, bf16[256,2048]{1,0:T(8,128)(2,1)} %edge_grads.1.gt_ref, bf16[256,2048]{1,0:T(8,128)(2,1)} %copy-done.8, bf16[4,256,1024]{2,1,0:T(8,128)(2,1)} %get-tuple-element.21.refs_8_.xt_ref, ...), custom_call_target="tpu_custom_call" | custom-call | flops 2013265920 | bytes 4194304 | tf_op jit(solution)/shard_map/basis_terms/pallas_call | solution.py:424
  101.8 1.5 %collective-permute-start.16 = (bf16[240,256]{1,0:T(8,128)(2,1)}, bf16[240,256]{1,0:T(8,128)(2,1)S(1)}, u32[]{:S(2)}, u32[]{:S(2)}) collective-permute-start(bf16[240,256]{1,0:T(8,128)(2,1)} %get-tuple-element.28), channel_id=1, source_target_pairs={{0,2},{1,3},{2,0},{3,1},{4,6},{5,7},{6,4},{7,5},{8,10},{9,11},{10,... | collective-permute-start | bytes 368648 | tf_op jit(solution)/shard_map/ppermute | solution.py:338
  103.4 4.2 %collective-permute-done.21 = bf16[240,256]{1,0:T(8,128)(2,1)S(1)} collective-permute-done((bf16[240,256]{1,0:T(8,128)(2,1)}, bf16[240,256]{1,0:T(8,128)(2,1)S(1)}, u32[]{:S(2)}, u32[]{:S(2)}) %collective-permute-start.21) | collective-permute-done | bytes 122912 | tf_op jit(solution)/shard_map/ppermute | solution.py:338
  107.7 1.0 add_convert_fusion.1
  108.7 2.7 %collective-permute-start.22 = (bf16[240,256]{1,0:T(8,128)(2,1)S(1)}, bf16[240,256]{1,0:T(8,128)(2,1)S(1)}, u32[]{:S(2)}, u32[]{:S(2)}) collective-permute-start(bf16[240,256]{1,0:T(8,128)(2,1)S(1)} %add_convert_fusion.1), channel_id=1, source_target_pairs={{0,24},{4,28},{8,0},{12,4},{16,8},{20,12},{24,16},{28,20},{1,25},{... | collective-permute-start | bytes 368648 | tf_op jit(solution)/shard_map/ppermute | solution.py:333
  111.5 0.7 slice.10
  112.1 3.0 %collective-permute-done.29.refs_3_ = f32[64,256]{1,0:T(8,128)S(1)} collective-permute-done((f32[64,256]{1,0:T(8,128)S(1)}, f32[64,256]{1,0:T(8,128)S(1)}, u32[]{:S(2)}, u32[]{:S(2)}) %collective-permute-start.29) | collective-permute-done | bytes 65568 | tf_op jit(solution)/shard_map/ppermute | solution.py:488
  115.2 0.6 copy-done.6
  115.8 1.7 %coef_rows.1 = f32[30,2000]{1,0:T(8,128)} custom-call(s32[4]{0:T(128)} %pad_add_fusion.place, f32[64,256]{1,0:T(8,128)} %copy-done.1, f32[64,256]{1,0:T(8,128)} %copy-done.4, f32[64,256]{1,0:T(8,128)} %copy-done.5, f32[64,256]{1,0:T(8,128)} %copy-done.6), custom_call_target="tpu_custom_call" | custom-call | flops 1048576 | bytes 4194304 | tf_op jit(solution)/shard_map/coef_rows/pallas_call | solution.py:489
  117.5 1.7 %add_multiply_fusion = f32[240,256]{1,0:T(8,128)} fusion(bf16[240,256]{1,0:T(8,128)(2,1)S(1)} %collective-permute-done.22, bf16[240,256]{1,0:T(8,128)(2,1)S(1)} %collective-permute-done.20, bf16[240,256]{1,0:T(8,128)(2,1)S(1)} %collective-permute-done.18, f32[240,256]{1,0:T(8,128)} %get-tuple-element.27, bf16[240,256]{1,0:T(8,128)(2,1)S(1)} %collective-permute-done.16), kind=kLoop, calls=%fused_computation.3 | loop fusion | flops 552960 | bytes 983040 | tf_op jit(solution)/shard_map/div | solution.py:465
  (68 shorter events, 2.6 us)
Async XLA Ops:
  0.6 7.5 %collective-permute-start.4 = (bf16[256,256]{1,0:T(8,128)(2,1)}, bf16[256,256]{1,0:T(8,128)(2,1)S(1)}, u32[]{:S(2)}, u32[]{:S(2)}) collective-permute-start(bf16[256,256]{1,0:T(8,128)(2,1)} %param.9), channel_id=1, source_target_pairs={{0,4},{4,0},{8,12},{12,8},{16,20},{20,16},{24,28},{28,24},{1,5},{5... | collective-permute-start | bytes 393224 | tf_op jit(solution)/shard_map/ppermute | solution.py:327
  3.6 6.5 %collective-permute-start.5 = (bf16[256,256]{1,0:T(8,128)(2,1)}, bf16[256,256]{1,0:T(8,128)(2,1)S(1)}, u32[]{:S(2)}, u32[]{:S(2)}) collective-permute-start(bf16[256,256]{1,0:T(8,128)(2,1)} %bitcast.21), channel_id=1, source_target_pairs={{0,4},{4,0},{8,12},{12,8},{16,20},{20,16},{24,28},{28,24},{1,5},{5... | collective-permute-start | bytes 393224 | tf_op jit(solution)/shard_map/ppermute | solution.py:327
  10.1 34.6 %copy-start.10 = (bf16[256,256]{1,0:T(8,128)(2,1)}, bf16[256,256]{1,0:T(8,128)(2,1)S(1)}, u32[]{:S(2)}) copy-start(bf16[256,256]{1,0:T(8,128)(2,1)S(1)} %collective-permute-done.5.refs_4_) | copy-start | bytes 393220
  10.2 7.5 %collective-permute-start.10 = (bf16[2,256,256]{2,1,0:T(8,128)(2,1)S(1)}, bf16[2,256,256]{2,1,0:T(8,128)(2,1)S(1)}, u32[]{:S(2)}, u32[]{:S(2)}) collective-permute-start(bf16[2,256,256]{2,1,0:T(8,128)(2,1)S(1)} %pad_maximum_fusion.1), channel_id=1, source_target_pairs={{0,2},{1,3},{2,0},{3,1},{4,6},{5,7},{6,4},{7,5},{8,10},{9,11},{10,... | collective-permute-start | bytes 786440 | tf_op jit(solution)/shard_map/ppermute | solution.py:338
  17.7 18.4 %copy-start = (bf16[2,2,256,256]{3,2,1,0:T(8,128)(2,1)}, bf16[2,2,256,256]{3,2,1,0:T(8,128)(2,1)S(1)}, u32[]{:S(2)}) copy-start(bf16[2,2,256,256]{3,2,1,0:T(8,128)(2,1)S(1)} %pad_maximum_fusion.feats) | copy-start | bytes 1572868
  17.7 18.4 %collective-permute-start.11 = (bf16[2,2,256,256]{3,2,1,0:T(8,128)(2,1)S(1)}, bf16[2,2,256,256]{3,2,1,0:T(8,128)(2,1)S(1)}, u32[]{:S(2)}, u32[]{:S(2)}) collective-permute-start(bf16[2,2,256,256]{3,2,1,0:T(8,128)(2,1)S(1)} %pad_maximum_fusion.feats), channel_id=1, source_target_pairs={{0,1},{1,0},{2,3},{3,2},{4,5},{5,4},{6,7},{7,6},{8,9},{9,8},{10,11... | collective-permute-start | bytes 1572872 | tf_op jit(solution)/shard_map/ppermute | solution.py:330
  19.3 6.9 %collective-permute-start = (f32[4,1024]{1,0:T(4,128)}, f32[4,1024]{1,0:T(4,128)S(1)}, u32[]{:S(2)}, u32[]{:S(2)}) collective-permute-start(f32[4,1024]{1,0:T(4,128)} %edge_table.1), channel_id=1, source_target_pairs={{0,4},{4,0},{8,12},{12,8},{16,20},{20,16},{24,28},{28,24},{1,5},{5... | collective-permute-start | bytes 49160 | tf_op jit(solution)/shard_map/ppermute | solution.py:327
  20.7 8.4 %collective-permute-start.1 = (bf16[256,256]{1,0:T(8,128)(2,1)}, bf16[256,256]{1,0:T(8,128)(2,1)S(1)}, u32[]{:S(2)}, u32[]{:S(2)}) collective-permute-start(bf16[256,256]{1,0:T(8,128)(2,1)} %bitcast.22), channel_id=1, source_target_pairs={{0,8},{4,12},{8,16},{12,20},{16,24},{20,28},{24,0},{28,4},{1,9},{5... | collective-permute-start | bytes 393224 | tf_op jit(solution)/shard_map/ppermute | solution.py:333
  22.3 11.8 %collective-permute-start.2 = (bf16[256,256]{1,0:T(8,128)(2,1)}, bf16[256,256]{1,0:T(8,128)(2,1)S(1)}, u32[]{:S(2)}, u32[]{:S(2)}) collective-permute-start(bf16[256,256]{1,0:T(8,128)(2,1)} %bitcast.23), channel_id=1, source_target_pairs={{0,16},{4,20},{8,24},{12,28},{16,0},{20,4},{24,8},{28,12},{1,17},{... | collective-permute-start | bytes 393224 | tf_op jit(solution)/shard_map/ppermute | solution.py:333
  24.8 9.7 %collective-permute-start.3 = (bf16[256,256]{1,0:T(8,128)(2,1)}, bf16[256,256]{1,0:T(8,128)(2,1)S(1)}, u32[]{:S(2)}, u32[]{:S(2)}) collective-permute-start(bf16[256,256]{1,0:T(8,128)(2,1)} %bitcast.24), channel_id=1, source_target_pairs={{0,24},{4,28},{8,0},{12,4},{16,8},{20,12},{24,16},{28,20},{1,25},{... | collective-permute-start | bytes 393224 | tf_op jit(solution)/shard_map/ppermute | solution.py:333
  26.9 9.2 %copy-start.7 = (f32[2,4,1024]{2,1,0:T(4,128)}, f32[2,4,1024]{2,1,0:T(4,128)S(1)}, u32[]{:S(2)}) copy-start(f32[2,4,1024]{2,1,0:T(4,128)S(1)} %pad_maximum_fusion.2.meta) | copy-start | bytes 98308
  26.9 9.1 %collective-permute-start.9 = (f32[2,4,1024]{2,1,0:T(4,128)S(1)}, f32[2,4,1024]{2,1,0:T(4,128)S(1)}, u32[]{:S(2)}, u32[]{:S(2)}) collective-permute-start(f32[2,4,1024]{2,1,0:T(4,128)S(1)} %pad_maximum_fusion.2.meta), channel_id=1, source_target_pairs={{0,1},{1,0},{2,3},{3,2},{4,5},{5,4},{6,7},{7,6},{8,9},{9,8},{10,11... | collective-permute-start | bytes 98312 | tf_op jit(solution)/shard_map/ppermute | solution.py:330
  29.1 7.0 %copy-start.11 = (bf16[256,256]{1,0:T(8,128)(2,1)}, bf16[256,256]{1,0:T(8,128)(2,1)S(1)}, u32[]{:S(2)}) copy-start(bf16[256,256]{1,0:T(8,128)(2,1)S(1)} %collective-permute-done.1.refs_1_) | copy-start | bytes 393220
  29.1 15.6 %collective-permute-start.6 = (bf16[256,256]{1,0:T(8,128)(2,1)S(1)}, bf16[256,256]{1,0:T(8,128)(2,1)S(1)}, u32[]{:S(2)}, u32[]{:S(2)}) collective-permute-start(bf16[256,256]{1,0:T(8,128)(2,1)S(1)} %collective-permute-done.1.refs_1_), channel_id=1, source_target_pairs={{0,4},{4,0},{8,12},{12,8},{16,20},{20,16},{24,28},{28,24},{1,5},{5... | collective-permute-start | bytes 393224 | tf_op jit(solution)/shard_map/ppermute | solution.py:327
  34.0 2.1 %copy-start.12 = (bf16[256,256]{1,0:T(8,128)(2,1)}, bf16[256,256]{1,0:T(8,128)(2,1)S(1)}, u32[]{:S(2)}) copy-start(bf16[256,256]{1,0:T(8,128)(2,1)S(1)} %collective-permute-done.2.refs_2_) | copy-start | bytes 393220
  34.0 10.7 %collective-permute-start.7 = (bf16[256,256]{1,0:T(8,128)(2,1)S(1)}, bf16[256,256]{1,0:T(8,128)(2,1)S(1)}, u32[]{:S(2)}, u32[]{:S(2)}) collective-permute-start(bf16[256,256]{1,0:T(8,128)(2,1)S(1)} %collective-permute-done.2.refs_2_), channel_id=1, source_target_pairs={{0,4},{4,0},{8,12},{12,8},{16,20},{20,16},{24,28},{28,24},{1,5},{5... | collective-permute-start | bytes 393224 | tf_op jit(solution)/shard_map/ppermute | solution.py:327
  34.6 1.5 %copy-start.13 = (bf16[256,256]{1,0:T(8,128)(2,1)}, bf16[256,256]{1,0:T(8,128)(2,1)S(1)}, u32[]{:S(2)}) copy-start(bf16[256,256]{1,0:T(8,128)(2,1)S(1)} %collective-permute-done.3.refs_3_) | copy-start | bytes 393220
  34.6 10.2 %collective-permute-start.8 = (bf16[256,256]{1,0:T(8,128)(2,1)S(1)}, bf16[256,256]{1,0:T(8,128)(2,1)S(1)}, u32[]{:S(2)}, u32[]{:S(2)}) collective-permute-start(bf16[256,256]{1,0:T(8,128)(2,1)S(1)} %collective-permute-done.3.refs_3_), channel_id=1, source_target_pairs={{0,4},{4,0},{8,12},{12,8},{16,20},{20,16},{24,28},{28,24},{1,5},{5... | collective-permute-start | bytes 393224 | tf_op jit(solution)/shard_map/ppermute | solution.py:327
  36.1 0.6 copy-start.17
  36.1 0.8 copy-start.9
  44.7 0.7 copy-start.14
  44.8 0.7 copy-start.15
  44.8 0.7 copy-start.16
  51.2 35.2 %collective-permute-start.15 = (bf16[256,2048]{1,0:T(8,128)(2,1)}, bf16[256,2048]{1,0:T(8,128)(2,1)S(1)}, u32[]{:S(2)}, u32[]{:S(2)}) collective-permute-start(bf16[256,2048]{1,0:T(8,128)(2,1)} %edge_grads.1.gt_ref), channel_id=1, source_target_pairs={{0,1},{1,0},{2,3},{3,2},{4,5},{5,4},{6,7},{7,6},{8,9},{9,8},{10,11... | collective-permute-start | bytes 3145736 | tf_op jit(solution)/shard_map/ppermute | solution.py:330
  60.9 7.2 %collective-permute-start.12 = (bf16[320,256]{1,0:T(8,128)(2,1)}, bf16[320,256]{1,0:T(8,128)(2,1)S(1)}, u32[]{:S(2)}, u32[]{:S(2)}) collective-permute-start(bf16[320,256]{1,0:T(8,128)(2,1)} %get-tuple-element.24), channel_id=1, source_target_pairs={{0,2},{1,3},{2,0},{3,1},{4,6},{5,7},{6,4},{7,5},{8,10},{9,11},{10,... | collective-permute-start | bytes 491528 | tf_op jit(solution)/shard_map/ppermute | solution.py:474
  62.4 5.7 %collective-permute-start.13 = (bf16[320,256]{1,0:T(8,128)(2,1)}, bf16[320,256]{1,0:T(8,128)(2,1)S(1)}, u32[]{:S(2)}, u32[]{:S(2)}) collective-permute-start(bf16[320,256]{1,0:T(8,128)(2,1)} %get-tuple-element.25), channel_id=1, source_target_pairs={{0,1},{1,0},{2,3},{3,2},{4,5},{5,4},{6,7},{7,6},{8,9},{9,8},{10,11... | collective-permute-start | bytes 491528 | tf_op jit(solution)/shard_map/ppermute | solution.py:474
  62.7 8.2 %collective-permute-start.14 = (bf16[320,256]{1,0:T(8,128)(2,1)}, bf16[320,256]{1,0:T(8,128)(2,1)S(1)}, u32[]{:S(2)}, u32[]{:S(2)}) collective-permute-start(bf16[320,256]{1,0:T(8,128)(2,1)} %get-tuple-element.26), channel_id=1, source_target_pairs={{0,3},{1,2},{2,1},{3,0},{4,7},{5,6},{6,5},{7,4},{8,11},{9,10},{10,... | collective-permute-start | bytes 491528 | tf_op jit(solution)/shard_map/ppermute | solution.py:474
  71.9 4.0 %collective-permute-start.23 = (bf16[64,256]{1,0:T(8,128)(2,1)S(1)}, bf16[64,256]{1,0:T(8,128)(2,1)S(1)}, u32[]{:S(2)}, u32[]{:S(2)}) collective-permute-start(bf16[64,256]{1,0:T(8,128)(2,1)S(1)} %slice.11), channel_id=1, source_target_pairs={{0,4},{4,0},{8,12},{12,8},{16,20},{20,16},{24,28},{28,24},{1,5},{5... | collective-permute-start | bytes 98312 | tf_op jit(solution)/shard_map/ppermute | solution.py:327
  75.9 5.9 %collective-permute-start.24 = (bf16[64,256]{1,0:T(8,128)(2,1)S(1)}, bf16[64,256]{1,0:T(8,128)(2,1)S(1)}, u32[]{:S(2)}, u32[]{:S(2)}) collective-permute-start(bf16[64,256]{1,0:T(8,128)(2,1)S(1)} %add_convert_fusion.4), channel_id=1, source_target_pairs={{0,16},{4,20},{8,24},{12,28},{16,0},{20,4},{24,8},{28,12},{1,17},{... | collective-permute-start | bytes 98312 | tf_op jit(solution)/shard_map/ppermute | solution.py:333
  77.9 5.7 %collective-permute-start.25 = (bf16[64,256]{1,0:T(8,128)(2,1)S(1)}, bf16[64,256]{1,0:T(8,128)(2,1)S(1)}, u32[]{:S(2)}, u32[]{:S(2)}) collective-permute-start(bf16[64,256]{1,0:T(8,128)(2,1)S(1)} %add_convert_fusion.4), channel_id=1, source_target_pairs={{0,8},{4,12},{8,16},{12,20},{16,24},{20,28},{24,0},{28,4},{1,9},{5... | collective-permute-start | bytes 98312 | tf_op jit(solution)/shard_map/ppermute | solution.py:333
  80.9 3.9 %collective-permute-start.26 = (bf16[64,256]{1,0:T(8,128)(2,1)S(1)}, bf16[64,256]{1,0:T(8,128)(2,1)S(1)}, u32[]{:S(2)}, u32[]{:S(2)}) collective-permute-start(bf16[64,256]{1,0:T(8,128)(2,1)S(1)} %add_convert_fusion.4), channel_id=1, source_target_pairs={{0,24},{4,28},{8,0},{12,4},{16,8},{20,12},{24,16},{28,20},{1,25},{... | collective-permute-start | bytes 98312 | tf_op jit(solution)/shard_map/ppermute | solution.py:333
  84.8 26.6 %copy-start.1 = (f32[64,256]{1,0:T(8,128)}, f32[64,256]{1,0:T(8,128)S(1)}, u32[]{:S(2)}) copy-start(f32[64,256]{1,0:T(8,128)S(1)} %add_add_fusion.refs_0_) | copy-start | bytes 196612
  84.8 23.9 %collective-permute-start.27 = (f32[64,256]{1,0:T(8,128)S(1)}, f32[64,256]{1,0:T(8,128)S(1)}, u32[]{:S(2)}, u32[]{:S(2)}) collective-permute-start(f32[64,256]{1,0:T(8,128)S(1)} %add_add_fusion.refs_0_), channel_id=1, source_target_pairs={{0,2},{1,3},{2,0},{3,1},{4,6},{5,7},{6,4},{7,5},{8,10},{9,11},{10,... | collective-permute-start | bytes 196616 | tf_op jit(solution)/shard_map/ppermute | solution.py:488
  86.4 25.0 %collective-permute-start.28 = (f32[64,256]{1,0:T(8,128)S(1)}, f32[64,256]{1,0:T(8,128)S(1)}, u32[]{:S(2)}, u32[]{:S(2)}) collective-permute-start(f32[64,256]{1,0:T(8,128)S(1)} %add_add_fusion.refs_0_), channel_id=1, source_target_pairs={{0,1},{1,0},{2,3},{3,2},{4,5},{5,4},{6,7},{7,6},{8,9},{9,8},{10,11... | collective-permute-start | bytes 196616 | tf_op jit(solution)/shard_map/ppermute | solution.py:488
  86.4 1.0 copy-start.8
  93.3 10.0 %copy-start.3 = (f32[240,256]{1,0:T(8,128)S(1)}, f32[240,256]{1,0:T(8,128)}, u32[]{:S(2)}) copy-start(f32[240,256]{1,0:T(8,128)} %get-tuple-element.29) | copy-start | bytes 737284
  93.3 8.5 %collective-permute-start.17 = (bf16[240,256]{1,0:T(8,128)(2,1)}, bf16[240,256]{1,0:T(8,128)(2,1)S(1)}, u32[]{:S(2)}, u32[]{:S(2)}) collective-permute-start(bf16[240,256]{1,0:T(8,128)(2,1)} %get-tuple-element.30), channel_id=1, source_target_pairs={{0,2},{1,3},{2,0},{3,1},{4,6},{5,7},{6,4},{7,5},{8,10},{9,11},{10,... | collective-permute-start | bytes 368648 | tf_op jit(solution)/shard_map/ppermute | solution.py:338
  93.8 9.6 %copy-start.2 = (f32[240,256]{1,0:T(8,128)S(1)}, f32[240,256]{1,0:T(8,128)}, u32[]{:S(2)}) copy-start(f32[240,256]{1,0:T(8,128)} %get-tuple-element.31) | copy-start | bytes 737284
  93.8 9.5 %collective-permute-start.19 = (bf16[240,256]{1,0:T(8,128)(2,1)}, bf16[240,256]{1,0:T(8,128)(2,1)S(1)}, u32[]{:S(2)}, u32[]{:S(2)}) collective-permute-start(bf16[240,256]{1,0:T(8,128)(2,1)} %get-tuple-element.32), channel_id=1, source_target_pairs={{0,2},{1,3},{2,0},{3,1},{4,6},{5,7},{6,4},{7,5},{8,10},{9,11},{10,... | collective-permute-start | bytes 368648 | tf_op jit(solution)/shard_map/ppermute | solution.py:338
  101.3 6.4 %collective-permute-start.21 = (bf16[240,256]{1,0:T(8,128)(2,1)}, bf16[240,256]{1,0:T(8,128)(2,1)S(1)}, u32[]{:S(2)}, u32[]{:S(2)}) collective-permute-start(bf16[240,256]{1,0:T(8,128)(2,1)} %get-tuple-element.34), channel_id=1, source_target_pairs={{0,2},{1,3},{2,0},{3,1},{4,6},{5,7},{6,4},{7,5},{8,10},{9,11},{10,... | collective-permute-start | bytes 368648 | tf_op jit(solution)/shard_map/ppermute | solution.py:338
  101.8 15.7 %collective-permute-start.16 = (bf16[240,256]{1,0:T(8,128)(2,1)}, bf16[240,256]{1,0:T(8,128)(2,1)S(1)}, u32[]{:S(2)}, u32[]{:S(2)}) collective-permute-start(bf16[240,256]{1,0:T(8,128)(2,1)} %get-tuple-element.28), channel_id=1, source_target_pairs={{0,2},{1,3},{2,0},{3,1},{4,6},{5,7},{6,4},{7,5},{8,10},{9,11},{10,... | collective-permute-start | bytes 368648 | tf_op jit(solution)/shard_map/ppermute | solution.py:338
  103.3 14.2 %collective-permute-start.18 = (bf16[240,256]{1,0:T(8,128)(2,1)S(1)}, bf16[240,256]{1,0:T(8,128)(2,1)S(1)}, u32[]{:S(2)}, u32[]{:S(2)}) collective-permute-start(bf16[240,256]{1,0:T(8,128)(2,1)S(1)} %add_convert_fusion.3), channel_id=1, source_target_pairs={{0,8},{4,12},{8,16},{12,20},{16,24},{20,28},{24,0},{28,4},{1,9},{5... | collective-permute-start | bytes 368648 | tf_op jit(solution)/shard_map/ppermute | solution.py:333
  107.7 9.8 %collective-permute-start.20 = (bf16[240,256]{1,0:T(8,128)(2,1)S(1)}, bf16[240,256]{1,0:T(8,128)(2,1)S(1)}, u32[]{:S(2)}, u32[]{:S(2)}) collective-permute-start(bf16[240,256]{1,0:T(8,128)(2,1)S(1)} %add_convert_fusion.2), channel_id=1, source_target_pairs={{0,16},{4,20},{8,24},{12,28},{16,0},{20,4},{24,8},{28,12},{1,17},{... | collective-permute-start | bytes 368648 | tf_op jit(solution)/shard_map/ppermute | solution.py:333
  108.7 6.4 %copy-start.4 = (f32[64,256]{1,0:T(8,128)}, f32[64,256]{1,0:T(8,128)S(1)}, u32[]{:S(2)}) copy-start(f32[64,256]{1,0:T(8,128)S(1)} %collective-permute-done.27.refs_1_) | copy-start | bytes 196612
  108.7 8.8 %collective-permute-start.22 = (bf16[240,256]{1,0:T(8,128)(2,1)S(1)}, bf16[240,256]{1,0:T(8,128)(2,1)S(1)}, u32[]{:S(2)}, u32[]{:S(2)}) collective-permute-start(bf16[240,256]{1,0:T(8,128)(2,1)S(1)} %add_convert_fusion.1), channel_id=1, source_target_pairs={{0,24},{4,28},{8,0},{12,4},{16,8},{20,12},{24,16},{28,20},{1,25},{... | collective-permute-start | bytes 368648 | tf_op jit(solution)/shard_map/ppermute | solution.py:333
  111.4 3.8 %copy-start.5 = (f32[64,256]{1,0:T(8,128)}, f32[64,256]{1,0:T(8,128)S(1)}, u32[]{:S(2)}) copy-start(f32[64,256]{1,0:T(8,128)S(1)} %collective-permute-done.28.refs_2_) | copy-start | bytes 196612
  111.4 3.8 %collective-permute-start.29 = (f32[64,256]{1,0:T(8,128)S(1)}, f32[64,256]{1,0:T(8,128)S(1)}, u32[]{:S(2)}, u32[]{:S(2)}) collective-permute-start(f32[64,256]{1,0:T(8,128)S(1)} %add_add_fusion.refs_0_), channel_id=1, source_target_pairs={{0,3},{1,2},{2,1},{3,0},{4,7},{5,6},{6,5},{7,4},{8,11},{9,10},{10,... | collective-permute-start | bytes 196616 | tf_op jit(solution)/shard_map/ppermute | solution.py:488
  115.2 0.6 copy-start.6

commit v3 on v2

--- a/solution.py
+++ b/solution.py
@@ -13,7 +13,7 @@
 F32 = jnp.float32
 BF16 = jnp.bfloat16
 I32 = jnp.int32
-VMEM_LIMIT = 56 * 1024 * 1024
+VMEM_LIMIT = 32 * 1024 * 1024
 
 
 def round_up(value, unit):
@@ -177,60 +177,57 @@
 def forward_kernel(
     sizes, place, meta, gt_ref, xt_ref, ct_ref, bases_ref, *refs
 ):
-    cols, shard, span, heads, padded = sizes
+    cols, shard, span, heads, padded, group = sizes
     outs = refs[:cols]
     total, inner, wide, coef_sum = refs[cols:]
     count = cols // PAIR
     y, core = place[2], place[3]
     edges = meta.shape[-1]
     width = bases_ref.shape[-1]
-    group = bases_ref.shape[0]
-    step = pl.program_id(0)
-
-    @pl.when(step == 0)
-    def _():
-        total[...] = jnp.zeros_like(total)
-        inner[...] = jnp.zeros_like(inner)
-
-    stacked = bases_ref[...].reshape(group * width, width)
-    for index in range(edges // span):
-        at = slice(index * span, (index + 1) * span)
-        backed = dot(stacked, gt_ref[:, at])
-        rows = xt_ref[0, :, at].astype(F32)
-        sums = total[:, at]
-        for t in range(group):
-            base = step * group + t
-            mine = backed[t * width : (t + 1) * width]
-            sums = sums + ct_ref[0, pl.ds(base, 1), at] * mine
-            inner[pl.ds(base, 1), at] = jnp.sum(mine * rows, axis=0, keepdims=True)
-        total[:, at] = sums
-
-    @pl.when(step == pl.num_programs(0) - 1)
-    def _():
-        ids = meta[0, 0:1, :].astype(I32)
-        owner, local = split_index(ids, shard)
-        owner_y, owner_core = split_index(owner, PAIR)
-        slot = (owner_core ^ core) * count + wrap(owner_y - y, count)
-        values = total[...].astype(BF16)
-        for at in range(cols):
-            hot = one_hot(jnp.where(slot == at, local, -1), shard)
-            outs[at][0:shard, :] = dot_t(hot, values).astype(BF16)
-        high, low = split_index(meta[0, 2:3, :].astype(I32), LANES)
-        for head in range(heads):
-            wide[head * padded : (head + 1) * padded, :] = jnp.where(
-                high == head, inner[...], 0.0
-            ).astype(BF16)
-        coef_sum[...] = dot_t(wide[...], one_hot(low, LANES))
-        share = heads * padded // cols
-        half = share // 2
-        for far in range(PAIR):
-            for sy in range(count):
-                target = (y + sy) % count * PAIR + (core ^ far)
-                for side in range(2):
-                    rows = coef_sum[pl.ds(pl.multiple_of(target * share + side * half, 8), half), :]
-                    outs[far * count + sy][
-                        shard : shard + half, side * LANES : (side + 1) * LANES
-                    ] = rows.astype(BF16)
+    total[...] = jnp.zeros_like(total)
+    inner[...] = jnp.zeros_like(inner)
+
+    def step(number, carry):
+        stacked = bases_ref[pl.ds(number * group, group)].reshape(group * width, width)
+        for index in range(edges // span):
+            at = slice(index * span, (index + 1) * span)
+            backed = dot(stacked, gt_ref[:, at])
+            rows = xt_ref[0, :, at].astype(F32)
+            sums = total[:, at]
+            for t in range(group):
+                base = number * group + t
+                mine = backed[t * width : (t + 1) * width]
+                sums = sums + ct_ref[0, pl.ds(base, 1), at] * mine
+                inner[pl.ds(base, 1), at] = jnp.sum(mine * rows, axis=0, keepdims=True)
+            total[:, at] = sums
+        return carry
+
+    lax.fori_loop(0, bases_ref.shape[0] // group, step, 0)
+
+    ids = meta[0, 0:1, :].astype(I32)
+    owner, local = split_index(ids, shard)
+    owner_y, owner_core = split_index(owner, PAIR)
+    slot = (owner_core ^ core) * count + wrap(owner_y - y, count)
+    values = total[...].astype(BF16)
+    for at in range(cols):
+        hot = one_hot(jnp.where(slot == at, local, -1), shard)
+        outs[at][0:shard, :] = dot_t(hot, values).astype(BF16)
+    high, low = split_index(meta[0, 2:3, :].astype(I32), LANES)
+    for head in range(heads):
+        wide[head * padded : (head + 1) * padded, :] = jnp.where(
+            high == head, inner[...], 0.0
+        ).astype(BF16)
+    coef_sum[...] = dot_t(wide[...], one_hot(low, LANES))
+    share = heads * padded // cols
+    half = share // 2
+    for far in range(PAIR):
+        for sy in range(count):
+            target = (y + sy) % count * PAIR + (core ^ far)
+            for side in range(2):
+                rows = coef_sum[pl.ds(pl.multiple_of(target * share + side * half, 8), half), :]
+                outs[far * count + sy][
+                    shard : shard + half, side * LANES : (side + 1) * LANES
+                ] = rows.astype(BF16)
 
 
 def basis_kernel(sizes, place, gt_ref, gt_core, xt_ref, ct_ref, *refs):
@@ -338,10 +335,9 @@
         return lax.ppermute(value, "col", [(c, (c + by * PAIR) % cols) for c in range(cols)])
 
     own_dest = dest_grad[0]
-    dest = [own_dest] + [turn_z(own_dest, s) for s in range(1, a_count)]
-    across = [flip_x(own_dest)]
+    turned = [turn_z(own_dest, s) for s in range(1, a_count)]
+    across_own = flip_x(own_dest)
     near = flip_x(node_feats)
-
     meta = pl.pallas_call(
         prepare_kernel,
         out_shape=jax.ShapeDtypeStruct((4, edges), F32),
@@ -350,12 +346,15 @@
         name="edge_table",
     )(block_fill, src_ids, dst_ids, rel_ids, edge_norm)
     meta = jnp.stack([meta, flip_x(meta)])
+    feats, turned[0] = lax.optimization_barrier((jnp.stack([node_feats, near]), turned[0]))
+    feats = jnp.stack([feats] + [turn_y(feats, s) for s in range(1, y_count)])
+    across = [across_own, flip_x(turned[0])]
+    feats, meta, across[0], across[1], *turned[1:] = lax.optimization_barrier(
+        (feats, meta, *across, *turned[1:])
+    )
+    dest = [own_dest] + turned
+    across += [flip_x(value) for value in turned[1:]]
     meta_core = flip_core(meta)
-
-    feats = jnp.stack([node_feats, near])
-    feats, across[0] = lax.optimization_barrier((feats, across[0]))
-    feats = jnp.stack([feats] + [turn_y(feats, s) for s in range(1, y_count)])
-    across += [flip_x(value) for value in dest[1:]]
     feats_core = flip_core(feats)
 
     xt, ct = call(
@@ -388,38 +387,24 @@
 
     group = max(g for g in range(1, 6) if basis_count % g == 0)
     share_rows = heads * padded // cols // 2
-    packed = pl.pallas_call(
-        functools.partial(forward_kernel, (cols, shard, span, heads, padded)),
-        grid=(basis_count // group,),
-        in_specs=[
-            smem(),
-            pl.BlockSpec(meta.shape, lambda s: (0, 0, 0)),
-            pl.BlockSpec((width, edges), lambda s: (0, 0)),
-            pl.BlockSpec((1, width, edges), lambda s: (0, 0, 0)),
-            pl.BlockSpec((1, padded, edges), lambda s: (0, 0, 0)),
-            pl.BlockSpec((group, width, width), lambda s: (s, 0, 0)),
-        ],
-        out_specs=[pl.BlockSpec((shard + share_rows, width), lambda s: (0, 0))] * cols,
-        out_shape=[jax.ShapeDtypeStruct((shard + share_rows, width), BF16)] * cols,
-        scratch_shapes=[
+    packed = call(
+        functools.partial(forward_kernel, (cols, shard, span, heads, padded, group)),
+        [jax.ShapeDtypeStruct((shard + share_rows, width), BF16)] * cols,
+        5,
+        [
             pltpu.VMEM((width, edges), F32),
             pltpu.VMEM((padded, edges), F32),
             pltpu.VMEM((heads * padded, edges), BF16),
             pltpu.VMEM((heads * padded, LANES), F32),
         ],
-        compiler_params=pltpu.CompilerParams(vmem_limit_bytes=VMEM_LIMIT),
-        cost_estimate=pl.CostEstimate(
-            flops=2 * edges * width * width * basis_count,
-            bytes_accessed=bases.size * 2,
-            transcendentals=0,
-        ),
-        name="backed_sums",
+        2 * edges * width * width * basis_count,
+        "backed_sums",
     )(place, meta, gt, xt, ct, bases)
 
     block = basis_count * width // (rows_total * cols)
     cover = block if block % TILE == 0 else round_up(block, TILE) + TILE
 
-    def basis_blocks(turns):
+    def basis_blocks(place, turns):
         count = len(turns) * y_count
         return call(
             functools.partial(
@@ -442,50 +427,51 @@
             "basis_terms",
         )(place, gt, gt_core, xt, ct)
 
-    def over_y(turns):
-        blocks = basis_blocks(turns)
-        for order, sz in enumerate(turns):
-            mine = blocks[order * y_count : (order + 1) * y_count]
-            value = mine[0]
-            for sy in range(1, y_count):
-                value = value + turn_y(mine[sy], sy).astype(F32)
-            sums[sz] = value
-
-    sums = {}
+    def to_col(value, far, sy):
+        return lax.ppermute(
+            value,
+            "col",
+            [(c, (c // PAIR + sy) % y_count * PAIR + (c % PAIR ^ far)) for c in range(cols)],
+        )
+
+    def after(value, other):
+        return lax.optimization_barrier((value, other))[0]
+
+    others = [(far, sy) for far in range(PAIR) for sy in range(y_count) if far or sy]
+    received = [to_col(packed[far * y_count + sy], far, sy) for far, sy in others]
+
+    sums, passed, marks = {}, [], []
     order = tuple(range(1, a_count)) + (0,)
-    half = a_count // 2
-    over_y(order[:half])
-    over_y(order[half:])
+    for at, sz in enumerate(order):
+        where = place
+        if at >= 2:
+            where = after(where, passed[at - 2])
+        blocks = basis_blocks(where, (sz,))
+        value = blocks[0]
+        arrived = [turn_y(blocks[sy], sy) for sy in range(1, y_count)]
+        for piece in arrived:
+            value = value + piece.astype(F32)
+        sums[sz] = turn_z(value.astype(BF16), sz) if sz else value
+        passed.append(arrived[-1] if arrived else blocks[0])
+        marks.append(blocks[0])
+    joined = packed[0].astype(F32)
+    for value in received:
+        joined = joined + after(value, marks[min(1, a_count - 1)]).astype(F32)
     basis_sum = sums[0]
     for sz in range(1, a_count):
-        basis_sum = basis_sum + turn_z(sums[sz].astype(BF16), sz).astype(F32)
+        basis_sum = basis_sum + sums[sz].astype(F32)
     if cover != block:
         owner = i * cols + j
         basis_sum = lax.dynamic_slice_in_dim(basis_sum, owner * block % TILE, block, axis=0)
     basis_grad = basis_sum / cols
 
-    joined = packed[0].astype(F32)
-    for far in range(PAIR):
-        for sy in range(y_count):
-            if far or sy:
-                target = [
-                    (c, ((c // PAIR + sy) % y_count) * PAIR + (c % PAIR ^ far)) for c in range(cols)
-                ]
-                joined = joined + lax.ppermute(packed[far * y_count + sy], "col", target).astype(
-                    F32
-                )
     node_grad = joined[:shard].astype(BF16)
     coef_part = joined[shard:]
     low = coef_part.astype(BF16)
-    low = (low.astype(F32) + flip_x(low).astype(F32)).astype(BF16)
-    coef_part = tree_sum([low.astype(F32)] + [turn_z(low, s).astype(F32) for s in range(1, a_count)])
-    shares = []
-    for far in range(PAIR):
-        for sy in range(y_count):
-            target = [
-                (c, ((c // PAIR + sy) % y_count) * PAIR + (c % PAIR ^ far)) for c in range(cols)
-            ]
-            shares.append(lax.ppermute(coef_part, "col", target) if far or sy else coef_part)
+    low = (low.astype(F32) + after(flip_x(low), marks[max(a_count - 2, 0)]).astype(F32)).astype(BF16)
+    around = [after(turn_z(low, s), marks[-1]).astype(F32) for s in range(1, a_count)]
+    coef_part = tree_sum([low.astype(F32)] + around)
+    shares = [coef_part] + [to_col(coef_part, far, sy) for far, sy in others]
     coef_grad = call(
         functools.partial(coef_kernel, (cols, heads, padded, cols)),
         jax.ShapeDtypeStruct((basis_count, relation_count), F32),

time: 120 us -> 92.4 us (0.77)
  waiting for transfers between devices: 38.4 us -> 24.1 us
  Pallas kernels: 38.3 us -> 29 us
  other arithmetic: 6.16 us -> 2.76 us
  local copies, waits for them, and re-layouts: 3.76 us -> 2.49 us
    ppermute x5, waiting for transfers between devices: 9.95 us -> 2.9 us  [turn_y(): lax.ppermute(value, 'col', [(c, (c + by * PAIR) % cols) for c in range(co...]
    ppermute x7, waiting for transfers between devices: 8.88 us -> 2.83 us  [flip_x(): return lax.ppermute(value, 'row', [(r, r ^ 1) for r in range(rows_total)])]
    pallas_call x2 -> x4, Pallas kernels: 11.8 us -> 8.48 us  [basis_blocks(): call(functools.partial(basis_kernel, (rows_total, cols, block, cover // T...]
    ppermute x9, waiting for transfers between devices: 8.77 us -> 5.42 us  [turn_z(): lax.ppermute(value, 'row', [(r, (r + by * PAIR) % rows_total) for r in ra...]
    pallas_call x1, Pallas kernels: 7.87 us -> 5.65 us  [on_device(): call(functools.partial(source_kernel, (cols, shard, span, heads, padded,...]
    ppermute x6, waiting for transfers between devices: 10.8 us -> 13 us  [to_col(): lax.ppermute(value, 'col', [(c, (c // PAIR + sy) % y_count * PAIR + (c %...]
    pallas_call x1, Pallas kernels: 5.74 us -> 4 us  [on_device(): call(functools.partial(grad_kernel, (rows_total, dest_shard, span)), jax....]
    ppermute x7, starting transfers between devices: 7.76 us -> 9.36 us  [flip_x(): return lax.ppermute(value, 'row', [(r, r ^ 1) for r in range(rows_total)])]
  transfers between devices with their start and end apart: 30 -> 30, of which waited for: 12 -> 9; matrix products, arithmetic and copies ran while one was open for 4% -> 3% of each run, Pallas kernels for 27% -> 25%
where the time goes in v3:
time: 92.4 us; the launch traced here: 92.1 us
  starting transfers between devices  32.8 us (35%)
  Pallas kernels  29 us (31%)
  waiting for transfers between devices  24.1 us (26%)
  other arithmetic  2.76 us (3%)
  local copies, waits for them, and re-layouts  2.49 us (3%)
    ppermute x9, starting transfers between devices, turn_z(): lax.ppermute(value, 'row', [(r, (r + by * PAIR) % rows_total) for r in ra...  14.5 us
    ppermute x6, waiting for transfers between devices, to_col(): lax.ppermute(value, 'col', [(c, (c // PAIR + sy) % y_count * PAIR + (c %...  13 us
    ppermute x7, starting transfers between devices, flip_x(): return lax.ppermute(value, 'row', [(r, r ^ 1) for r in range(rows_total)])  9.36 us
    pallas_call x4, Pallas kernels, basis_blocks(): call(functools.partial(basis_kernel, (rows_total, cols, block, cover // T...  8.48 us
    pallas_call x1, Pallas kernels, on_device(): call(functools.partial(forward_kernel, (cols, shard, span, heads, padded,...  8.2 us
    pallas_call x1, Pallas kernels, on_device(): call(functools.partial(source_kernel, (cols, shard, span, heads, padded,...  5.65 us
    ppermute x5, starting transfers between devices, turn_y(): lax.ppermute(value, 'col', [(c, (c + by * PAIR) % cols) for c in range(co...  5.64 us
    ppermute x9, waiting for transfers between devices, turn_z(): lax.ppermute(value, 'row', [(r, (r + by * PAIR) % rows_total) for r in ra...  5.42 us
  transfers between devices with their start and end apart: 30, of which 9 were waited for; matrix products, arithmetic and copies ran while one was open for 3% of the time, Pallas kernels for 25%

profile of v3, /device:TPU:0, one launch (start us, length us, event | category | flops | bytes accessed | tf_op | source)
XLA Modules:
  0.0 92.1 jit_solution(14685932451230077135)
XLA Ops:
  0.6 3.0 %collective-permute-start = (bf16[256,256]{1,0:T(8,128)(2,1)}, bf16[256,256]{1,0:T(8,128)(2,1)S(1)}, u32[]{:S(2)}, u32[]{:S(2)}) collective-permute-start(bf16[256,256]{1,0:T(8,128)(2,1)} %param.9), channel_id=1, source_target_pairs={{0,4},{4,0},{8,12},{12,8},{16,20},{20,16},{24,28},{28,24},{1,5},{5... | collective-permute-start | bytes 393224 | tf_op jit(solution)/shard_map/ppermute | solution.py:324
  3.6 1.6 %collective-permute-start.1 = (bf16[256,256]{1,0:T(8,128)(2,1)}, bf16[256,256]{1,0:T(8,128)(2,1)S(1)}, u32[]{:S(2)}, u32[]{:S(2)}) collective-permute-start(bf16[256,256]{1,0:T(8,128)(2,1)} %bitcast.14), channel_id=1, source_target_pairs={{0,8},{4,12},{8,16},{12,20},{16,24},{20,28},{24,0},{28,4},{1,9},{5... | collective-permute-start | bytes 393224 | tf_op jit(solution)/shard_map/ppermute | solution.py:330
  5.2 2.1 %collective-permute-done = bf16[256,256]{1,0:T(8,128)(2,1)S(1)} collective-permute-done((bf16[256,256]{1,0:T(8,128)(2,1)}, bf16[256,256]{1,0:T(8,128)(2,1)S(1)}, u32[]{:S(2)}, u32[]{:S(2)}) %collective-permute-start) | collective-permute-done | bytes 131104 | tf_op jit(solution)/shard_map/ppermute | solution.py:324
  7.3 0.9 %pad_maximum_fusion.1 = bf16[2,256,256]{2,1,0:T(8,128)(2,1)S(1)} fusion(bf16[1,256,256]{2,1,0:T(8,128)(2,1)S(1)} %bitcast.24, bf16[1,256,256]{2,1,0:T(8,128)(2,1)} %bitcast.23), kind=kLoop, calls=%fused_computation.2 | loop fusion | flops 131072 | bytes 524288 | tf_op jit(solution)/shard_map/stack | solution.py:349
  8.3 2.4 %collective-permute-done.1.refs_1_ = bf16[256,256]{1,0:T(8,128)(2,1)S(1)} collective-permute-done((bf16[256,256]{1,0:T(8,128)(2,1)}, bf16[256,256]{1,0:T(8,128)(2,1)S(1)}, u32[]{:S(2)}, u32[]{:S(2)}) %collective-permute-start.1) | collective-permute-done | bytes 131104 | tf_op jit(solution)/shard_map/ppermute | solution.py:330
  10.7 1.5 %collective-permute-start.2 = (bf16[2,256,256]{2,1,0:T(8,128)(2,1)S(1)}, bf16[2,256,256]{2,1,0:T(8,128)(2,1)S(1)}, u32[]{:S(2)}, u32[]{:S(2)}) collective-permute-start(bf16[2,256,256]{2,1,0:T(8,128)(2,1)S(1)} %pad_maximum_fusion.1), channel_id=1, source_target_pairs={{0,2},{1,3},{2,0},{3,1},{4,6},{5,7},{6,4},{7,5},{8,10},{9,11},{10,... | collective-permute-start | bytes 786440 | tf_op jit(solution)/shard_map/ppermute | solution.py:335
  12.2 1.4 %edge_table.1 = f32[4,1024]{1,0:T(4,128)} custom-call(s32[1,1,8]{2,1,0:T(1,128)} %fills.1, s32[1,1,1024]{2,1,0:T(1,128)} %src.1, s32[1,1,1024]{2,1,0:T(1,128)} %dst.1, s32[1,1,1024]{2,1,0:T(1,128)} %rel.1, f32[1,1,1024]{2,1,0:T(1,128)} %norm.1), custom_call_target="tpu_custom_call" | custom-call | tf_op jit(solution)/shard_map/edge_table/pallas_call | solution.py:341
  13.6 0.5 collective-permute-start.3
  14.1 1.5 %collective-permute-start.4 = (bf16[256,256]{1,0:T(8,128)(2,1)}, bf16[256,256]{1,0:T(8,128)(2,1)S(1)}, u32[]{:S(2)}, u32[]{:S(2)}) collective-permute-start(bf16[256,256]{1,0:T(8,128)(2,1)} %bitcast.15), channel_id=1, source_target_pairs={{0,4},{4,0},{8,12},{12,8},{16,20},{20,16},{24,28},{28,24},{1,5},{5... | collective-permute-start | bytes 393224 | tf_op jit(solution)/shard_map/ppermute | solution.py:324
  15.6 0.7 collective-permute-start.6
  16.4 1.3 %collective-permute-start.7 = (bf16[256,256]{1,0:T(8,128)(2,1)}, bf16[256,256]{1,0:T(8,128)(2,1)S(1)}, u32[]{:S(2)}, u32[]{:S(2)}) collective-permute-start(bf16[256,256]{1,0:T(8,128)(2,1)} %bitcast.17), channel_id=1, source_target_pairs={{0,24},{4,28},{8,0},{12,4},{16,8},{20,12},{24,16},{28,20},{1,25},{... | collective-permute-start | bytes 393224 | tf_op jit(solution)/shard_map/ppermute | solution.py:330
  17.7 1.3 %collective-permute-start.5 = (bf16[256,256]{1,0:T(8,128)(2,1)S(1)}, bf16[256,256]{1,0:T(8,128)(2,1)S(1)}, u32[]{:S(2)}, u32[]{:S(2)}) collective-permute-start(bf16[256,256]{1,0:T(8,128)(2,1)S(1)} %collective-permute-done.1.refs_1_), channel_id=1, source_target_pairs={{0,4},{4,0},{8,12},{12,8},{16,20},{20,16},{24,28},{28,24},{1,5},{5... | collective-permute-start | bytes 393224 | tf_op jit(solution)/shard_map/ppermute | solution.py:324
  19.0 0.7 pad_maximum_fusion.2.meta
  19.8 0.7 collective-permute-done.4.refs_4_
  20.5 3.0 %collective-permute-done.6.refs_2_ = bf16[256,256]{1,0:T(8,128)(2,1)S(1)} collective-permute-done((bf16[256,256]{1,0:T(8,128)(2,1)}, bf16[256,256]{1,0:T(8,128)(2,1)S(1)}, u32[]{:S(2)}, u32[]{:S(2)}) %collective-permute-start.6) | collective-permute-done | bytes 131104 | tf_op jit(solution)/shard_map/ppermute | solution.py:330
  23.5 0.5 collective-permute-start.10
  24.1 1.0 %collective-permute-start.8 = (bf16[256,256]{1,0:T(8,128)(2,1)S(1)}, bf16[256,256]{1,0:T(8,128)(2,1)S(1)}, u32[]{:S(2)}, u32[]{:S(2)}) collective-permute-start(bf16[256,256]{1,0:T(8,128)(2,1)S(1)} %collective-permute-done.6.refs_2_), channel_id=1, source_target_pairs={{0,4},{4,0},{8,12},{12,8},{16,20},{20,16},{24,28},{28,24},{1,5},{5... | collective-permute-start | bytes 393224 | tf_op jit(solution)/shard_map/ppermute | solution.py:324
  25.1 1.1 %collective-permute-start.9 = (bf16[256,256]{1,0:T(8,128)(2,1)S(1)}, bf16[256,256]{1,0:T(8,128)(2,1)S(1)}, u32[]{:S(2)}, u32[]{:S(2)}) collective-permute-start(bf16[256,256]{1,0:T(8,128)(2,1)S(1)} %collective-permute-done.7.refs_3_), channel_id=1, source_target_pairs={{0,4},{4,0},{8,12},{12,8},{16,20},{20,16},{24,28},{28,24},{1,5},{5... | collective-permute-start | bytes 393224 | tf_op jit(solution)/shard_map/ppermute | solution.py:324
  26.1 0.9 copy-done.1
  27.0 0.9 copy-done.2
  27.9 5.7 %source_rows.1 = (bf16[4,256,1024]{2,1,0:T(8,128)(2,1)S(1)}, f32[4,32,1024]{2,1,0:T(8,128)S(1)}) custom-call(s32[4]{0:T(128)S(1)} %pad_add_fusion.place, f32[2,4,1024]{2,1,0:T(4,128)S(1)} %pad_maximum_fusion.2.meta, f32[2,4,1024]{2,1,0:T(4,128)S(1)} %collective-permute-done.10.meta_core, bf16[2,2,256,256]{3,2,1,0:T(8,128)(2,1)S(1)} %pad_maximum_fusion.feats, ...), custom_call_target="tpu_custom_call" | custom-call | flops 2147483648 | bytes 4194304 | tf_op jit(solution)/shard_map/source_rows/pallas_call | solution.py:360
  33.6 4.0 %edge_grads.1.gt_ref = bf16[256,2048]{1,0:T(8,128)(2,1)S(1)} custom-call(s32[4]{0:T(128)S(1)} %pad_add_fusion.place, f32[2,4,1024]{2,1,0:T(4,128)S(1)} %pad_maximum_fusion.2.meta, bf16[256,256]{1,0:T(8,128)(2,1)S(1)} %bitcast.19, bf16[256,256]{1,0:T(8,128)(2,1)S(1)} %collective-permute-done.1.refs_1_, bf16[256,256]{1,0:T(8,128)(2,1)S(1)} %collective-permute-done.6.refs_2_, ...), custom_call_target="tpu_custom_call" | custom-call | flops 2147483648 | bytes 4194304 | tf_op jit(solution)/shard_map/edge_grads/pallas_call | solution.py:377
  37.7 8.2 %backed_sums.1 = (bf16[320,256]{1,0:T(8,128)(2,1)S(1)}, bf16[320,256]{1,0:T(8,128)(2,1)S(1)}, bf16[320,256]{1,0:T(8,128)(2,1)S(1)}, bf16[320,256]{1,0:T(8,128)(2,1)S(1)}) custom-call(s32[4]{0:T(128)S(1)} %pad_add_fusion.place, f32[2,4,1024]{2,1,0:T(4,128)S(1)} %pad_maximum_fusion.2.meta, bf16[256,2048]{1,0:T(8,128)(2,1)S(1)} %edge_grads.1.gt_ref, ...), custom_call_target="tpu_custom_call" | custom-call | flops 4026531840 | bytes 4194304 | tf_op jit(solution)/shard_map/backed_sums/pallas_call | solution.py:390
  45.9 0.6 collective-permute-start.15
  46.6 1.5 %collective-permute-start.12 = (bf16[320,256]{1,0:T(8,128)(2,1)S(1)}, bf16[320,256]{1,0:T(8,128)(2,1)S(1)}, u32[]{:S(2)}, u32[]{:S(2)}) collective-permute-start(bf16[320,256]{1,0:T(8,128)(2,1)S(1)} %get-tuple-element.45), channel_id=1, source_target_pairs={{0,2},{1,3},{2,0},{3,1},{4,6},{5,7},{6,4},{7,5},{8,10},{9,11},{10,... | collective-permute-start | bytes 491528 | tf_op jit(solution)/shard_map/ppermute | solution.py:431
  48.2 2.1 %basis_terms.4 = (f32[240,256]{1,0:T(8,128)S(1)}, bf16[240,256]{1,0:T(8,128)(2,1)S(1)}) custom-call(s32[4]{0:T(128)S(1)} %pad_add_fusion.place, bf16[256,2048]{1,0:T(8,128)(2,1)S(1)} %edge_grads.1.gt_ref, bf16[256,2048]{1,0:T(8,128)(2,1)S(1)} %collective-permute-done.13.gt_core, bf16[4,256,1024]{2,1,0:T(8,128)(2,1)S(1)} %get-tuple-element.42.refs_8_.xt_ref, ...), custom_call_target="tpu_custom_call" | custom-call | flops 1006632960 | bytes 4194304 | tf_op jit(solution)/shard_map/basis_terms/pallas_call | solution.py:409
  50.3 1.6 %collective-permute-done.15 = bf16[320,256]{1,0:T(8,128)(2,1)S(1)} collective-permute-done((bf16[320,256]{1,0:T(8,128)(2,1)S(1)}, bf16[320,256]{1,0:T(8,128)(2,1)S(1)}, u32[]{:S(2)}, u32[]{:S(2)}) %collective-permute-start.15) | collective-permute-done | bytes 163872 | tf_op jit(solution)/shard_map/ppermute | solution.py:431
  51.9 4.1 %collective-permute-done.12 = bf16[320,256]{1,0:T(8,128)(2,1)S(1)} collective-permute-done((bf16[320,256]{1,0:T(8,128)(2,1)S(1)}, bf16[320,256]{1,0:T(8,128)(2,1)S(1)}, u32[]{:S(2)}, u32[]{:S(2)}) %collective-permute-start.12) | collective-permute-done | bytes 163872 | tf_op jit(solution)/shard_map/ppermute | solution.py:431
  56.0 2.1 %basis_terms.6 = (f32[240,256]{1,0:T(8,128)S(1)}, bf16[240,256]{1,0:T(8,128)(2,1)S(1)}) custom-call(s32[4]{0:T(128)S(1)} %pad_add_fusion.place, bf16[256,2048]{1,0:T(8,128)(2,1)S(1)} %edge_grads.1.gt_ref, bf16[256,2048]{1,0:T(8,128)(2,1)S(1)} %collective-permute-done.13.gt_core, bf16[4,256,1024]{2,1,0:T(8,128)(2,1)S(1)} %get-tuple-element.42.refs_8_.xt_ref, ...), custom_call_target="tpu_custom_call" | custom-call | flops 1006632960 | bytes 4194304 | tf_op jit(solution)/shard_map/basis_terms/pallas_call | solution.py:409
  58.1 0.6 collective-permute-start.18
  58.7 1.5 %collective-permute-start.16 = (bf16[240,256]{1,0:T(8,128)(2,1)S(1)}, bf16[240,256]{1,0:T(8,128)(2,1)S(1)}, u32[]{:S(2)}, u32[]{:S(2)}) collective-permute-start(bf16[240,256]{1,0:T(8,128)(2,1)S(1)} %get-tuple-element.52), channel_id=1, source_target_pairs={{0,2},{1,3},{2,0},{3,1},{4,6},{5,7},{6,4},{7,5},{8,10},{9,11},{10,... | collective-permute-start | bytes 368648 | tf_op jit(solution)/shard_map/ppermute | solution.py:335
  60.3 1.0 %collective-permute-start.23 = (bf16[64,256]{1,0:T(8,128)(2,1)S(1)}, bf16[64,256]{1,0:T(8,128)(2,1)S(1)}, u32[]{:S(2)}, u32[]{:S(2)}) collective-permute-start(bf16[64,256]{1,0:T(8,128)(2,1)S(1)} %slice.11), channel_id=1, source_target_pairs={{0,4},{4,0},{8,12},{12,8},{16,20},{20,16},{24,28},{28,24},{1,5},{5... | collective-permute-start | bytes 98312 | tf_op jit(solution)/shard_map/ppermute | solution.py:324
  61.4 2.9 %collective-permute-done.18 = bf16[240,256]{1,0:T(8,128)(2,1)S(1)} collective-permute-done((bf16[240,256]{1,0:T(8,128)(2,1)S(1)}, bf16[240,256]{1,0:T(8,128)(2,1)S(1)}, u32[]{:S(2)}, u32[]{:S(2)}) %collective-permute-start.18) | collective-permute-done | bytes 122912 | tf_op jit(solution)/shard_map/ppermute | solution.py:335
  64.3 2.1 %basis_terms.7 = (f32[240,256]{1,0:T(8,128)S(1)}, bf16[240,256]{1,0:T(8,128)(2,1)S(1)}) custom-call(s32[4]{0:T(128)S(1)} %pad_add_fusion.place, bf16[256,2048]{1,0:T(8,128)(2,1)S(1)} %edge_grads.1.gt_ref, bf16[256,2048]{1,0:T(8,128)(2,1)S(1)} %collective-permute-done.13.gt_core, bf16[4,256,1024]{2,1,0:T(8,128)(2,1)S(1)} %get-tuple-element.42.refs_8_.xt_ref, ...), custom_call_target="tpu_custom_call" | custom-call | flops 1006632960 | bytes 4194304 | tf_op jit(solution)/shard_map/basis_terms/pallas_call | solution.py:409
  66.4 3.9 %collective-permute-start.26 = (bf16[64,256]{1,0:T(8,128)(2,1)S(1)}, bf16[64,256]{1,0:T(8,128)(2,1)S(1)}, u32[]{:S(2)}, u32[]{:S(2)}) collective-permute-start(bf16[64,256]{1,0:T(8,128)(2,1)S(1)} %add_convert_fusion.4), channel_id=1, source_target_pairs={{0,24},{4,28},{8,0},{12,4},{16,8},{20,12},{24,16},{28,20},{1,25},{... | collective-permute-start | bytes 98312 | tf_op jit(solution)/shard_map/ppermute | solution.py:330
  70.3 0.8 collective-permute-start.24
  71.1 0.5 collective-permute-start.21
  71.6 2.2 %collective-permute-start.20 = (bf16[240,256]{1,0:T(8,128)(2,1)S(1)}, bf16[240,256]{1,0:T(8,128)(2,1)S(1)}, u32[]{:S(2)}, u32[]{:S(2)}) collective-permute-start(bf16[240,256]{1,0:T(8,128)(2,1)S(1)} %add_convert_fusion.2), channel_id=1, source_target_pairs={{0,16},{4,20},{8,24},{12,28},{16,0},{20,4},{24,8},{28,12},{1,17},{... | collective-permute-start | bytes 368648 | tf_op jit(solution)/shard_map/ppermute | solution.py:330
  73.8 2.1 %basis_terms.5 = (f32[240,256]{1,0:T(8,128)S(1)}, bf16[240,256]{1,0:T(8,128)(2,1)S(1)}) custom-call(s32[4]{0:T(128)S(1)} %pad_add_fusion.place, bf16[256,2048]{1,0:T(8,128)(2,1)S(1)} %edge_grads.1.gt_ref, bf16[256,2048]{1,0:T(8,128)(2,1)S(1)} %collective-permute-done.13.gt_core, bf16[4,256,1024]{2,1,0:T(8,128)(2,1)S(1)} %get-tuple-element.42.refs_8_.xt_ref, ...), custom_call_target="tpu_custom_call" | custom-call | flops 1006632960 | bytes 4194304 | tf_op jit(solution)/shard_map/basis_terms/pallas_call | solution.py:409
  76.0 1.5 %collective-permute-start.19 = (bf16[240,256]{1,0:T(8,128)(2,1)S(1)}, bf16[240,256]{1,0:T(8,128)(2,1)S(1)}, u32[]{:S(2)}, u32[]{:S(2)}) collective-permute-start(bf16[240,256]{1,0:T(8,128)(2,1)S(1)} %add_convert_fusion.3), channel_id=1, source_target_pairs={{0,8},{4,12},{8,16},{12,20},{16,24},{20,28},{24,0},{28,4},{1,9},{5... | collective-permute-start | bytes 368648 | tf_op jit(solution)/shard_map/ppermute | solution.py:330
  77.5 1.5 %collective-permute-start.17 = (bf16[240,256]{1,0:T(8,128)(2,1)S(1)}, bf16[240,256]{1,0:T(8,128)(2,1)S(1)}, u32[]{:S(2)}, u32[]{:S(2)}) collective-permute-start(bf16[240,256]{1,0:T(8,128)(2,1)S(1)} %get-tuple-element.55), channel_id=1, source_target_pairs={{0,2},{1,3},{2,0},{3,1},{4,6},{5,7},{6,4},{7,5},{8,10},{9,11},{10,... | collective-permute-start | bytes 368648 | tf_op jit(solution)/shard_map/ppermute | solution.py:335
  79.1 0.6 collective-permute-start.27
  79.7 3.7 %collective-permute-done.27.refs_1_ = f32[64,256]{1,0:T(8,128)S(1)} collective-permute-done((f32[64,256]{1,0:T(8,128)S(1)}, f32[64,256]{1,0:T(8,128)S(1)}, u32[]{:S(2)}, u32[]{:S(2)}) %collective-permute-start.27) | collective-permute-done | bytes 65568 | tf_op jit(solution)/shard_map/ppermute | solution.py:431
  83.4 2.4 %collective-permute-start.22 = (bf16[240,256]{1,0:T(8,128)(2,1)S(1)}, bf16[240,256]{1,0:T(8,128)(2,1)S(1)}, u32[]{:S(2)}, u32[]{:S(2)}) collective-permute-start(bf16[240,256]{1,0:T(8,128)(2,1)S(1)} %add_convert_fusion.1), channel_id=1, source_target_pairs={{0,24},{4,28},{8,0},{12,4},{16,8},{20,12},{24,16},{28,20},{1,25},{... | collective-permute-start | bytes 368648 | tf_op jit(solution)/shard_map/ppermute | solution.py:330
  85.8 0.7 slice.10
  86.5 3.5 %collective-permute-done.29.refs_3_ = f32[64,256]{1,0:T(8,128)S(1)} collective-permute-done((f32[64,256]{1,0:T(8,128)S(1)}, f32[64,256]{1,0:T(8,128)S(1)}, u32[]{:S(2)}, u32[]{:S(2)}) %collective-permute-start.29) | collective-permute-done | bytes 65568 | tf_op jit(solution)/shard_map/ppermute | solution.py:431
  90.0 1.3 %coef_rows.1 = f32[30,2000]{1,0:T(8,128)} custom-call(s32[4]{0:T(128)S(1)} %pad_add_fusion.place, f32[64,256]{1,0:T(8,128)S(1)} %add_add_fusion.refs_0_, f32[64,256]{1,0:T(8,128)S(1)} %collective-permute-done.27.refs_1_, f32[64,256]{1,0:T(8,128)S(1)} %collective-permute-done.28.refs_2_, f32[64,256]{1,0:T(8,128)S(1)} %collective-permute-done.29.refs_3_), custom_call_target="tpu_custom_call" | custom-call | flops 1048576 | bytes 4194304 | tf_op jit(solution)/shard_map/coef_rows/pallas_call | solution.py:475
  91.3 0.8 add_multiply_fusion
  (42 shorter events, 0.5 us)
Async XLA Ops:
  0.6 6.7 %collective-permute-start = (bf16[256,256]{1,0:T(8,128)(2,1)}, bf16[256,256]{1,0:T(8,128)(2,1)S(1)}, u32[]{:S(2)}, u32[]{:S(2)}) collective-permute-start(bf16[256,256]{1,0:T(8,128)(2,1)} %param.9), channel_id=1, source_target_pairs={{0,4},{4,0},{8,12},{12,8},{16,20},{20,16},{24,28},{28,24},{1,5},{5... | collective-permute-start | bytes 393224 | tf_op jit(solution)/shard_map/ppermute | solution.py:324
  3.6 7.0 %collective-permute-start.1 = (bf16[256,256]{1,0:T(8,128)(2,1)}, bf16[256,256]{1,0:T(8,128)(2,1)S(1)}, u32[]{:S(2)}, u32[]{:S(2)}) collective-permute-start(bf16[256,256]{1,0:T(8,128)(2,1)} %bitcast.14), channel_id=1, source_target_pairs={{0,8},{4,12},{8,16},{12,20},{16,24},{20,28},{24,0},{28,4},{1,9},{5... | collective-permute-start | bytes 393224 | tf_op jit(solution)/shard_map/ppermute | solution.py:330
  10.7 9.1 %collective-permute-start.2 = (bf16[2,256,256]{2,1,0:T(8,128)(2,1)S(1)}, bf16[2,256,256]{2,1,0:T(8,128)(2,1)S(1)}, u32[]{:S(2)}, u32[]{:S(2)}) collective-permute-start(bf16[2,256,256]{2,1,0:T(8,128)(2,1)S(1)} %pad_maximum_fusion.1), channel_id=1, source_target_pairs={{0,2},{1,3},{2,0},{3,1},{4,6},{5,7},{6,4},{7,5},{8,10},{9,11},{10,... | collective-permute-start | bytes 786440 | tf_op jit(solution)/shard_map/ppermute | solution.py:335
  13.6 4.1 %collective-permute-start.3 = (f32[4,1024]{1,0:T(4,128)}, f32[4,1024]{1,0:T(4,128)S(1)}, u32[]{:S(2)}, u32[]{:S(2)}) collective-permute-start(f32[4,1024]{1,0:T(4,128)} %edge_table.1), channel_id=1, source_target_pairs={{0,4},{4,0},{8,12},{12,8},{16,20},{20,16},{24,28},{28,24},{1,5},{5... | collective-permute-start | bytes 49160 | tf_op jit(solution)/shard_map/ppermute | solution.py:324
  14.1 6.3 %collective-permute-start.4 = (bf16[256,256]{1,0:T(8,128)(2,1)}, bf16[256,256]{1,0:T(8,128)(2,1)S(1)}, u32[]{:S(2)}, u32[]{:S(2)}) collective-permute-start(bf16[256,256]{1,0:T(8,128)(2,1)} %bitcast.15), channel_id=1, source_target_pairs={{0,4},{4,0},{8,12},{12,8},{16,20},{20,16},{24,28},{28,24},{1,5},{5... | collective-permute-start | bytes 393224 | tf_op jit(solution)/shard_map/ppermute | solution.py:324
  15.6 7.9 %collective-permute-start.6 = (bf16[256,256]{1,0:T(8,128)(2,1)}, bf16[256,256]{1,0:T(8,128)(2,1)S(1)}, u32[]{:S(2)}, u32[]{:S(2)}) collective-permute-start(bf16[256,256]{1,0:T(8,128)(2,1)} %bitcast.16), channel_id=1, source_target_pairs={{0,16},{4,20},{8,24},{12,28},{16,0},{20,4},{24,8},{28,12},{1,17},{... | collective-permute-start | bytes 393224 | tf_op jit(solution)/shard_map/ppermute | solution.py:330
  16.4 7.1 %collective-permute-start.7 = (bf16[256,256]{1,0:T(8,128)(2,1)}, bf16[256,256]{1,0:T(8,128)(2,1)S(1)}, u32[]{:S(2)}, u32[]{:S(2)}) collective-permute-start(bf16[256,256]{1,0:T(8,128)(2,1)} %bitcast.17), channel_id=1, source_target_pairs={{0,24},{4,28},{8,0},{12,4},{16,8},{20,12},{24,16},{28,20},{1,25},{... | collective-permute-start | bytes 393224 | tf_op jit(solution)/shard_map/ppermute | solution.py:330
  17.7 5.8 %collective-permute-start.5 = (bf16[256,256]{1,0:T(8,128)(2,1)S(1)}, bf16[256,256]{1,0:T(8,128)(2,1)S(1)}, u32[]{:S(2)}, u32[]{:S(2)}) collective-permute-start(bf16[256,256]{1,0:T(8,128)(2,1)S(1)} %collective-permute-done.1.refs_1_), channel_id=1, source_target_pairs={{0,4},{4,0},{8,12},{12,8},{16,20},{20,16},{24,28},{28,24},{1,5},{5... | collective-permute-start | bytes 393224 | tf_op jit(solution)/shard_map/ppermute | solution.py:324
  23.5 2.6 %collective-permute-start.11 = (bf16[2,2,256,256]{3,2,1,0:T(8,128)(2,1)S(1)}, bf16[2,2,256,256]{3,2,1,0:T(8,128)(2,1)S(1)}, u32[]{:S(2)}, u32[]{:S(2)}) collective-permute-start(bf16[2,2,256,256]{3,2,1,0:T(8,128)(2,1)S(1)} %pad_maximum_fusion.feats), channel_id=1, source_target_pairs={{0,1},{1,0},{2,3},{3,2},{4,5},{5,4},{6,7},{7,6},{8,9},{9,8},{10,11... | collective-permute-start | bytes 1572872 | tf_op jit(solution)/shard_map/ppermute | solution.py:327
  23.5 2.6 %collective-permute-start.10 = (f32[2,4,1024]{2,1,0:T(4,128)S(1)}, f32[2,4,1024]{2,1,0:T(4,128)S(1)}, u32[]{:S(2)}, u32[]{:S(2)}) collective-permute-start(f32[2,4,1024]{2,1,0:T(4,128)S(1)} %pad_maximum_fusion.2.meta), channel_id=1, source_target_pairs={{0,1},{1,0},{2,3},{3,2},{4,5},{5,4},{6,7},{7,6},{8,9},{9,8},{10,11... | collective-permute-start | bytes 98312 | tf_op jit(solution)/shard_map/ppermute | solution.py:327
  24.1 9.5 %collective-permute-start.8 = (bf16[256,256]{1,0:T(8,128)(2,1)S(1)}, bf16[256,256]{1,0:T(8,128)(2,1)S(1)}, u32[]{:S(2)}, u32[]{:S(2)}) collective-permute-start(bf16[256,256]{1,0:T(8,128)(2,1)S(1)} %collective-permute-done.6.refs_2_), channel_id=1, source_target_pairs={{0,4},{4,0},{8,12},{12,8},{16,20},{20,16},{24,28},{28,24},{1,5},{5... | collective-permute-start | bytes 393224 | tf_op jit(solution)/shard_map/ppermute | solution.py:324
  25.1 8.5 %collective-permute-start.9 = (bf16[256,256]{1,0:T(8,128)(2,1)S(1)}, bf16[256,256]{1,0:T(8,128)(2,1)S(1)}, u32[]{:S(2)}, u32[]{:S(2)}) collective-permute-start(bf16[256,256]{1,0:T(8,128)(2,1)S(1)} %collective-permute-done.7.refs_3_), channel_id=1, source_target_pairs={{0,4},{4,0},{8,12},{12,8},{16,20},{20,16},{24,28},{28,24},{1,5},{5... | collective-permute-start | bytes 393224 | tf_op jit(solution)/shard_map/ppermute | solution.py:324
  26.1 0.9 copy-start.1
  27.0 0.9 copy-start.2
  27.9 5.7 %copy-start.3 = (bf16[1,256,256]{2,1,0:T(8,128)(2,1)S(1)}, bf16[1,256,256]{2,1,0:T(8,128)(2,1)}, u32[]{:S(2)}) copy-start(bf16[1,256,256]{2,1,0:T(8,128)(2,1)} %param.10) | copy-start | bytes 393220
  33.6 4.1 %copy-start = (bf16[30,256,256]{2,1,0:T(8,128)(2,1)S(1)}, bf16[30,256,256]{2,1,0:T(8,128)(2,1)}, u32[]{:S(2)}) copy-start(bf16[30,256,256]{2,1,0:T(8,128)(2,1)} %bases_ref.1) | copy-start | bytes 11796484
  37.6 10.5 %collective-permute-start.13 = (bf16[256,2048]{1,0:T(8,128)(2,1)S(1)}, bf16[256,2048]{1,0:T(8,128)(2,1)S(1)}, u32[]{:S(2)}, u32[]{:S(2)}) collective-permute-start(bf16[256,2048]{1,0:T(8,128)(2,1)S(1)} %edge_grads.1.gt_ref), channel_id=1, source_target_pairs={{0,1},{1,0},{2,3},{3,2},{4,5},{5,4},{6,7},{7,6},{8,9},{9,8},{10,11... | collective-permute-start | bytes 3145736 | tf_op jit(solution)/shard_map/ppermute | solution.py:327
  45.9 5.9 %collective-permute-start.15 = (bf16[320,256]{1,0:T(8,128)(2,1)S(1)}, bf16[320,256]{1,0:T(8,128)(2,1)S(1)}, u32[]{:S(2)}, u32[]{:S(2)}) collective-permute-start(bf16[320,256]{1,0:T(8,128)(2,1)S(1)} %get-tuple-element.50), channel_id=1, source_target_pairs={{0,3},{1,2},{2,1},{3,0},{4,7},{5,6},{6,5},{7,4},{8,11},{9,10},{10,... | collective-permute-start | bytes 491528 | tf_op jit(solution)/shard_map/ppermute | solution.py:431
  46.6 5.3 %collective-permute-start.14 = (bf16[320,256]{1,0:T(8,128)(2,1)S(1)}, bf16[320,256]{1,0:T(8,128)(2,1)S(1)}, u32[]{:S(2)}, u32[]{:S(2)}) collective-permute-start(bf16[320,256]{1,0:T(8,128)(2,1)S(1)} %get-tuple-element.48), channel_id=1, source_target_pairs={{0,1},{1,0},{2,3},{3,2},{4,5},{5,4},{6,7},{7,6},{8,9},{9,8},{10,11... | collective-permute-start | bytes 491528 | tf_op jit(solution)/shard_map/ppermute | solution.py:431
  46.6 9.4 %collective-permute-start.12 = (bf16[320,256]{1,0:T(8,128)(2,1)S(1)}, bf16[320,256]{1,0:T(8,128)(2,1)S(1)}, u32[]{:S(2)}, u32[]{:S(2)}) collective-permute-start(bf16[320,256]{1,0:T(8,128)(2,1)S(1)} %get-tuple-element.45), channel_id=1, source_target_pairs={{0,2},{1,3},{2,0},{3,1},{4,6},{5,7},{6,4},{7,5},{8,10},{9,11},{10,... | collective-permute-start | bytes 491528 | tf_op jit(solution)/shard_map/ppermute | solution.py:431
  58.1 6.1 %collective-permute-start.18 = (bf16[240,256]{1,0:T(8,128)(2,1)S(1)}, bf16[240,256]{1,0:T(8,128)(2,1)S(1)}, u32[]{:S(2)}, u32[]{:S(2)}) collective-permute-start(bf16[240,256]{1,0:T(8,128)(2,1)S(1)} %get-tuple-element.57), channel_id=1, source_target_pairs={{0,2},{1,3},{2,0},{3,1},{4,6},{5,7},{6,4},{7,5},{8,10},{9,11},{10,... | collective-permute-start | bytes 368648 | tf_op jit(solution)/shard_map/ppermute | solution.py:335
  58.7 12.9 %collective-permute-start.16 = (bf16[240,256]{1,0:T(8,128)(2,1)S(1)}, bf16[240,256]{1,0:T(8,128)(2,1)S(1)}, u32[]{:S(2)}, u32[]{:S(2)}) collective-permute-start(bf16[240,256]{1,0:T(8,128)(2,1)S(1)} %get-tuple-element.52), channel_id=1, source_target_pairs={{0,2},{1,3},{2,0},{3,1},{4,6},{5,7},{6,4},{7,5},{8,10},{9,11},{10,... | collective-permute-start | bytes 368648 | tf_op jit(solution)/shard_map/ppermute | solution.py:335
  60.3 6.0 %collective-permute-start.23 = (bf16[64,256]{1,0:T(8,128)(2,1)S(1)}, bf16[64,256]{1,0:T(8,128)(2,1)S(1)}, u32[]{:S(2)}, u32[]{:S(2)}) collective-permute-start(bf16[64,256]{1,0:T(8,128)(2,1)S(1)} %slice.11), channel_id=1, source_target_pairs={{0,4},{4,0},{8,12},{12,8},{16,20},{20,16},{24,28},{28,24},{1,5},{5... | collective-permute-start | bytes 98312 | tf_op jit(solution)/shard_map/ppermute | solution.py:324
  66.4 9.6 %collective-permute-start.26 = (bf16[64,256]{1,0:T(8,128)(2,1)S(1)}, bf16[64,256]{1,0:T(8,128)(2,1)S(1)}, u32[]{:S(2)}, u32[]{:S(2)}) collective-permute-start(bf16[64,256]{1,0:T(8,128)(2,1)S(1)} %add_convert_fusion.4), channel_id=1, source_target_pairs={{0,24},{4,28},{8,0},{12,4},{16,8},{20,12},{24,16},{28,20},{1,25},{... | collective-permute-start | bytes 98312 | tf_op jit(solution)/shard_map/ppermute | solution.py:330
  70.3 7.2 %collective-permute-start.25 = (bf16[64,256]{1,0:T(8,128)(2,1)S(1)}, bf16[64,256]{1,0:T(8,128)(2,1)S(1)}, u32[]{:S(2)}, u32[]{:S(2)}) collective-permute-start(bf16[64,256]{1,0:T(8,128)(2,1)S(1)} %add_convert_fusion.4), channel_id=1, source_target_pairs={{0,8},{4,12},{8,16},{12,20},{16,24},{20,28},{24,0},{28,4},{1,9},{5... | collective-permute-start | bytes 98312 | tf_op jit(solution)/shard_map/ppermute | solution.py:330
  70.3 8.8 %collective-permute-start.24 = (bf16[64,256]{1,0:T(8,128)(2,1)S(1)}, bf16[64,256]{1,0:T(8,128)(2,1)S(1)}, u32[]{:S(2)}, u32[]{:S(2)}) collective-permute-start(bf16[64,256]{1,0:T(8,128)(2,1)S(1)} %add_convert_fusion.4), channel_id=1, source_target_pairs={{0,16},{4,20},{8,24},{12,28},{16,0},{20,4},{24,8},{28,12},{1,17},{... | collective-permute-start | bytes 98312 | tf_op jit(solution)/shard_map/ppermute | solution.py:330
  71.1 8.5 %collective-permute-start.21 = (bf16[240,256]{1,0:T(8,128)(2,1)S(1)}, bf16[240,256]{1,0:T(8,128)(2,1)S(1)}, u32[]{:S(2)}, u32[]{:S(2)}) collective-permute-start(bf16[240,256]{1,0:T(8,128)(2,1)S(1)} %get-tuple-element.60), channel_id=1, source_target_pairs={{0,2},{1,3},{2,0},{3,1},{4,6},{5,7},{6,4},{7,5},{8,10},{9,11},{10,... | collective-permute-start | bytes 368648 | tf_op jit(solution)/shard_map/ppermute | solution.py:335
  71.6 19.7 %collective-permute-start.20 = (bf16[240,256]{1,0:T(8,128)(2,1)S(1)}, bf16[240,256]{1,0:T(8,128)(2,1)S(1)}, u32[]{:S(2)}, u32[]{:S(2)}) collective-permute-start(bf16[240,256]{1,0:T(8,128)(2,1)S(1)} %add_convert_fusion.2), channel_id=1, source_target_pairs={{0,16},{4,20},{8,24},{12,28},{16,0},{20,4},{24,8},{28,12},{1,17},{... | collective-permute-start | bytes 368648 | tf_op jit(solution)/shard_map/ppermute | solution.py:330
  76.0 15.3 %collective-permute-start.19 = (bf16[240,256]{1,0:T(8,128)(2,1)S(1)}, bf16[240,256]{1,0:T(8,128)(2,1)S(1)}, u32[]{:S(2)}, u32[]{:S(2)}) collective-permute-start(bf16[240,256]{1,0:T(8,128)(2,1)S(1)} %add_convert_fusion.3), channel_id=1, source_target_pairs={{0,8},{4,12},{8,16},{12,20},{16,24},{20,28},{24,0},{28,4},{1,9},{5... | collective-permute-start | bytes 368648 | tf_op jit(solution)/shard_map/ppermute | solution.py:330
  77.5 13.8 %collective-permute-start.17 = (bf16[240,256]{1,0:T(8,128)(2,1)S(1)}, bf16[240,256]{1,0:T(8,128)(2,1)S(1)}, u32[]{:S(2)}, u32[]{:S(2)}) collective-permute-start(bf16[240,256]{1,0:T(8,128)(2,1)S(1)} %get-tuple-element.55), channel_id=1, source_target_pairs={{0,2},{1,3},{2,0},{3,1},{4,6},{5,7},{6,4},{7,5},{8,10},{9,11},{10,... | collective-permute-start | bytes 368648 | tf_op jit(solution)/shard_map/ppermute | solution.py:335
  79.1 4.3 %collective-permute-start.27 = (f32[64,256]{1,0:T(8,128)S(1)}, f32[64,256]{1,0:T(8,128)S(1)}, u32[]{:S(2)}, u32[]{:S(2)}) collective-permute-start(f32[64,256]{1,0:T(8,128)S(1)} %add_add_fusion.refs_0_), channel_id=1, source_target_pairs={{0,2},{1,3},{2,0},{3,1},{4,6},{5,7},{6,4},{7,5},{8,10},{9,11},{10,... | collective-permute-start | bytes 196616 | tf_op jit(solution)/shard_map/ppermute | solution.py:431
  79.6 6.2 %collective-permute-start.28 = (f32[64,256]{1,0:T(8,128)S(1)}, f32[64,256]{1,0:T(8,128)S(1)}, u32[]{:S(2)}, u32[]{:S(2)}) collective-permute-start(f32[64,256]{1,0:T(8,128)S(1)} %add_add_fusion.refs_0_), channel_id=1, source_target_pairs={{0,1},{1,0},{2,3},{3,2},{4,5},{5,4},{6,7},{7,6},{8,9},{9,8},{10,11... | collective-permute-start | bytes 196616 | tf_op jit(solution)/shard_map/ppermute | solution.py:431
  83.4 7.9 %collective-permute-start.22 = (bf16[240,256]{1,0:T(8,128)(2,1)S(1)}, bf16[240,256]{1,0:T(8,128)(2,1)S(1)}, u32[]{:S(2)}, u32[]{:S(2)}) collective-permute-start(bf16[240,256]{1,0:T(8,128)(2,1)S(1)} %add_convert_fusion.1), channel_id=1, source_target_pairs={{0,24},{4,28},{8,0},{12,4},{16,8},{20,12},{24,16},{28,20},{1,25},{... | collective-permute-start | bytes 368648 | tf_op jit(solution)/shard_map/ppermute | solution.py:330
  85.8 4.2 %collective-permute-start.29 = (f32[64,256]{1,0:T(8,128)S(1)}, f32[64,256]{1,0:T(8,128)S(1)}, u32[]{:S(2)}, u32[]{:S(2)}) collective-permute-start(f32[64,256]{1,0:T(8,128)S(1)} %add_add_fusion.refs_0_), channel_id=1, source_target_pairs={{0,3},{1,2},{2,1},{3,0},{4,7},{5,6},{6,5},{7,4},{8,11},{9,10},{10,... | collective-permute-start | bytes 196616 | tf_op jit(solution)/shard_map/ppermute | solution.py:431

commit v4 on v3

--- a/solution.py
+++ b/solution.py
@@ -8,6 +8,7 @@
 
 EDGE_BLOCK = 128
 TILE = 16
+DIGIT = 256
 LANES = 128
 PAIR = 2
 F32 = jnp.float32
@@ -58,12 +59,6 @@
 
 def dot_t(left, right):
     return lax.dot_general(left, right, (((1,), (1,)), ((), ())), preferred_element_type=F32)
-
-
-def tree_sum(values):
-    if len(values) == 1:
-        return values[0]
-    return tree_sum(values[0::2]) + tree_sum(values[1::2])
 
 
 def vmem():
@@ -89,32 +84,77 @@
     )
 
 
-def prepare_kernel(fills, src, dst, rel, norm, out_ref):
-    blocks = fills.shape[-1]
-    out_ref[0:1, :] = src[0].astype(F32)
-    out_ref[1:2, :] = dst[0].astype(F32)
-    out_ref[2:3, :] = rel[0].astype(F32)
+def prepare_kernel(fills, src, dst, rel, norm, dest, feats, out_ref):
+    rows = dest.shape[0]
+    out_ref[0:rows, :] = dest[...]
+    out_ref[rows : rows + feats.shape[0], :] = feats[...]
+    base = rows + feats.shape[0]
+    span = out_ref.shape[1]
     lane = lax.broadcasted_iota(I32, (1, EDGE_BLOCK), 1)
-    for at in range(blocks):
-        here = slice(at * EDGE_BLOCK, (at + 1) * EDGE_BLOCK)
-        live = jnp.where(lane < fills[0, 0, at], 1.0, 0.0)
-        out_ref[3:4, here] = norm[0, :, here] * live
-
-
-def source_kernel(sizes, place, meta, meta_core, feats, feats_core, coefs_t, *refs):
-    cols, shard, span, heads, padded, extra = sizes
+    for q in range(src.shape[-1] // span):
+        here = slice(q * span, (q + 1) * span)
+        lines = []
+        for ids in (src, dst, rel):
+            high, low = split_index(ids[0, :, here], DIGIT)
+            lines += [low.astype(F32), high.astype(F32)]
+        live = []
+        for at in range(q * span // EDGE_BLOCK, (q + 1) * span // EDGE_BLOCK):
+            live.append(jnp.where(lane < fills[0, 0, at], 1.0, 0.0))
+        rest = norm[0, :, here] * jnp.concatenate(live, axis=1)
+        for _ in range(3):
+            digit = rest.astype(BF16).astype(F32)
+            lines.append(digit)
+            rest = rest - digit
+        lines.append(jnp.zeros((TILE - len(lines), span), F32))
+        out_ref[base + q * TILE : base + (q + 1) * TILE, :] = jnp.concatenate(
+            lines, axis=0
+        ).astype(BF16)
+
+
+def read_table(ref, at):
+    tile = ref[pl.ds(at, TILE), :].astype(F32)
+    ids = []
+    for kind in range(3):
+        low, high = tile[2 * kind : 2 * kind + 1], tile[2 * kind + 1 : 2 * kind + 2]
+        ids.append((high * DIGIT + low).astype(I32))
+    return (*ids, (tile[6:7] + tile[7:8]) + tile[8:9])
+
+
+def near_kernel(own, other, out_ref):
+    shard = out_ref.shape[0] // PAIR
+    for xr, source in enumerate((own, other)):
+        out_ref[xr * shard : (xr + 1) * shard, :] = source[shard : 2 * shard, :]
+
+
+def pack_kernel(own, other, *refs):
+    parts, out_ref = refs[:-1], refs[-1]
+    size = parts[0].shape[0]
+    for at, part in enumerate(parts):
+        out_ref[at * size : (at + 1) * size, :] = part[...]
+    base = len(parts) * size
+    lines = (out_ref.shape[0] - base) // PAIR
+    for xr, source in enumerate((own, other)):
+        out_ref[base + xr * lines : base + (xr + 1) * lines, :] = source[
+            source.shape[0] - lines :, :
+        ]
+
+
+def source_kernel(sizes, place, own, other, coefs_t, *refs):
+    cols, shard, edges, heads, padded, extra = sizes
     xt_ref, ct_ref, table, coefs = refs[extra:]
     count = cols // PAIR
     y, core = place[2], place[3]
-    width = feats.shape[-1]
-    edges = meta.shape[-1]
+    span = width = own.shape[-1]
+    base = cols * shard
+    lines = edges // span * TILE
     basis_count, relation_count = coefs_t.shape
     unit = eye(width)
-    for far, block in enumerate((feats, feats_core)):
+    for far, block in enumerate((own, other)):
         for sy in range(count):
             for xr in range(PAIR):
                 at = (far * count + sy) * shard
-                table[xr, :, at : at + shard] = dot_t(unit, block[sy, xr]).astype(BF16)
+                rows = block[(sy * PAIR + xr) * shard : (sy * PAIR + xr + 1) * shard, :]
+                table[xr, :, at : at + shard] = dot_t(unit, rows).astype(BF16)
     coefs[...] = jnp.zeros_like(coefs)
     for head in range(heads):
         live = min(LANES, relation_count - head * LANES)
@@ -122,18 +162,17 @@
             coefs[head * padded : head * padded + basis_count, 0:live] = coefs_t[
                 :, head * LANES : head * LANES + live
             ]
-    for far, source in enumerate((meta, meta_core)):
+    for far, source in enumerate((own, other)):
 
         def step(index, carry, far=far, source=source):
             xr = index // (edges // span)
             at = pl.multiple_of(index % (edges // span) * span, span)
-            ids = source[xr, 0:1, pl.ds(at, span)].astype(I32)
+            ids, _, relation, _ = read_table(source, pl.multiple_of(base + index * TILE, TILE))
             owner, local = split_index(ids, shard)
             owner_y, owner_core = split_index(owner, PAIR)
             slot = (owner_core ^ core) * count + wrap(y - owner_y, count)
             rows = dot(table[xr], slot_hot(slot, local, cols, shard))
             xt_ref[far * PAIR + xr, :, pl.ds(at, span)] = rows.astype(BF16)
-            relation = source[xr, 2:3, pl.ds(at, span)].astype(I32)
             high, low = split_index(relation, LANES)
             parts = dot(coefs[...], one_hot(low, LANES))
             total = jnp.zeros((padded, span), F32)
@@ -147,27 +186,25 @@
         lax.fori_loop(0, PAIR * (edges // span), step, 0, unroll=2)
 
 
-def grad_kernel(sizes, place, meta, *refs):
-    rows_total, shard, span = sizes
+def grad_kernel(sizes, place, packed, *refs):
+    rows_total, shard, edges = sizes
     count = rows_total // PAIR
     blocks = refs[:rows_total]
     gt_ref, table = refs[rows_total + 1 :]
     a, x = place[0], place[1]
-    width = blocks[0].shape[-1]
-    edges = meta.shape[-1]
+    span = width = blocks[0].shape[-1]
+    lines = edges // span * TILE
+    base = packed.shape[0] - PAIR * lines
     unit = eye(width)
     for at, block in enumerate(blocks):
-        table[:, at * shard : (at + 1) * shard] = dot_t(unit, block[...]).astype(BF16)
+        table[:, at * shard : (at + 1) * shard] = dot_t(unit, block[0:shard, :]).astype(BF16)
 
     def step(index, carry):
-        xr = index // (edges // span)
-        at = pl.multiple_of(index % (edges // span) * span, span)
-        ids = meta[xr, 1:2, pl.ds(at, span)].astype(I32)
+        _, ids, _, weight = read_table(packed, pl.multiple_of(base + index * TILE, TILE))
         owner, local = split_index(ids, shard)
         owner_a, owner_x = split_index(owner, PAIR)
         slot = (owner_x ^ x) * count + wrap(a - owner_a, count)
         rows = dot(table[...], slot_hot(slot, local, rows_total, shard))
-        weight = meta[xr, 3:4, pl.ds(at, span)]
         gt_ref[:, pl.ds(pl.multiple_of(index * span, span), span)] = (rows * weight).astype(BF16)
         return carry
 
@@ -175,15 +212,16 @@
 
 
 def forward_kernel(
-    sizes, place, meta, gt_ref, xt_ref, ct_ref, bases_ref, *refs
+    sizes, place, table, gt_ref, xt_ref, ct_ref, bases_ref, *refs
 ):
-    cols, shard, span, heads, padded, group = sizes
+    cols, shard, edges, heads, padded, group = sizes
     outs = refs[:cols]
     total, inner, wide, coef_sum = refs[cols:]
     count = cols // PAIR
     y, core = place[2], place[3]
-    edges = meta.shape[-1]
-    width = bases_ref.shape[-1]
+    span = width = bases_ref.shape[-1]
+    lines = edges // span * TILE
+    base_row = table.shape[0] - PAIR * lines
     total[...] = jnp.zeros_like(total)
     inner[...] = jnp.zeros_like(inner)
 
@@ -204,7 +242,8 @@
 
     lax.fori_loop(0, bases_ref.shape[0] // group, step, 0)
 
-    ids = meta[0, 0:1, :].astype(I32)
+    tables = [read_table(table, base_row + q * TILE) for q in range(edges // span)]
+    ids = jnp.concatenate([part[0] for part in tables], axis=1)
     owner, local = split_index(ids, shard)
     owner_y, owner_core = split_index(owner, PAIR)
     slot = (owner_core ^ core) * count + wrap(owner_y - y, count)
@@ -212,7 +251,7 @@
     for at in range(cols):
         hot = one_hot(jnp.where(slot == at, local, -1), shard)
         outs[at][0:shard, :] = dot_t(hot, values).astype(BF16)
-    high, low = split_index(meta[0, 2:3, :].astype(I32), LANES)
+    high, low = split_index(jnp.concatenate([part[2] for part in tables], axis=1), LANES)
     for head in range(heads):
         wide[head * padded : (head + 1) * padded, :] = jnp.where(
             high == head, inner[...], 0.0
@@ -234,16 +273,16 @@
     rows_total, cols, block, groups, basis_count, span, turns = sizes
     a_count, y_count = rows_total // PAIR, cols // PAIR
     a, x, y, core = place[0], place[1], place[2], place[3]
-    outs = refs[: y_count * len(turns)]
+    outs = refs[:y_count]
     acc, left_even, left_odd, tiles = refs[len(outs) :]
     width, edges = xt_ref.shape[1], xt_ref.shape[2]
     tiles_wide = width // TILE
     cover = groups * TILE
-    spread = tiles.shape[0] // len(outs)
+    spread = tiles.shape[0] // (y_count * len(turns))
     steps = edges // span
     firsts = []
-    for sz in turns:
-        for sy in range(y_count):
+    for sy in range(y_count):
+        for sz in turns:
             owner = ((a + sz) % a_count * PAIR + x) * cols + (y + sy) % y_count * PAIR + core
             firsts.append(owner * block // TILE)
 
@@ -274,24 +313,19 @@
             acc[...] += term
         else:
             acc[...] = term
-    for order, out in enumerate(outs):
-        out[...] = acc[order * cover : (order + 1) * cover, :].astype(out.dtype)
-
-
-def coef_kernel(sizes, place, *refs):
+    size = len(turns) * cover
+    for sy, out in enumerate(outs):
+        out[...] = acc[sy * size : (sy + 1) * size, :].astype(out.dtype)
+
+
+def coef_kernel(sizes, parts, out_ref, whole):
     cols, heads, padded, divisor = sizes
-    count = cols // PAIR
-    parts, (out_ref, whole) = refs[:cols], refs[cols:]
-    y, core = place[2], place[3]
     share = heads * padded // cols
     half = share // 2
-    for far in range(PAIR):
-        for sy in range(count):
-            target = wrap(y - sy, count) * PAIR + (core ^ far)
-            for side in range(2):
-                whole[pl.ds(pl.multiple_of(target * share + side * half, 8), half), :] = (
-                    parts[far * count + sy][:, side * LANES : (side + 1) * LANES]
-                )
+    for target in range(cols):
+        for side in range(2):
+            at = target * share + side * half
+            whole[at : at + half, :] = parts[target, :, side * LANES : (side + 1) * LANES]
     width, total = out_ref.shape
     for head in range(heads):
         live = min(LANES, total - head * LANES)
@@ -315,10 +349,18 @@
     heads = round_up(relation_count, LANES) // LANES
     while heads * padded % (cols * 2 * TILE):
         heads += 1
-    span = 256
     i = lax.axis_index("row")
     j = lax.axis_index("col")
     place = jnp.stack([i // PAIR, i % PAIR, j // PAIR, j % PAIR]).astype(I32)
+
+    def plain(body, rows, n_in, name, *first):
+        return pl.pallas_call(
+            body,
+            out_shape=jax.ShapeDtypeStruct((rows, width), BF16),
+            in_specs=[*first] + [vmem()] * n_in,
+            out_specs=vmem(),
+            name=name,
+        )
 
     def flip_x(value):
         return lax.ppermute(value, "row", [(r, r ^ 1) for r in range(rows_total)])
@@ -335,35 +377,33 @@
         return lax.ppermute(value, "col", [(c, (c + by * PAIR) % cols) for c in range(cols)])
 
     own_dest = dest_grad[0]
+    dest_shard = own_dest.shape[0]
     turned = [turn_z(own_dest, s) for s in range(1, a_count)]
-    across_own = flip_x(own_dest)
-    near = flip_x(node_feats)
-    meta = pl.pallas_call(
-        prepare_kernel,
-        out_shape=jax.ShapeDtypeStruct((4, edges), F32),
-        in_specs=[smem()] + [vmem()] * 4,
-        out_specs=vmem(),
-        name="edge_table",
-    )(block_fill, src_ids, dst_ids, rel_ids, edge_norm)
-    meta = jnp.stack([meta, flip_x(meta)])
-    feats, turned[0] = lax.optimization_barrier((jnp.stack([node_feats, near]), turned[0]))
-    feats = jnp.stack([feats] + [turn_y(feats, s) for s in range(1, y_count)])
-    across = [across_own, flip_x(turned[0])]
-    feats, meta, across[0], across[1], *turned[1:] = lax.optimization_barrier(
-        (feats, meta, *across, *turned[1:])
+    lines = edges // width * TILE
+    mine = plain(
+        prepare_kernel, dest_shard + shard + lines, 6, "edge_table", smem()
+    )(block_fill, src_ids, dst_ids, rel_ids, edge_norm, own_dest, node_feats)
+    other = flip_x(mine)
+    feats = plain(near_kernel, PAIR * shard, 2, "near_rows")(mine, other)
+    feats, *turned[:2] = lax.optimization_barrier((feats, *turned[:2]))
+    feats = [feats] + [turn_y(feats, s) for s in range(1, y_count)]
+    across = [other] + [flip_x(value) for value in turned[:2]]
+    feats[-1], *rest = lax.optimization_barrier((feats[-1], *across[1:], *turned[2:]))
+    across[1:], turned[2:] = rest[: len(across) - 1], rest[len(across) - 1 :]
+    across += [flip_x(value) for value in turned[2:]]
+    dest = [own_dest] + turned
+    packed = plain(pack_kernel, cols * shard + PAIR * lines, 2 + y_count, "packed_rows")(
+        mine, other, *feats
     )
-    dest = [own_dest] + turned
-    across += [flip_x(value) for value in turned[1:]]
-    meta_core = flip_core(meta)
-    feats_core = flip_core(feats)
+    packed_core = flip_core(packed)
 
     xt, ct = call(
-        functools.partial(source_kernel, (cols, shard, span, heads, padded, a_count)),
+        functools.partial(source_kernel, (cols, shard, edges, heads, padded, a_count)),
         (
             jax.ShapeDtypeStruct((2 * PAIR, width, edges), BF16),
             jax.ShapeDtypeStruct((2 * PAIR, padded, edges), F32),
         ),
-        5,
+        3,
         [
             pltpu.VMEM((PAIR, width, cols * shard), BF16),
             pltpu.VMEM((heads * padded, LANES), BF16),
@@ -371,24 +411,23 @@
         2 * 4 * edges * cols * shard * width,
         "source_rows",
         a_count,
-    )(place, meta, meta_core, feats, feats_core, coefs.T, *dest)
-
-    dest_shard = own_dest.shape[0]
+    )(place, packed, packed_core, coefs.T, *dest)
+
     gt = call(
-        functools.partial(grad_kernel, (rows_total, dest_shard, span)),
+        functools.partial(grad_kernel, (rows_total, dest_shard, edges)),
         jax.ShapeDtypeStruct((width, PAIR * edges), BF16),
         1 + rows_total,
         [pltpu.VMEM((width, rows_total * dest_shard), BF16)],
         2 * 2 * edges * rows_total * dest_shard * width,
         "edge_grads",
         1,
-    )(place, meta, *dest, *across, xt)
+    )(place, packed, *dest, *across, xt)
     gt_core = flip_core(gt)
 
     group = max(g for g in range(1, 6) if basis_count % g == 0)
     share_rows = heads * padded // cols // 2
-    packed = call(
-        functools.partial(forward_kernel, (cols, shard, span, heads, padded, group)),
+    partial = call(
+        functools.partial(forward_kernel, (cols, shard, edges, heads, padded, group)),
         [jax.ShapeDtypeStruct((shard + share_rows, width), BF16)] * cols,
         5,
         [
@@ -399,7 +438,7 @@
         ],
         2 * edges * width * width * basis_count,
         "backed_sums",
-    )(place, meta, gt, xt, ct, bases)
+    )(place, packed, gt, xt, ct, bases)
 
     block = basis_count * width // (rows_total * cols)
     cover = block if block % TILE == 0 else round_up(block, TILE) + TILE
@@ -409,19 +448,18 @@
         return call(
             functools.partial(
                 basis_kernel,
-                (rows_total, cols, block, cover // TILE, basis_count, 2 * span, turns),
+                (rows_total, cols, block, cover // TILE, basis_count, 2 * width, turns),
             ),
             [
-                jax.ShapeDtypeStruct((cover, width), BF16 if sy else F32)
-                for _ in turns
+                jax.ShapeDtypeStruct((len(turns) * cover, width), BF16 if sy else F32)
                 for sy in range(y_count)
             ],
             4,
             [
                 pltpu.VMEM((count * cover, width), F32),
-                pltpu.VMEM((count * cover, 2 * span), BF16),
-                pltpu.VMEM((count * cover, 2 * span), BF16),
-                pltpu.VMEM((count * (round_up(cover, width) // width + 1), TILE, 2 * span), BF16),
+                pltpu.VMEM((count * cover, 2 * width), BF16),
+                pltpu.VMEM((count * cover, 2 * width), BF16),
+                pltpu.VMEM((count * (round_up(cover, width) // width + 1), TILE, 2 * width), BF16),
             ],
             2 * 4 * edges * count * cover * width,
             "basis_terms",
@@ -438,25 +476,23 @@
         return lax.optimization_barrier((value, other))[0]
 
     others = [(far, sy) for far in range(PAIR) for sy in range(y_count) if far or sy]
-    received = [to_col(packed[far * y_count + sy], far, sy) for far, sy in others]
-
-    sums, passed, marks = {}, [], []
+    received = [to_col(partial[far * y_count + sy], far, sy) for far, sy in others]
+
     order = tuple(range(1, a_count)) + (0,)
-    for at, sz in enumerate(order):
-        where = place
-        if at >= 2:
-            where = after(where, passed[at - 2])
-        blocks = basis_blocks(where, (sz,))
-        value = blocks[0]
-        arrived = [turn_y(blocks[sy], sy) for sy in range(1, y_count)]
-        for piece in arrived:
-            value = value + piece.astype(F32)
-        sums[sz] = turn_z(value.astype(BF16), sz) if sz else value
-        passed.append(arrived[-1] if arrived else blocks[0])
-        marks.append(blocks[0])
-    joined = packed[0].astype(F32)
+    half = (a_count + 1) // 2
+    sums = {}
+    for turns in (order[:half], order[half:]):
+        if turns:
+            blocks = basis_blocks(place, turns)
+            value = blocks[0]
+            for sy in range(1, y_count):
+                value = value + turn_y(blocks[sy], sy).astype(F32)
+            for at, sz in enumerate(turns):
+                piece = value[at * cover : (at + 1) * cover]
+                sums[sz] = turn_z(piece.astype(BF16), sz) if sz else piece
+    joined = partial[0].astype(F32)
     for value in received:
-        joined = joined + after(value, marks[min(1, a_count - 1)]).astype(F32)
+        joined = joined + after(value, blocks[0]).astype(F32)
     basis_sum = sums[0]
     for sz in range(1, a_count):
         basis_sum = basis_sum + sums[sz].astype(F32)
@@ -467,19 +503,16 @@
 
     node_grad = joined[:shard].astype(BF16)
     coef_part = joined[shard:]
-    low = coef_part.astype(BF16)
-    low = (low.astype(F32) + after(flip_x(low), marks[max(a_count - 2, 0)]).astype(F32)).astype(BF16)
-    around = [after(turn_z(low, s), marks[-1]).astype(F32) for s in range(1, a_count)]
-    coef_part = tree_sum([low.astype(F32)] + around)
-    shares = [coef_part] + [to_col(coef_part, far, sy) for far, sy in others]
-    coef_grad = call(
+    rows_of = lax.all_gather(coef_part.astype(BF16), "row")
+    coef_part = jnp.sum(rows_of.astype(F32), axis=0)
+    coef_grad = pl.pallas_call(
         functools.partial(coef_kernel, (cols, heads, padded, cols)),
-        jax.ShapeDtypeStruct((basis_count, relation_count), F32),
-        cols,
-        [pltpu.VMEM((heads * padded, LANES), F32)],
-        1 << 20,
-        "coef_rows",
-    )(place, *shares)
+        out_shape=jax.ShapeDtypeStruct((basis_count, relation_count), F32),
+        in_specs=[vmem()],
+        out_specs=vmem(),
+        scratch_shapes=[pltpu.VMEM((heads * padded, LANES), F32)],
+        name="coef_rows",
+    )(lax.all_gather(coef_part, "col"))
     return (node_grad, basis_grad, coef_grad.T)
 
 

time: 92.4 us -> 110 us (1.19)
  blocking collectives: 0 us -> 37.3 us
  waiting for transfers between devices: 24.1 us -> 11.5 us
  starting transfers between devices: 32.8 us -> 21.8 us
  Pallas kernels: 29 us -> 32.2 us
  local copies, waits for them, and re-layouts: 2.49 us -> 5.01 us
  other arithmetic: 2.76 us -> 1.07 us
    all_gather x0 -> x2, blocking collectives: none -> 37.3 us  [the longest x1 31.1 us: on_device(): rows_of = lax.all_gather(coef_part.astype(BF16), 'row')]
    ppermute x6 -> x3, waiting for transfers between devices: 13 us -> 0.01 us  [to_col(): lax.ppermute(value, 'col', [(c, (c // PAIR + sy) % y_count * PAIR + (c %...]
    ppermute x9 -> x6, starting transfers between devices: 14.5 us -> 9.72 us  [turn_z(): lax.ppermute(value, 'row', [(r, (r + by * PAIR) % rows_total) for r in ra...]
    pallas_call x5 -> x7, Pallas kernels: 20.6 us -> 25.1 us  [the longest x1 8.1 us: on_device(): call(functools.partial(forward_kernel, (cols, shard, edges, heads, padded...]
    ppermute x7 -> x4, starting transfers between devices: 9.36 us -> 5.99 us  [flip_x(): return lax.ppermute(value, 'row', [(r, r ^ 1) for r in range(rows_total)])]
    ppermute x5 -> x3, waiting for transfers between devices: 2.9 us -> 0.01 us  [turn_y(): lax.ppermute(value, 'col', [(c, (c + by * PAIR) % cols) for c in range(co...]
    ppermute x7 -> x4, waiting for transfers between devices: 2.83 us -> 5.7 us  [flip_x(): return lax.ppermute(value, 'row', [(r, r ^ 1) for r in range(rows_total)])]
    unnamed x8 -> x18, local copies, waits for them, and re-layouts: 1.82 us -> 4.31 us
  transfers between devices with their start and end apart: 30 -> 18, of which waited for: 9 -> 6; matrix products, arithmetic and copies ran while one was open for 3% -> 1% of each run, Pallas kernels for 25% -> 22%
where the time goes in v4:
time: 110 us
  blocking collectives  37.3 us (34%)
  Pallas kernels  32.2 us (29%)
  starting transfers between devices  21.8 us (20%)
  waiting for transfers between devices  11.5 us (10%)
  local copies, waits for them, and re-layouts  5.01 us (5%)
    all_gather x1, blocking collectives, on_device(): rows_of = lax.all_gather(coef_part.astype(BF16), 'row')  31.1 us
    ppermute x6, starting transfers between devices, turn_z(): lax.ppermute(value, 'row', [(r, (r + by * PAIR) % rows_total) for r in ra...  9.72 us
    pallas_call x1, Pallas kernels, on_device(): call(functools.partial(forward_kernel, (cols, shard, edges, heads, padded...  8.1 us
    pallas_call x2, Pallas kernels, basis_blocks(): call(functools.partial(basis_kernel, (rows_total, cols, block, cover // T...  7.14 us
    all_gather x1, blocking collectives, on_device(): lax.all_gather(coef_part, 'col')  6.22 us
    ppermute x4, starting transfers between devices, flip_x(): return lax.ppermute(value, 'row', [(r, r ^ 1) for r in range(rows_total)])  5.99 us
    ppermute x4, waiting for transfers between devices, flip_x(): return lax.ppermute(value, 'row', [(r, r ^ 1) for r in range(rows_total)])  5.7 us
    pallas_call x1, Pallas kernels, on_device(): call(functools.partial(source_kernel, (cols, shard, edges, heads, padded,...  5.65 us
  transfers between devices with their start and end apart: 18, of which 6 were waited for; matrix products, arithmetic and copies ran while one was open for 1% of the time, Pallas kernels for 22%

profile of v4, /device:TPU:0, one launch (start us, length us, event | category | flops | bytes accessed | tf_op | source)
XLA Modules:
  0.0 109.7 jit_solution(5418920986054487415)
XLA Ops:
  0.6 1.8 %edge_table.1.own = bf16[576,256]{1,0:T(8,128)(2,1)} custom-call(s32[1,1,8]{2,1,0:T(1,128)} %fills.1, s32[1,1,1024]{2,1,0:T(1,128)} %src.1, s32[1,1,1024]{2,1,0:T(1,128)} %dst.1, s32[1,1,1024]{2,1,0:T(1,128)} %rel.1, f32[1,1,1024]{2,1,0:T(1,128)} %norm.1, bf16[256,256]{1,0:T(8,128)(2,1)} %bitcast.10, bf16[256,256]{1,0:T(8,128)(2,1)} %feats.1), custom_call_target="tpu_custom_call" | custom-call | tf_op jit(solution)/shard_map/edge_table/pallas_call | solution.py:383
  2.5 2.9 %collective-permute-start = (bf16[576,256]{1,0:T(8,128)(2,1)}, bf16[576,256]{1,0:T(8,128)(2,1)S(1)}, u32[]{:S(2)}, u32[]{:S(2)}) collective-permute-start(bf16[576,256]{1,0:T(8,128)(2,1)} %edge_table.1.own), channel_id=1, source_target_pairs={{0,4},{4,0},{8,12},{12,8},{16,20},{20,16},{24,28},{28,24},{1,5},{5... | collective-permute-start | bytes 884744 | tf_op jit(solution)/shard_map/ppermute | solution.py:366
  5.4 1.6 %collective-permute-start.1 = (bf16[256,256]{1,0:T(8,128)(2,1)}, bf16[256,256]{1,0:T(8,128)(2,1)S(1)}, u32[]{:S(2)}, u32[]{:S(2)}) collective-permute-start(bf16[256,256]{1,0:T(8,128)(2,1)} %bitcast.11), channel_id=1, source_target_pairs={{0,8},{4,12},{8,16},{12,20},{16,24},{20,28},{24,0},{28,4},{1,9},{5... | collective-permute-start | bytes 393224 | tf_op jit(solution)/shard_map/ppermute | solution.py:372
  7.0 2.6 %collective-permute-start.2 = (bf16[256,256]{1,0:T(8,128)(2,1)}, bf16[256,256]{1,0:T(8,128)(2,1)S(1)}, u32[]{:S(2)}, u32[]{:S(2)}) collective-permute-start(bf16[256,256]{1,0:T(8,128)(2,1)} %bitcast.12), channel_id=1, source_target_pairs={{0,16},{4,20},{8,24},{12,28},{16,0},{20,4},{24,8},{28,12},{1,17},{... | collective-permute-start | bytes 393224 | tf_op jit(solution)/shard_map/ppermute | solution.py:372
  9.6 3.0 %collective-permute-done.other.refs_4_ = bf16[576,256]{1,0:T(8,128)(2,1)S(1)} collective-permute-done((bf16[576,256]{1,0:T(8,128)(2,1)}, bf16[576,256]{1,0:T(8,128)(2,1)S(1)}, u32[]{:S(2)}, u32[]{:S(2)}) %collective-permute-start) | collective-permute-done | bytes 294944 | tf_op jit(solution)/shard_map/ppermute | solution.py:366
  12.6 0.7 copy-done
  13.3 1.8 %near_rows.1.refs_0_ = bf16[512,256]{1,0:T(8,128)(2,1)} custom-call(bf16[576,256]{1,0:T(8,128)(2,1)} %edge_table.1.own, bf16[576,256]{1,0:T(8,128)(2,1)} %copy-done), custom_call_target="tpu_custom_call" | custom-call | tf_op jit(solution)/shard_map/near_rows/pallas_call | solution.py:387
  15.1 0.0 collective-permute-done.1.refs_1_
  15.1 2.9 %collective-permute-done.2.refs_2_ = bf16[256,256]{1,0:T(8,128)(2,1)S(1)} collective-permute-done((bf16[256,256]{1,0:T(8,128)(2,1)}, bf16[256,256]{1,0:T(8,128)(2,1)S(1)}, u32[]{:S(2)}, u32[]{:S(2)}) %collective-permute-start.2) | collective-permute-done | bytes 131104 | tf_op jit(solution)/shard_map/ppermute | solution.py:372
  18.0 1.5 %collective-permute-start.3 = (bf16[512,256]{1,0:T(8,128)(2,1)}, bf16[512,256]{1,0:T(8,128)(2,1)S(1)}, u32[]{:S(2)}, u32[]{:S(2)}) collective-permute-start(bf16[512,256]{1,0:T(8,128)(2,1)} %near_rows.1.refs_0_), channel_id=1, source_target_pairs={{0,2},{1,3},{2,0},{3,1},{4,6},{5,7},{6,4},{7,5},{8,10},{9,11},{10,... | collective-permute-start | bytes 786440 | tf_op jit(solution)/shard_map/ppermute | solution.py:377
  19.6 1.6 %collective-permute-start.6 = (bf16[256,256]{1,0:T(8,128)(2,1)}, bf16[256,256]{1,0:T(8,128)(2,1)S(1)}, u32[]{:S(2)}, u32[]{:S(2)}) collective-permute-start(bf16[256,256]{1,0:T(8,128)(2,1)} %bitcast.13), channel_id=1, source_target_pairs={{0,24},{4,28},{8,0},{12,4},{16,8},{20,12},{24,16},{28,20},{1,25},{... | collective-permute-start | bytes 393224 | tf_op jit(solution)/shard_map/ppermute | solution.py:372
  21.2 0.8 collective-permute-start.4
  22.0 1.2 %collective-permute-start.5 = (bf16[256,256]{1,0:T(8,128)(2,1)S(1)}, bf16[256,256]{1,0:T(8,128)(2,1)S(1)}, u32[]{:S(2)}, u32[]{:S(2)}) collective-permute-start(bf16[256,256]{1,0:T(8,128)(2,1)S(1)} %collective-permute-done.2.refs_2_), channel_id=1, source_target_pairs={{0,4},{4,0},{8,12},{12,8},{16,20},{20,16},{24,28},{28,24},{1,5},{5... | collective-permute-start | bytes 393224 | tf_op jit(solution)/shard_map/ppermute | solution.py:366
  23.2 1.7 %collective-permute-done.6.refs_3_ = bf16[256,256]{1,0:T(8,128)(2,1)S(1)} collective-permute-done((bf16[256,256]{1,0:T(8,128)(2,1)}, bf16[256,256]{1,0:T(8,128)(2,1)S(1)}, u32[]{:S(2)}, u32[]{:S(2)}) %collective-permute-start.6) | collective-permute-done | bytes 131104 | tf_op jit(solution)/shard_map/ppermute | solution.py:372
  24.9 1.2 %collective-permute-done.4.refs_5_ = bf16[256,256]{1,0:T(8,128)(2,1)S(1)} collective-permute-done((bf16[256,256]{1,0:T(8,128)(2,1)S(1)}, bf16[256,256]{1,0:T(8,128)(2,1)S(1)}, u32[]{:S(2)}, u32[]{:S(2)}) %collective-permute-start.4) | collective-permute-done | bytes 131104 | tf_op jit(solution)/shard_map/ppermute | solution.py:366
  26.2 1.4 %collective-permute-done.5.refs_6_ = bf16[256,256]{1,0:T(8,128)(2,1)S(1)} collective-permute-done((bf16[256,256]{1,0:T(8,128)(2,1)S(1)}, bf16[256,256]{1,0:T(8,128)(2,1)S(1)}, u32[]{:S(2)}, u32[]{:S(2)}) %collective-permute-start.5) | collective-permute-done | bytes 131104 | tf_op jit(solution)/shard_map/ppermute | solution.py:366
  27.6 0.0 collective-permute-done.3.refs_1_
  27.6 0.7 copy-done.8
  28.3 2.1 %packed_rows.1.own.packed.table = bf16[1152,256]{1,0:T(8,128)(2,1)} custom-call(bf16[576,256]{1,0:T(8,128)(2,1)} %edge_table.1.own, bf16[576,256]{1,0:T(8,128)(2,1)} %copy-done, bf16[512,256]{1,0:T(8,128)(2,1)} %near_rows.1.refs_0_, bf16[512,256]{1,0:T(8,128)(2,1)} %copy-done.8), custom_call_target="tpu_custom_call" | custom-call | tf_op jit(solution)/shard_map/packed_rows/pallas_call | solution.py:395
  30.3 0.0 collective-permute-start.8
  30.3 0.1 pad_add_fusion.place
  30.4 1.0 collective-permute-start.7
  31.4 1.1 %collective-permute-done.8.other = bf16[1152,256]{1,0:T(8,128)(2,1)S(1)} collective-permute-done((bf16[1152,256]{1,0:T(8,128)(2,1)}, bf16[1152,256]{1,0:T(8,128)(2,1)S(1)}, u32[]{:S(2)}, u32[]{:S(2)}) %collective-permute-start.8) | collective-permute-done | bytes 589856 | tf_op jit(solution)/shard_map/ppermute | solution.py:369
  32.6 1.1 copy-done.2
  33.6 0.9 copy-done.4
  34.5 0.9 copy-done.7
  35.4 5.7 %source_rows.1 = (bf16[4,256,1024]{2,1,0:T(8,128)(2,1)S(1)}, f32[4,32,1024]{2,1,0:T(8,128)S(1)}) custom-call(s32[4]{0:T(128)S(1)} %pad_add_fusion.place, bf16[1152,256]{1,0:T(8,128)(2,1)S(1)} %copy-done.2, bf16[1152,256]{1,0:T(8,128)(2,1)S(1)} %collective-permute-done.8.other, bf16[30,2000]{1,0:T(8,128)(2,1)S(1)} %bitcast.16, bf16[256,256]{1,0:T(8,128)(2,1)S(1)} %bitcast.14, ...), custom_call_target="tpu_custom_call" | custom-call | flops 2147483648 | bytes 4194304 | tf_op jit(solution)/shard_map/source_rows/pallas_call | solution.py:400
  41.1 0.0 copy-start.6
  41.1 4.0 %edge_grads.1.gt_ref = bf16[256,2048]{1,0:T(8,128)(2,1)S(1)} custom-call(s32[4]{0:T(128)S(1)} %pad_add_fusion.place, bf16[1152,256]{1,0:T(8,128)(2,1)S(1)} %copy-done.3, bf16[256,256]{1,0:T(8,128)(2,1)S(1)} %bitcast.15, bf16[256,256]{1,0:T(8,128)(2,1)S(1)} %collective-permute-done.1.refs_1_, bf16[256,256]{1,0:T(8,128)(2,1)S(1)} %collective-permute-done.2.refs_2_, ...), custom_call_target="tpu_custom_call" | custom-call | flops 2147483648 | bytes 4194304 | tf_op jit(solution)/shard_map/edge_grads/pallas_call | solution.py:416
  45.2 0.2 collective-permute-start.10
  45.4 8.1 %backed_sums.1 = (bf16[320,256]{1,0:T(8,128)(2,1)S(1)}, bf16[320,256]{1,0:T(8,128)(2,1)S(1)}, bf16[320,256]{1,0:T(8,128)(2,1)S(1)}, bf16[320,256]{1,0:T(8,128)(2,1)S(1)}) custom-call(s32[4]{0:T(128)S(1)} %pad_add_fusion.place, bf16[1152,256]{1,0:T(8,128)(2,1)S(1)} %copy-done.3, bf16[256,2048]{1,0:T(8,128)(2,1)S(1)} %edge_grads.1.gt_ref, ...), custom_call_target="tpu_custom_call" | custom-call | flops 4026531840 | bytes 4194304 | tf_op jit(solution)/shard_map/backed_sums/pallas_call | solution.py:429
  53.5 0.6 collective-permute-start.9
  54.1 0.1 collective-permute-start.11
  54.1 1.6 %collective-permute-start.12 = (bf16[320,256]{1,0:T(8,128)(2,1)S(1)}, bf16[320,256]{1,0:T(8,128)(2,1)S(1)}, u32[]{:S(2)}, u32[]{:S(2)}) collective-permute-start(bf16[320,256]{1,0:T(8,128)(2,1)S(1)} %get-tuple-element.38), channel_id=1, source_target_pairs={{0,3},{1,2},{2,1},{3,0},{4,7},{5,6},{6,5},{7,4},{8,11},{9,10},{10,... | collective-permute-start | bytes 491528 | tf_op jit(solution)/shard_map/ppermute | solution.py:469
  55.7 3.6 %basis_terms.3 = (f32[480,256]{1,0:T(8,128)S(1)}, bf16[480,256]{1,0:T(8,128)(2,1)S(1)}) custom-call(s32[4]{0:T(128)S(1)} %pad_add_fusion.place, bf16[256,2048]{1,0:T(8,128)(2,1)S(1)} %edge_grads.1.gt_ref, bf16[256,2048]{1,0:T(8,128)(2,1)S(1)} %collective-permute-done.10.gt_core, bf16[4,256,1024]{2,1,0:T(8,128)(2,1)S(1)} %get-tuple-element.30.refs_8_.xt_ref, ...), custom_call_target="tpu_custom_call" | custom-call | flops 2013265920 | bytes 4194304 | tf_op jit(solution)/shard_map/basis_terms/pallas_call | solution.py:448
  59.3 0.6 collective-permute-start.14
  59.9 3.6 %basis_terms.2 = (f32[480,256]{1,0:T(8,128)S(1)}, bf16[480,256]{1,0:T(8,128)(2,1)S(1)}) custom-call(s32[4]{0:T(128)S(1)} %pad_add_fusion.place, bf16[256,2048]{1,0:T(8,128)(2,1)S(1)} %edge_grads.1.gt_ref, bf16[256,2048]{1,0:T(8,128)(2,1)S(1)} %collective-permute-done.10.gt_core, bf16[4,256,1024]{2,1,0:T(8,128)(2,1)S(1)} %get-tuple-element.30.refs_8_.xt_ref, ...), custom_call_target="tpu_custom_call" | custom-call | flops 2013265920 | bytes 4194304 | tf_op jit(solution)/shard_map/basis_terms/pallas_call | solution.py:448
  63.4 1.6 %collective-permute-start.13 = (bf16[480,256]{1,0:T(8,128)(2,1)S(1)}, bf16[480,256]{1,0:T(8,128)(2,1)S(1)}, u32[]{:S(2)}, u32[]{:S(2)}) collective-permute-start(bf16[480,256]{1,0:T(8,128)(2,1)S(1)} %get-tuple-element.40), channel_id=1, source_target_pairs={{0,2},{1,3},{2,0},{3,1},{4,6},{5,7},{6,4},{7,5},{8,10},{9,11},{10,... | collective-permute-start | bytes 737288 | tf_op jit(solution)/shard_map/ppermute | solution.py:377
  65.0 0.1 add_convert_fusion.1
  65.1 31.1 %all-gather = bf16[512,256]{1,0:T(8,128)(2,1)S(1)} all-gather(bf16[64,256]{1,0:T(8,128)(2,1)S(1)} %slice.34), channel_id=2, replica_groups=mesh['row'=8,'col'=4] {'row'}, dimensions={0}, use_global_device_ids=true | all-gather | bytes 294912 | tf_op jit(solution)/shard_map/all_gather | solution.py:506
  96.2 0.1 add_convert_fusion
  96.3 0.1 collective-permute-start.15
  96.4 1.0 collective-permute-start.16
  97.4 2.9 %collective-permute-start.17 = (bf16[240,256]{1,0:T(8,128)(2,1)S(1)}, bf16[240,256]{1,0:T(8,128)(2,1)S(1)}, u32[]{:S(2)}, u32[]{:S(2)}) collective-permute-start(bf16[240,256]{1,0:T(8,128)(2,1)S(1)} %slice.43), channel_id=1, source_target_pairs={{0,24},{4,28},{8,0},{12,4},{16,8},{20,12},{24,16},{28,20},{1,25},{... | collective-permute-start | bytes 368648 | tf_op jit(solution)/shard_map/ppermute | solution.py:372
  100.3 0.7 slice.29
  101.0 6.2 %all-gather.1 = f32[256,256]{1,0:T(8,128)} all-gather(f32[64,256]{1,0:T(8,128)S(1)} %convert_reduce_fusion), channel_id=3, replica_groups=mesh['row'=8,'col'=4] {'col'}, dimensions={0}, use_global_device_ids=true | all-gather | bytes 327680 | tf_op jit(solution)/shard_map/all_gather | solution.py:515
  107.2 1.7 %coef_rows.1 = f32[30,2000]{1,0:T(8,128)} custom-call(f32[4,64,256]{2,1,0:T(8,128)} %bitcast.18), custom_call_target="tpu_custom_call" | custom-call | tf_op jit(solution)/shard_map/coef_rows/pallas_call | solution.py:508
  108.9 0.8 fusion.2
  (27 shorter events, 0.2 us)
Async XLA Ops:
  2.5 10.2 %collective-permute-start = (bf16[576,256]{1,0:T(8,128)(2,1)}, bf16[576,256]{1,0:T(8,128)(2,1)S(1)}, u32[]{:S(2)}, u32[]{:S(2)}) collective-permute-start(bf16[576,256]{1,0:T(8,128)(2,1)} %edge_table.1.own), channel_id=1, source_target_pairs={{0,4},{4,0},{8,12},{12,8},{16,20},{20,16},{24,28},{28,24},{1,5},{5... | collective-permute-start | bytes 884744 | tf_op jit(solution)/shard_map/ppermute | solution.py:366
  5.4 9.7 %collective-permute-start.1 = (bf16[256,256]{1,0:T(8,128)(2,1)}, bf16[256,256]{1,0:T(8,128)(2,1)S(1)}, u32[]{:S(2)}, u32[]{:S(2)}) collective-permute-start(bf16[256,256]{1,0:T(8,128)(2,1)} %bitcast.11), channel_id=1, source_target_pairs={{0,8},{4,12},{8,16},{12,20},{16,24},{20,28},{24,0},{28,4},{1,9},{5... | collective-permute-start | bytes 393224 | tf_op jit(solution)/shard_map/ppermute | solution.py:372
  7.0 11.1 %collective-permute-start.2 = (bf16[256,256]{1,0:T(8,128)(2,1)}, bf16[256,256]{1,0:T(8,128)(2,1)S(1)}, u32[]{:S(2)}, u32[]{:S(2)}) collective-permute-start(bf16[256,256]{1,0:T(8,128)(2,1)} %bitcast.12), channel_id=1, source_target_pairs={{0,16},{4,20},{8,24},{12,28},{16,0},{20,4},{24,8},{28,12},{1,17},{... | collective-permute-start | bytes 393224 | tf_op jit(solution)/shard_map/ppermute | solution.py:372
  12.6 0.7 copy-start
  18.0 9.5 %collective-permute-start.3 = (bf16[512,256]{1,0:T(8,128)(2,1)}, bf16[512,256]{1,0:T(8,128)(2,1)S(1)}, u32[]{:S(2)}, u32[]{:S(2)}) collective-permute-start(bf16[512,256]{1,0:T(8,128)(2,1)} %near_rows.1.refs_0_), channel_id=1, source_target_pairs={{0,2},{1,3},{2,0},{3,1},{4,6},{5,7},{6,4},{7,5},{8,10},{9,11},{10,... | collective-permute-start | bytes 786440 | tf_op jit(solution)/shard_map/ppermute | solution.py:377
  19.6 5.3 %collective-permute-start.6 = (bf16[256,256]{1,0:T(8,128)(2,1)}, bf16[256,256]{1,0:T(8,128)(2,1)S(1)}, u32[]{:S(2)}, u32[]{:S(2)}) collective-permute-start(bf16[256,256]{1,0:T(8,128)(2,1)} %bitcast.13), channel_id=1, source_target_pairs={{0,24},{4,28},{8,0},{12,4},{16,8},{20,12},{24,16},{28,20},{1,25},{... | collective-permute-start | bytes 393224 | tf_op jit(solution)/shard_map/ppermute | solution.py:372
  21.2 5.0 %collective-permute-start.4 = (bf16[256,256]{1,0:T(8,128)(2,1)S(1)}, bf16[256,256]{1,0:T(8,128)(2,1)S(1)}, u32[]{:S(2)}, u32[]{:S(2)}) collective-permute-start(bf16[256,256]{1,0:T(8,128)(2,1)S(1)} %collective-permute-done.1.refs_1_), channel_id=1, source_target_pairs={{0,4},{4,0},{8,12},{12,8},{16,20},{20,16},{24,28},{28,24},{1,5},{5... | collective-permute-start | bytes 393224 | tf_op jit(solution)/shard_map/ppermute | solution.py:366
  22.0 5.6 %collective-permute-start.5 = (bf16[256,256]{1,0:T(8,128)(2,1)S(1)}, bf16[256,256]{1,0:T(8,128)(2,1)S(1)}, u32[]{:S(2)}, u32[]{:S(2)}) collective-permute-start(bf16[256,256]{1,0:T(8,128)(2,1)S(1)} %collective-permute-done.2.refs_2_), channel_id=1, source_target_pairs={{0,4},{4,0},{8,12},{12,8},{16,20},{20,16},{24,28},{28,24},{1,5},{5... | collective-permute-start | bytes 393224 | tf_op jit(solution)/shard_map/ppermute | solution.py:366
  27.6 0.7 copy-start.8
  30.3 2.2 %collective-permute-start.8 = (bf16[1152,256]{1,0:T(8,128)(2,1)}, bf16[1152,256]{1,0:T(8,128)(2,1)S(1)}, u32[]{:S(2)}, u32[]{:S(2)}) collective-permute-start(bf16[1152,256]{1,0:T(8,128)(2,1)} %packed_rows.1.own.packed.table), channel_id=1, source_target_pairs={{0,1},{1,0},{2,3},{3,2},{4,5},{5,4},{6,7},{7,6},{8,9},{9,8},{10,11... | collective-permute-start | bytes 1769480 | tf_op jit(solution)/shard_map/ppermute | solution.py:369
  30.4 10.7 %collective-permute-start.7 = (bf16[256,256]{1,0:T(8,128)(2,1)S(1)}, bf16[256,256]{1,0:T(8,128)(2,1)S(1)}, u32[]{:S(2)}, u32[]{:S(2)}) collective-permute-start(bf16[256,256]{1,0:T(8,128)(2,1)S(1)} %collective-permute-done.6.refs_3_), channel_id=1, source_target_pairs={{0,4},{4,0},{8,12},{12,8},{16,20},{20,16},{24,28},{28,24},{1,5},{5... | collective-permute-start | bytes 393224 | tf_op jit(solution)/shard_map/ppermute | solution.py:366
  32.6 1.1 copy-start.2
  33.6 0.9 copy-start.4
  34.5 0.9 copy-start.7
  35.4 5.7 %copy-start.1 = (bf16[576,256]{1,0:T(8,128)(2,1)S(1)}, bf16[576,256]{1,0:T(8,128)(2,1)}, u32[]{:S(2)}) copy-start(bf16[576,256]{1,0:T(8,128)(2,1)} %copy-done) | copy-start | bytes 884740
  35.4 5.7 %copy-start.3 = (bf16[1152,256]{1,0:T(8,128)(2,1)S(1)}, bf16[1152,256]{1,0:T(8,128)(2,1)}, u32[]{:S(2)}) copy-start(bf16[1152,256]{1,0:T(8,128)(2,1)} %packed_rows.1.own.packed.table) | copy-start | bytes 1769476
  35.4 5.7 %copy-start.5 = (bf16[1,256,256]{2,1,0:T(8,128)(2,1)S(1)}, bf16[1,256,256]{2,1,0:T(8,128)(2,1)}, u32[]{:S(2)}) copy-start(bf16[1,256,256]{2,1,0:T(8,128)(2,1)} %param.10) | copy-start | bytes 393220
  41.1 4.2 %copy-start.6 = (bf16[30,256,256]{2,1,0:T(8,128)(2,1)S(1)}, bf16[30,256,256]{2,1,0:T(8,128)(2,1)}, u32[]{:S(2)}) copy-start(bf16[30,256,256]{2,1,0:T(8,128)(2,1)} %bases_ref.1) | copy-start | bytes 11796484
  45.2 10.6 %collective-permute-start.10 = (bf16[256,2048]{1,0:T(8,128)(2,1)S(1)}, bf16[256,2048]{1,0:T(8,128)(2,1)S(1)}, u32[]{:S(2)}, u32[]{:S(2)}) collective-permute-start(bf16[256,2048]{1,0:T(8,128)(2,1)S(1)} %edge_grads.1.gt_ref), channel_id=1, source_target_pairs={{0,1},{1,0},{2,3},{3,2},{4,5},{5,4},{6,7},{7,6},{8,9},{9,8},{10,11... | collective-permute-start | bytes 3145736 | tf_op jit(solution)/shard_map/ppermute | solution.py:369
  53.5 11.5 %collective-permute-start.9 = (bf16[320,256]{1,0:T(8,128)(2,1)S(1)}, bf16[320,256]{1,0:T(8,128)(2,1)S(1)}, u32[]{:S(2)}, u32[]{:S(2)}) collective-permute-start(bf16[320,256]{1,0:T(8,128)(2,1)S(1)} %get-tuple-element.33), channel_id=1, source_target_pairs={{0,2},{1,3},{2,0},{3,1},{4,6},{5,7},{6,4},{7,5},{8,10},{9,11},{10,... | collective-permute-start | bytes 491528 | tf_op jit(solution)/shard_map/ppermute | solution.py:469
  54.1 10.9 %collective-permute-start.11 = (bf16[320,256]{1,0:T(8,128)(2,1)S(1)}, bf16[320,256]{1,0:T(8,128)(2,1)S(1)}, u32[]{:S(2)}, u32[]{:S(2)}) collective-permute-start(bf16[320,256]{1,0:T(8,128)(2,1)S(1)} %get-tuple-element.36), channel_id=1, source_target_pairs={{0,1},{1,0},{2,3},{3,2},{4,5},{5,4},{6,7},{7,6},{8,9},{9,8},{10,11... | collective-permute-start | bytes 491528 | tf_op jit(solution)/shard_map/ppermute | solution.py:469
  54.1 10.9 %collective-permute-start.12 = (bf16[320,256]{1,0:T(8,128)(2,1)S(1)}, bf16[320,256]{1,0:T(8,128)(2,1)S(1)}, u32[]{:S(2)}, u32[]{:S(2)}) collective-permute-start(bf16[320,256]{1,0:T(8,128)(2,1)S(1)} %get-tuple-element.38), channel_id=1, source_target_pairs={{0,3},{1,2},{2,1},{3,0},{4,7},{5,6},{6,5},{7,4},{8,11},{9,10},{10,... | collective-permute-start | bytes 491528 | tf_op jit(solution)/shard_map/ppermute | solution.py:469
  59.3 36.9 %collective-permute-start.14 = (bf16[480,256]{1,0:T(8,128)(2,1)S(1)}, bf16[480,256]{1,0:T(8,128)(2,1)S(1)}, u32[]{:S(2)}, u32[]{:S(2)}) collective-permute-start(bf16[480,256]{1,0:T(8,128)(2,1)S(1)} %get-tuple-element.42), channel_id=1, source_target_pairs={{0,2},{1,3},{2,0},{3,1},{4,6},{5,7},{6,4},{7,5},{8,10},{9,11},{10,... | collective-permute-start | bytes 737288 | tf_op jit(solution)/shard_map/ppermute | solution.py:377
  63.4 33.9 %collective-permute-start.13 = (bf16[480,256]{1,0:T(8,128)(2,1)S(1)}, bf16[480,256]{1,0:T(8,128)(2,1)S(1)}, u32[]{:S(2)}, u32[]{:S(2)}) collective-permute-start(bf16[480,256]{1,0:T(8,128)(2,1)S(1)} %get-tuple-element.40), channel_id=1, source_target_pairs={{0,2},{1,3},{2,0},{3,1},{4,6},{5,7},{6,4},{7,5},{8,10},{9,11},{10,... | collective-permute-start | bytes 737288 | tf_op jit(solution)/shard_map/ppermute | solution.py:377
  96.3 12.6 %collective-permute-start.15 = (bf16[240,256]{1,0:T(8,128)(2,1)S(1)}, bf16[240,256]{1,0:T(8,128)(2,1)S(1)}, u32[]{:S(2)}, u32[]{:S(2)}) collective-permute-start(bf16[240,256]{1,0:T(8,128)(2,1)S(1)} %get-tuple-element.43), channel_id=1, source_target_pairs={{0,8},{4,12},{8,16},{12,20},{16,24},{20,28},{24,0},{28,4},{1,9},{5... | collective-permute-start | bytes 368648 | tf_op jit(solution)/shard_map/ppermute | solution.py:372
  96.4 12.6 %collective-permute-start.16 = (bf16[240,256]{1,0:T(8,128)(2,1)S(1)}, bf16[240,256]{1,0:T(8,128)(2,1)S(1)}, u32[]{:S(2)}, u32[]{:S(2)}) collective-permute-start(bf16[240,256]{1,0:T(8,128)(2,1)S(1)} %get-tuple-element.44), channel_id=1, source_target_pairs={{0,16},{4,20},{8,24},{12,28},{16,0},{20,4},{24,8},{28,12},{1,17},{... | collective-permute-start | bytes 368648 | tf_op jit(solution)/shard_map/ppermute | solution.py:372
  97.4 11.5 %collective-permute-start.17 = (bf16[240,256]{1,0:T(8,128)(2,1)S(1)}, bf16[240,256]{1,0:T(8,128)(2,1)S(1)}, u32[]{:S(2)}, u32[]{:S(2)}) collective-permute-start(bf16[240,256]{1,0:T(8,128)(2,1)S(1)} %slice.43), channel_id=1, source_target_pairs={{0,24},{4,28},{8,0},{12,4},{16,8},{20,12},{24,16},{28,20},{1,25},{... | collective-permute-start | bytes 368648 | tf_op jit(solution)/shard_map/ppermute | solution.py:372

commit v5 on v3

--- a/solution.py
+++ b/solution.py
@@ -8,6 +8,7 @@
 
 EDGE_BLOCK = 128
 TILE = 16
+BAND = 64
 LANES = 128
 PAIR = 2
 F32 = jnp.float32
@@ -89,7 +90,8 @@
     )
 
 
-def prepare_kernel(fills, src, dst, rel, norm, out_ref):
+def prepare_kernel(heads, padded, fills, src, dst, rel, norm, coefs_t, dest, *outs):
+    out_ref, coefs, dest_out = outs
     blocks = fills.shape[-1]
     out_ref[0:1, :] = src[0].astype(F32)
     out_ref[1:2, :] = dst[0].astype(F32)
@@ -99,22 +101,8 @@
         here = slice(at * EDGE_BLOCK, (at + 1) * EDGE_BLOCK)
         live = jnp.where(lane < fills[0, 0, at], 1.0, 0.0)
         out_ref[3:4, here] = norm[0, :, here] * live
-
-
-def source_kernel(sizes, place, meta, meta_core, feats, feats_core, coefs_t, *refs):
-    cols, shard, span, heads, padded, extra = sizes
-    xt_ref, ct_ref, table, coefs = refs[extra:]
-    count = cols // PAIR
-    y, core = place[2], place[3]
-    width = feats.shape[-1]
-    edges = meta.shape[-1]
+    dest_out[...] = dest[...]
     basis_count, relation_count = coefs_t.shape
-    unit = eye(width)
-    for far, block in enumerate((feats, feats_core)):
-        for sy in range(count):
-            for xr in range(PAIR):
-                at = (far * count + sy) * shard
-                table[xr, :, at : at + shard] = dot_t(unit, block[sy, xr]).astype(BF16)
     coefs[...] = jnp.zeros_like(coefs)
     for head in range(heads):
         live = min(LANES, relation_count - head * LANES)
@@ -122,6 +110,21 @@
             coefs[head * padded : head * padded + basis_count, 0:live] = coefs_t[
                 :, head * LANES : head * LANES + live
             ]
+
+
+def source_kernel(sizes, place, meta, meta_core, feats, feats_core, coefs, *refs):
+    cols, shard, span, heads, padded, extra = sizes
+    xt_ref, ct_ref, table = refs[extra:]
+    count = cols // PAIR
+    y, core = place[2], place[3]
+    width = feats.shape[-1]
+    edges = meta.shape[-1]
+    unit = eye(width)
+    for far, block in enumerate((feats, feats_core)):
+        for sy in range(count):
+            for xr in range(PAIR):
+                at = (far * count + sy) * shard
+                table[xr, :, at : at + shard] = dot_t(unit, block[sy, xr]).astype(BF16)
     for far, source in enumerate((meta, meta_core)):
 
         def step(index, carry, far=far, source=source):
@@ -179,30 +182,47 @@
 ):
     cols, shard, span, heads, padded, group = sizes
     outs = refs[:cols]
-    total, inner, wide, coef_sum = refs[cols:]
+    total, inner, wide, coef_sum, *buffers = refs[cols:]
     count = cols // PAIR
     y, core = place[2], place[3]
     edges = meta.shape[-1]
     width = bases_ref.shape[-1]
     total[...] = jnp.zeros_like(total)
     inner[...] = jnp.zeros_like(inner)
+    steps = bases_ref.shape[0] // group
+    chunks = edges // span
+
+    def product(number, index, buffer):
+        stacked = bases_ref[pl.ds(number * group, group)].reshape(group * width, width)
+        buffer[...] = dot(stacked, gt_ref[:, index * span : (index + 1) * span])
+
+    def reduce(number, index, buffer):
+        at = slice(index * span, (index + 1) * span)
+        scales = [ct_ref[0, pl.ds(number * group + t, 1), at] for t in range(group)]
+        parts = [jnp.zeros((8, span), F32) for _ in range(group)]
+        for low in range(0, width, BAND):
+            sums = total[low : low + BAND, at]
+            rows = xt_ref[0, low : low + BAND, at].astype(F32)
+            for t in range(group):
+                mine = buffer[t * width + low : t * width + low + BAND, :]
+                sums = sums + scales[t] * mine
+                parts[t] = parts[t] + jnp.sum((mine * rows).reshape(BAND // 8, 8, span), axis=0)
+            total[low : low + BAND, at] = sums
+        for t in range(group):
+            inner[pl.ds(number * group + t, 1), at] = jnp.sum(parts[t], axis=0, keepdims=True)
+
+    product(0, 0, buffers[0])
 
     def step(number, carry):
-        stacked = bases_ref[pl.ds(number * group, group)].reshape(group * width, width)
-        for index in range(edges // span):
-            at = slice(index * span, (index + 1) * span)
-            backed = dot(stacked, gt_ref[:, at])
-            rows = xt_ref[0, :, at].astype(F32)
-            sums = total[:, at]
-            for t in range(group):
-                base = number * group + t
-                mine = backed[t * width : (t + 1) * width]
-                sums = sums + ct_ref[0, pl.ds(base, 1), at] * mine
-                inner[pl.ds(base, 1), at] = jnp.sum(mine * rows, axis=0, keepdims=True)
-            total[:, at] = sums
+        for index in range(chunks):
+            if index + 1 < chunks:
+                product(number, index + 1, buffers[(index + 1) % 2])
+            else:
+                product(jnp.minimum(number + 1, steps - 1), 0, buffers[(index + 1) % 2])
+            reduce(number, index, buffers[index % 2])
         return carry
 
-    lax.fori_loop(0, bases_ref.shape[0] // group, step, 0)
+    lax.fori_loop(0, steps, step, 0)
 
     ids = meta[0, 0:1, :].astype(I32)
     owner, local = split_index(ids, shard)
@@ -218,32 +238,32 @@
             high == head, inner[...], 0.0
         ).astype(BF16)
     coef_sum[...] = dot_t(wide[...], one_hot(low, LANES))
-    share = heads * padded // cols
+    share = heads * padded // PAIR
     half = share // 2
     for far in range(PAIR):
-        for sy in range(count):
-            target = (y + sy) % count * PAIR + (core ^ far)
-            for side in range(2):
-                rows = coef_sum[pl.ds(pl.multiple_of(target * share + side * half, 8), half), :]
+        for side in range(2):
+            at = pl.multiple_of((core ^ far) * share + side * half, 8)
+            rows = coef_sum[pl.ds(at, half), :].astype(BF16)
+            for sy in range(count):
                 outs[far * count + sy][
                     shard : shard + half, side * LANES : (side + 1) * LANES
-                ] = rows.astype(BF16)
+                ] = rows
 
 
 def basis_kernel(sizes, place, gt_ref, gt_core, xt_ref, ct_ref, *refs):
     rows_total, cols, block, groups, basis_count, span, turns = sizes
     a_count, y_count = rows_total // PAIR, cols // PAIR
     a, x, y, core = place[0], place[1], place[2], place[3]
-    outs = refs[: y_count * len(turns)]
+    outs = refs[:y_count]
     acc, left_even, left_odd, tiles = refs[len(outs) :]
     width, edges = xt_ref.shape[1], xt_ref.shape[2]
     tiles_wide = width // TILE
     cover = groups * TILE
-    spread = tiles.shape[0] // len(outs)
+    spread = tiles.shape[0] // (y_count * len(turns))
     steps = edges // span
     firsts = []
-    for sz in turns:
-        for sy in range(y_count):
+    for sy in range(y_count):
+        for sz in turns:
             owner = ((a + sz) % a_count * PAIR + x) * cols + (y + sy) % y_count * PAIR + core
             firsts.append(owner * block // TILE)
 
@@ -274,24 +294,20 @@
             acc[...] += term
         else:
             acc[...] = term
-    for order, out in enumerate(outs):
-        out[...] = acc[order * cover : (order + 1) * cover, :].astype(out.dtype)
-
-
-def coef_kernel(sizes, place, *refs):
-    cols, heads, padded, divisor = sizes
-    count = cols // PAIR
-    parts, (out_ref, whole) = refs[:cols], refs[cols:]
-    y, core = place[2], place[3]
-    share = heads * padded // cols
+    size = len(turns) * cover
+    for sy, out in enumerate(outs):
+        out[...] = acc[sy * size : (sy + 1) * size, :].astype(out.dtype)
+
+
+def coef_kernel(sizes, place, own, other, out_ref, whole):
+    heads, padded, divisor = sizes
+    core = place[3]
+    share = heads * padded // PAIR
     half = share // 2
-    for far in range(PAIR):
-        for sy in range(count):
-            target = wrap(y - sy, count) * PAIR + (core ^ far)
-            for side in range(2):
-                whole[pl.ds(pl.multiple_of(target * share + side * half, 8), half), :] = (
-                    parts[far * count + sy][:, side * LANES : (side + 1) * LANES]
-                )
+    for far, part in enumerate((own, other)):
+        for side in range(2):
+            at = pl.multiple_of((core ^ far) * share + side * half, 8)
+            whole[pl.ds(at, half), :] = part[:, side * LANES : (side + 1) * LANES]
     width, total = out_ref.shape
     for head in range(heads):
         live = min(LANES, total - head * LANES)
@@ -313,7 +329,7 @@
     edges = src_ids.size
     padded = round_up(basis_count, TILE)
     heads = round_up(relation_count, LANES) // LANES
-    while heads * padded % (cols * 2 * TILE):
+    while heads * padded % (PAIR * 2 * TILE):
         heads += 1
     span = 256
     i = lax.axis_index("row")
@@ -338,22 +354,31 @@
     turned = [turn_z(own_dest, s) for s in range(1, a_count)]
     across_own = flip_x(own_dest)
     near = flip_x(node_feats)
-    meta = pl.pallas_call(
-        prepare_kernel,
-        out_shape=jax.ShapeDtypeStruct((4, edges), F32),
-        in_specs=[smem()] + [vmem()] * 4,
-        out_specs=vmem(),
+    meta, coefs, own_dest = pl.pallas_call(
+        functools.partial(prepare_kernel, heads, padded),
+        out_shape=(
+            jax.ShapeDtypeStruct((4, edges), F32),
+            jax.ShapeDtypeStruct((heads * padded, LANES), BF16),
+            jax.ShapeDtypeStruct(own_dest.shape, BF16),
+        ),
+        in_specs=[smem()] + [vmem()] * 6,
+        out_specs=[vmem()] * 3,
         name="edge_table",
-    )(block_fill, src_ids, dst_ids, rel_ids, edge_norm)
+    )(block_fill, src_ids, dst_ids, rel_ids, edge_norm, coefs.T, own_dest)
     meta = jnp.stack([meta, flip_x(meta)])
-    feats, turned[0] = lax.optimization_barrier((jnp.stack([node_feats, near]), turned[0]))
+    first = a_count // 2 - 1
+    feats, turned[first] = lax.optimization_barrier(
+        (jnp.stack([node_feats, near]), turned[first])
+    )
     feats = jnp.stack([feats] + [turn_y(feats, s) for s in range(1, y_count)])
-    across = [across_own, flip_x(turned[0])]
-    feats, meta, across[0], across[1], *turned[1:] = lax.optimization_barrier(
-        (feats, meta, *across, *turned[1:])
+    across = [flip_x(turned[s]) if s == first else None for s in range(a_count - 1)]
+    feats, meta, across_own, across[first], *turned = lax.optimization_barrier(
+        (feats, meta, across_own, across[first], *turned)
     )
     dest = [own_dest] + turned
-    across += [flip_x(value) for value in turned[1:]]
+    across = [across_own] + [
+        across[s] if s == first else flip_x(turned[s]) for s in range(a_count - 1)
+    ]
     meta_core = flip_core(meta)
     feats_core = flip_core(feats)
 
@@ -366,12 +391,11 @@
         5,
         [
             pltpu.VMEM((PAIR, width, cols * shard), BF16),
-            pltpu.VMEM((heads * padded, LANES), BF16),
         ],
         2 * 4 * edges * cols * shard * width,
         "source_rows",
         a_count,
-    )(place, meta, meta_core, feats, feats_core, coefs.T, *dest)
+    )(place, meta, meta_core, feats, feats_core, coefs, *dest)
 
     dest_shard = own_dest.shape[0]
     gt = call(
@@ -386,7 +410,7 @@
     gt_core = flip_core(gt)
 
     group = max(g for g in range(1, 6) if basis_count % g == 0)
-    share_rows = heads * padded // cols // 2
+    share_rows = heads * padded // PAIR // 2
     packed = call(
         functools.partial(forward_kernel, (cols, shard, span, heads, padded, group)),
         [jax.ShapeDtypeStruct((shard + share_rows, width), BF16)] * cols,
@@ -396,6 +420,8 @@
             pltpu.VMEM((padded, edges), F32),
             pltpu.VMEM((heads * padded, edges), BF16),
             pltpu.VMEM((heads * padded, LANES), F32),
+            pltpu.VMEM((group * width, span), F32),
+            pltpu.VMEM((group * width, span), F32),
         ],
         2 * edges * width * width * basis_count,
         "backed_sums",
@@ -412,8 +438,7 @@
                 (rows_total, cols, block, cover // TILE, basis_count, 2 * span, turns),
             ),
             [
-                jax.ShapeDtypeStruct((cover, width), BF16 if sy else F32)
-                for _ in turns
+                jax.ShapeDtypeStruct((len(turns) * cover, width), BF16 if sy else F32)
                 for sy in range(y_count)
             ],
             4,
@@ -440,23 +465,23 @@
     others = [(far, sy) for far in range(PAIR) for sy in range(y_count) if far or sy]
     received = [to_col(packed[far * y_count + sy], far, sy) for far, sy in others]
 
-    sums, passed, marks = {}, [], []
     order = tuple(range(1, a_count)) + (0,)
-    for at, sz in enumerate(order):
-        where = place
-        if at >= 2:
-            where = after(where, passed[at - 2])
-        blocks = basis_blocks(where, (sz,))
-        value = blocks[0]
-        arrived = [turn_y(blocks[sy], sy) for sy in range(1, y_count)]
-        for piece in arrived:
-            value = value + piece.astype(F32)
-        sums[sz] = turn_z(value.astype(BF16), sz) if sz else value
-        passed.append(arrived[-1] if arrived else blocks[0])
-        marks.append(blocks[0])
+    half = (a_count + 1) // 2
+    sums, where, landed = {}, place, []
+    for turns in (order[:half], order[half:]):
+        if turns:
+            blocks = basis_blocks(where, turns)
+            where = after(place, blocks[0])
+            value = blocks[0]
+            for sy in range(1, y_count):
+                landed.append(turn_y(blocks[sy], sy))
+                value = value + landed[-1].astype(F32)
+            for at, sz in enumerate(turns):
+                piece = value[at * cover : (at + 1) * cover]
+                sums[sz] = turn_z(piece.astype(BF16), sz) if sz else piece
     joined = packed[0].astype(F32)
     for value in received:
-        joined = joined + after(value, marks[min(1, a_count - 1)]).astype(F32)
+        joined = joined + after(value, blocks[0]).astype(F32)
     basis_sum = sums[0]
     for sz in range(1, a_count):
         basis_sum = basis_sum + sums[sz].astype(F32)
@@ -468,18 +493,18 @@
     node_grad = joined[:shard].astype(BF16)
     coef_part = joined[shard:]
     low = coef_part.astype(BF16)
-    low = (low.astype(F32) + after(flip_x(low), marks[max(a_count - 2, 0)]).astype(F32)).astype(BF16)
-    around = [after(turn_z(low, s), marks[-1]).astype(F32) for s in range(1, a_count)]
+    low = (low.astype(F32) + flip_x(low).astype(F32)).astype(BF16)
+    low = after(low, landed[0])
+    around = [turn_z(low, s).astype(F32) for s in range(1, a_count)]
     coef_part = tree_sum([low.astype(F32)] + around)
-    shares = [coef_part] + [to_col(coef_part, far, sy) for far, sy in others]
     coef_grad = call(
-        functools.partial(coef_kernel, (cols, heads, padded, cols)),
+        functools.partial(coef_kernel, (heads, padded, cols)),
         jax.ShapeDtypeStruct((basis_count, relation_count), F32),
-        cols,
+        2,
         [pltpu.VMEM((heads * padded, LANES), F32)],
         1 << 20,
         "coef_rows",
-    )(place, *shares)
+    )(place, coef_part, flip_core(coef_part))
     return (node_grad, basis_grad, coef_grad.T)
 
 

time: 92.4 us -> 89.4 us (0.968)
  starting transfers between devices: 32.8 us -> 30.1 us
    ppermute x6 -> x3, waiting for transfers between devices: 13 us -> 1.86 us  [to_col(): lax.ppermute(value, 'col', [(c, (c // PAIR + sy) % y_count * PAIR + (c %...]
    ppermute x9, waiting for transfers between devices: 5.42 us -> 14.2 us  [turn_z(): lax.ppermute(value, 'row', [(r, (r + by * PAIR) % rows_total) for r in ra...]
    ppermute x5 -> x3, waiting for transfers between devices: 2.9 us -> 5.08 us  [turn_y(): lax.ppermute(value, 'col', [(c, (c + by * PAIR) % cols) for c in range(co...]
    ppermute x5 -> x3, starting transfers between devices: 5.64 us -> 3.55 us  [turn_y(): lax.ppermute(value, 'col', [(c, (c + by * PAIR) % cols) for c in range(co...]
    pallas_call x4 -> x2, Pallas kernels: 8.48 us -> 7.09 us  [basis_blocks(): call(functools.partial(basis_kernel, (rows_total, cols, block, cover // T...]
    ppermute x7, starting transfers between devices: 9.36 us -> 8.19 us  [flip_x(): return lax.ppermute(value, 'row', [(r, r ^ 1) for r in range(rows_total)])]
    ppermute x9, starting transfers between devices: 14.5 us -> 15.5 us  [turn_z(): lax.ppermute(value, 'row', [(r, (r + by * PAIR) % rows_total) for r in ra...]
    ppermute x6 -> x3, starting transfers between devices: 2.79 us -> 2.21 us  [to_col(): lax.ppermute(value, 'col', [(c, (c // PAIR + sy) % y_count * PAIR + (c %...]
  transfers between devices with their start and end apart: 30 -> 26, of which waited for: 9 -> 11; matrix products, arithmetic and copies ran while one was open for 3% -> 4% of each run, Pallas kernels for 25% -> 27%
where the time goes in v5:
time: 89.4 us; the launch traced here: 89.1 us
  starting transfers between devices  30.1 us (34%)
  Pallas kernels  28.9 us (32%)
  waiting for transfers between devices  24 us (27%)
  other arithmetic  2.82 us (3%)
  local copies, waits for them, and re-layouts  2.52 us (3%)
    ppermute x9, starting transfers between devices, turn_z(): lax.ppermute(value, 'row', [(r, (r + by * PAIR) % rows_total) for r in ra...  15.5 us
    ppermute x9, waiting for transfers between devices, turn_z(): lax.ppermute(value, 'row', [(r, (r + by * PAIR) % rows_total) for r in ra...  14.2 us
    pallas_call x1, Pallas kernels, on_device(): call(functools.partial(forward_kernel, (cols, shard, span, heads, padded,...  9.1 us
    ppermute x7, starting transfers between devices, flip_x(): return lax.ppermute(value, 'row', [(r, r ^ 1) for r in range(rows_total)])  8.19 us
    pallas_call x2, Pallas kernels, basis_blocks(): call(functools.partial(basis_kernel, (rows_total, cols, block, cover // T...  7.09 us
    pallas_call x1, Pallas kernels, on_device(): call(functools.partial(source_kernel, (cols, shard, span, heads, padded,...  5.65 us
    ppermute x3, waiting for transfers between devices, turn_y(): lax.ppermute(value, 'col', [(c, (c + by * PAIR) % cols) for c in range(co...  5.08 us
    pallas_call x1, Pallas kernels, on_device(): call(functools.partial(grad_kernel, (rows_total, dest_shard, span)), jax....  4.01 us
  transfers between devices with their start and end apart: 26, of which 11 were waited for; matrix products, arithmetic and copies ran while one was open for 4% of the time, Pallas kernels for 27%

profile of v5, /device:TPU:0, one launch (start us, length us, event | category | flops | bytes accessed | tf_op | source)
XLA Modules:
  0.0 89.1 jit_solution(12351669104476555918)
XLA Ops:
  0.6 3.0 %collective-permute-start = (bf16[256,256]{1,0:T(8,128)(2,1)}, bf16[256,256]{1,0:T(8,128)(2,1)S(1)}, u32[]{:S(2)}, u32[]{:S(2)}) collective-permute-start(bf16[256,256]{1,0:T(8,128)(2,1)} %param.9), channel_id=1, source_target_pairs={{0,4},{4,0},{8,12},{12,8},{16,20},{20,16},{24,28},{28,24},{1,5},{5... | collective-permute-start | bytes 393224 | tf_op jit(solution)/shard_map/ppermute | solution.py:340
  3.6 2.6 %collective-permute-start.1 = (bf16[256,256]{1,0:T(8,128)(2,1)}, bf16[256,256]{1,0:T(8,128)(2,1)S(1)}, u32[]{:S(2)}, u32[]{:S(2)}) collective-permute-start(bf16[256,256]{1,0:T(8,128)(2,1)} %bitcast.17), channel_id=1, source_target_pairs={{0,16},{4,20},{8,24},{12,28},{16,0},{20,4},{24,8},{28,12},{1,17},{... | collective-permute-start | bytes 393224 | tf_op jit(solution)/shard_map/ppermute | solution.py:346
  6.2 1.1 %collective-permute-done = bf16[256,256]{1,0:T(8,128)(2,1)S(1)} collective-permute-done((bf16[256,256]{1,0:T(8,128)(2,1)}, bf16[256,256]{1,0:T(8,128)(2,1)S(1)}, u32[]{:S(2)}, u32[]{:S(2)}) %collective-permute-start) | collective-permute-done | bytes 131104 | tf_op jit(solution)/shard_map/ppermute | solution.py:340
  7.3 0.9 %pad_maximum_fusion.1 = bf16[2,256,256]{2,1,0:T(8,128)(2,1)S(1)} fusion(bf16[1,256,256]{2,1,0:T(8,128)(2,1)S(1)} %bitcast.23, bf16[1,256,256]{2,1,0:T(8,128)(2,1)} %bitcast.22), kind=kLoop, calls=%fused_computation.4 | loop fusion | flops 131072 | bytes 524288 | tf_op jit(solution)/shard_map/stack | solution.py:371
  8.3 4.2 %collective-permute-done.1.refs_2_ = bf16[256,256]{1,0:T(8,128)(2,1)S(1)} collective-permute-done((bf16[256,256]{1,0:T(8,128)(2,1)}, bf16[256,256]{1,0:T(8,128)(2,1)S(1)}, u32[]{:S(2)}, u32[]{:S(2)}) %collective-permute-start.1) | collective-permute-done | bytes 131104 | tf_op jit(solution)/shard_map/ppermute | solution.py:346
  12.5 1.5 %collective-permute-start.2 = (bf16[2,256,256]{2,1,0:T(8,128)(2,1)S(1)}, bf16[2,256,256]{2,1,0:T(8,128)(2,1)S(1)}, u32[]{:S(2)}, u32[]{:S(2)}) collective-permute-start(bf16[2,256,256]{2,1,0:T(8,128)(2,1)S(1)} %pad_maximum_fusion.1), channel_id=1, source_target_pairs={{0,2},{1,3},{2,0},{3,1},{4,6},{5,7},{6,4},{7,5},{8,10},{9,11},{10,... | collective-permute-start | bytes 786440 | tf_op jit(solution)/shard_map/ppermute | solution.py:351
  14.0 1.8 %edge_table.1 = (f32[4,1024]{1,0:T(4,128)}, bf16[512,128]{1,0:T(8,128)(2,1)}, bf16[256,256]{1,0:T(8,128)(2,1)}) custom-call(s32[1,1,8]{2,1,0:T(1,128)} %fills.1, s32[1,1,1024]{2,1,0:T(1,128)} %src.1, s32[1,1,1024]{2,1,0:T(1,128)} %dst.1, s32[1,1,1024]{2,1,0:T(1,128)} %rel.1, f32[1,1,1024]{2,1,0:T(1,128)} %norm.1, bf16[30,2000]{1,0:T(8,128)(2,1)} %bitcast.16, ...), custom_call_target="tpu_custom_call" | custom-call | tf_op jit(solution)/shard_map/edge_table/pallas_call | solution.py:357
  15.8 0.5 collective-permute-start.3
  16.3 1.5 %collective-permute-start.4 = (bf16[256,256]{1,0:T(8,128)(2,1)}, bf16[256,256]{1,0:T(8,128)(2,1)S(1)}, u32[]{:S(2)}, u32[]{:S(2)}) collective-permute-start(bf16[256,256]{1,0:T(8,128)(2,1)} %bitcast.19), channel_id=1, source_target_pairs={{0,4},{4,0},{8,12},{12,8},{16,20},{20,16},{24,28},{28,24},{1,5},{5... | collective-permute-start | bytes 393224 | tf_op jit(solution)/shard_map/ppermute | solution.py:340
  17.8 0.8 collective-permute-start.6
  18.6 3.0 %collective-permute-start.7 = (bf16[256,256]{1,0:T(8,128)(2,1)}, bf16[256,256]{1,0:T(8,128)(2,1)S(1)}, u32[]{:S(2)}, u32[]{:S(2)}) collective-permute-start(bf16[256,256]{1,0:T(8,128)(2,1)} %bitcast.21), channel_id=1, source_target_pairs={{0,24},{4,28},{8,0},{12,4},{16,8},{20,12},{24,16},{28,20},{1,25},{... | collective-permute-start | bytes 393224 | tf_op jit(solution)/shard_map/ppermute | solution.py:346
  21.7 0.5 collective-permute-start.5
  22.2 0.7 pad_maximum_fusion.2.meta
  23.0 2.9 %collective-permute-done.6.refs_1_ = bf16[256,256]{1,0:T(8,128)(2,1)S(1)} collective-permute-done((bf16[256,256]{1,0:T(8,128)(2,1)}, bf16[256,256]{1,0:T(8,128)(2,1)S(1)}, u32[]{:S(2)}, u32[]{:S(2)}) %collective-permute-start.6) | collective-permute-done | bytes 131104 | tf_op jit(solution)/shard_map/ppermute | solution.py:346
  25.9 0.7 collective-permute-done.5.refs_6_
  26.6 0.5 collective-permute-start.10
  27.1 0.1 pad_add_fusion.place
  27.2 0.5 collective-permute-start.8
  27.8 1.5 %collective-permute-start.9 = (bf16[256,256]{1,0:T(8,128)(2,1)S(1)}, bf16[256,256]{1,0:T(8,128)(2,1)S(1)}, u32[]{:S(2)}, u32[]{:S(2)}) collective-permute-start(bf16[256,256]{1,0:T(8,128)(2,1)S(1)} %collective-permute-done.7.refs_3_), channel_id=1, source_target_pairs={{0,4},{4,0},{8,12},{12,8},{16,20},{20,16},{24,28},{28,24},{1,5},{5... | collective-permute-start | bytes 393224 | tf_op jit(solution)/shard_map/ppermute | solution.py:340
  29.3 0.9 %copy-done.1 = bf16[256,256]{1,0:T(8,128)(2,1)S(1)} copy-done((bf16[256,256]{1,0:T(8,128)(2,1)S(1)}, bf16[256,256]{1,0:T(8,128)(2,1)}, u32[]{:S(2)}) %copy-start.1) | copy-done | bytes 131096
  30.2 0.9 %copy-done.3 = bf16[512,128]{1,0:T(8,128)(2,1)S(1)} copy-done((bf16[512,128]{1,0:T(8,128)(2,1)S(1)}, bf16[512,128]{1,0:T(8,128)(2,1)}, u32[]{:S(2)}) %copy-start.3) | copy-done | bytes 131096
  31.1 5.6 %source_rows.1 = (bf16[4,256,1024]{2,1,0:T(8,128)(2,1)S(1)}, f32[4,32,1024]{2,1,0:T(8,128)S(1)}) custom-call(s32[4]{0:T(128)S(1)} %pad_add_fusion.place, f32[2,4,1024]{2,1,0:T(4,128)S(1)} %pad_maximum_fusion.2.meta, f32[2,4,1024]{2,1,0:T(4,128)S(1)} %collective-permute-done.10.meta_core, bf16[2,2,256,256]{3,2,1,0:T(8,128)(2,1)S(1)} %pad_maximum_fusion.feats, ...), custom_call_target="tpu_custom_call" | custom-call | flops 2147483648 | bytes 4194304 | tf_op jit(solution)/shard_map/source_rows/pallas_call | solution.py:385
  36.8 4.0 %edge_grads.1.gt_ref = bf16[256,2048]{1,0:T(8,128)(2,1)S(1)} custom-call(s32[4]{0:T(128)S(1)} %pad_add_fusion.place, f32[2,4,1024]{2,1,0:T(4,128)S(1)} %pad_maximum_fusion.2.meta, bf16[256,256]{1,0:T(8,128)(2,1)S(1)} %copy-done.2, bf16[256,256]{1,0:T(8,128)(2,1)S(1)} %collective-permute-done.6.refs_1_, bf16[256,256]{1,0:T(8,128)(2,1)S(1)} %collective-permute-done.1.refs_2_, ...), custom_call_target="tpu_custom_call" | custom-call | flops 2147483648 | bytes 4194304 | tf_op jit(solution)/shard_map/edge_grads/pallas_call | solution.py:401
  40.9 9.1 %backed_sums.1 = (bf16[384,256]{1,0:T(8,128)(2,1)S(1)}, bf16[384,256]{1,0:T(8,128)(2,1)S(1)}, bf16[384,256]{1,0:T(8,128)(2,1)S(1)}, bf16[384,256]{1,0:T(8,128)(2,1)S(1)}) custom-call(s32[4]{0:T(128)S(1)} %pad_add_fusion.place, f32[2,4,1024]{2,1,0:T(4,128)S(1)} %pad_maximum_fusion.2.meta, bf16[256,2048]{1,0:T(8,128)(2,1)S(1)} %edge_grads.1.gt_ref, ...), custom_call_target="tpu_custom_call" | custom-call | flops 4026531840 | bytes 4194304 | tf_op jit(solution)/shard_map/backed_sums/pallas_call | solution.py:414
  50.0 0.6 collective-permute-start.12
  50.5 0.2 collective-permute-start.14
  50.8 1.4 %collective-permute-start.15 = (bf16[384,256]{1,0:T(8,128)(2,1)S(1)}, bf16[384,256]{1,0:T(8,128)(2,1)S(1)}, u32[]{:S(2)}, u32[]{:S(2)}) collective-permute-start(bf16[384,256]{1,0:T(8,128)(2,1)S(1)} %get-tuple-element.52), channel_id=1, source_target_pairs={{0,3},{1,2},{2,1},{3,0},{4,7},{5,6},{6,5},{7,4},{8,11},{9,10},{10,... | collective-permute-start | bytes 589832 | tf_op jit(solution)/shard_map/ppermute | solution.py:456
  52.2 3.5 %basis_terms.2 = (f32[480,256]{1,0:T(8,128)S(1)}, bf16[480,256]{1,0:T(8,128)(2,1)S(1)}) custom-call(s32[4]{0:T(128)S(1)} %pad_add_fusion.place, bf16[256,2048]{1,0:T(8,128)(2,1)S(1)} %edge_grads.1.gt_ref, bf16[256,2048]{1,0:T(8,128)(2,1)S(1)} %collective-permute-done.13.gt_core, bf16[4,256,1024]{2,1,0:T(8,128)(2,1)S(1)} %get-tuple-element.42.refs_8_.xt_ref, ...), custom_call_target="tpu_custom_call" | custom-call | flops 2013265920 | bytes 4194304 | tf_op jit(solution)/shard_map/basis_terms/pallas_call | solution.py:435
  55.7 3.5 %basis_terms.3 = (f32[480,256]{1,0:T(8,128)S(1)}, bf16[480,256]{1,0:T(8,128)(2,1)S(1)}) custom-call(s32[4]{0:T(128)S(1)} %pad_add_fusion.place, bf16[256,2048]{1,0:T(8,128)(2,1)S(1)} %edge_grads.1.gt_ref, bf16[256,2048]{1,0:T(8,128)(2,1)S(1)} %collective-permute-done.13.gt_core, bf16[4,256,1024]{2,1,0:T(8,128)(2,1)S(1)} %get-tuple-element.42.refs_8_.xt_ref, ...), custom_call_target="tpu_custom_call" | custom-call | flops 2013265920 | bytes 4194304 | tf_op jit(solution)/shard_map/basis_terms/pallas_call | solution.py:435
  59.3 1.9 %collective-permute-done.15 = bf16[384,256]{1,0:T(8,128)(2,1)S(1)} collective-permute-done((bf16[384,256]{1,0:T(8,128)(2,1)S(1)}, bf16[384,256]{1,0:T(8,128)(2,1)S(1)}, u32[]{:S(2)}, u32[]{:S(2)}) %collective-permute-start.15) | collective-permute-done | bytes 196640 | tf_op jit(solution)/shard_map/ppermute | solution.py:456
  61.2 0.1 add_convert_fusion.1
  61.3 0.6 collective-permute-start.21
  61.9 0.5 collective-permute-start.17
  62.4 0.7 slice.29
  63.0 1.6 %collective-permute-start.16 = (bf16[480,256]{1,0:T(8,128)(2,1)S(1)}, bf16[480,256]{1,0:T(8,128)(2,1)S(1)}, u32[]{:S(2)}, u32[]{:S(2)}) collective-permute-start(bf16[480,256]{1,0:T(8,128)(2,1)S(1)} %get-tuple-element.54), channel_id=1, source_target_pairs={{0,2},{1,3},{2,0},{3,1},{4,6},{5,7},{6,4},{7,5},{8,10},{9,11},{10,... | collective-permute-start | bytes 737288 | tf_op jit(solution)/shard_map/ppermute | solution.py:351
  64.6 1.0 %collective-permute-done.21 = bf16[128,256]{1,0:T(8,128)(2,1)S(1)} collective-permute-done((bf16[128,256]{1,0:T(8,128)(2,1)S(1)}, bf16[128,256]{1,0:T(8,128)(2,1)S(1)}, u32[]{:S(2)}, u32[]{:S(2)}) %collective-permute-start.21) | collective-permute-done | bytes 65568 | tf_op jit(solution)/shard_map/ppermute | solution.py:340
  65.7 5.1 %collective-permute-done.17 = bf16[480,256]{1,0:T(8,128)(2,1)S(1)} collective-permute-done((bf16[480,256]{1,0:T(8,128)(2,1)S(1)}, bf16[480,256]{1,0:T(8,128)(2,1)S(1)}, u32[]{:S(2)}, u32[]{:S(2)}) %collective-permute-start.17) | collective-permute-done | bytes 245792 | tf_op jit(solution)/shard_map/ppermute | solution.py:351
  70.7 1.2 %collective-permute-start.22 = (bf16[128,256]{1,0:T(8,128)(2,1)S(1)}, bf16[128,256]{1,0:T(8,128)(2,1)S(1)}, u32[]{:S(2)}, u32[]{:S(2)}) collective-permute-start(bf16[128,256]{1,0:T(8,128)(2,1)S(1)} %add_convert_fusion.2), channel_id=1, source_target_pairs={{0,16},{4,20},{8,24},{12,28},{16,0},{20,4},{24,8},{28,12},{1,17},{... | collective-permute-start | bytes 196616 | tf_op jit(solution)/shard_map/ppermute | solution.py:346
  71.9 2.1 %collective-permute-start.23 = (bf16[128,256]{1,0:T(8,128)(2,1)S(1)}, bf16[128,256]{1,0:T(8,128)(2,1)S(1)}, u32[]{:S(2)}, u32[]{:S(2)}) collective-permute-start(bf16[128,256]{1,0:T(8,128)(2,1)S(1)} %add_convert_fusion.2), channel_id=1, source_target_pairs={{0,8},{4,12},{8,16},{12,20},{16,24},{20,28},{24,0},{28,4},{1,9},{5... | collective-permute-start | bytes 196616 | tf_op jit(solution)/shard_map/ppermute | solution.py:346
  74.0 1.8 %collective-permute-start.24 = (bf16[128,256]{1,0:T(8,128)(2,1)S(1)}, bf16[128,256]{1,0:T(8,128)(2,1)S(1)}, u32[]{:S(2)}, u32[]{:S(2)}) collective-permute-start(bf16[128,256]{1,0:T(8,128)(2,1)S(1)} %add_convert_fusion.2), channel_id=1, source_target_pairs={{0,24},{4,28},{8,0},{12,4},{16,8},{20,12},{24,16},{28,20},{1,25},{... | collective-permute-start | bytes 196616 | tf_op jit(solution)/shard_map/ppermute | solution.py:346
  75.8 0.3 collective-permute-start.18
  76.1 0.8 collective-permute-start.19
  77.0 2.9 %collective-permute-start.20 = (bf16[240,256]{1,0:T(8,128)(2,1)S(1)}, bf16[240,256]{1,0:T(8,128)(2,1)S(1)}, u32[]{:S(2)}, u32[]{:S(2)}) collective-permute-start(bf16[240,256]{1,0:T(8,128)(2,1)S(1)} %slice.44), channel_id=1, source_target_pairs={{0,24},{4,28},{8,0},{12,4},{16,8},{20,12},{24,16},{28,20},{1,25},{... | collective-permute-start | bytes 368648 | tf_op jit(solution)/shard_map/ppermute | solution.py:346
  80.0 1.1 %collective-permute-done.24 = bf16[128,256]{1,0:T(8,128)(2,1)S(1)} collective-permute-done((bf16[128,256]{1,0:T(8,128)(2,1)S(1)}, bf16[128,256]{1,0:T(8,128)(2,1)S(1)}, u32[]{:S(2)}, u32[]{:S(2)}) %collective-permute-start.24) | collective-permute-done | bytes 65568 | tf_op jit(solution)/shard_map/ppermute | solution.py:346
  81.2 2.8 %collective-permute-done.18 = bf16[240,256]{1,0:T(8,128)(2,1)S(1)} collective-permute-done((bf16[240,256]{1,0:T(8,128)(2,1)S(1)}, bf16[240,256]{1,0:T(8,128)(2,1)S(1)}, u32[]{:S(2)}, u32[]{:S(2)}) %collective-permute-start.18) | collective-permute-done | bytes 122912 | tf_op jit(solution)/shard_map/ppermute | solution.py:346
  84.0 3.1 %collective-permute-done.19 = bf16[240,256]{1,0:T(8,128)(2,1)S(1)} collective-permute-done((bf16[240,256]{1,0:T(8,128)(2,1)S(1)}, bf16[240,256]{1,0:T(8,128)(2,1)S(1)}, u32[]{:S(2)}, u32[]{:S(2)}) %collective-permute-start.19) | collective-permute-done | bytes 122912 | tf_op jit(solution)/shard_map/ppermute | solution.py:346
  87.1 0.8 fusion.2
  87.9 1.3 %coef_rows.1 = f32[30,2000]{1,0:T(8,128)} custom-call(s32[4]{0:T(128)S(1)} %pad_add_fusion.place, f32[128,256]{1,0:T(8,128)S(1)} %add_add_fusion.own, f32[128,256]{1,0:T(8,128)S(1)} %collective-permute-done.25.other), custom_call_target="tpu_custom_call" | custom-call | flops 1048576 | bytes 4194304 | tf_op jit(solution)/shard_map/coef_rows/pallas_call | solution.py:500
  (33 shorter events, 0.5 us)
Async XLA Ops:
  0.6 6.7 %collective-permute-start = (bf16[256,256]{1,0:T(8,128)(2,1)}, bf16[256,256]{1,0:T(8,128)(2,1)S(1)}, u32[]{:S(2)}, u32[]{:S(2)}) collective-permute-start(bf16[256,256]{1,0:T(8,128)(2,1)} %param.9), channel_id=1, source_target_pairs={{0,4},{4,0},{8,12},{12,8},{16,20},{20,16},{24,28},{28,24},{1,5},{5... | collective-permute-start | bytes 393224 | tf_op jit(solution)/shard_map/ppermute | solution.py:340
  3.6 8.9 %collective-permute-start.1 = (bf16[256,256]{1,0:T(8,128)(2,1)}, bf16[256,256]{1,0:T(8,128)(2,1)S(1)}, u32[]{:S(2)}, u32[]{:S(2)}) collective-permute-start(bf16[256,256]{1,0:T(8,128)(2,1)} %bitcast.17), channel_id=1, source_target_pairs={{0,16},{4,20},{8,24},{12,28},{16,0},{20,4},{24,8},{28,12},{1,17},{... | collective-permute-start | bytes 393224 | tf_op jit(solution)/shard_map/ppermute | solution.py:346
  12.5 10.4 %collective-permute-start.2 = (bf16[2,256,256]{2,1,0:T(8,128)(2,1)S(1)}, bf16[2,256,256]{2,1,0:T(8,128)(2,1)S(1)}, u32[]{:S(2)}, u32[]{:S(2)}) collective-permute-start(bf16[2,256,256]{2,1,0:T(8,128)(2,1)S(1)} %pad_maximum_fusion.1), channel_id=1, source_target_pairs={{0,2},{1,3},{2,0},{3,1},{4,6},{5,7},{6,4},{7,5},{8,10},{9,11},{10,... | collective-permute-start | bytes 786440 | tf_op jit(solution)/shard_map/ppermute | solution.py:351
  15.8 5.9 %collective-permute-start.3 = (f32[4,1024]{1,0:T(4,128)}, f32[4,1024]{1,0:T(4,128)S(1)}, u32[]{:S(2)}, u32[]{:S(2)}) collective-permute-start(f32[4,1024]{1,0:T(4,128)} %get-tuple-element.31), channel_id=1, source_target_pairs={{0,4},{4,0},{8,12},{12,8},{16,20},{20,16},{24,28},{28,24},{1,5},{5... | collective-permute-start | bytes 49160 | tf_op jit(solution)/shard_map/ppermute | solution.py:340
  16.3 6.6 %collective-permute-start.4 = (bf16[256,256]{1,0:T(8,128)(2,1)}, bf16[256,256]{1,0:T(8,128)(2,1)S(1)}, u32[]{:S(2)}, u32[]{:S(2)}) collective-permute-start(bf16[256,256]{1,0:T(8,128)(2,1)} %bitcast.19), channel_id=1, source_target_pairs={{0,4},{4,0},{8,12},{12,8},{16,20},{20,16},{24,28},{28,24},{1,5},{5... | collective-permute-start | bytes 393224 | tf_op jit(solution)/shard_map/ppermute | solution.py:340
  17.8 8.0 %collective-permute-start.6 = (bf16[256,256]{1,0:T(8,128)(2,1)}, bf16[256,256]{1,0:T(8,128)(2,1)S(1)}, u32[]{:S(2)}, u32[]{:S(2)}) collective-permute-start(bf16[256,256]{1,0:T(8,128)(2,1)} %bitcast.20), channel_id=1, source_target_pairs={{0,8},{4,12},{8,16},{12,20},{16,24},{20,28},{24,0},{28,4},{1,9},{5... | collective-permute-start | bytes 393224 | tf_op jit(solution)/shard_map/ppermute | solution.py:346
  18.6 7.3 %collective-permute-start.7 = (bf16[256,256]{1,0:T(8,128)(2,1)}, bf16[256,256]{1,0:T(8,128)(2,1)S(1)}, u32[]{:S(2)}, u32[]{:S(2)}) collective-permute-start(bf16[256,256]{1,0:T(8,128)(2,1)} %bitcast.21), channel_id=1, source_target_pairs={{0,24},{4,28},{8,0},{12,4},{16,8},{20,12},{24,16},{28,20},{1,25},{... | collective-permute-start | bytes 393224 | tf_op jit(solution)/shard_map/ppermute | solution.py:346
  21.7 5.0 %collective-permute-start.5 = (bf16[256,256]{1,0:T(8,128)(2,1)S(1)}, bf16[256,256]{1,0:T(8,128)(2,1)S(1)}, u32[]{:S(2)}, u32[]{:S(2)}) collective-permute-start(bf16[256,256]{1,0:T(8,128)(2,1)S(1)} %collective-permute-done.1.refs_2_), channel_id=1, source_target_pairs={{0,4},{4,0},{8,12},{12,8},{16,20},{20,16},{24,28},{28,24},{1,5},{5... | collective-permute-start | bytes 393224 | tf_op jit(solution)/shard_map/ppermute | solution.py:340
  26.6 2.6 %collective-permute-start.11 = (bf16[2,2,256,256]{3,2,1,0:T(8,128)(2,1)S(1)}, bf16[2,2,256,256]{3,2,1,0:T(8,128)(2,1)S(1)}, u32[]{:S(2)}, u32[]{:S(2)}) collective-permute-start(bf16[2,2,256,256]{3,2,1,0:T(8,128)(2,1)S(1)} %pad_maximum_fusion.feats), channel_id=1, source_target_pairs={{0,1},{1,0},{2,3},{3,2},{4,5},{5,4},{6,7},{7,6},{8,9},{9,8},{10,11... | collective-permute-start | bytes 1572872 | tf_op jit(solution)/shard_map/ppermute | solution.py:343
  26.6 2.6 %collective-permute-start.10 = (f32[2,4,1024]{2,1,0:T(4,128)S(1)}, f32[2,4,1024]{2,1,0:T(4,128)S(1)}, u32[]{:S(2)}, u32[]{:S(2)}) collective-permute-start(f32[2,4,1024]{2,1,0:T(4,128)S(1)} %pad_maximum_fusion.2.meta), channel_id=1, source_target_pairs={{0,1},{1,0},{2,3},{3,2},{4,5},{5,4},{6,7},{7,6},{8,9},{9,8},{10,11... | collective-permute-start | bytes 98312 | tf_op jit(solution)/shard_map/ppermute | solution.py:343
  27.2 9.5 %collective-permute-start.8 = (bf16[256,256]{1,0:T(8,128)(2,1)S(1)}, bf16[256,256]{1,0:T(8,128)(2,1)S(1)}, u32[]{:S(2)}, u32[]{:S(2)}) collective-permute-start(bf16[256,256]{1,0:T(8,128)(2,1)S(1)} %collective-permute-done.6.refs_1_), channel_id=1, source_target_pairs={{0,4},{4,0},{8,12},{12,8},{16,20},{20,16},{24,28},{28,24},{1,5},{5... | collective-permute-start | bytes 393224 | tf_op jit(solution)/shard_map/ppermute | solution.py:340
  27.8 9.0 %collective-permute-start.9 = (bf16[256,256]{1,0:T(8,128)(2,1)S(1)}, bf16[256,256]{1,0:T(8,128)(2,1)S(1)}, u32[]{:S(2)}, u32[]{:S(2)}) collective-permute-start(bf16[256,256]{1,0:T(8,128)(2,1)S(1)} %collective-permute-done.7.refs_3_), channel_id=1, source_target_pairs={{0,4},{4,0},{8,12},{12,8},{16,20},{20,16},{24,28},{28,24},{1,5},{5... | collective-permute-start | bytes 393224 | tf_op jit(solution)/shard_map/ppermute | solution.py:340
  29.3 0.9 %copy-start.1 = (bf16[256,256]{1,0:T(8,128)(2,1)S(1)}, bf16[256,256]{1,0:T(8,128)(2,1)}, u32[]{:S(2)}) copy-start(bf16[256,256]{1,0:T(8,128)(2,1)} %get-tuple-element.34.refs_0_) | copy-start | bytes 393220
  30.2 0.9 %copy-start.3 = (bf16[512,128]{1,0:T(8,128)(2,1)S(1)}, bf16[512,128]{1,0:T(8,128)(2,1)}, u32[]{:S(2)}) copy-start(bf16[512,128]{1,0:T(8,128)(2,1)} %get-tuple-element.41.coefs) | copy-start | bytes 393220
  31.1 5.7 %copy-start.2 = (bf16[256,256]{1,0:T(8,128)(2,1)S(1)}, bf16[256,256]{1,0:T(8,128)(2,1)}, u32[]{:S(2)}) copy-start(bf16[256,256]{1,0:T(8,128)(2,1)} %get-tuple-element.34.refs_0_) | copy-start | bytes 393220
  36.8 4.1 %copy-start = (bf16[30,256,256]{2,1,0:T(8,128)(2,1)S(1)}, bf16[30,256,256]{2,1,0:T(8,128)(2,1)}, u32[]{:S(2)}) copy-start(bf16[30,256,256]{2,1,0:T(8,128)(2,1)} %bases_ref.1) | copy-start | bytes 11796484
  40.8 11.4 %collective-permute-start.13 = (bf16[256,2048]{1,0:T(8,128)(2,1)S(1)}, bf16[256,2048]{1,0:T(8,128)(2,1)S(1)}, u32[]{:S(2)}, u32[]{:S(2)}) collective-permute-start(bf16[256,2048]{1,0:T(8,128)(2,1)S(1)} %edge_grads.1.gt_ref), channel_id=1, source_target_pairs={{0,1},{1,0},{2,3},{3,2},{4,5},{5,4},{6,7},{7,6},{8,9},{9,8},{10,11... | collective-permute-start | bytes 3145736 | tf_op jit(solution)/shard_map/ppermute | solution.py:343
  50.0 9.3 %collective-permute-start.12 = (bf16[384,256]{1,0:T(8,128)(2,1)S(1)}, bf16[384,256]{1,0:T(8,128)(2,1)S(1)}, u32[]{:S(2)}, u32[]{:S(2)}) collective-permute-start(bf16[384,256]{1,0:T(8,128)(2,1)S(1)} %get-tuple-element.45), channel_id=1, source_target_pairs={{0,2},{1,3},{2,0},{3,1},{4,6},{5,7},{6,4},{7,5},{8,10},{9,11},{10,... | collective-permute-start | bytes 589832 | tf_op jit(solution)/shard_map/ppermute | solution.py:456
  50.5 8.8 %collective-permute-start.14 = (bf16[384,256]{1,0:T(8,128)(2,1)S(1)}, bf16[384,256]{1,0:T(8,128)(2,1)S(1)}, u32[]{:S(2)}, u32[]{:S(2)}) collective-permute-start(bf16[384,256]{1,0:T(8,128)(2,1)S(1)} %get-tuple-element.50), channel_id=1, source_target_pairs={{0,1},{1,0},{2,3},{3,2},{4,5},{5,4},{6,7},{7,6},{8,9},{9,8},{10,11... | collective-permute-start | bytes 589832 | tf_op jit(solution)/shard_map/ppermute | solution.py:456
  50.8 10.4 %collective-permute-start.15 = (bf16[384,256]{1,0:T(8,128)(2,1)S(1)}, bf16[384,256]{1,0:T(8,128)(2,1)S(1)}, u32[]{:S(2)}, u32[]{:S(2)}) collective-permute-start(bf16[384,256]{1,0:T(8,128)(2,1)S(1)} %get-tuple-element.52), channel_id=1, source_target_pairs={{0,3},{1,2},{2,1},{3,0},{4,7},{5,6},{6,5},{7,4},{8,11},{9,10},{10,... | collective-permute-start | bytes 589832 | tf_op jit(solution)/shard_map/ppermute | solution.py:456
  61.3 4.3 %collective-permute-start.21 = (bf16[128,256]{1,0:T(8,128)(2,1)S(1)}, bf16[128,256]{1,0:T(8,128)(2,1)S(1)}, u32[]{:S(2)}, u32[]{:S(2)}) collective-permute-start(bf16[128,256]{1,0:T(8,128)(2,1)S(1)} %slice.34), channel_id=1, source_target_pairs={{0,4},{4,0},{8,12},{12,8},{16,20},{20,16},{24,28},{28,24},{1,5},{5... | collective-permute-start | bytes 196616 | tf_op jit(solution)/shard_map/ppermute | solution.py:340
  61.9 8.8 %collective-permute-start.17 = (bf16[480,256]{1,0:T(8,128)(2,1)S(1)}, bf16[480,256]{1,0:T(8,128)(2,1)S(1)}, u32[]{:S(2)}, u32[]{:S(2)}) collective-permute-start(bf16[480,256]{1,0:T(8,128)(2,1)S(1)} %get-tuple-element.55), channel_id=1, source_target_pairs={{0,2},{1,3},{2,0},{3,1},{4,6},{5,7},{6,4},{7,5},{8,10},{9,11},{10,... | collective-permute-start | bytes 737288 | tf_op jit(solution)/shard_map/ppermute | solution.py:351
  63.0 13.1 %collective-permute-start.16 = (bf16[480,256]{1,0:T(8,128)(2,1)S(1)}, bf16[480,256]{1,0:T(8,128)(2,1)S(1)}, u32[]{:S(2)}, u32[]{:S(2)}) collective-permute-start(bf16[480,256]{1,0:T(8,128)(2,1)S(1)} %get-tuple-element.54), channel_id=1, source_target_pairs={{0,2},{1,3},{2,0},{3,1},{4,6},{5,7},{6,4},{7,5},{8,10},{9,11},{10,... | collective-permute-start | bytes 737288 | tf_op jit(solution)/shard_map/ppermute | solution.py:351
  70.7 6.3 %collective-permute-start.22 = (bf16[128,256]{1,0:T(8,128)(2,1)S(1)}, bf16[128,256]{1,0:T(8,128)(2,1)S(1)}, u32[]{:S(2)}, u32[]{:S(2)}) collective-permute-start(bf16[128,256]{1,0:T(8,128)(2,1)S(1)} %add_convert_fusion.2), channel_id=1, source_target_pairs={{0,16},{4,20},{8,24},{12,28},{16,0},{20,4},{24,8},{28,12},{1,17},{... | collective-permute-start | bytes 196616 | tf_op jit(solution)/shard_map/ppermute | solution.py:346
  71.9 8.1 %collective-permute-start.23 = (bf16[128,256]{1,0:T(8,128)(2,1)S(1)}, bf16[128,256]{1,0:T(8,128)(2,1)S(1)}, u32[]{:S(2)}, u32[]{:S(2)}) collective-permute-start(bf16[128,256]{1,0:T(8,128)(2,1)S(1)} %add_convert_fusion.2), channel_id=1, source_target_pairs={{0,8},{4,12},{8,16},{12,20},{16,24},{20,28},{24,0},{28,4},{1,9},{5... | collective-permute-start | bytes 196616 | tf_op jit(solution)/shard_map/ppermute | solution.py:346
  74.0 7.1 %collective-permute-start.24 = (bf16[128,256]{1,0:T(8,128)(2,1)S(1)}, bf16[128,256]{1,0:T(8,128)(2,1)S(1)}, u32[]{:S(2)}, u32[]{:S(2)}) collective-permute-start(bf16[128,256]{1,0:T(8,128)(2,1)S(1)} %add_convert_fusion.2), channel_id=1, source_target_pairs={{0,24},{4,28},{8,0},{12,4},{16,8},{20,12},{24,16},{28,20},{1,25},{... | collective-permute-start | bytes 196616 | tf_op jit(solution)/shard_map/ppermute | solution.py:346
  75.8 8.2 %collective-permute-start.18 = (bf16[240,256]{1,0:T(8,128)(2,1)S(1)}, bf16[240,256]{1,0:T(8,128)(2,1)S(1)}, u32[]{:S(2)}, u32[]{:S(2)}) collective-permute-start(bf16[240,256]{1,0:T(8,128)(2,1)S(1)} %get-tuple-element.57), channel_id=1, source_target_pairs={{0,8},{4,12},{8,16},{12,20},{16,24},{20,28},{24,0},{28,4},{1,9},{5... | collective-permute-start | bytes 368648 | tf_op jit(solution)/shard_map/ppermute | solution.py:346
  76.1 10.9 %collective-permute-start.19 = (bf16[240,256]{1,0:T(8,128)(2,1)S(1)}, bf16[240,256]{1,0:T(8,128)(2,1)S(1)}, u32[]{:S(2)}, u32[]{:S(2)}) collective-permute-start(bf16[240,256]{1,0:T(8,128)(2,1)S(1)} %get-tuple-element.58), channel_id=1, source_target_pairs={{0,16},{4,20},{8,24},{12,28},{16,0},{20,4},{24,8},{28,12},{1,17},{... | collective-permute-start | bytes 368648 | tf_op jit(solution)/shard_map/ppermute | solution.py:346
  77.0 10.0 %collective-permute-start.20 = (bf16[240,256]{1,0:T(8,128)(2,1)S(1)}, bf16[240,256]{1,0:T(8,128)(2,1)S(1)}, u32[]{:S(2)}, u32[]{:S(2)}) collective-permute-start(bf16[240,256]{1,0:T(8,128)(2,1)S(1)} %slice.44), channel_id=1, source_target_pairs={{0,24},{4,28},{8,0},{12,4},{16,8},{20,12},{24,16},{28,20},{1,25},{... | collective-permute-start | bytes 368648 | tf_op jit(solution)/shard_map/ppermute | solution.py:346
  81.1 6.8 %collective-permute-start.25 = (f32[128,256]{1,0:T(8,128)S(1)}, f32[128,256]{1,0:T(8,128)S(1)}, u32[]{:S(2)}, u32[]{:S(2)}) collective-permute-start(f32[128,256]{1,0:T(8,128)S(1)} %add_add_fusion.own), channel_id=1, source_target_pairs={{0,1},{1,0},{2,3},{3,2},{4,5},{5,4},{6,7},{7,6},{8,9},{9,8},{10,11... | collective-permute-start | bytes 393224 | tf_op jit(solution)/shard_map/ppermute | solution.py:343

commit v6 on v5

--- a/solution.py
+++ b/solution.py
@@ -8,7 +8,6 @@
 
 EDGE_BLOCK = 128
 TILE = 16
-BAND = 64
 LANES = 128
 PAIR = 2
 F32 = jnp.float32
@@ -182,47 +181,30 @@
 ):
     cols, shard, span, heads, padded, group = sizes
     outs = refs[:cols]
-    total, inner, wide, coef_sum, *buffers = refs[cols:]
+    total, inner, wide, coef_sum = refs[cols:]
     count = cols // PAIR
     y, core = place[2], place[3]
     edges = meta.shape[-1]
     width = bases_ref.shape[-1]
     total[...] = jnp.zeros_like(total)
     inner[...] = jnp.zeros_like(inner)
-    steps = bases_ref.shape[0] // group
-    chunks = edges // span
-
-    def product(number, index, buffer):
+
+    def step(number, carry):
         stacked = bases_ref[pl.ds(number * group, group)].reshape(group * width, width)
-        buffer[...] = dot(stacked, gt_ref[:, index * span : (index + 1) * span])
-
-    def reduce(number, index, buffer):
-        at = slice(index * span, (index + 1) * span)
-        scales = [ct_ref[0, pl.ds(number * group + t, 1), at] for t in range(group)]
-        parts = [jnp.zeros((8, span), F32) for _ in range(group)]
-        for low in range(0, width, BAND):
-            sums = total[low : low + BAND, at]
-            rows = xt_ref[0, low : low + BAND, at].astype(F32)
+        for index in range(edges // span):
+            at = slice(index * span, (index + 1) * span)
+            backed = dot(stacked, gt_ref[:, at])
+            rows = xt_ref[0, :, at].astype(F32)
+            sums = total[:, at]
             for t in range(group):
-                mine = buffer[t * width + low : t * width + low + BAND, :]
-                sums = sums + scales[t] * mine
-                parts[t] = parts[t] + jnp.sum((mine * rows).reshape(BAND // 8, 8, span), axis=0)
-            total[low : low + BAND, at] = sums
-        for t in range(group):
-            inner[pl.ds(number * group + t, 1), at] = jnp.sum(parts[t], axis=0, keepdims=True)
-
-    product(0, 0, buffers[0])
-
-    def step(number, carry):
-        for index in range(chunks):
-            if index + 1 < chunks:
-                product(number, index + 1, buffers[(index + 1) % 2])
-            else:
-                product(jnp.minimum(number + 1, steps - 1), 0, buffers[(index + 1) % 2])
-            reduce(number, index, buffers[index % 2])
+                base = number * group + t
+                mine = backed[t * width : (t + 1) * width]
+                sums = sums + ct_ref[0, pl.ds(base, 1), at] * mine
+                inner[pl.ds(base, 1), at] = jnp.sum(mine * rows, axis=0, keepdims=True)
+            total[:, at] = sums
         return carry
 
-    lax.fori_loop(0, steps, step, 0)
+    lax.fori_loop(0, bases_ref.shape[0] // group, step, 0)
 
     ids = meta[0, 0:1, :].astype(I32)
     owner, local = split_index(ids, shard)
@@ -363,22 +345,27 @@
         ),
         in_specs=[smem()] + [vmem()] * 6,
         out_specs=[vmem()] * 3,
+        compiler_params=pltpu.CompilerParams(vmem_limit_bytes=VMEM_LIMIT),
         name="edge_table",
     )(block_fill, src_ids, dst_ids, rel_ids, edge_norm, coefs.T, own_dest)
     meta = jnp.stack([meta, flip_x(meta)])
-    first = a_count // 2 - 1
-    feats, turned[first] = lax.optimization_barrier(
-        (jnp.stack([node_feats, near]), turned[first])
+    middle = (a_count - 1) // 2
+    sides = [s for s in range(a_count - 1) if s != middle]
+    feats, *early = lax.optimization_barrier(
+        (jnp.stack([node_feats, near]), *[turned[s] for s in sides])
     )
+    for s, value in zip(sides, early):
+        turned[s] = value
     feats = jnp.stack([feats] + [turn_y(feats, s) for s in range(1, y_count)])
-    across = [flip_x(turned[s]) if s == first else None for s in range(a_count - 1)]
-    feats, meta, across_own, across[first], *turned = lax.optimization_barrier(
-        (feats, meta, across_own, across[first], *turned)
+    across = [None if s == middle else flip_x(turned[s]) for s in range(a_count - 1)]
+    feats, meta, across_own, turned[middle], *early = lax.optimization_barrier(
+        (feats, meta, across_own, turned[middle], *[across[s] for s in sides])
     )
+    for s, value in zip(sides, early):
+        across[s] = value
+    across[middle] = flip_x(turned[middle])
     dest = [own_dest] + turned
-    across = [across_own] + [
-        across[s] if s == first else flip_x(turned[s]) for s in range(a_count - 1)
-    ]
+    across = [across_own] + across
     meta_core = flip_core(meta)
     feats_core = flip_core(feats)
 
@@ -420,8 +407,6 @@
             pltpu.VMEM((padded, edges), F32),
             pltpu.VMEM((heads * padded, edges), BF16),
             pltpu.VMEM((heads * padded, LANES), F32),
-            pltpu.VMEM((group * width, span), F32),
-            pltpu.VMEM((group * width, span), F32),
         ],
         2 * edges * width * width * basis_count,
         "backed_sums",
@@ -492,9 +477,8 @@
 
     node_grad = joined[:shard].astype(BF16)
     coef_part = joined[shard:]
-    low = coef_part.astype(BF16)
+    low = after(coef_part.astype(BF16), landed[0])
     low = (low.astype(F32) + flip_x(low).astype(F32)).astype(BF16)
-    low = after(low, landed[0])
     around = [turn_z(low, s).astype(F32) for s in range(1, a_count)]
     coef_part = tree_sum([low.astype(F32)] + around)
     coef_grad = call(

time: 89.4 us -> 95.2 us (1.065)
  local copies, waits for them, and re-layouts: 2.52 us -> 5.92 us
  waiting for transfers between devices: 24 us -> 27.2 us
  Pallas kernels: 28.9 us -> 27 us
  starting transfers between devices: 30.1 us -> 31.9 us
    unnamed x8 -> x16, local copies, waits for them, and re-layouts: 1.82 us -> 5.21 us
    ppermute x9, waiting for transfers between devices: 14.2 us -> 17.2 us  [turn_z(): lax.ppermute(value, 'row', [(r, (r + by * PAIR) % rows_total) for r in ra...]
    ppermute x7, starting transfers between devices: 8.19 us -> 9.79 us  [flip_x(): return lax.ppermute(value, 'row', [(r, r ^ 1) for r in range(rows_total)])]
    pallas_call x1, Pallas kernels: 1.78 us -> 0.59 us  [on_device(): pl.pallas_call(functools.partial(prepare_kernel, heads, padded), out_shap...]
  transfers between devices with their start and end apart: 26 -> 26, of which waited for: 11 -> 9; matrix products, arithmetic and copies ran while one was open for 4% -> 3% of each run, Pallas kernels for 27% -> 23%
where the time goes in v6:
time: 95.2 us; the launch traced here: 94.9 us
  starting transfers between devices  31.9 us (34%)
  waiting for transfers between devices  27.2 us (29%)
  Pallas kernels  27 us (28%)
  local copies, waits for them, and re-layouts  5.92 us (6%)
  other arithmetic  2.1 us (2%)
    ppermute x9, waiting for transfers between devices, turn_z(): lax.ppermute(value, 'row', [(r, (r + by * PAIR) % rows_total) for r in ra...  17.2 us
    ppermute x9, starting transfers between devices, turn_z(): lax.ppermute(value, 'row', [(r, (r + by * PAIR) % rows_total) for r in ra...  15.5 us
    ppermute x7, starting transfers between devices, flip_x(): return lax.ppermute(value, 'row', [(r, r ^ 1) for r in range(rows_total)])  9.79 us
    pallas_call x1, Pallas kernels, on_device(): call(functools.partial(forward_kernel, (cols, shard, span, heads, padded,...  8.33 us
    pallas_call x2, Pallas kernels, basis_blocks(): call(functools.partial(basis_kernel, (rows_total, cols, block, cover // T...  7.09 us
    ppermute x3, waiting for transfers between devices, turn_y(): lax.ppermute(value, 'col', [(c, (c + by * PAIR) % cols) for c in range(co...  5.96 us
    pallas_call x1, Pallas kernels, on_device(): call(functools.partial(source_kernel, (cols, shard, span, heads, padded,...  5.65 us
    unnamed x16, local copies, waits for them, and re-layouts  5.21 us
  transfers between devices with their start and end apart: 26, of which 9 were waited for; matrix products, arithmetic and copies ran while one was open for 3% of the time, Pallas kernels for 23%

profile of v6, /device:TPU:0, one launch (start us, length us, event | category | flops | bytes accessed | tf_op | source)
XLA Modules:
  0.0 94.9 jit_solution(10734072400188890307)
XLA Ops:
  0.6 3.0 %collective-permute-start = (bf16[256,256]{1,0:T(8,128)(2,1)}, bf16[256,256]{1,0:T(8,128)(2,1)S(1)}, u32[]{:S(2)}, u32[]{:S(2)}) collective-permute-start(bf16[256,256]{1,0:T(8,128)(2,1)} %param.9), channel_id=1, source_target_pairs={{0,4},{4,0},{8,12},{12,8},{16,20},{20,16},{24,28},{28,24},{1,5},{5... | collective-permute-start | bytes 393224 | tf_op jit(solution)/shard_map/ppermute | solution.py:322
  3.6 1.6 %collective-permute-start.1 = (bf16[256,256]{1,0:T(8,128)(2,1)}, bf16[256,256]{1,0:T(8,128)(2,1)S(1)}, u32[]{:S(2)}, u32[]{:S(2)}) collective-permute-start(bf16[256,256]{1,0:T(8,128)(2,1)} %bitcast.14), channel_id=1, source_target_pairs={{0,8},{4,12},{8,16},{12,20},{16,24},{20,28},{24,0},{28,4},{1,9},{5... | collective-permute-start | bytes 393224 | tf_op jit(solution)/shard_map/ppermute | solution.py:328
  5.2 2.2 %collective-permute-start.2 = (bf16[256,256]{1,0:T(8,128)(2,1)}, bf16[256,256]{1,0:T(8,128)(2,1)S(1)}, u32[]{:S(2)}, u32[]{:S(2)}) collective-permute-start(bf16[256,256]{1,0:T(8,128)(2,1)} %bitcast.15), channel_id=1, source_target_pairs={{0,24},{4,28},{8,0},{12,4},{16,8},{20,12},{24,16},{28,20},{1,25},{... | collective-permute-start | bytes 393224 | tf_op jit(solution)/shard_map/ppermute | solution.py:328
  7.5 0.9 pad_maximum_fusion.1
  8.4 3.6 %collective-permute-done.1.refs_1_ = bf16[256,256]{1,0:T(8,128)(2,1)S(1)} collective-permute-done((bf16[256,256]{1,0:T(8,128)(2,1)}, bf16[256,256]{1,0:T(8,128)(2,1)S(1)}, u32[]{:S(2)}, u32[]{:S(2)}) %collective-permute-start.1) | collective-permute-done | bytes 131104 | tf_op jit(solution)/shard_map/ppermute | solution.py:328
  12.0 0.9 collective-permute-done.2.refs_3_
  12.9 1.5 %collective-permute-start.3 = (bf16[2,256,256]{2,1,0:T(8,128)(2,1)S(1)}, bf16[2,256,256]{2,1,0:T(8,128)(2,1)S(1)}, u32[]{:S(2)}, u32[]{:S(2)}) collective-permute-start(bf16[2,256,256]{2,1,0:T(8,128)(2,1)S(1)} %pad_maximum_fusion.1), channel_id=1, source_target_pairs={{0,2},{1,3},{2,0},{3,1},{4,6},{5,7},{6,4},{7,5},{8,10},{9,11},{10,... | collective-permute-start | bytes 786440 | tf_op jit(solution)/shard_map/ppermute | solution.py:333
  14.4 0.9 copy-done
  15.3 0.9 copy-done.1
  16.2 0.7 copy-done.2
  16.9 0.7 copy-done.3
  17.6 0.7 copy-done.4
  18.3 0.7 copy-done.5
  19.0 0.7 copy-done.6
  19.6 0.6 edge_table.1
  20.2 0.6 collective-permute-start.4
  20.8 1.5 %collective-permute-start.5 = (bf16[256,256]{1,0:T(8,128)(2,1)S(1)}, bf16[256,256]{1,0:T(8,128)(2,1)S(1)}, u32[]{:S(2)}, u32[]{:S(2)}) collective-permute-start(bf16[256,256]{1,0:T(8,128)(2,1)S(1)} %bitcast.17), channel_id=1, source_target_pairs={{0,4},{4,0},{8,12},{12,8},{16,20},{20,16},{24,28},{28,24},{1,5},{5... | collective-permute-start | bytes 393224 | tf_op jit(solution)/shard_map/ppermute | solution.py:322
  22.3 1.3 %collective-permute-start.6 = (bf16[256,256]{1,0:T(8,128)(2,1)S(1)}, bf16[256,256]{1,0:T(8,128)(2,1)S(1)}, u32[]{:S(2)}, u32[]{:S(2)}) collective-permute-start(bf16[256,256]{1,0:T(8,128)(2,1)S(1)} %bitcast.18), channel_id=1, source_target_pairs={{0,16},{4,20},{8,24},{12,28},{16,0},{20,4},{24,8},{28,12},{1,17},{... | collective-permute-start | bytes 393224 | tf_op jit(solution)/shard_map/ppermute | solution.py:328
  23.6 0.5 collective-permute-start.7
  24.2 1.5 %collective-permute-start.8 = (bf16[256,256]{1,0:T(8,128)(2,1)S(1)}, bf16[256,256]{1,0:T(8,128)(2,1)S(1)}, u32[]{:S(2)}, u32[]{:S(2)}) collective-permute-start(bf16[256,256]{1,0:T(8,128)(2,1)S(1)} %collective-permute-done.2.refs_3_), channel_id=1, source_target_pairs={{0,4},{4,0},{8,12},{12,8},{16,20},{20,16},{24,28},{28,24},{1,5},{5... | collective-permute-start | bytes 393224 | tf_op jit(solution)/shard_map/ppermute | solution.py:322
  25.7 1.4 %collective-permute-done.5.refs_4_ = bf16[256,256]{1,0:T(8,128)(2,1)S(1)} collective-permute-done((bf16[256,256]{1,0:T(8,128)(2,1)S(1)}, bf16[256,256]{1,0:T(8,128)(2,1)S(1)}, u32[]{:S(2)}, u32[]{:S(2)}) %collective-permute-start.5) | collective-permute-done | bytes 131104 | tf_op jit(solution)/shard_map/ppermute | solution.py:322
  27.2 2.8 %collective-permute-done.6.refs_2_ = bf16[256,256]{1,0:T(8,128)(2,1)S(1)} collective-permute-done((bf16[256,256]{1,0:T(8,128)(2,1)S(1)}, bf16[256,256]{1,0:T(8,128)(2,1)S(1)}, u32[]{:S(2)}, u32[]{:S(2)}) %collective-permute-start.6) | collective-permute-done | bytes 131104 | tf_op jit(solution)/shard_map/ppermute | solution.py:328
  30.0 1.0 %collective-permute-done.8.refs_7_ = bf16[256,256]{1,0:T(8,128)(2,1)S(1)} collective-permute-done((bf16[256,256]{1,0:T(8,128)(2,1)S(1)}, bf16[256,256]{1,0:T(8,128)(2,1)S(1)}, u32[]{:S(2)}, u32[]{:S(2)}) %collective-permute-start.8) | collective-permute-done | bytes 131104 | tf_op jit(solution)/shard_map/ppermute | solution.py:322
  31.0 0.5 collective-permute-start.10
  31.6 1.4 %collective-permute-start.9 = (bf16[256,256]{1,0:T(8,128)(2,1)S(1)}, bf16[256,256]{1,0:T(8,128)(2,1)S(1)}, u32[]{:S(2)}, u32[]{:S(2)}) collective-permute-start(bf16[256,256]{1,0:T(8,128)(2,1)S(1)} %collective-permute-done.6.refs_2_), channel_id=1, source_target_pairs={{0,4},{4,0},{8,12},{12,8},{16,20},{20,16},{24,28},{28,24},{1,5},{5... | collective-permute-start | bytes 393224 | tf_op jit(solution)/shard_map/ppermute | solution.py:322
  32.9 5.7 %source_rows.1 = (bf16[4,256,1024]{2,1,0:T(8,128)(2,1)S(1)}, f32[4,32,1024]{2,1,0:T(8,128)S(1)}) custom-call(s32[4]{0:T(128)S(1)} %pad_add_fusion.place, f32[2,4,1024]{2,1,0:T(4,128)S(1)} %pad_maximum_fusion.2.meta, f32[2,4,1024]{2,1,0:T(4,128)S(1)} %collective-permute-done.10.meta_core, bf16[2,2,256,256]{3,2,1,0:T(8,128)(2,1)S(1)} %pad_maximum_fusion.feats, ...), custom_call_target="tpu_custom_call" | custom-call | flops 2147483648 | bytes 4194304 | tf_op jit(solution)/shard_map/source_rows/pallas_call | solution.py:372
  38.6 4.0 %edge_grads.1.gt_ref = bf16[256,2048]{1,0:T(8,128)(2,1)S(1)} custom-call(s32[4]{0:T(128)S(1)} %pad_add_fusion.place, f32[2,4,1024]{2,1,0:T(4,128)S(1)} %pad_maximum_fusion.2.meta, bf16[256,256]{1,0:T(8,128)(2,1)S(1)} %get-tuple-element.35.refs_0_, bf16[256,256]{1,0:T(8,128)(2,1)S(1)} %collective-permute-done.1.refs_1_, ...), custom_call_target="tpu_custom_call" | custom-call | flops 2147483648 | bytes 4194304 | tf_op jit(solution)/shard_map/edge_grads/pallas_call | solution.py:388
  42.8 8.3 %backed_sums.1 = (bf16[384,256]{1,0:T(8,128)(2,1)S(1)}, bf16[384,256]{1,0:T(8,128)(2,1)S(1)}, bf16[384,256]{1,0:T(8,128)(2,1)S(1)}, bf16[384,256]{1,0:T(8,128)(2,1)S(1)}) custom-call(s32[4]{0:T(128)S(1)} %pad_add_fusion.place, f32[2,4,1024]{2,1,0:T(4,128)S(1)} %pad_maximum_fusion.2.meta, bf16[256,2048]{1,0:T(8,128)(2,1)S(1)} %edge_grads.1.gt_ref, ...), custom_call_target="tpu_custom_call" | custom-call | flops 4026531840 | bytes 4194304 | tf_op jit(solution)/shard_map/backed_sums/pallas_call | solution.py:401
  51.2 0.6 collective-permute-start.12
  51.8 1.6 %collective-permute-start.15 = (bf16[384,256]{1,0:T(8,128)(2,1)S(1)}, bf16[384,256]{1,0:T(8,128)(2,1)S(1)}, u32[]{:S(2)}, u32[]{:S(2)}) collective-permute-start(bf16[384,256]{1,0:T(8,128)(2,1)S(1)} %get-tuple-element.52), channel_id=1, source_target_pairs={{0,3},{1,2},{2,1},{3,0},{4,7},{5,6},{6,5},{7,4},{8,11},{9,10},{10,... | collective-permute-start | bytes 589832 | tf_op jit(solution)/shard_map/ppermute | solution.py:441
  53.4 3.5 %basis_terms.2 = (f32[480,256]{1,0:T(8,128)S(1)}, bf16[480,256]{1,0:T(8,128)(2,1)S(1)}) custom-call(s32[4]{0:T(128)S(1)} %pad_add_fusion.place, bf16[256,2048]{1,0:T(8,128)(2,1)S(1)} %edge_grads.1.gt_ref, bf16[256,2048]{1,0:T(8,128)(2,1)S(1)} %collective-permute-done.13.gt_core, bf16[4,256,1024]{2,1,0:T(8,128)(2,1)S(1)} %get-tuple-element.42.refs_8_.xt_ref, ...), custom_call_target="tpu_custom_call" | custom-call | flops 2013265920 | bytes 4194304 | tf_op jit(solution)/shard_map/basis_terms/pallas_call | solution.py:420
  57.0 3.5 %basis_terms.3 = (f32[480,256]{1,0:T(8,128)S(1)}, bf16[480,256]{1,0:T(8,128)(2,1)S(1)}) custom-call(s32[4]{0:T(128)S(1)} %pad_add_fusion.place, bf16[256,2048]{1,0:T(8,128)(2,1)S(1)} %edge_grads.1.gt_ref, bf16[256,2048]{1,0:T(8,128)(2,1)S(1)} %collective-permute-done.13.gt_core, bf16[4,256,1024]{2,1,0:T(8,128)(2,1)S(1)} %get-tuple-element.42.refs_8_.xt_ref, ...), custom_call_target="tpu_custom_call" | custom-call | flops 2013265920 | bytes 4194304 | tf_op jit(solution)/shard_map/basis_terms/pallas_call | solution.py:420
  60.6 1.5 %collective-permute-done.15 = bf16[384,256]{1,0:T(8,128)(2,1)S(1)} collective-permute-done((bf16[384,256]{1,0:T(8,128)(2,1)S(1)}, bf16[384,256]{1,0:T(8,128)(2,1)S(1)}, u32[]{:S(2)}, u32[]{:S(2)}) %collective-permute-start.15) | collective-permute-done | bytes 196640 | tf_op jit(solution)/shard_map/ppermute | solution.py:441
  62.1 0.5 collective-permute-start.17
  62.7 0.7 slice.29
  63.4 1.5 %collective-permute-start.16 = (bf16[480,256]{1,0:T(8,128)(2,1)S(1)}, bf16[480,256]{1,0:T(8,128)(2,1)S(1)}, u32[]{:S(2)}, u32[]{:S(2)}) collective-permute-start(bf16[480,256]{1,0:T(8,128)(2,1)S(1)} %get-tuple-element.54), channel_id=1, source_target_pairs={{0,2},{1,3},{2,0},{3,1},{4,6},{5,7},{6,4},{7,5},{8,10},{9,11},{10,... | collective-permute-start | bytes 737288 | tf_op jit(solution)/shard_map/ppermute | solution.py:333
  64.9 6.0 %collective-permute-done.17 = bf16[480,256]{1,0:T(8,128)(2,1)S(1)} collective-permute-done((bf16[480,256]{1,0:T(8,128)(2,1)S(1)}, bf16[480,256]{1,0:T(8,128)(2,1)S(1)}, u32[]{:S(2)}, u32[]{:S(2)}) %collective-permute-start.17) | collective-permute-done | bytes 245792 | tf_op jit(solution)/shard_map/ppermute | solution.py:333
  70.9 1.4 %collective-permute-start.21 = (bf16[128,256]{1,0:T(8,128)(2,1)S(1)}, bf16[128,256]{1,0:T(8,128)(2,1)S(1)}, u32[]{:S(2)}, u32[]{:S(2)}) collective-permute-start(bf16[128,256]{1,0:T(8,128)(2,1)S(1)} %slice.34), channel_id=1, source_target_pairs={{0,4},{4,0},{8,12},{12,8},{16,20},{20,16},{24,28},{28,24},{1,5},{5... | collective-permute-start | bytes 196616 | tf_op jit(solution)/shard_map/ppermute | solution.py:322
  72.3 1.6 %collective-permute-start.18 = (bf16[240,256]{1,0:T(8,128)(2,1)S(1)}, bf16[240,256]{1,0:T(8,128)(2,1)S(1)}, u32[]{:S(2)}, u32[]{:S(2)}) collective-permute-start(bf16[240,256]{1,0:T(8,128)(2,1)S(1)} %get-tuple-element.57), channel_id=1, source_target_pairs={{0,8},{4,12},{8,16},{12,20},{16,24},{20,28},{24,0},{28,4},{1,9},{5... | collective-permute-start | bytes 368648 | tf_op jit(solution)/shard_map/ppermute | solution.py:328
  73.9 1.3 %collective-permute-start.19 = (bf16[240,256]{1,0:T(8,128)(2,1)S(1)}, bf16[240,256]{1,0:T(8,128)(2,1)S(1)}, u32[]{:S(2)}, u32[]{:S(2)}) collective-permute-start(bf16[240,256]{1,0:T(8,128)(2,1)S(1)} %get-tuple-element.58), channel_id=1, source_target_pairs={{0,16},{4,20},{8,24},{12,28},{16,0},{20,4},{24,8},{28,12},{1,17},{... | collective-permute-start | bytes 368648 | tf_op jit(solution)/shard_map/ppermute | solution.py:328
  75.2 1.8 %collective-permute-start.22 = (bf16[128,256]{1,0:T(8,128)(2,1)S(1)}, bf16[128,256]{1,0:T(8,128)(2,1)S(1)}, u32[]{:S(2)}, u32[]{:S(2)}) collective-permute-start(bf16[128,256]{1,0:T(8,128)(2,1)S(1)} %add_convert_fusion.2), channel_id=1, source_target_pairs={{0,16},{4,20},{8,24},{12,28},{16,0},{20,4},{24,8},{28,12},{1,17},{... | collective-permute-start | bytes 196616 | tf_op jit(solution)/shard_map/ppermute | solution.py:328
  77.0 1.6 %collective-permute-start.23 = (bf16[128,256]{1,0:T(8,128)(2,1)S(1)}, bf16[128,256]{1,0:T(8,128)(2,1)S(1)}, u32[]{:S(2)}, u32[]{:S(2)}) collective-permute-start(bf16[128,256]{1,0:T(8,128)(2,1)S(1)} %add_convert_fusion.2), channel_id=1, source_target_pairs={{0,8},{4,12},{8,16},{12,20},{16,24},{20,28},{24,0},{28,4},{1,9},{5... | collective-permute-start | bytes 196616 | tf_op jit(solution)/shard_map/ppermute | solution.py:328
  78.5 2.3 %collective-permute-start.24 = (bf16[128,256]{1,0:T(8,128)(2,1)S(1)}, bf16[128,256]{1,0:T(8,128)(2,1)S(1)}, u32[]{:S(2)}, u32[]{:S(2)}) collective-permute-start(bf16[128,256]{1,0:T(8,128)(2,1)S(1)} %add_convert_fusion.2), channel_id=1, source_target_pairs={{0,24},{4,28},{8,0},{12,4},{16,8},{20,12},{24,16},{28,20},{1,25},{... | collective-permute-start | bytes 196616 | tf_op jit(solution)/shard_map/ppermute | solution.py:328
  80.9 6.8 %collective-permute-done.22 = bf16[128,256]{1,0:T(8,128)(2,1)S(1)} collective-permute-done((bf16[128,256]{1,0:T(8,128)(2,1)S(1)}, bf16[128,256]{1,0:T(8,128)(2,1)S(1)}, u32[]{:S(2)}, u32[]{:S(2)}) %collective-permute-start.22) | collective-permute-done | bytes 65568 | tf_op jit(solution)/shard_map/ppermute | solution.py:328
  87.7 1.9 %collective-permute-start.20 = (bf16[240,256]{1,0:T(8,128)(2,1)S(1)}, bf16[240,256]{1,0:T(8,128)(2,1)S(1)}, u32[]{:S(2)}, u32[]{:S(2)}) collective-permute-start(bf16[240,256]{1,0:T(8,128)(2,1)S(1)} %slice.43), channel_id=1, source_target_pairs={{0,24},{4,28},{8,0},{12,4},{16,8},{20,12},{24,16},{28,20},{1,25},{... | collective-permute-start | bytes 368648 | tf_op jit(solution)/shard_map/ppermute | solution.py:328
  89.8 3.1 %collective-permute-done.20 = bf16[240,256]{1,0:T(8,128)(2,1)S(1)} collective-permute-done((bf16[240,256]{1,0:T(8,128)(2,1)S(1)}, bf16[240,256]{1,0:T(8,128)(2,1)S(1)}, u32[]{:S(2)}, u32[]{:S(2)}) %collective-permute-start.20) | collective-permute-done | bytes 122912 | tf_op jit(solution)/shard_map/ppermute | solution.py:328
  92.8 0.8 fusion.2
  93.6 1.3 %coef_rows.1 = f32[30,2000]{1,0:T(8,128)} custom-call(s32[4]{0:T(128)S(1)} %pad_add_fusion.place, f32[128,256]{1,0:T(8,128)S(1)} %add_add_fusion.own, f32[128,256]{1,0:T(8,128)S(1)} %collective-permute-done.25.other), custom_call_target="tpu_custom_call" | custom-call | flops 1048576 | bytes 4194304 | tf_op jit(solution)/shard_map/coef_rows/pallas_call | solution.py:484
  (41 shorter events, 0.9 us)
Async XLA Ops:
  0.6 6.8 %collective-permute-start = (bf16[256,256]{1,0:T(8,128)(2,1)}, bf16[256,256]{1,0:T(8,128)(2,1)S(1)}, u32[]{:S(2)}, u32[]{:S(2)}) collective-permute-start(bf16[256,256]{1,0:T(8,128)(2,1)} %param.9), channel_id=1, source_target_pairs={{0,4},{4,0},{8,12},{12,8},{16,20},{20,16},{24,28},{28,24},{1,5},{5... | collective-permute-start | bytes 393224 | tf_op jit(solution)/shard_map/ppermute | solution.py:322
  3.6 8.4 %collective-permute-start.1 = (bf16[256,256]{1,0:T(8,128)(2,1)}, bf16[256,256]{1,0:T(8,128)(2,1)S(1)}, u32[]{:S(2)}, u32[]{:S(2)}) collective-permute-start(bf16[256,256]{1,0:T(8,128)(2,1)} %bitcast.14), channel_id=1, source_target_pairs={{0,8},{4,12},{8,16},{12,20},{16,24},{20,28},{24,0},{28,4},{1,9},{5... | collective-permute-start | bytes 393224 | tf_op jit(solution)/shard_map/ppermute | solution.py:328
  5.2 7.7 %collective-permute-start.2 = (bf16[256,256]{1,0:T(8,128)(2,1)}, bf16[256,256]{1,0:T(8,128)(2,1)S(1)}, u32[]{:S(2)}, u32[]{:S(2)}) collective-permute-start(bf16[256,256]{1,0:T(8,128)(2,1)} %bitcast.15), channel_id=1, source_target_pairs={{0,24},{4,28},{8,0},{12,4},{16,8},{20,12},{24,16},{28,20},{1,25},{... | collective-permute-start | bytes 393224 | tf_op jit(solution)/shard_map/ppermute | solution.py:328
  12.9 12.8 %collective-permute-start.3 = (bf16[2,256,256]{2,1,0:T(8,128)(2,1)S(1)}, bf16[2,256,256]{2,1,0:T(8,128)(2,1)S(1)}, u32[]{:S(2)}, u32[]{:S(2)}) collective-permute-start(bf16[2,256,256]{2,1,0:T(8,128)(2,1)S(1)} %pad_maximum_fusion.1), channel_id=1, source_target_pairs={{0,2},{1,3},{2,0},{3,1},{4,6},{5,7},{6,4},{7,5},{8,10},{9,11},{10,... | collective-permute-start | bytes 786440 | tf_op jit(solution)/shard_map/ppermute | solution.py:333
  14.4 0.9 copy-start
  15.3 0.9 copy-start.1
  16.2 0.7 copy-start.2
  16.9 0.7 copy-start.3
  17.6 0.7 copy-start.4
  18.3 0.7 copy-start.5
  19.0 0.7 copy-start.6
  20.2 4.0 %collective-permute-start.4 = (f32[4,1024]{1,0:T(4,128)S(1)}, f32[4,1024]{1,0:T(4,128)S(1)}, u32[]{:S(2)}, u32[]{:S(2)}) collective-permute-start(f32[4,1024]{1,0:T(4,128)S(1)} %get-tuple-element.31), channel_id=1, source_target_pairs={{0,4},{4,0},{8,12},{12,8},{16,20},{20,16},{24,28},{28,24},{1,5},{5... | collective-permute-start | bytes 49160 | tf_op jit(solution)/shard_map/ppermute | solution.py:322
  20.8 6.3 %collective-permute-start.5 = (bf16[256,256]{1,0:T(8,128)(2,1)S(1)}, bf16[256,256]{1,0:T(8,128)(2,1)S(1)}, u32[]{:S(2)}, u32[]{:S(2)}) collective-permute-start(bf16[256,256]{1,0:T(8,128)(2,1)S(1)} %bitcast.17), channel_id=1, source_target_pairs={{0,4},{4,0},{8,12},{12,8},{16,20},{20,16},{24,28},{28,24},{1,5},{5... | collective-permute-start | bytes 393224 | tf_op jit(solution)/shard_map/ppermute | solution.py:322
  22.3 7.6 %collective-permute-start.6 = (bf16[256,256]{1,0:T(8,128)(2,1)S(1)}, bf16[256,256]{1,0:T(8,128)(2,1)S(1)}, u32[]{:S(2)}, u32[]{:S(2)}) collective-permute-start(bf16[256,256]{1,0:T(8,128)(2,1)S(1)} %bitcast.18), channel_id=1, source_target_pairs={{0,16},{4,20},{8,24},{12,28},{16,0},{20,4},{24,8},{28,12},{1,17},{... | collective-permute-start | bytes 393224 | tf_op jit(solution)/shard_map/ppermute | solution.py:328
  23.6 6.3 %collective-permute-start.7 = (bf16[256,256]{1,0:T(8,128)(2,1)S(1)}, bf16[256,256]{1,0:T(8,128)(2,1)S(1)}, u32[]{:S(2)}, u32[]{:S(2)}) collective-permute-start(bf16[256,256]{1,0:T(8,128)(2,1)S(1)} %collective-permute-done.1.refs_1_), channel_id=1, source_target_pairs={{0,4},{4,0},{8,12},{12,8},{16,20},{20,16},{24,28},{28,24},{1,5},{5... | collective-permute-start | bytes 393224 | tf_op jit(solution)/shard_map/ppermute | solution.py:322
  24.2 6.8 %collective-permute-start.8 = (bf16[256,256]{1,0:T(8,128)(2,1)S(1)}, bf16[256,256]{1,0:T(8,128)(2,1)S(1)}, u32[]{:S(2)}, u32[]{:S(2)}) collective-permute-start(bf16[256,256]{1,0:T(8,128)(2,1)S(1)} %collective-permute-done.2.refs_3_), channel_id=1, source_target_pairs={{0,4},{4,0},{8,12},{12,8},{16,20},{20,16},{24,28},{28,24},{1,5},{5... | collective-permute-start | bytes 393224 | tf_op jit(solution)/shard_map/ppermute | solution.py:322
  31.0 2.0 %collective-permute-start.11 = (bf16[2,2,256,256]{3,2,1,0:T(8,128)(2,1)S(1)}, bf16[2,2,256,256]{3,2,1,0:T(8,128)(2,1)S(1)}, u32[]{:S(2)}, u32[]{:S(2)}) collective-permute-start(bf16[2,2,256,256]{3,2,1,0:T(8,128)(2,1)S(1)} %pad_maximum_fusion.feats), channel_id=1, source_target_pairs={{0,1},{1,0},{2,3},{3,2},{4,5},{5,4},{6,7},{7,6},{8,9},{9,8},{10,11... | collective-permute-start | bytes 1572872 | tf_op jit(solution)/shard_map/ppermute | solution.py:325
  31.0 2.0 %collective-permute-start.10 = (f32[2,4,1024]{2,1,0:T(4,128)S(1)}, f32[2,4,1024]{2,1,0:T(4,128)S(1)}, u32[]{:S(2)}, u32[]{:S(2)}) collective-permute-start(f32[2,4,1024]{2,1,0:T(4,128)S(1)} %pad_maximum_fusion.2.meta), channel_id=1, source_target_pairs={{0,1},{1,0},{2,3},{3,2},{4,5},{5,4},{6,7},{7,6},{8,9},{9,8},{10,11... | collective-permute-start | bytes 98312 | tf_op jit(solution)/shard_map/ppermute | solution.py:325
  31.6 7.0 %collective-permute-start.9 = (bf16[256,256]{1,0:T(8,128)(2,1)S(1)}, bf16[256,256]{1,0:T(8,128)(2,1)S(1)}, u32[]{:S(2)}, u32[]{:S(2)}) collective-permute-start(bf16[256,256]{1,0:T(8,128)(2,1)S(1)} %collective-permute-done.6.refs_2_), channel_id=1, source_target_pairs={{0,4},{4,0},{8,12},{12,8},{16,20},{20,16},{24,28},{28,24},{1,5},{5... | collective-permute-start | bytes 393224 | tf_op jit(solution)/shard_map/ppermute | solution.py:322
  38.6 4.2 %copy-start.7 = (bf16[30,256,256]{2,1,0:T(8,128)(2,1)S(1)}, bf16[30,256,256]{2,1,0:T(8,128)(2,1)}, u32[]{:S(2)}) copy-start(bf16[30,256,256]{2,1,0:T(8,128)(2,1)} %bases_ref.1) | copy-start | bytes 11796484
  42.6 10.8 %collective-permute-start.13 = (bf16[256,2048]{1,0:T(8,128)(2,1)S(1)}, bf16[256,2048]{1,0:T(8,128)(2,1)S(1)}, u32[]{:S(2)}, u32[]{:S(2)}) collective-permute-start(bf16[256,2048]{1,0:T(8,128)(2,1)S(1)} %edge_grads.1.gt_ref), channel_id=1, source_target_pairs={{0,1},{1,0},{2,3},{3,2},{4,5},{5,4},{6,7},{7,6},{8,9},{9,8},{10,11... | collective-permute-start | bytes 3145736 | tf_op jit(solution)/shard_map/ppermute | solution.py:325
  51.2 9.4 %collective-permute-start.12 = (bf16[384,256]{1,0:T(8,128)(2,1)S(1)}, bf16[384,256]{1,0:T(8,128)(2,1)S(1)}, u32[]{:S(2)}, u32[]{:S(2)}) collective-permute-start(bf16[384,256]{1,0:T(8,128)(2,1)S(1)} %get-tuple-element.45), channel_id=1, source_target_pairs={{0,2},{1,3},{2,0},{3,1},{4,6},{5,7},{6,4},{7,5},{8,10},{9,11},{10,... | collective-permute-start | bytes 589832 | tf_op jit(solution)/shard_map/ppermute | solution.py:441
  51.8 8.8 %collective-permute-start.14 = (bf16[384,256]{1,0:T(8,128)(2,1)S(1)}, bf16[384,256]{1,0:T(8,128)(2,1)S(1)}, u32[]{:S(2)}, u32[]{:S(2)}) collective-permute-start(bf16[384,256]{1,0:T(8,128)(2,1)S(1)} %get-tuple-element.50), channel_id=1, source_target_pairs={{0,1},{1,0},{2,3},{3,2},{4,5},{5,4},{6,7},{7,6},{8,9},{9,8},{10,11... | collective-permute-start | bytes 589832 | tf_op jit(solution)/shard_map/ppermute | solution.py:441
  51.8 10.3 %collective-permute-start.15 = (bf16[384,256]{1,0:T(8,128)(2,1)S(1)}, bf16[384,256]{1,0:T(8,128)(2,1)S(1)}, u32[]{:S(2)}, u32[]{:S(2)}) collective-permute-start(bf16[384,256]{1,0:T(8,128)(2,1)S(1)} %get-tuple-element.52), channel_id=1, source_target_pairs={{0,3},{1,2},{2,1},{3,0},{4,7},{5,6},{6,5},{7,4},{8,11},{9,10},{10,... | collective-permute-start | bytes 589832 | tf_op jit(solution)/shard_map/ppermute | solution.py:441
  62.1 8.8 %collective-permute-start.17 = (bf16[480,256]{1,0:T(8,128)(2,1)S(1)}, bf16[480,256]{1,0:T(8,128)(2,1)S(1)}, u32[]{:S(2)}, u32[]{:S(2)}) collective-permute-start(bf16[480,256]{1,0:T(8,128)(2,1)S(1)} %get-tuple-element.55), channel_id=1, source_target_pairs={{0,2},{1,3},{2,0},{3,1},{4,6},{5,7},{6,4},{7,5},{8,10},{9,11},{10,... | collective-permute-start | bytes 737288 | tf_op jit(solution)/shard_map/ppermute | solution.py:333
  63.4 15.2 %collective-permute-start.16 = (bf16[480,256]{1,0:T(8,128)(2,1)S(1)}, bf16[480,256]{1,0:T(8,128)(2,1)S(1)}, u32[]{:S(2)}, u32[]{:S(2)}) collective-permute-start(bf16[480,256]{1,0:T(8,128)(2,1)S(1)} %get-tuple-element.54), channel_id=1, source_target_pairs={{0,2},{1,3},{2,0},{3,1},{4,6},{5,7},{6,4},{7,5},{8,10},{9,11},{10,... | collective-permute-start | bytes 737288 | tf_op jit(solution)/shard_map/ppermute | solution.py:333
  70.9 4.3 %collective-permute-start.21 = (bf16[128,256]{1,0:T(8,128)(2,1)S(1)}, bf16[128,256]{1,0:T(8,128)(2,1)S(1)}, u32[]{:S(2)}, u32[]{:S(2)}) collective-permute-start(bf16[128,256]{1,0:T(8,128)(2,1)S(1)} %slice.34), channel_id=1, source_target_pairs={{0,4},{4,0},{8,12},{12,8},{16,20},{20,16},{24,28},{28,24},{1,5},{5... | collective-permute-start | bytes 196616 | tf_op jit(solution)/shard_map/ppermute | solution.py:322
  72.3 17.4 %collective-permute-start.18 = (bf16[240,256]{1,0:T(8,128)(2,1)S(1)}, bf16[240,256]{1,0:T(8,128)(2,1)S(1)}, u32[]{:S(2)}, u32[]{:S(2)}) collective-permute-start(bf16[240,256]{1,0:T(8,128)(2,1)S(1)} %get-tuple-element.57), channel_id=1, source_target_pairs={{0,8},{4,12},{8,16},{12,20},{16,24},{20,28},{24,0},{28,4},{1,9},{5... | collective-permute-start | bytes 368648 | tf_op jit(solution)/shard_map/ppermute | solution.py:328
  73.9 15.9 %collective-permute-start.19 = (bf16[240,256]{1,0:T(8,128)(2,1)S(1)}, bf16[240,256]{1,0:T(8,128)(2,1)S(1)}, u32[]{:S(2)}, u32[]{:S(2)}) collective-permute-start(bf16[240,256]{1,0:T(8,128)(2,1)S(1)} %get-tuple-element.58), channel_id=1, source_target_pairs={{0,16},{4,20},{8,24},{12,28},{16,0},{20,4},{24,8},{28,12},{1,17},{... | collective-permute-start | bytes 368648 | tf_op jit(solution)/shard_map/ppermute | solution.py:328
  75.2 12.5 %collective-permute-start.22 = (bf16[128,256]{1,0:T(8,128)(2,1)S(1)}, bf16[128,256]{1,0:T(8,128)(2,1)S(1)}, u32[]{:S(2)}, u32[]{:S(2)}) collective-permute-start(bf16[128,256]{1,0:T(8,128)(2,1)S(1)} %add_convert_fusion.2), channel_id=1, source_target_pairs={{0,16},{4,20},{8,24},{12,28},{16,0},{20,4},{24,8},{28,12},{1,17},{... | collective-permute-start | bytes 196616 | tf_op jit(solution)/shard_map/ppermute | solution.py:328
  77.0 12.6 %collective-permute-start.23 = (bf16[128,256]{1,0:T(8,128)(2,1)S(1)}, bf16[128,256]{1,0:T(8,128)(2,1)S(1)}, u32[]{:S(2)}, u32[]{:S(2)}) collective-permute-start(bf16[128,256]{1,0:T(8,128)(2,1)S(1)} %add_convert_fusion.2), channel_id=1, source_target_pairs={{0,8},{4,12},{8,16},{12,20},{16,24},{20,28},{24,0},{28,4},{1,9},{5... | collective-permute-start | bytes 196616 | tf_op jit(solution)/shard_map/ppermute | solution.py:328
  78.5 11.1 %collective-permute-start.24 = (bf16[128,256]{1,0:T(8,128)(2,1)S(1)}, bf16[128,256]{1,0:T(8,128)(2,1)S(1)}, u32[]{:S(2)}, u32[]{:S(2)}) collective-permute-start(bf16[128,256]{1,0:T(8,128)(2,1)S(1)} %add_convert_fusion.2), channel_id=1, source_target_pairs={{0,24},{4,28},{8,0},{12,4},{16,8},{20,12},{24,16},{28,20},{1,25},{... | collective-permute-start | bytes 196616 | tf_op jit(solution)/shard_map/ppermute | solution.py:328
  87.7 5.2 %collective-permute-start.20 = (bf16[240,256]{1,0:T(8,128)(2,1)S(1)}, bf16[240,256]{1,0:T(8,128)(2,1)S(1)}, u32[]{:S(2)}, u32[]{:S(2)}) collective-permute-start(bf16[240,256]{1,0:T(8,128)(2,1)S(1)} %slice.43), channel_id=1, source_target_pairs={{0,24},{4,28},{8,0},{12,4},{16,8},{20,12},{24,16},{28,20},{1,25},{... | collective-permute-start | bytes 368648 | tf_op jit(solution)/shard_map/ppermute | solution.py:328
  89.7 3.9 %collective-permute-start.25 = (f32[128,256]{1,0:T(8,128)S(1)}, f32[128,256]{1,0:T(8,128)S(1)}, u32[]{:S(2)}, u32[]{:S(2)}) collective-permute-start(f32[128,256]{1,0:T(8,128)S(1)} %add_add_fusion.own), channel_id=1, source_target_pairs={{0,1},{1,0},{2,3},{3,2},{4,5},{5,4},{6,7},{7,6},{8,9},{9,8},{10,11... | collective-permute-start | bytes 393224 | tf_op jit(solution)/shard_map/ppermute | solution.py:325

commit v7 on v6

--- a/solution.py
+++ b/solution.py
@@ -89,8 +89,7 @@
     )
 
 
-def prepare_kernel(heads, padded, fills, src, dst, rel, norm, coefs_t, dest, *outs):
-    out_ref, coefs, dest_out = outs
+def prepare_kernel(fills, src, dst, rel, norm, out_ref):
     blocks = fills.shape[-1]
     out_ref[0:1, :] = src[0].astype(F32)
     out_ref[1:2, :] = dst[0].astype(F32)
@@ -100,20 +99,11 @@
         here = slice(at * EDGE_BLOCK, (at + 1) * EDGE_BLOCK)
         live = jnp.where(lane < fills[0, 0, at], 1.0, 0.0)
         out_ref[3:4, here] = norm[0, :, here] * live
-    dest_out[...] = dest[...]
-    basis_count, relation_count = coefs_t.shape
-    coefs[...] = jnp.zeros_like(coefs)
-    for head in range(heads):
-        live = min(LANES, relation_count - head * LANES)
-        if live > 0:
-            coefs[head * padded : head * padded + basis_count, 0:live] = coefs_t[
-                :, head * LANES : head * LANES + live
-            ]
-
-
-def source_kernel(sizes, place, meta, meta_core, feats, feats_core, coefs, *refs):
-    cols, shard, span, heads, padded, extra = sizes
-    xt_ref, ct_ref, table = refs[extra:]
+
+
+def source_kernel(sizes, place, meta, meta_core, feats, feats_core, *refs):
+    cols, shard, span, extra = sizes
+    xt_ref, table = refs[extra:]
     count = cols // PAIR
     y, core = place[2], place[3]
     width = feats.shape[-1]
@@ -135,31 +125,31 @@
             slot = (owner_core ^ core) * count + wrap(y - owner_y, count)
             rows = dot(table[xr], slot_hot(slot, local, cols, shard))
             xt_ref[far * PAIR + xr, :, pl.ds(at, span)] = rows.astype(BF16)
-            relation = source[xr, 2:3, pl.ds(at, span)].astype(I32)
-            high, low = split_index(relation, LANES)
-            parts = dot(coefs[...], one_hot(low, LANES))
-            total = jnp.zeros((padded, span), F32)
-            for head in range(heads):
-                total = total + jnp.where(
-                    high == head, parts[head * padded : (head + 1) * padded], 0.0
-                )
-            ct_ref[far * PAIR + xr, :, pl.ds(at, span)] = total
             return carry
 
         lax.fori_loop(0, PAIR * (edges // span), step, 0, unroll=2)
 
 
-def grad_kernel(sizes, place, meta, *refs):
-    rows_total, shard, span = sizes
+def grad_kernel(sizes, place, meta, meta_core, coefs_t, *refs):
+    rows_total, shard, span, heads, padded = sizes
     count = rows_total // PAIR
     blocks = refs[:rows_total]
-    gt_ref, table = refs[rows_total + 1 :]
+    gt_ref, ct_ref, table, coefs = refs[rows_total + 1 :]
     a, x = place[0], place[1]
     width = blocks[0].shape[-1]
     edges = meta.shape[-1]
     unit = eye(width)
     for at, block in enumerate(blocks):
         table[:, at * shard : (at + 1) * shard] = dot_t(unit, block[...]).astype(BF16)
+
+    basis_count, relation_count = coefs_t.shape
+    coefs[...] = jnp.zeros_like(coefs)
+    for head in range(heads):
+        live = min(LANES, relation_count - head * LANES)
+        if live > 0:
+            coefs[head * padded : head * padded + basis_count, 0:live] = coefs_t[
+                :, head * LANES : head * LANES + live
+            ]
 
     def step(index, carry):
         xr = index // (edges // span)
@@ -171,6 +161,16 @@
         rows = dot(table[...], slot_hot(slot, local, rows_total, shard))
         weight = meta[xr, 3:4, pl.ds(at, span)]
         gt_ref[:, pl.ds(pl.multiple_of(index * span, span), span)] = (rows * weight).astype(BF16)
+        for far, source in enumerate((meta, meta_core)):
+            relation = source[xr, 2:3, pl.ds(at, span)].astype(I32)
+            high, low = split_index(relation, LANES)
+            parts = dot(coefs[...], one_hot(low, LANES))
+            total = jnp.zeros((padded, span), F32)
+            for head in range(heads):
+                total = total + jnp.where(
+                    high == head, parts[head * padded : (head + 1) * padded], 0.0
+                )
+            ct_ref[far * PAIR + xr, :, pl.ds(at, span)] = total
         return carry
 
     lax.fori_loop(0, PAIR * (edges // span), step, 0, unroll=2)
@@ -336,30 +336,25 @@
     turned = [turn_z(own_dest, s) for s in range(1, a_count)]
     across_own = flip_x(own_dest)
     near = flip_x(node_feats)
-    meta, coefs, own_dest = pl.pallas_call(
-        functools.partial(prepare_kernel, heads, padded),
-        out_shape=(
-            jax.ShapeDtypeStruct((4, edges), F32),
-            jax.ShapeDtypeStruct((heads * padded, LANES), BF16),
-            jax.ShapeDtypeStruct(own_dest.shape, BF16),
-        ),
-        in_specs=[smem()] + [vmem()] * 6,
-        out_specs=[vmem()] * 3,
-        compiler_params=pltpu.CompilerParams(vmem_limit_bytes=VMEM_LIMIT),
+    meta = pl.pallas_call(
+        prepare_kernel,
+        out_shape=jax.ShapeDtypeStruct((4, edges), F32),
+        in_specs=[smem()] + [vmem()] * 4,
+        out_specs=vmem(),
         name="edge_table",
-    )(block_fill, src_ids, dst_ids, rel_ids, edge_norm, coefs.T, own_dest)
+    )(block_fill, src_ids, dst_ids, rel_ids, edge_norm)
     meta = jnp.stack([meta, flip_x(meta)])
     middle = (a_count - 1) // 2
     sides = [s for s in range(a_count - 1) if s != middle]
-    feats, *early = lax.optimization_barrier(
-        (jnp.stack([node_feats, near]), *[turned[s] for s in sides])
+    feats, meta, across_own, *early = lax.optimization_barrier(
+        (jnp.stack([node_feats, near]), meta, across_own, *[turned[s] for s in sides])
     )
     for s, value in zip(sides, early):
         turned[s] = value
     feats = jnp.stack([feats] + [turn_y(feats, s) for s in range(1, y_count)])
     across = [None if s == middle else flip_x(turned[s]) for s in range(a_count - 1)]
-    feats, meta, across_own, turned[middle], *early = lax.optimization_barrier(
-        (feats, meta, across_own, turned[middle], *[across[s] for s in sides])
+    feats, turned[middle], *early = lax.optimization_barrier(
+        (feats, turned[middle], *[across[s] for s in sides])
     )
     for s, value in zip(sides, early):
         across[s] = value
@@ -369,31 +364,32 @@
     meta_core = flip_core(meta)
     feats_core = flip_core(feats)
 
-    xt, ct = call(
-        functools.partial(source_kernel, (cols, shard, span, heads, padded, a_count)),
+    xt = call(
+        functools.partial(source_kernel, (cols, shard, span, a_count - 1)),
+        jax.ShapeDtypeStruct((2 * PAIR, width, edges), BF16),
+        4,
+        [pltpu.VMEM((PAIR, width, cols * shard), BF16)],
+        2 * 4 * edges * cols * shard * width,
+        "source_rows",
+        a_count - 1,
+    )(place, meta, meta_core, feats, feats_core, *turned)
+
+    dest_shard = own_dest.shape[0]
+    gt, ct = call(
+        functools.partial(grad_kernel, (rows_total, dest_shard, span, heads, padded)),
         (
-            jax.ShapeDtypeStruct((2 * PAIR, width, edges), BF16),
+            jax.ShapeDtypeStruct((width, PAIR * edges), BF16),
             jax.ShapeDtypeStruct((2 * PAIR, padded, edges), F32),
         ),
-        5,
+        3 + rows_total,
         [
-            pltpu.VMEM((PAIR, width, cols * shard), BF16),
+            pltpu.VMEM((width, rows_total * dest_shard), BF16),
+            pltpu.VMEM((heads * padded, LANES), BF16),
         ],
-        2 * 4 * edges * cols * shard * width,
-        "source_rows",
-        a_count,
-    )(place, meta, meta_core, feats, feats_core, coefs, *dest)
-
-    dest_shard = own_dest.shape[0]
-    gt = call(
-        functools.partial(grad_kernel, (rows_total, dest_shard, span)),
-        jax.ShapeDtypeStruct((width, PAIR * edges), BF16),
-        1 + rows_total,
-        [pltpu.VMEM((width, rows_total * dest_shard), BF16)],
         2 * 2 * edges * rows_total * dest_shard * width,
         "edge_grads",
         1,
-    )(place, meta, *dest, *across, xt)
+    )(place, meta, meta_core, coefs.T, *dest, *across, xt)
     gt_core = flip_core(gt)
 
     group = max(g for g in range(1, 6) if basis_count % g == 0)
@@ -452,11 +448,10 @@
 
     order = tuple(range(1, a_count)) + (0,)
     half = (a_count + 1) // 2
-    sums, where, landed = {}, place, []
+    sums, landed = {}, []
     for turns in (order[:half], order[half:]):
         if turns:
-            blocks = basis_blocks(where, turns)
-            where = after(place, blocks[0])
+            blocks = basis_blocks(place, turns)
             value = blocks[0]
             for sy in range(1, y_count):
                 landed.append(turn_y(blocks[sy], sy))

time: 95.2 us -> 86.3 us (0.907)
  local copies, waits for them, and re-layouts: 5.92 us -> 0.72 us
  waiting for transfers between devices: 27.2 us -> 24.2 us
  starting transfers between devices: 31.9 us -> 29.6 us
    unnamed x16 -> x6, local copies, waits for them, and re-layouts: 5.21 us -> 0.01 us
    ppermute x9, waiting for transfers between devices: 17.2 us -> 15 us  [turn_z(): lax.ppermute(value, 'row', [(r, (r + by * PAIR) % rows_total) for r in ra...]
    ppermute x7, waiting for transfers between devices: 2.46 us -> 0.37 us  [flip_x(): return lax.ppermute(value, 'row', [(r, r ^ 1) for r in range(rows_total)])]
    ppermute x7, starting transfers between devices: 9.79 us -> 8.17 us  [flip_x(): return lax.ppermute(value, 'row', [(r, r ^ 1) for r in range(rows_total)])]
    ppermute x3, waiting for transfers between devices: 5.96 us -> 7.09 us  [turn_y(): lax.ppermute(value, 'col', [(c, (c + by * PAIR) % cols) for c in range(co...]
  transfers between devices with their start and end apart: 26 -> 26, of which waited for: 9 -> 10; matrix products, arithmetic and copies ran while one was open for 3% -> 4% of each run, Pallas kernels for 23% -> 25%
where the time goes in v7:
time: 86.3 us; the launch traced here: 86 us
  starting transfers between devices  29.6 us (34%)
  Pallas kernels  27.8 us (32%)
  waiting for transfers between devices  24.2 us (28%)
  other arithmetic  2.82 us (3%)
    ppermute x9, starting transfers between devices, turn_z(): lax.ppermute(value, 'row', [(r, (r + by * PAIR) % rows_total) for r in ra...  15.7 us
    ppermute x9, waiting for transfers between devices, turn_z(): lax.ppermute(value, 'row', [(r, (r + by * PAIR) % rows_total) for r in ra...  15 us
    pallas_call x1, Pallas kernels, on_device(): call(functools.partial(forward_kernel, (cols, shard, span, heads, padded,...  8.22 us
    ppermute x7, starting transfers between devices, flip_x(): return lax.ppermute(value, 'row', [(r, r ^ 1) for r in range(rows_total)])  8.17 us
    pallas_call x2, Pallas kernels, basis_blocks(): call(functools.partial(basis_kernel, (rows_total, cols, block, cover // T...  7.14 us
    ppermute x3, waiting for transfers between devices, turn_y(): lax.ppermute(value, 'col', [(c, (c + by * PAIR) % cols) for c in range(co...  7.09 us
    pallas_call x1, Pallas kernels, on_device(): call(functools.partial(grad_kernel, (rows_total, dest_shard, span, heads,...  4.96 us
    pallas_call x1, Pallas kernels, on_device(): call(functools.partial(source_kernel, (cols, shard, span, a_count - 1)),...  4.79 us
  transfers between devices with their start and end apart: 26, of which 10 were waited for; matrix products, arithmetic and copies ran while one was open for 4% of the time, Pallas kernels for 25%

profile of v7, /device:TPU:0, one launch (start us, length us, event | category | flops | bytes accessed | tf_op | source)
XLA Modules:
  0.0 86.0 jit_solution(3279821358493646387)
XLA Ops:
  0.6 3.0 %collective-permute-start = (bf16[256,256]{1,0:T(8,128)(2,1)}, bf16[256,256]{1,0:T(8,128)(2,1)S(1)}, u32[]{:S(2)}, u32[]{:S(2)}) collective-permute-start(bf16[256,256]{1,0:T(8,128)(2,1)} %param.9), channel_id=1, source_target_pairs={{0,4},{4,0},{8,12},{12,8},{16,20},{20,16},{24,28},{28,24},{1,5},{5... | collective-permute-start | bytes 393224 | tf_op jit(solution)/shard_map/ppermute | solution.py:322
  3.6 1.4 %edge_table.1 = f32[4,1024]{1,0:T(4,128)} custom-call(s32[1,1,8]{2,1,0:T(1,128)} %fills.1, s32[1,1,1024]{2,1,0:T(1,128)} %src.1, s32[1,1,1024]{2,1,0:T(1,128)} %dst.1, s32[1,1,1024]{2,1,0:T(1,128)} %rel.1, f32[1,1,1024]{2,1,0:T(1,128)} %norm.1), custom_call_target="tpu_custom_call" | custom-call | tf_op jit(solution)/shard_map/edge_table/pallas_call | solution.py:339
  5.1 2.0 %collective-permute-start.2 = (bf16[256,256]{1,0:T(8,128)(2,1)}, bf16[256,256]{1,0:T(8,128)(2,1)S(1)}, u32[]{:S(2)}, u32[]{:S(2)}) collective-permute-start(bf16[256,256]{1,0:T(8,128)(2,1)} %bitcast.14), channel_id=1, source_target_pairs={{0,4},{4,0},{8,12},{12,8},{16,20},{20,16},{24,28},{28,24},{1,5},{5... | collective-permute-start | bytes 393224 | tf_op jit(solution)/shard_map/ppermute | solution.py:322
  7.1 1.6 %collective-permute-start.3 = (bf16[256,256]{1,0:T(8,128)(2,1)}, bf16[256,256]{1,0:T(8,128)(2,1)S(1)}, u32[]{:S(2)}, u32[]{:S(2)}) collective-permute-start(bf16[256,256]{1,0:T(8,128)(2,1)} %bitcast.15), channel_id=1, source_target_pairs={{0,8},{4,12},{8,16},{12,20},{16,24},{20,28},{24,0},{28,4},{1,9},{5... | collective-permute-start | bytes 393224 | tf_op jit(solution)/shard_map/ppermute | solution.py:328
  8.7 2.2 %collective-permute-start.4 = (bf16[256,256]{1,0:T(8,128)(2,1)}, bf16[256,256]{1,0:T(8,128)(2,1)S(1)}, u32[]{:S(2)}, u32[]{:S(2)}) collective-permute-start(bf16[256,256]{1,0:T(8,128)(2,1)} %bitcast.16), channel_id=1, source_target_pairs={{0,24},{4,28},{8,0},{12,4},{16,8},{20,12},{24,16},{28,20},{1,25},{... | collective-permute-start | bytes 393224 | tf_op jit(solution)/shard_map/ppermute | solution.py:328
  10.9 0.7 pad_maximum_fusion.2.meta
  11.6 0.9 %pad_maximum_fusion.1 = bf16[2,256,256]{2,1,0:T(8,128)(2,1)S(1)} fusion(bf16[1,256,256]{2,1,0:T(8,128)(2,1)S(1)} %bitcast.23, bf16[1,256,256]{2,1,0:T(8,128)(2,1)} %bitcast.22), kind=kLoop, calls=%fused_computation.4 | loop fusion | flops 131072 | bytes 524288 | tf_op jit(solution)/shard_map/stack | solution.py:350
  12.6 2.5 %collective-permute-done.3.refs_0_.refs_1_ = bf16[256,256]{1,0:T(8,128)(2,1)S(1)} collective-permute-done((bf16[256,256]{1,0:T(8,128)(2,1)}, bf16[256,256]{1,0:T(8,128)(2,1)S(1)}, u32[]{:S(2)}, u32[]{:S(2)}) %collective-permute-start.3) | collective-permute-done | bytes 131104 | tf_op jit(solution)/shard_map/ppermute | solution.py:328
  15.1 0.7 collective-permute-done.4.refs_2_.refs_3_
  15.8 1.5 %collective-permute-start.6 = (bf16[2,256,256]{2,1,0:T(8,128)(2,1)S(1)}, bf16[2,256,256]{2,1,0:T(8,128)(2,1)S(1)}, u32[]{:S(2)}, u32[]{:S(2)}) collective-permute-start(bf16[2,256,256]{2,1,0:T(8,128)(2,1)S(1)} %pad_maximum_fusion.1), channel_id=1, source_target_pairs={{0,2},{1,3},{2,0},{3,1},{4,6},{5,7},{6,4},{7,5},{8,10},{9,11},{10,... | collective-permute-start | bytes 786440 | tf_op jit(solution)/shard_map/ppermute | solution.py:333
  17.3 1.2 %collective-permute-start.7 = (bf16[256,256]{1,0:T(8,128)(2,1)}, bf16[256,256]{1,0:T(8,128)(2,1)S(1)}, u32[]{:S(2)}, u32[]{:S(2)}) collective-permute-start(bf16[256,256]{1,0:T(8,128)(2,1)} %bitcast.17), channel_id=1, source_target_pairs={{0,16},{4,20},{8,24},{12,28},{16,0},{20,4},{24,8},{28,12},{1,17},{... | collective-permute-start | bytes 393224 | tf_op jit(solution)/shard_map/ppermute | solution.py:328
  18.5 0.5 collective-permute-start.8
  19.0 1.5 %collective-permute-start.9 = (bf16[256,256]{1,0:T(8,128)(2,1)S(1)}, bf16[256,256]{1,0:T(8,128)(2,1)S(1)}, u32[]{:S(2)}, u32[]{:S(2)}) collective-permute-start(bf16[256,256]{1,0:T(8,128)(2,1)S(1)} %collective-permute-done.4.refs_2_.refs_3_), channel_id=1, source_target_pairs={{0,4},{4,0},{8,12},{12,8},{16,20},{20,16},{24,28},{28,24},{1,5},{5... | collective-permute-start | bytes 393224 | tf_op jit(solution)/shard_map/ppermute | solution.py:322
  20.5 2.2 %collective-permute-done.6 = bf16[2,256,256]{2,1,0:T(8,128)(2,1)S(1)} collective-permute-done((bf16[2,256,256]{2,1,0:T(8,128)(2,1)S(1)}, bf16[2,256,256]{2,1,0:T(8,128)(2,1)S(1)}, u32[]{:S(2)}, u32[]{:S(2)}) %collective-permute-start.6) | collective-permute-done | bytes 262176 | tf_op jit(solution)/shard_map/ppermute | solution.py:333
  22.7 2.3 %collective-permute-done.7.refs_1_.refs_2_ = bf16[256,256]{1,0:T(8,128)(2,1)S(1)} collective-permute-done((bf16[256,256]{1,0:T(8,128)(2,1)}, bf16[256,256]{1,0:T(8,128)(2,1)S(1)}, u32[]{:S(2)}, u32[]{:S(2)}) %collective-permute-start.7) | collective-permute-done | bytes 131104 | tf_op jit(solution)/shard_map/ppermute | solution.py:328
  25.1 0.5 collective-permute-start.5
  25.5 0.1 pad_add_fusion.place
  25.6 0.6 collective-permute-start.10
  26.2 0.8 collective-permute-done.5.meta_core
  27.0 4.8 %source_rows.1.refs_8_.xt_ref = bf16[4,256,1024]{2,1,0:T(8,128)(2,1)S(1)} custom-call(s32[4]{0:T(128)S(1)} %pad_add_fusion.place, f32[2,4,1024]{2,1,0:T(4,128)S(1)} %pad_maximum_fusion.2.meta, f32[2,4,1024]{2,1,0:T(4,128)S(1)} %collective-permute-done.5.meta_core, bf16[2,2,256,256]{3,2,1,0:T(8,128)(2,1)S(1)} %pad_maximum_fusion.feats, ...), custom_call_target="tpu_custom_call" | custom-call | flops 2147483648 | bytes 4194304 | tf_op jit(solution)/shard_map/source_rows/pallas_call | solution.py:367
  31.8 5.0 %edge_grads.1 = (bf16[256,2048]{1,0:T(8,128)(2,1)S(1)}, f32[4,32,1024]{2,1,0:T(8,128)S(1)}) custom-call(s32[4]{0:T(128)S(1)} %pad_add_fusion.place, f32[2,4,1024]{2,1,0:T(4,128)S(1)} %pad_maximum_fusion.2.meta, f32[2,4,1024]{2,1,0:T(4,128)S(1)} %collective-permute-done.5.meta_core, bf16[30,2000]{1,0:T(8,128)(2,1)S(1)} %bitcast.13, ...), custom_call_target="tpu_custom_call" | custom-call | flops 2147483648 | bytes 4194304 | tf_op jit(solution)/shard_map/edge_grads/pallas_call | solution.py:378
  36.8 0.2 collective-permute-start.13
  37.0 8.2 %backed_sums.1 = (bf16[384,256]{1,0:T(8,128)(2,1)S(1)}, bf16[384,256]{1,0:T(8,128)(2,1)S(1)}, bf16[384,256]{1,0:T(8,128)(2,1)S(1)}, bf16[384,256]{1,0:T(8,128)(2,1)S(1)}) custom-call(s32[4]{0:T(128)S(1)} %pad_add_fusion.place, f32[2,4,1024]{2,1,0:T(4,128)S(1)} %pad_maximum_fusion.2.meta, bf16[256,2048]{1,0:T(8,128)(2,1)S(1)} %get-tuple-element.35.gt_ref, ...), custom_call_target="tpu_custom_call" | custom-call | flops 4026531840 | bytes 4194304 | tf_op jit(solution)/shard_map/backed_sums/pallas_call | solution.py:397
  45.2 0.6 collective-permute-start.12
  45.8 0.1 collective-permute-start.14
  45.9 1.6 %collective-permute-start.15 = (bf16[384,256]{1,0:T(8,128)(2,1)S(1)}, bf16[384,256]{1,0:T(8,128)(2,1)S(1)}, u32[]{:S(2)}, u32[]{:S(2)}) collective-permute-start(bf16[384,256]{1,0:T(8,128)(2,1)S(1)} %get-tuple-element.43), channel_id=1, source_target_pairs={{0,3},{1,2},{2,1},{3,0},{4,7},{5,6},{6,5},{7,4},{8,11},{9,10},{10,... | collective-permute-start | bytes 589832 | tf_op jit(solution)/shard_map/ppermute | solution.py:437
  47.5 3.6 %basis_terms.3 = (f32[480,256]{1,0:T(8,128)S(1)}, bf16[480,256]{1,0:T(8,128)(2,1)S(1)}) custom-call(s32[4]{0:T(128)S(1)} %pad_add_fusion.place, bf16[256,2048]{1,0:T(8,128)(2,1)S(1)} %get-tuple-element.35.gt_ref, bf16[256,2048]{1,0:T(8,128)(2,1)S(1)} %collective-permute-done.13.gt_core, bf16[4,256,1024]{2,1,0:T(8,128)(2,1)S(1)} %source_rows.1.refs_8_.xt_ref, ...), custom_call_target="tpu_custom_call" | custom-call | flops 2013265920 | bytes 4194304 | tf_op jit(solution)/shard_map/basis_terms/pallas_call | solution.py:416
  51.0 0.6 collective-permute-start.17
  51.6 3.6 %basis_terms.2 = (f32[480,256]{1,0:T(8,128)S(1)}, bf16[480,256]{1,0:T(8,128)(2,1)S(1)}) custom-call(s32[4]{0:T(128)S(1)} %pad_add_fusion.place, bf16[256,2048]{1,0:T(8,128)(2,1)S(1)} %get-tuple-element.35.gt_ref, bf16[256,2048]{1,0:T(8,128)(2,1)S(1)} %collective-permute-done.13.gt_core, bf16[4,256,1024]{2,1,0:T(8,128)(2,1)S(1)} %source_rows.1.refs_8_.xt_ref, ...), custom_call_target="tpu_custom_call" | custom-call | flops 2013265920 | bytes 4194304 | tf_op jit(solution)/shard_map/basis_terms/pallas_call | solution.py:416
  55.2 0.9 %collective-permute-done.15 = bf16[384,256]{1,0:T(8,128)(2,1)S(1)} collective-permute-done((bf16[384,256]{1,0:T(8,128)(2,1)S(1)}, bf16[384,256]{1,0:T(8,128)(2,1)S(1)}, u32[]{:S(2)}, u32[]{:S(2)}) %collective-permute-start.15) | collective-permute-done | bytes 196640 | tf_op jit(solution)/shard_map/ppermute | solution.py:437
  56.1 0.1 add_convert_fusion.1
  56.2 0.7 slice.29
  56.9 0.7 collective-permute-start.16
  57.6 4.9 %collective-permute-done.17 = bf16[480,256]{1,0:T(8,128)(2,1)S(1)} collective-permute-done((bf16[480,256]{1,0:T(8,128)(2,1)S(1)}, bf16[480,256]{1,0:T(8,128)(2,1)S(1)}, u32[]{:S(2)}, u32[]{:S(2)}) %collective-permute-start.17) | collective-permute-done | bytes 245792 | tf_op jit(solution)/shard_map/ppermute | solution.py:333
  62.5 0.6 collective-permute-start.21
  63.1 0.1 add_convert_fusion
  63.2 2.1 %collective-permute-start.18 = (bf16[240,256]{1,0:T(8,128)(2,1)S(1)}, bf16[240,256]{1,0:T(8,128)(2,1)S(1)}, u32[]{:S(2)}, u32[]{:S(2)}) collective-permute-start(bf16[240,256]{1,0:T(8,128)(2,1)S(1)} %get-tuple-element.49), channel_id=1, source_target_pairs={{0,8},{4,12},{8,16},{12,20},{16,24},{20,28},{24,0},{28,4},{1,9},{5... | collective-permute-start | bytes 368648 | tf_op jit(solution)/shard_map/ppermute | solution.py:328
  65.3 1.2 %collective-permute-start.19 = (bf16[240,256]{1,0:T(8,128)(2,1)S(1)}, bf16[240,256]{1,0:T(8,128)(2,1)S(1)}, u32[]{:S(2)}, u32[]{:S(2)}) collective-permute-start(bf16[240,256]{1,0:T(8,128)(2,1)S(1)} %get-tuple-element.50), channel_id=1, source_target_pairs={{0,16},{4,20},{8,24},{12,28},{16,0},{20,4},{24,8},{28,12},{1,17},{... | collective-permute-start | bytes 368648 | tf_op jit(solution)/shard_map/ppermute | solution.py:328
  66.4 0.4 collective-permute-done.21
  66.8 1.6 %collective-permute-start.22 = (bf16[128,256]{1,0:T(8,128)(2,1)S(1)}, bf16[128,256]{1,0:T(8,128)(2,1)S(1)}, u32[]{:S(2)}, u32[]{:S(2)}) collective-permute-start(bf16[128,256]{1,0:T(8,128)(2,1)S(1)} %add_convert_fusion.2), channel_id=1, source_target_pairs={{0,16},{4,20},{8,24},{12,28},{16,0},{20,4},{24,8},{28,12},{1,17},{... | collective-permute-start | bytes 196616 | tf_op jit(solution)/shard_map/ppermute | solution.py:328
  68.4 1.6 %collective-permute-start.23 = (bf16[128,256]{1,0:T(8,128)(2,1)S(1)}, bf16[128,256]{1,0:T(8,128)(2,1)S(1)}, u32[]{:S(2)}, u32[]{:S(2)}) collective-permute-start(bf16[128,256]{1,0:T(8,128)(2,1)S(1)} %add_convert_fusion.2), channel_id=1, source_target_pairs={{0,8},{4,12},{8,16},{12,20},{16,24},{20,28},{24,0},{28,4},{1,9},{5... | collective-permute-start | bytes 196616 | tf_op jit(solution)/shard_map/ppermute | solution.py:328
  70.1 2.2 %collective-permute-start.24 = (bf16[128,256]{1,0:T(8,128)(2,1)S(1)}, bf16[128,256]{1,0:T(8,128)(2,1)S(1)}, u32[]{:S(2)}, u32[]{:S(2)}) collective-permute-start(bf16[128,256]{1,0:T(8,128)(2,1)S(1)} %add_convert_fusion.2), channel_id=1, source_target_pairs={{0,24},{4,28},{8,0},{12,4},{16,8},{20,12},{24,16},{28,20},{1,25},{... | collective-permute-start | bytes 196616 | tf_op jit(solution)/shard_map/ppermute | solution.py:328
  72.3 6.4 %collective-permute-done.22 = bf16[128,256]{1,0:T(8,128)(2,1)S(1)} collective-permute-done((bf16[128,256]{1,0:T(8,128)(2,1)S(1)}, bf16[128,256]{1,0:T(8,128)(2,1)S(1)}, u32[]{:S(2)}, u32[]{:S(2)}) %collective-permute-start.22) | collective-permute-done | bytes 65568 | tf_op jit(solution)/shard_map/ppermute | solution.py:328
  78.8 1.9 %collective-permute-start.20 = (bf16[240,256]{1,0:T(8,128)(2,1)S(1)}, bf16[240,256]{1,0:T(8,128)(2,1)S(1)}, u32[]{:S(2)}, u32[]{:S(2)}) collective-permute-start(bf16[240,256]{1,0:T(8,128)(2,1)S(1)} %slice.43), channel_id=1, source_target_pairs={{0,24},{4,28},{8,0},{12,4},{16,8},{20,12},{24,16},{28,20},{1,25},{... | collective-permute-start | bytes 368648 | tf_op jit(solution)/shard_map/ppermute | solution.py:328
  80.8 0.1 collective-permute-start.25
  80.9 3.1 %collective-permute-done.20 = bf16[240,256]{1,0:T(8,128)(2,1)S(1)} collective-permute-done((bf16[240,256]{1,0:T(8,128)(2,1)S(1)}, bf16[240,256]{1,0:T(8,128)(2,1)S(1)}, u32[]{:S(2)}, u32[]{:S(2)}) %collective-permute-start.20) | collective-permute-done | bytes 122912 | tf_op jit(solution)/shard_map/ppermute | solution.py:328
  83.9 0.8 fusion.2
  84.7 1.3 %coef_rows.1 = f32[30,2000]{1,0:T(8,128)} custom-call(s32[4]{0:T(128)S(1)} %pad_add_fusion.place, f32[128,256]{1,0:T(8,128)S(1)} %add_add_fusion.own, f32[128,256]{1,0:T(8,128)S(1)} %collective-permute-done.25.other), custom_call_target="tpu_custom_call" | custom-call | flops 1048576 | bytes 4194304 | tf_op jit(solution)/shard_map/coef_rows/pallas_call | solution.py:479
  (31 shorter events, 0.3 us)
Async XLA Ops:
  0.6 11.0 %collective-permute-start = (bf16[256,256]{1,0:T(8,128)(2,1)}, bf16[256,256]{1,0:T(8,128)(2,1)S(1)}, u32[]{:S(2)}, u32[]{:S(2)}) collective-permute-start(bf16[256,256]{1,0:T(8,128)(2,1)} %param.9), channel_id=1, source_target_pairs={{0,4},{4,0},{8,12},{12,8},{16,20},{20,16},{24,28},{28,24},{1,5},{5... | collective-permute-start | bytes 393224 | tf_op jit(solution)/shard_map/ppermute | solution.py:322
  5.1 5.9 %collective-permute-start.1 = (f32[4,1024]{1,0:T(4,128)}, f32[4,1024]{1,0:T(4,128)S(1)}, u32[]{:S(2)}, u32[]{:S(2)}) collective-permute-start(f32[4,1024]{1,0:T(4,128)} %edge_table.1), channel_id=1, source_target_pairs={{0,4},{4,0},{8,12},{12,8},{16,20},{20,16},{24,28},{28,24},{1,5},{5... | collective-permute-start | bytes 49160 | tf_op jit(solution)/shard_map/ppermute | solution.py:322
  5.1 7.5 %collective-permute-start.2 = (bf16[256,256]{1,0:T(8,128)(2,1)}, bf16[256,256]{1,0:T(8,128)(2,1)S(1)}, u32[]{:S(2)}, u32[]{:S(2)}) collective-permute-start(bf16[256,256]{1,0:T(8,128)(2,1)} %bitcast.14), channel_id=1, source_target_pairs={{0,4},{4,0},{8,12},{12,8},{16,20},{20,16},{24,28},{28,24},{1,5},{5... | collective-permute-start | bytes 393224 | tf_op jit(solution)/shard_map/ppermute | solution.py:322
  7.1 8.0 %collective-permute-start.3 = (bf16[256,256]{1,0:T(8,128)(2,1)}, bf16[256,256]{1,0:T(8,128)(2,1)S(1)}, u32[]{:S(2)}, u32[]{:S(2)}) collective-permute-start(bf16[256,256]{1,0:T(8,128)(2,1)} %bitcast.15), channel_id=1, source_target_pairs={{0,8},{4,12},{8,16},{12,20},{16,24},{20,28},{24,0},{28,4},{1,9},{5... | collective-permute-start | bytes 393224 | tf_op jit(solution)/shard_map/ppermute | solution.py:328
  8.7 7.1 %collective-permute-start.4 = (bf16[256,256]{1,0:T(8,128)(2,1)}, bf16[256,256]{1,0:T(8,128)(2,1)S(1)}, u32[]{:S(2)}, u32[]{:S(2)}) collective-permute-start(bf16[256,256]{1,0:T(8,128)(2,1)} %bitcast.16), channel_id=1, source_target_pairs={{0,24},{4,28},{8,0},{12,4},{16,8},{20,12},{24,16},{28,20},{1,25},{... | collective-permute-start | bytes 393224 | tf_op jit(solution)/shard_map/ppermute | solution.py:328
  15.8 6.9 %collective-permute-start.6 = (bf16[2,256,256]{2,1,0:T(8,128)(2,1)S(1)}, bf16[2,256,256]{2,1,0:T(8,128)(2,1)S(1)}, u32[]{:S(2)}, u32[]{:S(2)}) collective-permute-start(bf16[2,256,256]{2,1,0:T(8,128)(2,1)S(1)} %pad_maximum_fusion.1), channel_id=1, source_target_pairs={{0,2},{1,3},{2,0},{3,1},{4,6},{5,7},{6,4},{7,5},{8,10},{9,11},{10,... | collective-permute-start | bytes 786440 | tf_op jit(solution)/shard_map/ppermute | solution.py:333
  17.3 7.7 %collective-permute-start.7 = (bf16[256,256]{1,0:T(8,128)(2,1)}, bf16[256,256]{1,0:T(8,128)(2,1)S(1)}, u32[]{:S(2)}, u32[]{:S(2)}) collective-permute-start(bf16[256,256]{1,0:T(8,128)(2,1)} %bitcast.17), channel_id=1, source_target_pairs={{0,16},{4,20},{8,24},{12,28},{16,0},{20,4},{24,8},{28,12},{1,17},{... | collective-permute-start | bytes 393224 | tf_op jit(solution)/shard_map/ppermute | solution.py:328
  18.5 6.5 %collective-permute-start.8 = (bf16[256,256]{1,0:T(8,128)(2,1)S(1)}, bf16[256,256]{1,0:T(8,128)(2,1)S(1)}, u32[]{:S(2)}, u32[]{:S(2)}) collective-permute-start(bf16[256,256]{1,0:T(8,128)(2,1)S(1)} %collective-permute-done.3.refs_0_.refs_1_), channel_id=1, source_target_pairs={{0,4},{4,0},{8,12},{12,8},{16,20},{20,16},{24,28},{28,24},{1,5},{5... | collective-permute-start | bytes 393224 | tf_op jit(solution)/shard_map/ppermute | solution.py:322
  19.0 6.0 %collective-permute-start.9 = (bf16[256,256]{1,0:T(8,128)(2,1)S(1)}, bf16[256,256]{1,0:T(8,128)(2,1)S(1)}, u32[]{:S(2)}, u32[]{:S(2)}) collective-permute-start(bf16[256,256]{1,0:T(8,128)(2,1)S(1)} %collective-permute-done.4.refs_2_.refs_3_), channel_id=1, source_target_pairs={{0,4},{4,0},{8,12},{12,8},{16,20},{20,16},{24,28},{28,24},{1,5},{5... | collective-permute-start | bytes 393224 | tf_op jit(solution)/shard_map/ppermute | solution.py:322
  25.0 2.0 %collective-permute-start.11 = (bf16[2,2,256,256]{3,2,1,0:T(8,128)(2,1)S(1)}, bf16[2,2,256,256]{3,2,1,0:T(8,128)(2,1)S(1)}, u32[]{:S(2)}, u32[]{:S(2)}) collective-permute-start(bf16[2,2,256,256]{3,2,1,0:T(8,128)(2,1)S(1)} %pad_maximum_fusion.feats), channel_id=1, source_target_pairs={{0,1},{1,0},{2,3},{3,2},{4,5},{5,4},{6,7},{7,6},{8,9},{9,8},{10,11... | collective-permute-start | bytes 1572872 | tf_op jit(solution)/shard_map/ppermute | solution.py:325
  25.1 1.9 %collective-permute-start.5 = (f32[2,4,1024]{2,1,0:T(4,128)S(1)}, f32[2,4,1024]{2,1,0:T(4,128)S(1)}, u32[]{:S(2)}, u32[]{:S(2)}) collective-permute-start(f32[2,4,1024]{2,1,0:T(4,128)S(1)} %pad_maximum_fusion.2.meta), channel_id=1, source_target_pairs={{0,1},{1,0},{2,3},{3,2},{4,5},{5,4},{6,7},{7,6},{8,9},{9,8},{10,11... | collective-permute-start | bytes 98312 | tf_op jit(solution)/shard_map/ppermute | solution.py:325
  25.6 6.2 %copy-start.1 = (bf16[2000,30]{0,1:T(8,128)(2,1)S(1)}, bf16[2000,30]{0,1:T(8,128)(2,1)}, u32[]{:S(2)}) copy-start(bf16[2000,30]{0,1:T(8,128)(2,1)} %param.12) | copy-start | bytes 360004
  25.6 6.2 %copy-start.2 = (bf16[1,256,256]{2,1,0:T(8,128)(2,1)S(1)}, bf16[1,256,256]{2,1,0:T(8,128)(2,1)}, u32[]{:S(2)}) copy-start(bf16[1,256,256]{2,1,0:T(8,128)(2,1)} %param.10) | copy-start | bytes 393220
  25.6 6.2 %collective-permute-start.10 = (bf16[256,256]{1,0:T(8,128)(2,1)S(1)}, bf16[256,256]{1,0:T(8,128)(2,1)S(1)}, u32[]{:S(2)}, u32[]{:S(2)}) collective-permute-start(bf16[256,256]{1,0:T(8,128)(2,1)S(1)} %collective-permute-done.7.refs_1_.refs_2_), channel_id=1, source_target_pairs={{0,4},{4,0},{8,12},{12,8},{16,20},{20,16},{24,28},{28,24},{1,5},{5... | collective-permute-start | bytes 393224 | tf_op jit(solution)/shard_map/ppermute | solution.py:322
  31.8 5.2 %copy-start = (bf16[30,256,256]{2,1,0:T(8,128)(2,1)S(1)}, bf16[30,256,256]{2,1,0:T(8,128)(2,1)}, u32[]{:S(2)}) copy-start(bf16[30,256,256]{2,1,0:T(8,128)(2,1)} %bases_ref.1) | copy-start | bytes 11796484
  36.8 10.7 %collective-permute-start.13 = (bf16[256,2048]{1,0:T(8,128)(2,1)S(1)}, bf16[256,2048]{1,0:T(8,128)(2,1)S(1)}, u32[]{:S(2)}, u32[]{:S(2)}) collective-permute-start(bf16[256,2048]{1,0:T(8,128)(2,1)S(1)} %get-tuple-element.35.gt_ref), channel_id=1, source_target_pairs={{0,1},{1,0},{2,3},{3,2},{4,5},{5,4},{6,7},{7,6},{8,9},{9,8},{10,11... | collective-permute-start | bytes 3145736 | tf_op jit(solution)/shard_map/ppermute | solution.py:325
  45.2 9.9 %collective-permute-start.12 = (bf16[384,256]{1,0:T(8,128)(2,1)S(1)}, bf16[384,256]{1,0:T(8,128)(2,1)S(1)}, u32[]{:S(2)}, u32[]{:S(2)}) collective-permute-start(bf16[384,256]{1,0:T(8,128)(2,1)S(1)} %get-tuple-element.38), channel_id=1, source_target_pairs={{0,2},{1,3},{2,0},{3,1},{4,6},{5,7},{6,4},{7,5},{8,10},{9,11},{10,... | collective-permute-start | bytes 589832 | tf_op jit(solution)/shard_map/ppermute | solution.py:437
  45.8 9.4 %collective-permute-start.14 = (bf16[384,256]{1,0:T(8,128)(2,1)S(1)}, bf16[384,256]{1,0:T(8,128)(2,1)S(1)}, u32[]{:S(2)}, u32[]{:S(2)}) collective-permute-start(bf16[384,256]{1,0:T(8,128)(2,1)S(1)} %get-tuple-element.41), channel_id=1, source_target_pairs={{0,1},{1,0},{2,3},{3,2},{4,5},{5,4},{6,7},{7,6},{8,9},{9,8},{10,11... | collective-permute-start | bytes 589832 | tf_op jit(solution)/shard_map/ppermute | solution.py:437
  45.9 10.2 %collective-permute-start.15 = (bf16[384,256]{1,0:T(8,128)(2,1)S(1)}, bf16[384,256]{1,0:T(8,128)(2,1)S(1)}, u32[]{:S(2)}, u32[]{:S(2)}) collective-permute-start(bf16[384,256]{1,0:T(8,128)(2,1)S(1)} %get-tuple-element.43), channel_id=1, source_target_pairs={{0,3},{1,2},{2,1},{3,0},{4,7},{5,6},{6,5},{7,4},{8,11},{9,10},{10,... | collective-permute-start | bytes 589832 | tf_op jit(solution)/shard_map/ppermute | solution.py:437
  51.0 11.5 %collective-permute-start.17 = (bf16[480,256]{1,0:T(8,128)(2,1)S(1)}, bf16[480,256]{1,0:T(8,128)(2,1)S(1)}, u32[]{:S(2)}, u32[]{:S(2)}) collective-permute-start(bf16[480,256]{1,0:T(8,128)(2,1)S(1)} %get-tuple-element.47), channel_id=1, source_target_pairs={{0,2},{1,3},{2,0},{3,1},{4,6},{5,7},{6,4},{7,5},{8,10},{9,11},{10,... | collective-permute-start | bytes 737288 | tf_op jit(solution)/shard_map/ppermute | solution.py:333
  56.9 13.2 %collective-permute-start.16 = (bf16[480,256]{1,0:T(8,128)(2,1)S(1)}, bf16[480,256]{1,0:T(8,128)(2,1)S(1)}, u32[]{:S(2)}, u32[]{:S(2)}) collective-permute-start(bf16[480,256]{1,0:T(8,128)(2,1)S(1)} %get-tuple-element.45), channel_id=1, source_target_pairs={{0,2},{1,3},{2,0},{3,1},{4,6},{5,7},{6,4},{7,5},{8,10},{9,11},{10,... | collective-permute-start | bytes 737288 | tf_op jit(solution)/shard_map/ppermute | solution.py:333
  62.5 4.3 %collective-permute-start.21 = (bf16[128,256]{1,0:T(8,128)(2,1)S(1)}, bf16[128,256]{1,0:T(8,128)(2,1)S(1)}, u32[]{:S(2)}, u32[]{:S(2)}) collective-permute-start(bf16[128,256]{1,0:T(8,128)(2,1)S(1)} %slice.34), channel_id=1, source_target_pairs={{0,4},{4,0},{8,12},{12,8},{16,20},{20,16},{24,28},{28,24},{1,5},{5... | collective-permute-start | bytes 196616 | tf_op jit(solution)/shard_map/ppermute | solution.py:322
  63.2 17.7 %collective-permute-start.18 = (bf16[240,256]{1,0:T(8,128)(2,1)S(1)}, bf16[240,256]{1,0:T(8,128)(2,1)S(1)}, u32[]{:S(2)}, u32[]{:S(2)}) collective-permute-start(bf16[240,256]{1,0:T(8,128)(2,1)S(1)} %get-tuple-element.49), channel_id=1, source_target_pairs={{0,8},{4,12},{8,16},{12,20},{16,24},{20,28},{24,0},{28,4},{1,9},{5... | collective-permute-start | bytes 368648 | tf_op jit(solution)/shard_map/ppermute | solution.py:328
  65.3 15.6 %collective-permute-start.19 = (bf16[240,256]{1,0:T(8,128)(2,1)S(1)}, bf16[240,256]{1,0:T(8,128)(2,1)S(1)}, u32[]{:S(2)}, u32[]{:S(2)}) collective-permute-start(bf16[240,256]{1,0:T(8,128)(2,1)S(1)} %get-tuple-element.50), channel_id=1, source_target_pairs={{0,16},{4,20},{8,24},{12,28},{16,0},{20,4},{24,8},{28,12},{1,17},{... | collective-permute-start | bytes 368648 | tf_op jit(solution)/shard_map/ppermute | solution.py:328
  66.8 12.0 %collective-permute-start.22 = (bf16[128,256]{1,0:T(8,128)(2,1)S(1)}, bf16[128,256]{1,0:T(8,128)(2,1)S(1)}, u32[]{:S(2)}, u32[]{:S(2)}) collective-permute-start(bf16[128,256]{1,0:T(8,128)(2,1)S(1)} %add_convert_fusion.2), channel_id=1, source_target_pairs={{0,16},{4,20},{8,24},{12,28},{16,0},{20,4},{24,8},{28,12},{1,17},{... | collective-permute-start | bytes 196616 | tf_op jit(solution)/shard_map/ppermute | solution.py:328
  68.4 12.3 %collective-permute-start.23 = (bf16[128,256]{1,0:T(8,128)(2,1)S(1)}, bf16[128,256]{1,0:T(8,128)(2,1)S(1)}, u32[]{:S(2)}, u32[]{:S(2)}) collective-permute-start(bf16[128,256]{1,0:T(8,128)(2,1)S(1)} %add_convert_fusion.2), channel_id=1, source_target_pairs={{0,8},{4,12},{8,16},{12,20},{16,24},{20,28},{24,0},{28,4},{1,9},{5... | collective-permute-start | bytes 196616 | tf_op jit(solution)/shard_map/ppermute | solution.py:328
  70.1 10.6 %collective-permute-start.24 = (bf16[128,256]{1,0:T(8,128)(2,1)S(1)}, bf16[128,256]{1,0:T(8,128)(2,1)S(1)}, u32[]{:S(2)}, u32[]{:S(2)}) collective-permute-start(bf16[128,256]{1,0:T(8,128)(2,1)S(1)} %add_convert_fusion.2), channel_id=1, source_target_pairs={{0,24},{4,28},{8,0},{12,4},{16,8},{20,12},{24,16},{28,20},{1,25},{... | collective-permute-start | bytes 196616 | tf_op jit(solution)/shard_map/ppermute | solution.py:328
  78.8 5.2 %collective-permute-start.20 = (bf16[240,256]{1,0:T(8,128)(2,1)S(1)}, bf16[240,256]{1,0:T(8,128)(2,1)S(1)}, u32[]{:S(2)}, u32[]{:S(2)}) collective-permute-start(bf16[240,256]{1,0:T(8,128)(2,1)S(1)} %slice.43), channel_id=1, source_target_pairs={{0,24},{4,28},{8,0},{12,4},{16,8},{20,12},{24,16},{28,20},{1,25},{... | collective-permute-start | bytes 368648 | tf_op jit(solution)/shard_map/ppermute | solution.py:328
  80.8 3.9 %collective-permute-start.25 = (f32[128,256]{1,0:T(8,128)S(1)}, f32[128,256]{1,0:T(8,128)S(1)}, u32[]{:S(2)}, u32[]{:S(2)}) collective-permute-start(f32[128,256]{1,0:T(8,128)S(1)} %add_add_fusion.own), channel_id=1, source_target_pairs={{0,1},{1,0},{2,3},{3,2},{4,5},{5,4},{6,7},{7,6},{8,9},{9,8},{10,11... | collective-permute-start | bytes 393224 | tf_op jit(solution)/shard_map/ppermute | solution.py:325

commit v8 on v7

--- a/solution.py
+++ b/solution.py
@@ -180,8 +180,8 @@
     sizes, place, meta, gt_ref, xt_ref, ct_ref, bases_ref, *refs
 ):
     cols, shard, span, heads, padded, group = sizes
-    outs = refs[:cols]
-    total, inner, wide, coef_sum = refs[cols:]
+    outs, halves = refs[:cols], refs[cols : cols + PAIR]
+    total, inner, wide, coef_sum = refs[cols + PAIR :]
     count = cols // PAIR
     y, core = place[2], place[3]
     edges = meta.shape[-1]
@@ -213,7 +213,7 @@
     values = total[...].astype(BF16)
     for at in range(cols):
         hot = one_hot(jnp.where(slot == at, local, -1), shard)
-        outs[at][0:shard, :] = dot_t(hot, values).astype(BF16)
+        outs[at][...] = dot_t(hot, values).astype(BF16)
     high, low = split_index(meta[0, 2:3, :].astype(I32), LANES)
     for head in range(heads):
         wide[head * padded : (head + 1) * padded, :] = jnp.where(
@@ -225,11 +225,7 @@
     for far in range(PAIR):
         for side in range(2):
             at = pl.multiple_of((core ^ far) * share + side * half, 8)
-            rows = coef_sum[pl.ds(at, half), :].astype(BF16)
-            for sy in range(count):
-                outs[far * count + sy][
-                    shard : shard + half, side * LANES : (side + 1) * LANES
-                ] = rows
+            halves[far][:, side * LANES : (side + 1) * LANES] = coef_sum[pl.ds(at, half), :]
 
 
 def basis_kernel(sizes, place, gt_ref, gt_core, xt_ref, ct_ref, *refs):
@@ -396,7 +392,8 @@
     share_rows = heads * padded // PAIR // 2
     packed = call(
         functools.partial(forward_kernel, (cols, shard, span, heads, padded, group)),
-        [jax.ShapeDtypeStruct((shard + share_rows, width), BF16)] * cols,
+        [jax.ShapeDtypeStruct((shard, width), BF16)] * cols
+        + [jax.ShapeDtypeStruct((share_rows, width), F32)] * PAIR,
         5,
         [
             pltpu.VMEM((width, edges), F32),
@@ -446,12 +443,21 @@
     others = [(far, sy) for far in range(PAIR) for sy in range(y_count) if far or sy]
     received = [to_col(packed[far * y_count + sy], far, sy) for far, sy in others]
 
+    coef_part = packed[cols] + flip_core(packed[cols + 1])
+    where = [after(place, coef_part)]
+    coef_part = coef_part + flip_x(coef_part)
+    where.append(after(place, coef_part))
+    low = coef_part.astype(BF16)
+    around = [turn_z(low, s) for s in range(1, a_count)]
+
     order = tuple(range(1, a_count)) + (0,)
     half = (a_count + 1) // 2
     sums, landed = {}, []
-    for turns in (order[:half], order[half:]):
+    for start, turns in zip(where, (order[:half], order[half:])):
         if turns:
-            blocks = basis_blocks(place, turns)
+            if sums:
+                start = after(start, blocks[0])
+            blocks = basis_blocks(start, turns)
             value = blocks[0]
             for sy in range(1, y_count):
                 landed.append(turn_y(blocks[sy], sy))
@@ -459,6 +465,8 @@
             for at, sz in enumerate(turns):
                 piece = value[at * cover : (at + 1) * cover]
                 sums[sz] = turn_z(piece.astype(BF16), sz) if sz else piece
+    around = [after(value, landed[0]) for value in around]
+    coef_part = tree_sum([low.astype(F32)] + [value.astype(F32) for value in around])
     joined = packed[0].astype(F32)
     for value in received:
         joined = joined + after(value, blocks[0]).astype(F32)
@@ -470,12 +478,9 @@
         basis_sum = lax.dynamic_slice_in_dim(basis_sum, owner * block % TILE, block, axis=0)
     basis_grad = basis_sum / cols
 
-    node_grad = joined[:shard].astype(BF16)
-    coef_part = joined[shard:]
+    node_grad = joined.astype(BF16)
     low = after(coef_part.astype(BF16), landed[0])
-    low = (low.astype(F32) + flip_x(low).astype(F32)).astype(BF16)
-    around = [turn_z(low, s).astype(F32) for s in range(1, a_count)]
-    coef_part = tree_sum([low.astype(F32)] + around)
+    coef_part = tree_sum([low.astype(F32)] + [turn_y(low, s).astype(F32) for s in range(1, y_count)])
     coef_grad = call(
         functools.partial(coef_kernel, (heads, padded, cols)),
         jax.ShapeDtypeStruct((basis_count, relation_count), F32),

time: 86.3 us -> 83.6 us (0.969)
  waiting for transfers between devices: 24.2 us -> 19.4 us
  starting transfers between devices: 29.6 us -> 31.7 us
    ppermute x3 -> x4, waiting for transfers between devices: 7.09 us -> 2.16 us  [turn_y(): lax.ppermute(value, 'col', [(c, (c + by * PAIR) % cols) for c in range(co...]
    ppermute x7, waiting for transfers between devices: 0.37 us -> 2.93 us  [flip_x(): return lax.ppermute(value, 'row', [(r, r ^ 1) for r in range(rows_total)])]
    ppermute x9, waiting for transfers between devices: 15 us -> 12.5 us  [turn_z(): lax.ppermute(value, 'row', [(r, (r + by * PAIR) % rows_total) for r in ra...]
    ppermute x3 -> x4, starting transfers between devices: 2.76 us -> 5.19 us  [turn_y(): lax.ppermute(value, 'col', [(c, (c + by * PAIR) % cols) for c in range(co...]
    ppermute x4 -> x5, waiting for transfers between devices: 0.82 us -> 1.8 us  [flip_core(): return lax.ppermute(value, 'col', [(c, c ^ 1) for c in range(cols)])]
    ppermute x3, waiting for transfers between devices: 0.93 us -> 0.01 us  [to_col(): lax.ppermute(value, 'col', [(c, (c // PAIR + sy) % y_count * PAIR + (c %...]
  transfers between devices with their start and end apart: 26 -> 28, of which waited for: 10 -> 11; matrix products, arithmetic and copies ran while one was open for 4% -> 4% of each run, Pallas kernels for 25% -> 26%
where the time goes in v8:
time: 83.6 us; the launch traced here: 83.3 us
  starting transfers between devices  31.7 us (38%)
  Pallas kernels  27.8 us (33%)
  waiting for transfers between devices  19.4 us (23%)
  other arithmetic  3.47 us (4%)
  between operations  0.85 us (1%)
    ppermute x9, starting transfers between devices, turn_z(): lax.ppermute(value, 'row', [(r, (r + by * PAIR) % rows_total) for r in ra...  14.8 us
    ppermute x9, waiting for transfers between devices, turn_z(): lax.ppermute(value, 'row', [(r, (r + by * PAIR) % rows_total) for r in ra...  12.5 us
    ppermute x7, starting transfers between devices, flip_x(): return lax.ppermute(value, 'row', [(r, r ^ 1) for r in range(rows_total)])  8.38 us
    pallas_call x1, Pallas kernels, on_device(): call(functools.partial(forward_kernel, (cols, shard, span, heads, padded,...  8.2 us
    pallas_call x2, Pallas kernels, basis_blocks(): call(functools.partial(basis_kernel, (rows_total, cols, block, cover // T...  7.14 us
    ppermute x4, starting transfers between devices, turn_y(): lax.ppermute(value, 'col', [(c, (c + by * PAIR) % cols) for c in range(co...  5.19 us
    pallas_call x1, Pallas kernels, on_device(): call(functools.partial(grad_kernel, (rows_total, dest_shard, span, heads,...  4.96 us
    pallas_call x1, Pallas kernels, on_device(): call(functools.partial(source_kernel, (cols, shard, span, a_count - 1)),...  4.79 us
  transfers between devices with their start and end apart: 28, of which 11 were waited for; matrix products, arithmetic and copies ran while one was open for 4% of the time, Pallas kernels for 26%

profile of v8, /device:TPU:0, one launch (start us, length us, event | category | flops | bytes accessed | tf_op | source)
XLA Modules:
  0.0 83.3 jit_solution(16697520457574166948)
XLA Ops:
  0.6 3.0 %collective-permute-start = (bf16[256,256]{1,0:T(8,128)(2,1)}, bf16[256,256]{1,0:T(8,128)(2,1)S(1)}, u32[]{:S(2)}, u32[]{:S(2)}) collective-permute-start(bf16[256,256]{1,0:T(8,128)(2,1)} %param.9), channel_id=1, source_target_pairs={{0,4},{4,0},{8,12},{12,8},{16,20},{20,16},{24,28},{28,24},{1,5},{5... | collective-permute-start | bytes 393224 | tf_op jit(solution)/shard_map/ppermute | solution.py:318
  3.6 1.4 %edge_table.1 = f32[4,1024]{1,0:T(4,128)} custom-call(s32[1,1,8]{2,1,0:T(1,128)} %fills.1, s32[1,1,1024]{2,1,0:T(1,128)} %src.1, s32[1,1,1024]{2,1,0:T(1,128)} %dst.1, s32[1,1,1024]{2,1,0:T(1,128)} %rel.1, f32[1,1,1024]{2,1,0:T(1,128)} %norm.1), custom_call_target="tpu_custom_call" | custom-call | tf_op jit(solution)/shard_map/edge_table/pallas_call | solution.py:335
  5.1 2.0 %collective-permute-start.2 = (bf16[256,256]{1,0:T(8,128)(2,1)}, bf16[256,256]{1,0:T(8,128)(2,1)S(1)}, u32[]{:S(2)}, u32[]{:S(2)}) collective-permute-start(bf16[256,256]{1,0:T(8,128)(2,1)} %bitcast.14), channel_id=1, source_target_pairs={{0,4},{4,0},{8,12},{12,8},{16,20},{20,16},{24,28},{28,24},{1,5},{5... | collective-permute-start | bytes 393224 | tf_op jit(solution)/shard_map/ppermute | solution.py:318
  7.1 1.6 %collective-permute-start.3 = (bf16[256,256]{1,0:T(8,128)(2,1)}, bf16[256,256]{1,0:T(8,128)(2,1)S(1)}, u32[]{:S(2)}, u32[]{:S(2)}) collective-permute-start(bf16[256,256]{1,0:T(8,128)(2,1)} %bitcast.15), channel_id=1, source_target_pairs={{0,8},{4,12},{8,16},{12,20},{16,24},{20,28},{24,0},{28,4},{1,9},{5... | collective-permute-start | bytes 393224 | tf_op jit(solution)/shard_map/ppermute | solution.py:324
  8.7 2.2 %collective-permute-start.4 = (bf16[256,256]{1,0:T(8,128)(2,1)}, bf16[256,256]{1,0:T(8,128)(2,1)S(1)}, u32[]{:S(2)}, u32[]{:S(2)}) collective-permute-start(bf16[256,256]{1,0:T(8,128)(2,1)} %bitcast.16), channel_id=1, source_target_pairs={{0,24},{4,28},{8,0},{12,4},{16,8},{20,12},{24,16},{28,20},{1,25},{... | collective-permute-start | bytes 393224 | tf_op jit(solution)/shard_map/ppermute | solution.py:324
  10.9 0.7 pad_maximum_fusion.2.meta
  11.6 0.9 %pad_maximum_fusion.1 = bf16[2,256,256]{2,1,0:T(8,128)(2,1)S(1)} fusion(bf16[1,256,256]{2,1,0:T(8,128)(2,1)S(1)} %bitcast.23, bf16[1,256,256]{2,1,0:T(8,128)(2,1)} %bitcast.22), kind=kLoop, calls=%fused_computation.3 | loop fusion | flops 131072 | bytes 524288 | tf_op jit(solution)/shard_map/stack | solution.py:346
  12.6 2.5 %collective-permute-done.3.refs_0_.refs_1_ = bf16[256,256]{1,0:T(8,128)(2,1)S(1)} collective-permute-done((bf16[256,256]{1,0:T(8,128)(2,1)}, bf16[256,256]{1,0:T(8,128)(2,1)S(1)}, u32[]{:S(2)}, u32[]{:S(2)}) %collective-permute-start.3) | collective-permute-done | bytes 131104 | tf_op jit(solution)/shard_map/ppermute | solution.py:324
  15.1 0.7 collective-permute-done.4.refs_2_.refs_3_
  15.8 1.5 %collective-permute-start.6 = (bf16[2,256,256]{2,1,0:T(8,128)(2,1)S(1)}, bf16[2,256,256]{2,1,0:T(8,128)(2,1)S(1)}, u32[]{:S(2)}, u32[]{:S(2)}) collective-permute-start(bf16[2,256,256]{2,1,0:T(8,128)(2,1)S(1)} %pad_maximum_fusion.1), channel_id=1, source_target_pairs={{0,2},{1,3},{2,0},{3,1},{4,6},{5,7},{6,4},{7,5},{8,10},{9,11},{10,... | collective-permute-start | bytes 786440 | tf_op jit(solution)/shard_map/ppermute | solution.py:329
  17.3 1.2 %collective-permute-start.7 = (bf16[256,256]{1,0:T(8,128)(2,1)}, bf16[256,256]{1,0:T(8,128)(2,1)S(1)}, u32[]{:S(2)}, u32[]{:S(2)}) collective-permute-start(bf16[256,256]{1,0:T(8,128)(2,1)} %bitcast.17), channel_id=1, source_target_pairs={{0,16},{4,20},{8,24},{12,28},{16,0},{20,4},{24,8},{28,12},{1,17},{... | collective-permute-start | bytes 393224 | tf_op jit(solution)/shard_map/ppermute | solution.py:324
  18.5 0.5 collective-permute-start.8
  19.0 1.5 %collective-permute-start.9 = (bf16[256,256]{1,0:T(8,128)(2,1)S(1)}, bf16[256,256]{1,0:T(8,128)(2,1)S(1)}, u32[]{:S(2)}, u32[]{:S(2)}) collective-permute-start(bf16[256,256]{1,0:T(8,128)(2,1)S(1)} %collective-permute-done.4.refs_2_.refs_3_), channel_id=1, source_target_pairs={{0,4},{4,0},{8,12},{12,8},{16,20},{20,16},{24,28},{28,24},{1,5},{5... | collective-permute-start | bytes 393224 | tf_op jit(solution)/shard_map/ppermute | solution.py:318
  20.5 2.2 %collective-permute-done.6 = bf16[2,256,256]{2,1,0:T(8,128)(2,1)S(1)} collective-permute-done((bf16[2,256,256]{2,1,0:T(8,128)(2,1)S(1)}, bf16[2,256,256]{2,1,0:T(8,128)(2,1)S(1)}, u32[]{:S(2)}, u32[]{:S(2)}) %collective-permute-start.6) | collective-permute-done | bytes 262176 | tf_op jit(solution)/shard_map/ppermute | solution.py:329
  22.7 2.3 %collective-permute-done.7.refs_1_.refs_2_ = bf16[256,256]{1,0:T(8,128)(2,1)S(1)} collective-permute-done((bf16[256,256]{1,0:T(8,128)(2,1)}, bf16[256,256]{1,0:T(8,128)(2,1)S(1)}, u32[]{:S(2)}, u32[]{:S(2)}) %collective-permute-start.7) | collective-permute-done | bytes 131104 | tf_op jit(solution)/shard_map/ppermute | solution.py:324
  25.1 0.5 collective-permute-start.5
  25.5 0.1 pad_add_fusion.place
  25.6 0.6 collective-permute-start.10
  26.2 0.8 collective-permute-done.5.meta_core
  27.0 4.8 %source_rows.1.refs_8_.xt_ref = bf16[4,256,1024]{2,1,0:T(8,128)(2,1)S(1)} custom-call(s32[4]{0:T(128)S(1)} %pad_add_fusion.place, f32[2,4,1024]{2,1,0:T(4,128)S(1)} %pad_maximum_fusion.2.meta, f32[2,4,1024]{2,1,0:T(4,128)S(1)} %collective-permute-done.5.meta_core, bf16[2,2,256,256]{3,2,1,0:T(8,128)(2,1)S(1)} %pad_maximum_fusion.feats, ...), custom_call_target="tpu_custom_call" | custom-call | flops 2147483648 | bytes 4194304 | tf_op jit(solution)/shard_map/source_rows/pallas_call | solution.py:363
  31.8 5.0 %edge_grads.1 = (bf16[256,2048]{1,0:T(8,128)(2,1)S(1)}, f32[4,32,1024]{2,1,0:T(8,128)S(1)}) custom-call(s32[4]{0:T(128)S(1)} %pad_add_fusion.place, f32[2,4,1024]{2,1,0:T(4,128)S(1)} %pad_maximum_fusion.2.meta, f32[2,4,1024]{2,1,0:T(4,128)S(1)} %collective-permute-done.5.meta_core, bf16[30,2000]{1,0:T(8,128)(2,1)S(1)} %bitcast.13, ...), custom_call_target="tpu_custom_call" | custom-call | flops 2147483648 | bytes 4194304 | tf_op jit(solution)/shard_map/edge_grads/pallas_call | solution.py:374
  36.8 0.2 collective-permute-start.15
  37.0 8.2 %backed_sums.1 = (bf16[256,256]{1,0:T(8,128)(2,1)S(1)}, bf16[256,256]{1,0:T(8,128)(2,1)S(1)}, bf16[256,256]{1,0:T(8,128)(2,1)S(1)}, bf16[256,256]{1,0:T(8,128)(2...) custom-call(s32[4]{0:T(128)S(1)} %pad_add_fusion.place, f32[2,4,1024]{2,1,0:T(4,128)S(1)} %pad_maximum_fusion.2.meta, ...), custom_call_target="tpu_custom_call" | custom-call | flops 4026531840 | bytes 4194304 | tf_op jit(solution)/shard_map/backed_sums/pallas_call | solution.py:393
  45.2 0.4 collective-permute-start.13
  45.6 1.0 %collective-permute-done.13 = f32[128,256]{1,0:T(8,128)S(1)} collective-permute-done((f32[128,256]{1,0:T(8,128)S(1)}, f32[128,256]{1,0:T(8,128)S(1)}, u32[]{:S(2)}, u32[]{:S(2)}) %collective-permute-start.13) | collective-permute-done | bytes 131104 | tf_op jit(solution)/shard_map/ppermute | solution.py:321
  46.7 0.8 collective-permute-start.14
  47.4 0.5 collective-permute-start.12
  47.9 1.6 %collective-permute-start.17 = (bf16[256,256]{1,0:T(8,128)(2,1)S(1)}, bf16[256,256]{1,0:T(8,128)(2,1)S(1)}, u32[]{:S(2)}, u32[]{:S(2)}) collective-permute-start(bf16[256,256]{1,0:T(8,128)(2,1)S(1)} %get-tuple-element.57), channel_id=1, source_target_pairs={{0,3},{1,2},{2,1},{3,0},{4,7},{5,6},{6,5},{7,4},{8,11},{9,10},{10,... | collective-permute-start | bytes 393224 | tf_op jit(solution)/shard_map/ppermute | solution.py:434
  49.6 2.9 %collective-permute-done.14 = f32[128,256]{1,0:T(8,128)S(1)} collective-permute-done((f32[128,256]{1,0:T(8,128)S(1)}, f32[128,256]{1,0:T(8,128)S(1)}, u32[]{:S(2)}, u32[]{:S(2)}) %collective-permute-start.14) | collective-permute-done | bytes 131104 | tf_op jit(solution)/shard_map/ppermute | solution.py:318
  52.5 1.6 %collective-permute-start.23 = (bf16[128,256]{1,0:T(8,128)(2,1)S(1)}, bf16[128,256]{1,0:T(8,128)(2,1)S(1)}, u32[]{:S(2)}, u32[]{:S(2)}) collective-permute-start(bf16[128,256]{1,0:T(8,128)(2,1)S(1)} %add.54), channel_id=1, source_target_pairs={{0,16},{4,20},{8,24},{12,28},{16,0},{20,4},{24,8},{28,12},{1,17},{... | collective-permute-start | bytes 196616 | tf_op jit(solution)/shard_map/ppermute | solution.py:324
  54.2 3.6 %basis_terms.2 = (f32[480,256]{1,0:T(8,128)S(1)}, bf16[480,256]{1,0:T(8,128)(2,1)S(1)}) custom-call(s32[4]{0:T(128)S(1)} %pad_add_fusion.place, bf16[256,2048]{1,0:T(8,128)(2,1)S(1)} %get-tuple-element.43.gt_ref, bf16[256,2048]{1,0:T(8,128)(2,1)S(1)} %collective-permute-done.15.gt_core, bf16[4,256,1024]{2,1,0:T(8,128)(2,1)S(1)} %source_rows.1.refs_8_.xt_ref, ...), custom_call_target="tpu_custom_call" | custom-call | flops 2013265920 | bytes 4194304 | tf_op jit(solution)/shard_map/basis_terms/pallas_call | solution.py:413
  57.7 0.6 collective-permute-start.19
  58.3 3.6 %basis_terms.3 = (f32[480,256]{1,0:T(8,128)S(1)}, bf16[480,256]{1,0:T(8,128)(2,1)S(1)}) custom-call(s32[4]{0:T(128)S(1)} %pad_add_fusion.place, bf16[256,2048]{1,0:T(8,128)(2,1)S(1)} %get-tuple-element.43.gt_ref, bf16[256,2048]{1,0:T(8,128)(2,1)S(1)} %collective-permute-done.15.gt_core, bf16[4,256,1024]{2,1,0:T(8,128)(2,1)S(1)} %source_rows.1.refs_8_.xt_ref, ...), custom_call_target="tpu_custom_call" | custom-call | flops 2013265920 | bytes 4194304 | tf_op jit(solution)/shard_map/basis_terms/pallas_call | solution.py:413
  61.9 1.7 %collective-permute-start.24 = (bf16[128,256]{1,0:T(8,128)(2,1)S(1)}, bf16[128,256]{1,0:T(8,128)(2,1)S(1)}, u32[]{:S(2)}, u32[]{:S(2)}) collective-permute-start(bf16[128,256]{1,0:T(8,128)(2,1)S(1)} %add.54), channel_id=1, source_target_pairs={{0,8},{4,12},{8,16},{12,20},{16,24},{20,28},{24,0},{28,4},{1,9},{5... | collective-permute-start | bytes 196616 | tf_op jit(solution)/shard_map/ppermute | solution.py:324
  63.6 2.2 %collective-permute-start.25 = (bf16[128,256]{1,0:T(8,128)(2,1)S(1)}, bf16[128,256]{1,0:T(8,128)(2,1)S(1)}, u32[]{:S(2)}, u32[]{:S(2)}) collective-permute-start(bf16[128,256]{1,0:T(8,128)(2,1)S(1)} %add.54), channel_id=1, source_target_pairs={{0,24},{4,28},{8,0},{12,4},{16,8},{20,12},{24,16},{28,20},{1,25},{... | collective-permute-start | bytes 196616 | tf_op jit(solution)/shard_map/ppermute | solution.py:324
  65.8 1.5 %collective-permute-start.18 = (bf16[480,256]{1,0:T(8,128)(2,1)S(1)}, bf16[480,256]{1,0:T(8,128)(2,1)S(1)}, u32[]{:S(2)}, u32[]{:S(2)}) collective-permute-start(bf16[480,256]{1,0:T(8,128)(2,1)S(1)} %get-tuple-element.59), channel_id=1, source_target_pairs={{0,2},{1,3},{2,0},{3,1},{4,6},{5,7},{6,4},{7,5},{8,10},{9,11},{10,... | collective-permute-start | bytes 737288 | tf_op jit(solution)/shard_map/ppermute | solution.py:329
  67.3 0.7 add_convert_fusion.1
  68.0 0.1 collective-permute-done.24
  68.1 0.4 collective-permute-done.25
  68.6 1.6 %collective-permute-start.26 = (bf16[128,256]{1,0:T(8,128)(2,1)S(1)}, bf16[128,256]{1,0:T(8,128)(2,1)S(1)}, u32[]{:S(2)}, u32[]{:S(2)}) collective-permute-start(bf16[128,256]{1,0:T(8,128)(2,1)S(1)} %add_convert_fusion.2), channel_id=1, source_target_pairs={{0,2},{1,3},{2,0},{3,1},{4,6},{5,7},{6,4},{7,5},{8,10},{9,11},{10,... | collective-permute-start | bytes 196616 | tf_op jit(solution)/shard_map/ppermute | solution.py:329
  70.3 0.3 collective-permute-start.20
  70.6 3.9 %collective-permute-start.21 = (bf16[240,256]{1,0:T(8,128)(2,1)S(1)}, bf16[240,256]{1,0:T(8,128)(2,1)S(1)}, u32[]{:S(2)}, u32[]{:S(2)}) collective-permute-start(bf16[240,256]{1,0:T(8,128)(2,1)S(1)} %get-tuple-element.66), channel_id=1, source_target_pairs={{0,16},{4,20},{8,24},{12,28},{16,0},{20,4},{24,8},{28,12},{1,17},{... | collective-permute-start | bytes 368648 | tf_op jit(solution)/shard_map/ppermute | solution.py:324
  74.6 0.1 collective-permute-start.22
  74.7 0.1 collective-permute-start.27
  74.8 2.9 %collective-permute-done.20 = bf16[240,256]{1,0:T(8,128)(2,1)S(1)} collective-permute-done((bf16[240,256]{1,0:T(8,128)(2,1)S(1)}, bf16[240,256]{1,0:T(8,128)(2,1)S(1)}, u32[]{:S(2)}, u32[]{:S(2)}) %collective-permute-start.20) | collective-permute-done | bytes 122912 | tf_op jit(solution)/shard_map/ppermute | solution.py:324
  77.7 3.5 %collective-permute-done.21 = bf16[240,256]{1,0:T(8,128)(2,1)S(1)} collective-permute-done((bf16[240,256]{1,0:T(8,128)(2,1)S(1)}, bf16[240,256]{1,0:T(8,128)(2,1)S(1)}, u32[]{:S(2)}, u32[]{:S(2)}) %collective-permute-start.21) | collective-permute-done | bytes 122912 | tf_op jit(solution)/shard_map/ppermute | solution.py:324
  81.3 0.8 fusion.2
  82.0 1.3 %coef_rows.1 = f32[30,2000]{1,0:T(8,128)} custom-call(s32[4]{0:T(128)S(1)} %pad_add_fusion.place, f32[128,256]{1,0:T(8,128)S(1)} %convert_add_fusion.1.own, f32[128,256]{1,0:T(8,128)S(1)} %collective-permute-done.27.other), custom_call_target="tpu_custom_call" | custom-call | flops 1048576 | bytes 4194304 | tf_op jit(solution)/shard_map/coef_rows/pallas_call | solution.py:484
  (35 shorter events, 0.4 us)
Async XLA Ops:
  0.6 11.0 %collective-permute-start = (bf16[256,256]{1,0:T(8,128)(2,1)}, bf16[256,256]{1,0:T(8,128)(2,1)S(1)}, u32[]{:S(2)}, u32[]{:S(2)}) collective-permute-start(bf16[256,256]{1,0:T(8,128)(2,1)} %param.9), channel_id=1, source_target_pairs={{0,4},{4,0},{8,12},{12,8},{16,20},{20,16},{24,28},{28,24},{1,5},{5... | collective-permute-start | bytes 393224 | tf_op jit(solution)/shard_map/ppermute | solution.py:318
  5.1 5.9 %collective-permute-start.1 = (f32[4,1024]{1,0:T(4,128)}, f32[4,1024]{1,0:T(4,128)S(1)}, u32[]{:S(2)}, u32[]{:S(2)}) collective-permute-start(f32[4,1024]{1,0:T(4,128)} %edge_table.1), channel_id=1, source_target_pairs={{0,4},{4,0},{8,12},{12,8},{16,20},{20,16},{24,28},{28,24},{1,5},{5... | collective-permute-start | bytes 49160 | tf_op jit(solution)/shard_map/ppermute | solution.py:318
  5.1 7.5 %collective-permute-start.2 = (bf16[256,256]{1,0:T(8,128)(2,1)}, bf16[256,256]{1,0:T(8,128)(2,1)S(1)}, u32[]{:S(2)}, u32[]{:S(2)}) collective-permute-start(bf16[256,256]{1,0:T(8,128)(2,1)} %bitcast.14), channel_id=1, source_target_pairs={{0,4},{4,0},{8,12},{12,8},{16,20},{20,16},{24,28},{28,24},{1,5},{5... | collective-permute-start | bytes 393224 | tf_op jit(solution)/shard_map/ppermute | solution.py:318
  7.1 8.0 %collective-permute-start.3 = (bf16[256,256]{1,0:T(8,128)(2,1)}, bf16[256,256]{1,0:T(8,128)(2,1)S(1)}, u32[]{:S(2)}, u32[]{:S(2)}) collective-permute-start(bf16[256,256]{1,0:T(8,128)(2,1)} %bitcast.15), channel_id=1, source_target_pairs={{0,8},{4,12},{8,16},{12,20},{16,24},{20,28},{24,0},{28,4},{1,9},{5... | collective-permute-start | bytes 393224 | tf_op jit(solution)/shard_map/ppermute | solution.py:324
  8.7 7.1 %collective-permute-start.4 = (bf16[256,256]{1,0:T(8,128)(2,1)}, bf16[256,256]{1,0:T(8,128)(2,1)S(1)}, u32[]{:S(2)}, u32[]{:S(2)}) collective-permute-start(bf16[256,256]{1,0:T(8,128)(2,1)} %bitcast.16), channel_id=1, source_target_pairs={{0,24},{4,28},{8,0},{12,4},{16,8},{20,12},{24,16},{28,20},{1,25},{... | collective-permute-start | bytes 393224 | tf_op jit(solution)/shard_map/ppermute | solution.py:324
  15.8 6.9 %collective-permute-start.6 = (bf16[2,256,256]{2,1,0:T(8,128)(2,1)S(1)}, bf16[2,256,256]{2,1,0:T(8,128)(2,1)S(1)}, u32[]{:S(2)}, u32[]{:S(2)}) collective-permute-start(bf16[2,256,256]{2,1,0:T(8,128)(2,1)S(1)} %pad_maximum_fusion.1), channel_id=1, source_target_pairs={{0,2},{1,3},{2,0},{3,1},{4,6},{5,7},{6,4},{7,5},{8,10},{9,11},{10,... | collective-permute-start | bytes 786440 | tf_op jit(solution)/shard_map/ppermute | solution.py:329
  17.3 7.7 %collective-permute-start.7 = (bf16[256,256]{1,0:T(8,128)(2,1)}, bf16[256,256]{1,0:T(8,128)(2,1)S(1)}, u32[]{:S(2)}, u32[]{:S(2)}) collective-permute-start(bf16[256,256]{1,0:T(8,128)(2,1)} %bitcast.17), channel_id=1, source_target_pairs={{0,16},{4,20},{8,24},{12,28},{16,0},{20,4},{24,8},{28,12},{1,17},{... | collective-permute-start | bytes 393224 | tf_op jit(solution)/shard_map/ppermute | solution.py:324
  18.5 6.5 %collective-permute-start.8 = (bf16[256,256]{1,0:T(8,128)(2,1)S(1)}, bf16[256,256]{1,0:T(8,128)(2,1)S(1)}, u32[]{:S(2)}, u32[]{:S(2)}) collective-permute-start(bf16[256,256]{1,0:T(8,128)(2,1)S(1)} %collective-permute-done.3.refs_0_.refs_1_), channel_id=1, source_target_pairs={{0,4},{4,0},{8,12},{12,8},{16,20},{20,16},{24,28},{28,24},{1,5},{5... | collective-permute-start | bytes 393224 | tf_op jit(solution)/shard_map/ppermute | solution.py:318
  19.0 6.0 %collective-permute-start.9 = (bf16[256,256]{1,0:T(8,128)(2,1)S(1)}, bf16[256,256]{1,0:T(8,128)(2,1)S(1)}, u32[]{:S(2)}, u32[]{:S(2)}) collective-permute-start(bf16[256,256]{1,0:T(8,128)(2,1)S(1)} %collective-permute-done.4.refs_2_.refs_3_), channel_id=1, source_target_pairs={{0,4},{4,0},{8,12},{12,8},{16,20},{20,16},{24,28},{28,24},{1,5},{5... | collective-permute-start | bytes 393224 | tf_op jit(solution)/shard_map/ppermute | solution.py:318
  25.0 2.0 %collective-permute-start.11 = (bf16[2,2,256,256]{3,2,1,0:T(8,128)(2,1)S(1)}, bf16[2,2,256,256]{3,2,1,0:T(8,128)(2,1)S(1)}, u32[]{:S(2)}, u32[]{:S(2)}) collective-permute-start(bf16[2,2,256,256]{3,2,1,0:T(8,128)(2,1)S(1)} %pad_maximum_fusion.feats), channel_id=1, source_target_pairs={{0,1},{1,0},{2,3},{3,2},{4,5},{5,4},{6,7},{7,6},{8,9},{9,8},{10,11... | collective-permute-start | bytes 1572872 | tf_op jit(solution)/shard_map/ppermute | solution.py:321
  25.1 1.9 %collective-permute-start.5 = (f32[2,4,1024]{2,1,0:T(4,128)S(1)}, f32[2,4,1024]{2,1,0:T(4,128)S(1)}, u32[]{:S(2)}, u32[]{:S(2)}) collective-permute-start(f32[2,4,1024]{2,1,0:T(4,128)S(1)} %pad_maximum_fusion.2.meta), channel_id=1, source_target_pairs={{0,1},{1,0},{2,3},{3,2},{4,5},{5,4},{6,7},{7,6},{8,9},{9,8},{10,11... | collective-permute-start | bytes 98312 | tf_op jit(solution)/shard_map/ppermute | solution.py:321
  25.6 6.2 %copy-start.1 = (bf16[2000,30]{0,1:T(8,128)(2,1)S(1)}, bf16[2000,30]{0,1:T(8,128)(2,1)}, u32[]{:S(2)}) copy-start(bf16[2000,30]{0,1:T(8,128)(2,1)} %param.12) | copy-start | bytes 360004
  25.6 6.2 %copy-start.2 = (bf16[1,256,256]{2,1,0:T(8,128)(2,1)S(1)}, bf16[1,256,256]{2,1,0:T(8,128)(2,1)}, u32[]{:S(2)}) copy-start(bf16[1,256,256]{2,1,0:T(8,128)(2,1)} %param.10) | copy-start | bytes 393220
  25.6 6.2 %collective-permute-start.10 = (bf16[256,256]{1,0:T(8,128)(2,1)S(1)}, bf16[256,256]{1,0:T(8,128)(2,1)S(1)}, u32[]{:S(2)}, u32[]{:S(2)}) collective-permute-start(bf16[256,256]{1,0:T(8,128)(2,1)S(1)} %collective-permute-done.7.refs_1_.refs_2_), channel_id=1, source_target_pairs={{0,4},{4,0},{8,12},{12,8},{16,20},{20,16},{24,28},{28,24},{1,5},{5... | collective-permute-start | bytes 393224 | tf_op jit(solution)/shard_map/ppermute | solution.py:318
  31.8 5.2 %copy-start = (bf16[30,256,256]{2,1,0:T(8,128)(2,1)S(1)}, bf16[30,256,256]{2,1,0:T(8,128)(2,1)}, u32[]{:S(2)}) copy-start(bf16[30,256,256]{2,1,0:T(8,128)(2,1)} %bases_ref.1) | copy-start | bytes 11796484
  36.8 17.4 %collective-permute-start.15 = (bf16[256,2048]{1,0:T(8,128)(2,1)S(1)}, bf16[256,2048]{1,0:T(8,128)(2,1)S(1)}, u32[]{:S(2)}, u32[]{:S(2)}) collective-permute-start(bf16[256,2048]{1,0:T(8,128)(2,1)S(1)} %get-tuple-element.43.gt_ref), channel_id=1, source_target_pairs={{0,1},{1,0},{2,3},{3,2},{4,5},{5,4},{6,7},{7,6},{8,9},{9,8},{10,11... | collective-permute-start | bytes 3145736 | tf_op jit(solution)/shard_map/ppermute | solution.py:321
  45.2 1.4 %collective-permute-start.13 = (f32[128,256]{1,0:T(8,128)S(1)}, f32[128,256]{1,0:T(8,128)S(1)}, u32[]{:S(2)}, u32[]{:S(2)}) collective-permute-start(f32[128,256]{1,0:T(8,128)S(1)} %get-tuple-element.48), channel_id=1, source_target_pairs={{0,1},{1,0},{2,3},{3,2},{4,5},{5,4},{6,7},{7,6},{8,9},{9,8},{10,11... | collective-permute-start | bytes 393224 | tf_op jit(solution)/shard_map/ppermute | solution.py:321
  46.7 5.8 %collective-permute-start.14 = (f32[128,256]{1,0:T(8,128)S(1)}, f32[128,256]{1,0:T(8,128)S(1)}, u32[]{:S(2)}, u32[]{:S(2)}) collective-permute-start(f32[128,256]{1,0:T(8,128)S(1)} %add.53), channel_id=1, source_target_pairs={{0,4},{4,0},{8,12},{12,8},{16,20},{20,16},{24,28},{28,24},{1,5},{5... | collective-permute-start | bytes 393224 | tf_op jit(solution)/shard_map/ppermute | solution.py:318
  47.4 14.4 %collective-permute-start.12 = (bf16[256,256]{1,0:T(8,128)(2,1)S(1)}, bf16[256,256]{1,0:T(8,128)(2,1)S(1)}, u32[]{:S(2)}, u32[]{:S(2)}) collective-permute-start(bf16[256,256]{1,0:T(8,128)(2,1)S(1)} %get-tuple-element.46), channel_id=1, source_target_pairs={{0,2},{1,3},{2,0},{3,1},{4,6},{5,7},{6,4},{7,5},{8,10},{9,11},{10,... | collective-permute-start | bytes 393224 | tf_op jit(solution)/shard_map/ppermute | solution.py:434
  47.9 15.7 %collective-permute-start.16 = (bf16[256,256]{1,0:T(8,128)(2,1)S(1)}, bf16[256,256]{1,0:T(8,128)(2,1)S(1)}, u32[]{:S(2)}, u32[]{:S(2)}) collective-permute-start(bf16[256,256]{1,0:T(8,128)(2,1)S(1)} %get-tuple-element.55), channel_id=1, source_target_pairs={{0,1},{1,0},{2,3},{3,2},{4,5},{5,4},{6,7},{7,6},{8,9},{9,8},{10,11... | collective-permute-start | bytes 393224 | tf_op jit(solution)/shard_map/ppermute | solution.py:434
  47.9 17.8 %collective-permute-start.17 = (bf16[256,256]{1,0:T(8,128)(2,1)S(1)}, bf16[256,256]{1,0:T(8,128)(2,1)S(1)}, u32[]{:S(2)}, u32[]{:S(2)}) collective-permute-start(bf16[256,256]{1,0:T(8,128)(2,1)S(1)} %get-tuple-element.57), channel_id=1, source_target_pairs={{0,3},{1,2},{2,1},{3,0},{4,7},{5,6},{6,5},{7,4},{8,11},{9,10},{10,... | collective-permute-start | bytes 393224 | tf_op jit(solution)/shard_map/ppermute | solution.py:434
  52.5 15.5 %collective-permute-start.23 = (bf16[128,256]{1,0:T(8,128)(2,1)S(1)}, bf16[128,256]{1,0:T(8,128)(2,1)S(1)}, u32[]{:S(2)}, u32[]{:S(2)}) collective-permute-start(bf16[128,256]{1,0:T(8,128)(2,1)S(1)} %add.54), channel_id=1, source_target_pairs={{0,16},{4,20},{8,24},{12,28},{16,0},{20,4},{24,8},{28,12},{1,17},{... | collective-permute-start | bytes 196616 | tf_op jit(solution)/shard_map/ppermute | solution.py:324
  57.7 10.3 %collective-permute-start.19 = (bf16[480,256]{1,0:T(8,128)(2,1)S(1)}, bf16[480,256]{1,0:T(8,128)(2,1)S(1)}, u32[]{:S(2)}, u32[]{:S(2)}) collective-permute-start(bf16[480,256]{1,0:T(8,128)(2,1)S(1)} %get-tuple-element.60), channel_id=1, source_target_pairs={{0,2},{1,3},{2,0},{3,1},{4,6},{5,7},{6,4},{7,5},{8,10},{9,11},{10,... | collective-permute-start | bytes 737288 | tf_op jit(solution)/shard_map/ppermute | solution.py:329
  61.9 6.3 %collective-permute-start.24 = (bf16[128,256]{1,0:T(8,128)(2,1)S(1)}, bf16[128,256]{1,0:T(8,128)(2,1)S(1)}, u32[]{:S(2)}, u32[]{:S(2)}) collective-permute-start(bf16[128,256]{1,0:T(8,128)(2,1)S(1)} %add.54), channel_id=1, source_target_pairs={{0,8},{4,12},{8,16},{12,20},{16,24},{20,28},{24,0},{28,4},{1,9},{5... | collective-permute-start | bytes 196616 | tf_op jit(solution)/shard_map/ppermute | solution.py:324
  63.6 5.0 %collective-permute-start.25 = (bf16[128,256]{1,0:T(8,128)(2,1)S(1)}, bf16[128,256]{1,0:T(8,128)(2,1)S(1)}, u32[]{:S(2)}, u32[]{:S(2)}) collective-permute-start(bf16[128,256]{1,0:T(8,128)(2,1)S(1)} %add.54), channel_id=1, source_target_pairs={{0,24},{4,28},{8,0},{12,4},{16,8},{20,12},{24,16},{28,20},{1,25},{... | collective-permute-start | bytes 196616 | tf_op jit(solution)/shard_map/ppermute | solution.py:324
  65.8 8.8 %collective-permute-start.18 = (bf16[480,256]{1,0:T(8,128)(2,1)S(1)}, bf16[480,256]{1,0:T(8,128)(2,1)S(1)}, u32[]{:S(2)}, u32[]{:S(2)}) collective-permute-start(bf16[480,256]{1,0:T(8,128)(2,1)S(1)} %get-tuple-element.59), channel_id=1, source_target_pairs={{0,2},{1,3},{2,0},{3,1},{4,6},{5,7},{6,4},{7,5},{8,10},{9,11},{10,... | collective-permute-start | bytes 737288 | tf_op jit(solution)/shard_map/ppermute | solution.py:329
  68.6 6.1 %collective-permute-start.26 = (bf16[128,256]{1,0:T(8,128)(2,1)S(1)}, bf16[128,256]{1,0:T(8,128)(2,1)S(1)}, u32[]{:S(2)}, u32[]{:S(2)}) collective-permute-start(bf16[128,256]{1,0:T(8,128)(2,1)S(1)} %add_convert_fusion.2), channel_id=1, source_target_pairs={{0,2},{1,3},{2,0},{3,1},{4,6},{5,7},{6,4},{7,5},{8,10},{9,11},{10,... | collective-permute-start | bytes 196616 | tf_op jit(solution)/shard_map/ppermute | solution.py:329
  70.3 7.5 %collective-permute-start.20 = (bf16[240,256]{1,0:T(8,128)(2,1)S(1)}, bf16[240,256]{1,0:T(8,128)(2,1)S(1)}, u32[]{:S(2)}, u32[]{:S(2)}) collective-permute-start(bf16[240,256]{1,0:T(8,128)(2,1)S(1)} %get-tuple-element.65), channel_id=1, source_target_pairs={{0,8},{4,12},{8,16},{12,20},{16,24},{20,28},{24,0},{28,4},{1,9},{5... | collective-permute-start | bytes 368648 | tf_op jit(solution)/shard_map/ppermute | solution.py:324
  70.6 10.7 %collective-permute-start.21 = (bf16[240,256]{1,0:T(8,128)(2,1)S(1)}, bf16[240,256]{1,0:T(8,128)(2,1)S(1)}, u32[]{:S(2)}, u32[]{:S(2)}) collective-permute-start(bf16[240,256]{1,0:T(8,128)(2,1)S(1)} %get-tuple-element.66), channel_id=1, source_target_pairs={{0,16},{4,20},{8,24},{12,28},{16,0},{20,4},{24,8},{28,12},{1,17},{... | collective-permute-start | bytes 368648 | tf_op jit(solution)/shard_map/ppermute | solution.py:324
  74.6 6.7 %collective-permute-start.22 = (bf16[240,256]{1,0:T(8,128)(2,1)S(1)}, bf16[240,256]{1,0:T(8,128)(2,1)S(1)}, u32[]{:S(2)}, u32[]{:S(2)}) collective-permute-start(bf16[240,256]{1,0:T(8,128)(2,1)S(1)} %slice.31), channel_id=1, source_target_pairs={{0,24},{4,28},{8,0},{12,4},{16,8},{20,12},{24,16},{28,20},{1,25},{... | collective-permute-start | bytes 368648 | tf_op jit(solution)/shard_map/ppermute | solution.py:324
  74.7 7.3 %collective-permute-start.27 = (f32[128,256]{1,0:T(8,128)S(1)}, f32[128,256]{1,0:T(8,128)S(1)}, u32[]{:S(2)}, u32[]{:S(2)}) collective-permute-start(f32[128,256]{1,0:T(8,128)S(1)} %convert_add_fusion.1.own), channel_id=1, source_target_pairs={{0,1},{1,0},{2,3},{3,2},{4,5},{5,4},{6,7},{7,6},{8,9},{9,8},{10,11... | collective-permute-start | bytes 393224 | tf_op jit(solution)/shard_map/ppermute | solution.py:321

commit v9 on v8

--- a/solution.py
+++ b/solution.py
@@ -441,35 +441,32 @@
         return lax.optimization_barrier((value, other))[0]
 
     others = [(far, sy) for far in range(PAIR) for sy in range(y_count) if far or sy]
-    received = [to_col(packed[far * y_count + sy], far, sy) for far, sy in others]
-
-    coef_part = packed[cols] + flip_core(packed[cols + 1])
-    where = [after(place, coef_part)]
-    coef_part = coef_part + flip_x(coef_part)
-    where.append(after(place, coef_part))
-    low = coef_part.astype(BF16)
-    around = [turn_z(low, s) for s in range(1, a_count)]
 
     order = tuple(range(1, a_count)) + (0,)
     half = (a_count + 1) // 2
-    sums, landed = {}, []
-    for start, turns in zip(where, (order[:half], order[half:])):
-        if turns:
-            if sums:
-                start = after(start, blocks[0])
-            blocks = basis_blocks(start, turns)
-            value = blocks[0]
-            for sy in range(1, y_count):
-                landed.append(turn_y(blocks[sy], sy))
-                value = value + landed[-1].astype(F32)
-            for at, sz in enumerate(turns):
-                piece = value[at * cover : (at + 1) * cover]
-                sums[sz] = turn_z(piece.astype(BF16), sz) if sz else piece
-    around = [after(value, landed[0]) for value in around]
-    coef_part = tree_sum([low.astype(F32)] + [value.astype(F32) for value in around])
+    sums, landed, marks = {}, [], []
+
+    def add_blocks(start, turns):
+        blocks = basis_blocks(start, turns)
+        marks.append(blocks[0])
+        value = blocks[0]
+        for sy in range(1, y_count):
+            landed.append(turn_y(blocks[sy], sy))
+            value = value + landed[-1].astype(F32)
+        for at, sz in enumerate(turns):
+            piece = value[at * cover : (at + 1) * cover]
+            sums[sz] = turn_z(piece.astype(BF16), sz) if sz else piece
+
+    coef_part = packed[cols] + flip_core(packed[cols + 1])
+    add_blocks(after(place, coef_part), order[:half])
+    coef_part = coef_part + after(flip_x(coef_part), marks[0])
+    low = coef_part.astype(BF16)
+    coef_part = tree_sum([low.astype(F32)] + [turn_z(low, s).astype(F32) for s in range(1, a_count)])
+    add_blocks(after(after(place, low), marks[0]), order[half:])
     joined = packed[0].astype(F32)
-    for value in received:
-        joined = joined + after(value, blocks[0]).astype(F32)
+    for far, sy in others:
+        value = after(packed[far * y_count + sy], landed[-1])
+        joined = joined + to_col(value, far, sy).astype(F32)
     basis_sum = sums[0]
     for sz in range(1, a_count):
         basis_sum = basis_sum + sums[sz].astype(F32)

time: 83.6 us -> 81.4 us (0.974)
  starting transfers between devices: 31.7 us -> 27.3 us
  waiting for transfers between devices: 19.4 us -> 21.6 us
    ppermute x4, waiting for transfers between devices: 2.16 us -> 7.27 us  [turn_y(): lax.ppermute(value, 'col', [(c, (c + by * PAIR) % cols) for c in range(co...]
    ppermute x9, waiting for transfers between devices: 12.5 us -> 8.88 us  [turn_z(): lax.ppermute(value, 'row', [(r, (r + by * PAIR) % rows_total) for r in ra...]
    ppermute x3, waiting for transfers between devices: 0.01 us -> 2.12 us  [to_col(): lax.ppermute(value, 'col', [(c, (c // PAIR + sy) % y_count * PAIR + (c %...]
    ppermute x9, starting transfers between devices: 14.8 us -> 13.1 us  [turn_z(): lax.ppermute(value, 'row', [(r, (r + by * PAIR) % rows_total) for r in ra...]
    ppermute x4, starting transfers between devices: 5.19 us -> 3.61 us  [turn_y(): lax.ppermute(value, 'col', [(c, (c + by * PAIR) % cols) for c in range(co...]
    ppermute x7, waiting for transfers between devices: 2.93 us -> 1.5 us  [flip_x(): return lax.ppermute(value, 'row', [(r, r ^ 1) for r in range(rows_total)])]
    ppermute x3, starting transfers between devices: 2.14 us -> 1.13 us  [to_col(): lax.ppermute(value, 'col', [(c, (c // PAIR + sy) % y_count * PAIR + (c %...]
  transfers between devices with their start and end apart: 28 -> 28, of which waited for: 11 -> 13; matrix products, arithmetic and copies ran while one was open for 4% -> 4% of each run, Pallas kernels for 26% -> 27%
where the time goes in v9:
time: 81.4 us; the launch traced here: 81.1 us
  Pallas kernels  27.8 us (34%)
  starting transfers between devices  27.3 us (34%)
  waiting for transfers between devices  21.6 us (27%)
  other arithmetic  3.51 us (4%)
  between operations  0.83 us (1%)
    ppermute x9, starting transfers between devices, turn_z(): lax.ppermute(value, 'row', [(r, (r + by * PAIR) % rows_total) for r in ra...  13.1 us
    ppermute x9, waiting for transfers between devices, turn_z(): lax.ppermute(value, 'row', [(r, (r + by * PAIR) % rows_total) for r in ra...  8.88 us
    ppermute x7, starting transfers between devices, flip_x(): return lax.ppermute(value, 'row', [(r, r ^ 1) for r in range(rows_total)])  8.38 us
    pallas_call x1, Pallas kernels, on_device(): call(functools.partial(forward_kernel, (cols, shard, span, heads, padded,...  8.2 us
    ppermute x4, waiting for transfers between devices, turn_y(): lax.ppermute(value, 'col', [(c, (c + by * PAIR) % cols) for c in range(co...  7.27 us
    pallas_call x2, Pallas kernels, basis_blocks(): call(functools.partial(basis_kernel, (rows_total, cols, block, cover // T...  7.14 us
    pallas_call x1, Pallas kernels, on_device(): call(functools.partial(grad_kernel, (rows_total, dest_shard, span, heads,...  4.96 us
    pallas_call x1, Pallas kernels, on_device(): call(functools.partial(source_kernel, (cols, shard, span, a_count - 1)),...  4.79 us
  transfers between devices with their start and end apart: 28, of which 13 were waited for; matrix products, arithmetic and copies ran while one was open for 4% of the time, Pallas kernels for 27%

profile of v9, /device:TPU:0, one launch (start us, length us, event | category | flops | bytes accessed | tf_op | source)
XLA Modules:
  0.0 81.1 jit_solution(5925733006755758508)
XLA Ops:
  0.6 3.0 %collective-permute-start = (bf16[256,256]{1,0:T(8,128)(2,1)}, bf16[256,256]{1,0:T(8,128)(2,1)S(1)}, u32[]{:S(2)}, u32[]{:S(2)}) collective-permute-start(bf16[256,256]{1,0:T(8,128)(2,1)} %param.9), channel_id=1, source_target_pairs={{0,4},{4,0},{8,12},{12,8},{16,20},{20,16},{24,28},{28,24},{1,5},{5... | collective-permute-start | bytes 393224 | tf_op jit(solution)/shard_map/ppermute | solution.py:318
  3.6 1.4 %edge_table.1 = f32[4,1024]{1,0:T(4,128)} custom-call(s32[1,1,8]{2,1,0:T(1,128)} %fills.1, s32[1,1,1024]{2,1,0:T(1,128)} %src.1, s32[1,1,1024]{2,1,0:T(1,128)} %dst.1, s32[1,1,1024]{2,1,0:T(1,128)} %rel.1, f32[1,1,1024]{2,1,0:T(1,128)} %norm.1), custom_call_target="tpu_custom_call" | custom-call | tf_op jit(solution)/shard_map/edge_table/pallas_call | solution.py:335
  5.1 2.0 %collective-permute-start.2 = (bf16[256,256]{1,0:T(8,128)(2,1)}, bf16[256,256]{1,0:T(8,128)(2,1)S(1)}, u32[]{:S(2)}, u32[]{:S(2)}) collective-permute-start(bf16[256,256]{1,0:T(8,128)(2,1)} %bitcast.14), channel_id=1, source_target_pairs={{0,4},{4,0},{8,12},{12,8},{16,20},{20,16},{24,28},{28,24},{1,5},{5... | collective-permute-start | bytes 393224 | tf_op jit(solution)/shard_map/ppermute | solution.py:318
  7.1 1.6 %collective-permute-start.3 = (bf16[256,256]{1,0:T(8,128)(2,1)}, bf16[256,256]{1,0:T(8,128)(2,1)S(1)}, u32[]{:S(2)}, u32[]{:S(2)}) collective-permute-start(bf16[256,256]{1,0:T(8,128)(2,1)} %bitcast.15), channel_id=1, source_target_pairs={{0,8},{4,12},{8,16},{12,20},{16,24},{20,28},{24,0},{28,4},{1,9},{5... | collective-permute-start | bytes 393224 | tf_op jit(solution)/shard_map/ppermute | solution.py:324
  8.7 2.2 %collective-permute-start.4 = (bf16[256,256]{1,0:T(8,128)(2,1)}, bf16[256,256]{1,0:T(8,128)(2,1)S(1)}, u32[]{:S(2)}, u32[]{:S(2)}) collective-permute-start(bf16[256,256]{1,0:T(8,128)(2,1)} %bitcast.16), channel_id=1, source_target_pairs={{0,24},{4,28},{8,0},{12,4},{16,8},{20,12},{24,16},{28,20},{1,25},{... | collective-permute-start | bytes 393224 | tf_op jit(solution)/shard_map/ppermute | solution.py:324
  10.9 0.7 pad_maximum_fusion.2.meta
  11.6 0.9 %pad_maximum_fusion.1 = bf16[2,256,256]{2,1,0:T(8,128)(2,1)S(1)} fusion(bf16[1,256,256]{2,1,0:T(8,128)(2,1)S(1)} %bitcast.23, bf16[1,256,256]{2,1,0:T(8,128)(2,1)} %bitcast.22), kind=kLoop, calls=%fused_computation.3 | loop fusion | flops 131072 | bytes 524288 | tf_op jit(solution)/shard_map/stack | solution.py:346
  12.6 2.5 %collective-permute-done.3.refs_0_.refs_1_ = bf16[256,256]{1,0:T(8,128)(2,1)S(1)} collective-permute-done((bf16[256,256]{1,0:T(8,128)(2,1)}, bf16[256,256]{1,0:T(8,128)(2,1)S(1)}, u32[]{:S(2)}, u32[]{:S(2)}) %collective-permute-start.3) | collective-permute-done | bytes 131104 | tf_op jit(solution)/shard_map/ppermute | solution.py:324
  15.1 0.7 collective-permute-done.4.refs_2_.refs_3_
  15.8 1.5 %collective-permute-start.6 = (bf16[2,256,256]{2,1,0:T(8,128)(2,1)S(1)}, bf16[2,256,256]{2,1,0:T(8,128)(2,1)S(1)}, u32[]{:S(2)}, u32[]{:S(2)}) collective-permute-start(bf16[2,256,256]{2,1,0:T(8,128)(2,1)S(1)} %pad_maximum_fusion.1), channel_id=1, source_target_pairs={{0,2},{1,3},{2,0},{3,1},{4,6},{5,7},{6,4},{7,5},{8,10},{9,11},{10,... | collective-permute-start | bytes 786440 | tf_op jit(solution)/shard_map/ppermute | solution.py:329
  17.3 1.2 %collective-permute-start.7 = (bf16[256,256]{1,0:T(8,128)(2,1)}, bf16[256,256]{1,0:T(8,128)(2,1)S(1)}, u32[]{:S(2)}, u32[]{:S(2)}) collective-permute-start(bf16[256,256]{1,0:T(8,128)(2,1)} %bitcast.17), channel_id=1, source_target_pairs={{0,16},{4,20},{8,24},{12,28},{16,0},{20,4},{24,8},{28,12},{1,17},{... | collective-permute-start | bytes 393224 | tf_op jit(solution)/shard_map/ppermute | solution.py:324
  18.5 0.5 collective-permute-start.8
  19.0 1.5 %collective-permute-start.9 = (bf16[256,256]{1,0:T(8,128)(2,1)S(1)}, bf16[256,256]{1,0:T(8,128)(2,1)S(1)}, u32[]{:S(2)}, u32[]{:S(2)}) collective-permute-start(bf16[256,256]{1,0:T(8,128)(2,1)S(1)} %collective-permute-done.4.refs_2_.refs_3_), channel_id=1, source_target_pairs={{0,4},{4,0},{8,12},{12,8},{16,20},{20,16},{24,28},{28,24},{1,5},{5... | collective-permute-start | bytes 393224 | tf_op jit(solution)/shard_map/ppermute | solution.py:318
  20.5 2.2 %collective-permute-done.6 = bf16[2,256,256]{2,1,0:T(8,128)(2,1)S(1)} collective-permute-done((bf16[2,256,256]{2,1,0:T(8,128)(2,1)S(1)}, bf16[2,256,256]{2,1,0:T(8,128)(2,1)S(1)}, u32[]{:S(2)}, u32[]{:S(2)}) %collective-permute-start.6) | collective-permute-done | bytes 262176 | tf_op jit(solution)/shard_map/ppermute | solution.py:329
  22.7 2.3 %collective-permute-done.7.refs_1_.refs_2_ = bf16[256,256]{1,0:T(8,128)(2,1)S(1)} collective-permute-done((bf16[256,256]{1,0:T(8,128)(2,1)}, bf16[256,256]{1,0:T(8,128)(2,1)S(1)}, u32[]{:S(2)}, u32[]{:S(2)}) %collective-permute-start.7) | collective-permute-done | bytes 131104 | tf_op jit(solution)/shard_map/ppermute | solution.py:324
  25.1 0.5 collective-permute-start.5
  25.5 0.1 pad_add_fusion.place
  25.6 0.6 collective-permute-start.10
  26.2 0.8 collective-permute-done.5.meta_core
  27.0 4.8 %source_rows.1.refs_8_.xt_ref = bf16[4,256,1024]{2,1,0:T(8,128)(2,1)S(1)} custom-call(s32[4]{0:T(128)S(1)} %pad_add_fusion.place, f32[2,4,1024]{2,1,0:T(4,128)S(1)} %pad_maximum_fusion.2.meta, f32[2,4,1024]{2,1,0:T(4,128)S(1)} %collective-permute-done.5.meta_core, bf16[2,2,256,256]{3,2,1,0:T(8,128)(2,1)S(1)} %pad_maximum_fusion.feats, ...), custom_call_target="tpu_custom_call" | custom-call | flops 2147483648 | bytes 4194304 | tf_op jit(solution)/shard_map/source_rows/pallas_call | solution.py:363
  31.8 5.0 %edge_grads.1 = (bf16[256,2048]{1,0:T(8,128)(2,1)S(1)}, f32[4,32,1024]{2,1,0:T(8,128)S(1)}) custom-call(s32[4]{0:T(128)S(1)} %pad_add_fusion.place, f32[2,4,1024]{2,1,0:T(4,128)S(1)} %pad_maximum_fusion.2.meta, f32[2,4,1024]{2,1,0:T(4,128)S(1)} %collective-permute-done.5.meta_core, bf16[30,2000]{1,0:T(8,128)(2,1)S(1)} %bitcast.13, ...), custom_call_target="tpu_custom_call" | custom-call | flops 2147483648 | bytes 4194304 | tf_op jit(solution)/shard_map/edge_grads/pallas_call | solution.py:374
  36.8 0.2 collective-permute-start.14
  37.0 8.2 %backed_sums.1 = (bf16[256,256]{1,0:T(8,128)(2,1)S(1)}, bf16[256,256]{1,0:T(8,128)(2,1)S(1)}, bf16[256,256]{1,0:T(8,128)(2,1)S(1)}, bf16[256,256]{1,0:T(8,128)(2...) custom-call(s32[4]{0:T(128)S(1)} %pad_add_fusion.place, f32[2,4,1024]{2,1,0:T(4,128)S(1)} %pad_maximum_fusion.2.meta, ...), custom_call_target="tpu_custom_call" | custom-call | flops 4026531840 | bytes 4194304 | tf_op jit(solution)/shard_map/backed_sums/pallas_call | solution.py:393
  45.2 0.4 collective-permute-start.12
  45.6 1.0 %collective-permute-done.12 = f32[128,256]{1,0:T(8,128)S(1)} collective-permute-done((f32[128,256]{1,0:T(8,128)S(1)}, f32[128,256]{1,0:T(8,128)S(1)}, u32[]{:S(2)}, u32[]{:S(2)}) %collective-permute-start.12) | collective-permute-done | bytes 131104 | tf_op jit(solution)/shard_map/ppermute | solution.py:321
  46.7 0.8 collective-permute-start.13
  47.4 3.6 %basis_terms.2 = (f32[480,256]{1,0:T(8,128)S(1)}, bf16[480,256]{1,0:T(8,128)(2,1)S(1)}) custom-call(s32[4]{0:T(128)S(1)} %pad_add_fusion.place, bf16[256,2048]{1,0:T(8,128)(2,1)S(1)} %get-tuple-element.41.gt_ref, bf16[256,2048]{1,0:T(8,128)(2,1)S(1)} %collective-permute-done.14.gt_core, bf16[4,256,1024]{2,1,0:T(8,128)(2,1)S(1)} %source_rows.1.refs_8_.xt_ref, ...), custom_call_target="tpu_custom_call" | custom-call | flops 2013265920 | bytes 4194304 | tf_op jit(solution)/shard_map/basis_terms/pallas_call | solution.py:413
  51.0 1.5 %collective-permute-done.13 = f32[128,256]{1,0:T(8,128)S(1)} collective-permute-done((f32[128,256]{1,0:T(8,128)S(1)}, f32[128,256]{1,0:T(8,128)S(1)}, u32[]{:S(2)}, u32[]{:S(2)}) %collective-permute-start.13) | collective-permute-done | bytes 131104 | tf_op jit(solution)/shard_map/ppermute | solution.py:318
  52.5 1.6 %collective-permute-start.23 = (bf16[128,256]{1,0:T(8,128)(2,1)S(1)}, bf16[128,256]{1,0:T(8,128)(2,1)S(1)}, u32[]{:S(2)}, u32[]{:S(2)}) collective-permute-start(bf16[128,256]{1,0:T(8,128)(2,1)S(1)} %add_convert_fusion.3), channel_id=1, source_target_pairs={{0,16},{4,20},{8,24},{12,28},{16,0},{20,4},{24,8},{28,12},{1,17},{... | collective-permute-start | bytes 196616 | tf_op jit(solution)/shard_map/ppermute | solution.py:324
  54.1 1.6 %collective-permute-start.24 = (bf16[128,256]{1,0:T(8,128)(2,1)S(1)}, bf16[128,256]{1,0:T(8,128)(2,1)S(1)}, u32[]{:S(2)}, u32[]{:S(2)}) collective-permute-start(bf16[128,256]{1,0:T(8,128)(2,1)S(1)} %add_convert_fusion.3), channel_id=1, source_target_pairs={{0,8},{4,12},{8,16},{12,20},{16,24},{20,28},{24,0},{28,4},{1,9},{5... | collective-permute-start | bytes 196616 | tf_op jit(solution)/shard_map/ppermute | solution.py:324
  55.8 2.2 %collective-permute-start.25 = (bf16[128,256]{1,0:T(8,128)(2,1)S(1)}, bf16[128,256]{1,0:T(8,128)(2,1)S(1)}, u32[]{:S(2)}, u32[]{:S(2)}) collective-permute-start(bf16[128,256]{1,0:T(8,128)(2,1)S(1)} %add_convert_fusion.3), channel_id=1, source_target_pairs={{0,24},{4,28},{8,0},{12,4},{16,8},{20,12},{24,16},{28,20},{1,25},{... | collective-permute-start | bytes 196616 | tf_op jit(solution)/shard_map/ppermute | solution.py:324
  58.0 0.5 collective-permute-start.19
  58.5 3.6 %basis_terms.3 = (f32[480,256]{1,0:T(8,128)S(1)}, bf16[480,256]{1,0:T(8,128)(2,1)S(1)}) custom-call(s32[4]{0:T(128)S(1)} %pad_add_fusion.place, bf16[256,2048]{1,0:T(8,128)(2,1)S(1)} %get-tuple-element.41.gt_ref, bf16[256,2048]{1,0:T(8,128)(2,1)S(1)} %collective-permute-done.14.gt_core, bf16[4,256,1024]{2,1,0:T(8,128)(2,1)S(1)} %source_rows.1.refs_8_.xt_ref, ...), custom_call_target="tpu_custom_call" | custom-call | flops 2013265920 | bytes 4194304 | tf_op jit(solution)/shard_map/basis_terms/pallas_call | solution.py:413
  62.0 1.6 %collective-permute-start.15 = (bf16[480,256]{1,0:T(8,128)(2,1)S(1)}, bf16[480,256]{1,0:T(8,128)(2,1)S(1)}, u32[]{:S(2)}, u32[]{:S(2)}) collective-permute-start(bf16[480,256]{1,0:T(8,128)(2,1)S(1)} %get-tuple-element.52), channel_id=1, source_target_pairs={{0,2},{1,3},{2,0},{3,1},{4,6},{5,7},{6,4},{7,5},{8,10},{9,11},{10,... | collective-permute-start | bytes 737288 | tf_op jit(solution)/shard_map/ppermute | solution.py:329
  63.7 2.2 %collective-permute-done.19 = bf16[480,256]{1,0:T(8,128)(2,1)S(1)} collective-permute-done((bf16[480,256]{1,0:T(8,128)(2,1)S(1)}, bf16[480,256]{1,0:T(8,128)(2,1)S(1)}, u32[]{:S(2)}, u32[]{:S(2)}) %collective-permute-start.19) | collective-permute-done | bytes 245792 | tf_op jit(solution)/shard_map/ppermute | solution.py:329
  66.0 1.5 %collective-permute-start.21 = (bf16[240,256]{1,0:T(8,128)(2,1)S(1)}, bf16[240,256]{1,0:T(8,128)(2,1)S(1)}, u32[]{:S(2)}, u32[]{:S(2)}) collective-permute-start(bf16[240,256]{1,0:T(8,128)(2,1)S(1)} %get-tuple-element.62), channel_id=1, source_target_pairs={{0,16},{4,20},{8,24},{12,28},{16,0},{20,4},{24,8},{28,12},{1,17},{... | collective-permute-start | bytes 368648 | tf_op jit(solution)/shard_map/ppermute | solution.py:324
  67.6 2.9 %collective-permute-done.15 = bf16[480,256]{1,0:T(8,128)(2,1)S(1)} collective-permute-done((bf16[480,256]{1,0:T(8,128)(2,1)S(1)}, bf16[480,256]{1,0:T(8,128)(2,1)S(1)}, u32[]{:S(2)}, u32[]{:S(2)}) %collective-permute-start.15) | collective-permute-done | bytes 245792 | tf_op jit(solution)/shard_map/ppermute | solution.py:329
  70.5 0.1 convert_add_fusion
  70.6 1.0 %collective-permute-start.22 = (bf16[240,256]{1,0:T(8,128)(2,1)S(1)}, bf16[240,256]{1,0:T(8,128)(2,1)S(1)}, u32[]{:S(2)}, u32[]{:S(2)}) collective-permute-start(bf16[240,256]{1,0:T(8,128)(2,1)S(1)} %slice.31), channel_id=1, source_target_pairs={{0,24},{4,28},{8,0},{12,4},{16,8},{20,12},{24,16},{28,20},{1,25},{... | collective-permute-start | bytes 368648 | tf_op jit(solution)/shard_map/ppermute | solution.py:324
  71.7 0.5 collective-permute-start.16
  72.2 1.1 %collective-permute-done.20 = bf16[240,256]{1,0:T(8,128)(2,1)S(1)} collective-permute-done((bf16[240,256]{1,0:T(8,128)(2,1)S(1)}, bf16[240,256]{1,0:T(8,128)(2,1)S(1)}, u32[]{:S(2)}, u32[]{:S(2)}) %collective-permute-start.20) | collective-permute-done | bytes 122912 | tf_op jit(solution)/shard_map/ppermute | solution.py:324
  73.3 0.6 collective-permute-start.18
  73.9 1.9 %collective-permute-done.21 = bf16[240,256]{1,0:T(8,128)(2,1)S(1)} collective-permute-done((bf16[240,256]{1,0:T(8,128)(2,1)S(1)}, bf16[240,256]{1,0:T(8,128)(2,1)S(1)}, u32[]{:S(2)}, u32[]{:S(2)}) %collective-permute-start.21) | collective-permute-done | bytes 122912 | tf_op jit(solution)/shard_map/ppermute | solution.py:324
  75.8 0.4 collective-permute-done.22
  76.2 0.8 fusion.2
  77.0 2.1 %collective-permute-done.18 = bf16[256,256]{1,0:T(8,128)(2,1)S(1)} collective-permute-done((bf16[256,256]{1,0:T(8,128)(2,1)S(1)}, bf16[256,256]{1,0:T(8,128)(2,1)S(1)}, u32[]{:S(2)}, u32[]{:S(2)}) %collective-permute-start.18) | collective-permute-done | bytes 131104 | tf_op jit(solution)/shard_map/ppermute | solution.py:434
  79.1 0.7 add_convert_fusion.1
  79.8 1.3 %coef_rows.1 = f32[30,2000]{1,0:T(8,128)} custom-call(s32[4]{0:T(128)S(1)} %pad_add_fusion.place, f32[128,256]{1,0:T(8,128)S(1)} %convert_add_fusion.1.own, f32[128,256]{1,0:T(8,128)S(1)} %collective-permute-done.27.other), custom_call_target="tpu_custom_call" | custom-call | flops 1048576 | bytes 4194304 | tf_op jit(solution)/shard_map/coef_rows/pallas_call | solution.py:481
  (35 shorter events, 0.4 us)
Async XLA Ops:
  0.6 11.0 %collective-permute-start = (bf16[256,256]{1,0:T(8,128)(2,1)}, bf16[256,256]{1,0:T(8,128)(2,1)S(1)}, u32[]{:S(2)}, u32[]{:S(2)}) collective-permute-start(bf16[256,256]{1,0:T(8,128)(2,1)} %param.9), channel_id=1, source_target_pairs={{0,4},{4,0},{8,12},{12,8},{16,20},{20,16},{24,28},{28,24},{1,5},{5... | collective-permute-start | bytes 393224 | tf_op jit(solution)/shard_map/ppermute | solution.py:318
  5.1 5.9 %collective-permute-start.1 = (f32[4,1024]{1,0:T(4,128)}, f32[4,1024]{1,0:T(4,128)S(1)}, u32[]{:S(2)}, u32[]{:S(2)}) collective-permute-start(f32[4,1024]{1,0:T(4,128)} %edge_table.1), channel_id=1, source_target_pairs={{0,4},{4,0},{8,12},{12,8},{16,20},{20,16},{24,28},{28,24},{1,5},{5... | collective-permute-start | bytes 49160 | tf_op jit(solution)/shard_map/ppermute | solution.py:318
  5.1 7.5 %collective-permute-start.2 = (bf16[256,256]{1,0:T(8,128)(2,1)}, bf16[256,256]{1,0:T(8,128)(2,1)S(1)}, u32[]{:S(2)}, u32[]{:S(2)}) collective-permute-start(bf16[256,256]{1,0:T(8,128)(2,1)} %bitcast.14), channel_id=1, source_target_pairs={{0,4},{4,0},{8,12},{12,8},{16,20},{20,16},{24,28},{28,24},{1,5},{5... | collective-permute-start | bytes 393224 | tf_op jit(solution)/shard_map/ppermute | solution.py:318
  7.1 8.0 %collective-permute-start.3 = (bf16[256,256]{1,0:T(8,128)(2,1)}, bf16[256,256]{1,0:T(8,128)(2,1)S(1)}, u32[]{:S(2)}, u32[]{:S(2)}) collective-permute-start(bf16[256,256]{1,0:T(8,128)(2,1)} %bitcast.15), channel_id=1, source_target_pairs={{0,8},{4,12},{8,16},{12,20},{16,24},{20,28},{24,0},{28,4},{1,9},{5... | collective-permute-start | bytes 393224 | tf_op jit(solution)/shard_map/ppermute | solution.py:324
  8.7 7.1 %collective-permute-start.4 = (bf16[256,256]{1,0:T(8,128)(2,1)}, bf16[256,256]{1,0:T(8,128)(2,1)S(1)}, u32[]{:S(2)}, u32[]{:S(2)}) collective-permute-start(bf16[256,256]{1,0:T(8,128)(2,1)} %bitcast.16), channel_id=1, source_target_pairs={{0,24},{4,28},{8,0},{12,4},{16,8},{20,12},{24,16},{28,20},{1,25},{... | collective-permute-start | bytes 393224 | tf_op jit(solution)/shard_map/ppermute | solution.py:324
  15.8 6.9 %collective-permute-start.6 = (bf16[2,256,256]{2,1,0:T(8,128)(2,1)S(1)}, bf16[2,256,256]{2,1,0:T(8,128)(2,1)S(1)}, u32[]{:S(2)}, u32[]{:S(2)}) collective-permute-start(bf16[2,256,256]{2,1,0:T(8,128)(2,1)S(1)} %pad_maximum_fusion.1), channel_id=1, source_target_pairs={{0,2},{1,3},{2,0},{3,1},{4,6},{5,7},{6,4},{7,5},{8,10},{9,11},{10,... | collective-permute-start | bytes 786440 | tf_op jit(solution)/shard_map/ppermute | solution.py:329
  17.3 7.7 %collective-permute-start.7 = (bf16[256,256]{1,0:T(8,128)(2,1)}, bf16[256,256]{1,0:T(8,128)(2,1)S(1)}, u32[]{:S(2)}, u32[]{:S(2)}) collective-permute-start(bf16[256,256]{1,0:T(8,128)(2,1)} %bitcast.17), channel_id=1, source_target_pairs={{0,16},{4,20},{8,24},{12,28},{16,0},{20,4},{24,8},{28,12},{1,17},{... | collective-permute-start | bytes 393224 | tf_op jit(solution)/shard_map/ppermute | solution.py:324
  18.5 6.5 %collective-permute-start.8 = (bf16[256,256]{1,0:T(8,128)(2,1)S(1)}, bf16[256,256]{1,0:T(8,128)(2,1)S(1)}, u32[]{:S(2)}, u32[]{:S(2)}) collective-permute-start(bf16[256,256]{1,0:T(8,128)(2,1)S(1)} %collective-permute-done.3.refs_0_.refs_1_), channel_id=1, source_target_pairs={{0,4},{4,0},{8,12},{12,8},{16,20},{20,16},{24,28},{28,24},{1,5},{5... | collective-permute-start | bytes 393224 | tf_op jit(solution)/shard_map/ppermute | solution.py:318
  19.0 6.0 %collective-permute-start.9 = (bf16[256,256]{1,0:T(8,128)(2,1)S(1)}, bf16[256,256]{1,0:T(8,128)(2,1)S(1)}, u32[]{:S(2)}, u32[]{:S(2)}) collective-permute-start(bf16[256,256]{1,0:T(8,128)(2,1)S(1)} %collective-permute-done.4.refs_2_.refs_3_), channel_id=1, source_target_pairs={{0,4},{4,0},{8,12},{12,8},{16,20},{20,16},{24,28},{28,24},{1,5},{5... | collective-permute-start | bytes 393224 | tf_op jit(solution)/shard_map/ppermute | solution.py:318
  25.0 2.0 %collective-permute-start.11 = (bf16[2,2,256,256]{3,2,1,0:T(8,128)(2,1)S(1)}, bf16[2,2,256,256]{3,2,1,0:T(8,128)(2,1)S(1)}, u32[]{:S(2)}, u32[]{:S(2)}) collective-permute-start(bf16[2,2,256,256]{3,2,1,0:T(8,128)(2,1)S(1)} %pad_maximum_fusion.feats), channel_id=1, source_target_pairs={{0,1},{1,0},{2,3},{3,2},{4,5},{5,4},{6,7},{7,6},{8,9},{9,8},{10,11... | collective-permute-start | bytes 1572872 | tf_op jit(solution)/shard_map/ppermute | solution.py:321
  25.1 1.9 %collective-permute-start.5 = (f32[2,4,1024]{2,1,0:T(4,128)S(1)}, f32[2,4,1024]{2,1,0:T(4,128)S(1)}, u32[]{:S(2)}, u32[]{:S(2)}) collective-permute-start(f32[2,4,1024]{2,1,0:T(4,128)S(1)} %pad_maximum_fusion.2.meta), channel_id=1, source_target_pairs={{0,1},{1,0},{2,3},{3,2},{4,5},{5,4},{6,7},{7,6},{8,9},{9,8},{10,11... | collective-permute-start | bytes 98312 | tf_op jit(solution)/shard_map/ppermute | solution.py:321
  25.6 6.2 %copy-start.1 = (bf16[2000,30]{0,1:T(8,128)(2,1)S(1)}, bf16[2000,30]{0,1:T(8,128)(2,1)}, u32[]{:S(2)}) copy-start(bf16[2000,30]{0,1:T(8,128)(2,1)} %param.12) | copy-start | bytes 360004
  25.6 6.2 %copy-start.2 = (bf16[1,256,256]{2,1,0:T(8,128)(2,1)S(1)}, bf16[1,256,256]{2,1,0:T(8,128)(2,1)}, u32[]{:S(2)}) copy-start(bf16[1,256,256]{2,1,0:T(8,128)(2,1)} %param.10) | copy-start | bytes 393220
  25.6 6.2 %collective-permute-start.10 = (bf16[256,256]{1,0:T(8,128)(2,1)S(1)}, bf16[256,256]{1,0:T(8,128)(2,1)S(1)}, u32[]{:S(2)}, u32[]{:S(2)}) collective-permute-start(bf16[256,256]{1,0:T(8,128)(2,1)S(1)} %collective-permute-done.7.refs_1_.refs_2_), channel_id=1, source_target_pairs={{0,4},{4,0},{8,12},{12,8},{16,20},{20,16},{24,28},{28,24},{1,5},{5... | collective-permute-start | bytes 393224 | tf_op jit(solution)/shard_map/ppermute | solution.py:318
  31.8 5.2 %copy-start = (bf16[30,256,256]{2,1,0:T(8,128)(2,1)S(1)}, bf16[30,256,256]{2,1,0:T(8,128)(2,1)}, u32[]{:S(2)}) copy-start(bf16[30,256,256]{2,1,0:T(8,128)(2,1)} %bases_ref.1) | copy-start | bytes 11796484
  36.8 10.6 %collective-permute-start.14 = (bf16[256,2048]{1,0:T(8,128)(2,1)S(1)}, bf16[256,2048]{1,0:T(8,128)(2,1)S(1)}, u32[]{:S(2)}, u32[]{:S(2)}) collective-permute-start(bf16[256,2048]{1,0:T(8,128)(2,1)S(1)} %get-tuple-element.41.gt_ref), channel_id=1, source_target_pairs={{0,1},{1,0},{2,3},{3,2},{4,5},{5,4},{6,7},{7,6},{8,9},{9,8},{10,11... | collective-permute-start | bytes 3145736 | tf_op jit(solution)/shard_map/ppermute | solution.py:321
  45.2 1.4 %collective-permute-start.12 = (f32[128,256]{1,0:T(8,128)S(1)}, f32[128,256]{1,0:T(8,128)S(1)}, u32[]{:S(2)}, u32[]{:S(2)}) collective-permute-start(f32[128,256]{1,0:T(8,128)S(1)} %get-tuple-element.46), channel_id=1, source_target_pairs={{0,1},{1,0},{2,3},{3,2},{4,5},{5,4},{6,7},{7,6},{8,9},{9,8},{10,11... | collective-permute-start | bytes 393224 | tf_op jit(solution)/shard_map/ppermute | solution.py:321
  46.7 5.8 %collective-permute-start.13 = (f32[128,256]{1,0:T(8,128)S(1)}, f32[128,256]{1,0:T(8,128)S(1)}, u32[]{:S(2)}, u32[]{:S(2)}) collective-permute-start(f32[128,256]{1,0:T(8,128)S(1)} %add.53), channel_id=1, source_target_pairs={{0,4},{4,0},{8,12},{12,8},{16,20},{20,16},{24,28},{28,24},{1,5},{5... | collective-permute-start | bytes 393224 | tf_op jit(solution)/shard_map/ppermute | solution.py:318
  52.5 11.1 %collective-permute-start.23 = (bf16[128,256]{1,0:T(8,128)(2,1)S(1)}, bf16[128,256]{1,0:T(8,128)(2,1)S(1)}, u32[]{:S(2)}, u32[]{:S(2)}) collective-permute-start(bf16[128,256]{1,0:T(8,128)(2,1)S(1)} %add_convert_fusion.3), channel_id=1, source_target_pairs={{0,16},{4,20},{8,24},{12,28},{16,0},{20,4},{24,8},{28,12},{1,17},{... | collective-permute-start | bytes 196616 | tf_op jit(solution)/shard_map/ppermute | solution.py:324
  54.1 9.5 %collective-permute-start.24 = (bf16[128,256]{1,0:T(8,128)(2,1)S(1)}, bf16[128,256]{1,0:T(8,128)(2,1)S(1)}, u32[]{:S(2)}, u32[]{:S(2)}) collective-permute-start(bf16[128,256]{1,0:T(8,128)(2,1)S(1)} %add_convert_fusion.3), channel_id=1, source_target_pairs={{0,8},{4,12},{8,16},{12,20},{16,24},{20,28},{24,0},{28,4},{1,9},{5... | collective-permute-start | bytes 196616 | tf_op jit(solution)/shard_map/ppermute | solution.py:324
  55.8 7.9 %collective-permute-start.25 = (bf16[128,256]{1,0:T(8,128)(2,1)S(1)}, bf16[128,256]{1,0:T(8,128)(2,1)S(1)}, u32[]{:S(2)}, u32[]{:S(2)}) collective-permute-start(bf16[128,256]{1,0:T(8,128)(2,1)S(1)} %add_convert_fusion.3), channel_id=1, source_target_pairs={{0,24},{4,28},{8,0},{12,4},{16,8},{20,12},{24,16},{28,20},{1,25},{... | collective-permute-start | bytes 196616 | tf_op jit(solution)/shard_map/ppermute | solution.py:324
  58.0 7.9 %collective-permute-start.19 = (bf16[480,256]{1,0:T(8,128)(2,1)S(1)}, bf16[480,256]{1,0:T(8,128)(2,1)S(1)}, u32[]{:S(2)}, u32[]{:S(2)}) collective-permute-start(bf16[480,256]{1,0:T(8,128)(2,1)S(1)} %get-tuple-element.59), channel_id=1, source_target_pairs={{0,2},{1,3},{2,0},{3,1},{4,6},{5,7},{6,4},{7,5},{8,10},{9,11},{10,... | collective-permute-start | bytes 737288 | tf_op jit(solution)/shard_map/ppermute | solution.py:329
  62.0 8.5 %collective-permute-start.15 = (bf16[480,256]{1,0:T(8,128)(2,1)S(1)}, bf16[480,256]{1,0:T(8,128)(2,1)S(1)}, u32[]{:S(2)}, u32[]{:S(2)}) collective-permute-start(bf16[480,256]{1,0:T(8,128)(2,1)S(1)} %get-tuple-element.52), channel_id=1, source_target_pairs={{0,2},{1,3},{2,0},{3,1},{4,6},{5,7},{6,4},{7,5},{8,10},{9,11},{10,... | collective-permute-start | bytes 737288 | tf_op jit(solution)/shard_map/ppermute | solution.py:329
  65.9 6.3 %collective-permute-start.26 = (bf16[128,256]{1,0:T(8,128)(2,1)S(1)}, bf16[128,256]{1,0:T(8,128)(2,1)S(1)}, u32[]{:S(2)}, u32[]{:S(2)}) collective-permute-start(bf16[128,256]{1,0:T(8,128)(2,1)S(1)} %add_convert_fusion.2), channel_id=1, source_target_pairs={{0,2},{1,3},{2,0},{3,1},{4,6},{5,7},{6,4},{7,5},{8,10},{9,11},{10,... | collective-permute-start | bytes 196616 | tf_op jit(solution)/shard_map/ppermute | solution.py:329
  66.0 7.3 %collective-permute-start.20 = (bf16[240,256]{1,0:T(8,128)(2,1)S(1)}, bf16[240,256]{1,0:T(8,128)(2,1)S(1)}, u32[]{:S(2)}, u32[]{:S(2)}) collective-permute-start(bf16[240,256]{1,0:T(8,128)(2,1)S(1)} %get-tuple-element.61), channel_id=1, source_target_pairs={{0,8},{4,12},{8,16},{12,20},{16,24},{20,28},{24,0},{28,4},{1,9},{5... | collective-permute-start | bytes 368648 | tf_op jit(solution)/shard_map/ppermute | solution.py:324
  66.0 9.7 %collective-permute-start.21 = (bf16[240,256]{1,0:T(8,128)(2,1)S(1)}, bf16[240,256]{1,0:T(8,128)(2,1)S(1)}, u32[]{:S(2)}, u32[]{:S(2)}) collective-permute-start(bf16[240,256]{1,0:T(8,128)(2,1)S(1)} %get-tuple-element.62), channel_id=1, source_target_pairs={{0,16},{4,20},{8,24},{12,28},{16,0},{20,4},{24,8},{28,12},{1,17},{... | collective-permute-start | bytes 368648 | tf_op jit(solution)/shard_map/ppermute | solution.py:324
  70.6 5.6 %collective-permute-start.22 = (bf16[240,256]{1,0:T(8,128)(2,1)S(1)}, bf16[240,256]{1,0:T(8,128)(2,1)S(1)}, u32[]{:S(2)}, u32[]{:S(2)}) collective-permute-start(bf16[240,256]{1,0:T(8,128)(2,1)S(1)} %slice.31), channel_id=1, source_target_pairs={{0,24},{4,28},{8,0},{12,4},{16,8},{20,12},{24,16},{28,20},{1,25},{... | collective-permute-start | bytes 368648 | tf_op jit(solution)/shard_map/ppermute | solution.py:324
  71.7 5.3 %collective-permute-start.16 = (bf16[256,256]{1,0:T(8,128)(2,1)S(1)}, bf16[256,256]{1,0:T(8,128)(2,1)S(1)}, u32[]{:S(2)}, u32[]{:S(2)}) collective-permute-start(bf16[256,256]{1,0:T(8,128)(2,1)S(1)} %get-tuple-element.53), channel_id=1, source_target_pairs={{0,2},{1,3},{2,0},{3,1},{4,6},{5,7},{6,4},{7,5},{8,10},{9,11},{10,... | collective-permute-start | bytes 393224 | tf_op jit(solution)/shard_map/ppermute | solution.py:434
  72.2 4.8 %collective-permute-start.17 = (bf16[256,256]{1,0:T(8,128)(2,1)S(1)}, bf16[256,256]{1,0:T(8,128)(2,1)S(1)}, u32[]{:S(2)}, u32[]{:S(2)}) collective-permute-start(bf16[256,256]{1,0:T(8,128)(2,1)S(1)} %get-tuple-element.55), channel_id=1, source_target_pairs={{0,1},{1,0},{2,3},{3,2},{4,5},{5,4},{6,7},{7,6},{8,9},{9,8},{10,11... | collective-permute-start | bytes 393224 | tf_op jit(solution)/shard_map/ppermute | solution.py:434
  73.3 5.8 %collective-permute-start.18 = (bf16[256,256]{1,0:T(8,128)(2,1)S(1)}, bf16[256,256]{1,0:T(8,128)(2,1)S(1)}, u32[]{:S(2)}, u32[]{:S(2)}) collective-permute-start(bf16[256,256]{1,0:T(8,128)(2,1)S(1)} %get-tuple-element.57), channel_id=1, source_target_pairs={{0,3},{1,2},{2,1},{3,0},{4,7},{5,6},{6,5},{7,4},{8,11},{9,10},{10,... | collective-permute-start | bytes 393224 | tf_op jit(solution)/shard_map/ppermute | solution.py:434
  75.8 4.0 %collective-permute-start.27 = (f32[128,256]{1,0:T(8,128)S(1)}, f32[128,256]{1,0:T(8,128)S(1)}, u32[]{:S(2)}, u32[]{:S(2)}) collective-permute-start(f32[128,256]{1,0:T(8,128)S(1)} %convert_add_fusion.1.own), channel_id=1, source_target_pairs={{0,1},{1,0},{2,3},{3,2},{4,5},{5,4},{6,7},{7,6},{8,9},{9,8},{10,11... | collective-permute-start | bytes 393224 | tf_op jit(solution)/shard_map/ppermute | solution.py:321

commit v10 on v9

--- a/solution.py
+++ b/solution.py
@@ -180,8 +180,8 @@
     sizes, place, meta, gt_ref, xt_ref, ct_ref, bases_ref, *refs
 ):
     cols, shard, span, heads, padded, group = sizes
-    outs, halves = refs[:cols], refs[cols : cols + PAIR]
-    total, inner, wide, coef_sum = refs[cols + PAIR :]
+    outs, halves = refs[:PAIR], refs[PAIR : 2 * PAIR]
+    total, inner, wide, coef_sum = refs[2 * PAIR :]
     count = cols // PAIR
     y, core = place[2], place[3]
     edges = meta.shape[-1]
@@ -213,7 +213,8 @@
     values = total[...].astype(BF16)
     for at in range(cols):
         hot = one_hot(jnp.where(slot == at, local, -1), shard)
-        outs[at][...] = dot_t(hot, values).astype(BF16)
+        row = at % count * shard
+        outs[at // count][row : row + shard, :] = dot_t(hot, values).astype(BF16)
     high, low = split_index(meta[0, 2:3, :].astype(I32), LANES)
     for head in range(heads):
         wide[head * padded : (head + 1) * padded, :] = jnp.where(
@@ -392,7 +393,7 @@
     share_rows = heads * padded // PAIR // 2
     packed = call(
         functools.partial(forward_kernel, (cols, shard, span, heads, padded, group)),
-        [jax.ShapeDtypeStruct((shard, width), BF16)] * cols
+        [jax.ShapeDtypeStruct((y_count * shard, width), BF16)] * PAIR
         + [jax.ShapeDtypeStruct((share_rows, width), F32)] * PAIR,
         5,
         [
@@ -430,17 +431,8 @@
             "basis_terms",
         )(place, gt, gt_core, xt, ct)
 
-    def to_col(value, far, sy):
-        return lax.ppermute(
-            value,
-            "col",
-            [(c, (c // PAIR + sy) % y_count * PAIR + (c % PAIR ^ far)) for c in range(cols)],
-        )
-
     def after(value, other):
         return lax.optimization_barrier((value, other))[0]
-
-    others = [(far, sy) for far in range(PAIR) for sy in range(y_count) if far or sy]
 
     order = tuple(range(1, a_count)) + (0,)
     half = (a_count + 1) // 2
@@ -457,25 +449,18 @@
             piece = value[at * cover : (at + 1) * cover]
             sums[sz] = turn_z(piece.astype(BF16), sz) if sz else piece
 
-    coef_part = packed[cols] + flip_core(packed[cols + 1])
+    coef_part = packed[PAIR] + flip_core(packed[PAIR + 1])
     add_blocks(after(place, coef_part), order[:half])
     coef_part = coef_part + after(flip_x(coef_part), marks[0])
     low = coef_part.astype(BF16)
     coef_part = tree_sum([low.astype(F32)] + [turn_z(low, s).astype(F32) for s in range(1, a_count)])
     add_blocks(after(after(place, low), marks[0]), order[half:])
-    joined = packed[0].astype(F32)
-    for far, sy in others:
-        value = after(packed[far * y_count + sy], landed[-1])
-        joined = joined + to_col(value, far, sy).astype(F32)
-    basis_sum = sums[0]
-    for sz in range(1, a_count):
-        basis_sum = basis_sum + sums[sz].astype(F32)
-    if cover != block:
-        owner = i * cols + j
-        basis_sum = lax.dynamic_slice_in_dim(basis_sum, owner * block % TILE, block, axis=0)
-    basis_grad = basis_sum / cols
-
-    node_grad = joined.astype(BF16)
+    joined = packed[0].astype(F32) + after(flip_core(packed[1]), marks[-1]).astype(F32)
+    node_sum = joined[:shard]
+    for sy in range(1, y_count):
+        value = joined[sy * shard : (sy + 1) * shard].astype(BF16)
+        node_sum = node_sum + turn_y(after(value, landed[-1]), sy).astype(F32)
+    node_grad = node_sum.astype(BF16)
     low = after(coef_part.astype(BF16), landed[0])
     coef_part = tree_sum([low.astype(F32)] + [turn_y(low, s).astype(F32) for s in range(1, y_count)])
     coef_grad = call(
@@ -486,6 +471,13 @@
         1 << 20,
         "coef_rows",
     )(place, coef_part, flip_core(coef_part))
+    basis_sum = sums[0]
+    for sz in range(1, a_count):
+        basis_sum = basis_sum + after(sums[sz], coef_grad).astype(F32)
+    if cover != block:
+        owner = i * cols + j
+        basis_sum = lax.dynamic_slice_in_dim(basis_sum, owner * block % TILE, block, axis=0)
+    basis_grad = basis_sum / cols
     return (node_grad, basis_grad, coef_grad.T)
 
 

time: 81.4 us -> 79.6 us (0.978)
  waiting for transfers between devices: 21.6 us -> 20.2 us
    ppermute x4 -> x5, waiting for transfers between devices: 7.27 us -> 11.5 us  [turn_y(): lax.ppermute(value, 'col', [(c, (c + by * PAIR) % cols) for c in range(co...]
    ppermute x9, waiting for transfers between devices: 8.88 us -> 5.52 us  [turn_z(): lax.ppermute(value, 'row', [(r, (r + by * PAIR) % rows_total) for r in ra...]
    ppermute x3 -> x0, waiting for transfers between devices: 2.12 us -> none  [to_col(): lax.ppermute(value, 'col', [(c, (c // PAIR + sy) % y_count * PAIR + (c %...]
    ppermute x3 -> x0, starting transfers between devices: 1.13 us -> none  [to_col(): lax.ppermute(value, 'col', [(c, (c // PAIR + sy) % y_count * PAIR + (c %...]
    ppermute x4 -> x5, starting transfers between devices: 3.61 us -> 4.18 us  [turn_y(): lax.ppermute(value, 'col', [(c, (c + by * PAIR) % cols) for c in range(co...]
    ppermute x5 -> x6, waiting for transfers between devices: 1.8 us -> 1.66 us  [flip_core(): return lax.ppermute(value, 'col', [(c, c ^ 1) for c in range(cols)])]
  transfers between devices with their start and end apart: 28 -> 27, of which waited for: 13 -> 10; matrix products, arithmetic and copies ran while one was open for 4% -> 4% of each run, Pallas kernels for 27% -> 29%
where the time goes in v10:
time: 79.6 us; the launch traced here: 79.3 us
  Pallas kernels  27.8 us (35%)
  starting transfers between devices  26.9 us (34%)
  waiting for transfers between devices  20.2 us (25%)
  other arithmetic  3.49 us (4%)
  between operations  0.88 us (1%)
    ppermute x9, starting transfers between devices, turn_z(): lax.ppermute(value, 'row', [(r, (r + by * PAIR) % rows_total) for r in ra...  13 us
    ppermute x5, waiting for transfers between devices, turn_y(): lax.ppermute(value, 'col', [(c, (c + by * PAIR) % cols) for c in range(co...  11.5 us
    ppermute x7, starting transfers between devices, flip_x(): return lax.ppermute(value, 'row', [(r, r ^ 1) for r in range(rows_total)])  8.38 us
    pallas_call x1, Pallas kernels, on_device(): call(functools.partial(forward_kernel, (cols, shard, span, heads, padded,...  8.2 us
    pallas_call x2, Pallas kernels, basis_blocks(): call(functools.partial(basis_kernel, (rows_total, cols, block, cover // T...  7.14 us
    ppermute x9, waiting for transfers between devices, turn_z(): lax.ppermute(value, 'row', [(r, (r + by * PAIR) % rows_total) for r in ra...  5.52 us
    pallas_call x1, Pallas kernels, on_device(): call(functools.partial(grad_kernel, (rows_total, dest_shard, span, heads,...  4.96 us
    pallas_call x1, Pallas kernels, on_device(): call(functools.partial(source_kernel, (cols, shard, span, a_count - 1)),...  4.79 us
  transfers between devices with their start and end apart: 27, of which 10 were waited for; matrix products, arithmetic and copies ran while one was open for 4% of the time, Pallas kernels for 29%

profile of v10, /device:TPU:0, one launch (start us, length us, event | category | flops | bytes accessed | tf_op | source)
XLA Modules:
  0.0 79.3 jit_solution(10249105829015755585)
XLA Ops:
  0.6 3.0 %collective-permute-start = (bf16[256,256]{1,0:T(8,128)(2,1)}, bf16[256,256]{1,0:T(8,128)(2,1)S(1)}, u32[]{:S(2)}, u32[]{:S(2)}) collective-permute-start(bf16[256,256]{1,0:T(8,128)(2,1)} %param.9), channel_id=1, source_target_pairs={{0,4},{4,0},{8,12},{12,8},{16,20},{20,16},{24,28},{28,24},{1,5},{5... | collective-permute-start | bytes 393224 | tf_op jit(solution)/shard_map/ppermute | solution.py:319
  3.6 1.4 %edge_table.1 = f32[4,1024]{1,0:T(4,128)} custom-call(s32[1,1,8]{2,1,0:T(1,128)} %fills.1, s32[1,1,1024]{2,1,0:T(1,128)} %src.1, s32[1,1,1024]{2,1,0:T(1,128)} %dst.1, s32[1,1,1024]{2,1,0:T(1,128)} %rel.1, f32[1,1,1024]{2,1,0:T(1,128)} %norm.1), custom_call_target="tpu_custom_call" | custom-call | tf_op jit(solution)/shard_map/edge_table/pallas_call | solution.py:336
  5.1 2.0 %collective-permute-start.2 = (bf16[256,256]{1,0:T(8,128)(2,1)}, bf16[256,256]{1,0:T(8,128)(2,1)S(1)}, u32[]{:S(2)}, u32[]{:S(2)}) collective-permute-start(bf16[256,256]{1,0:T(8,128)(2,1)} %bitcast.14), channel_id=1, source_target_pairs={{0,4},{4,0},{8,12},{12,8},{16,20},{20,16},{24,28},{28,24},{1,5},{5... | collective-permute-start | bytes 393224 | tf_op jit(solution)/shard_map/ppermute | solution.py:319
  7.1 1.6 %collective-permute-start.3 = (bf16[256,256]{1,0:T(8,128)(2,1)}, bf16[256,256]{1,0:T(8,128)(2,1)S(1)}, u32[]{:S(2)}, u32[]{:S(2)}) collective-permute-start(bf16[256,256]{1,0:T(8,128)(2,1)} %bitcast.15), channel_id=1, source_target_pairs={{0,8},{4,12},{8,16},{12,20},{16,24},{20,28},{24,0},{28,4},{1,9},{5... | collective-permute-start | bytes 393224 | tf_op jit(solution)/shard_map/ppermute | solution.py:325
  8.7 2.2 %collective-permute-start.4 = (bf16[256,256]{1,0:T(8,128)(2,1)}, bf16[256,256]{1,0:T(8,128)(2,1)S(1)}, u32[]{:S(2)}, u32[]{:S(2)}) collective-permute-start(bf16[256,256]{1,0:T(8,128)(2,1)} %bitcast.16), channel_id=1, source_target_pairs={{0,24},{4,28},{8,0},{12,4},{16,8},{20,12},{24,16},{28,20},{1,25},{... | collective-permute-start | bytes 393224 | tf_op jit(solution)/shard_map/ppermute | solution.py:325
  10.9 0.7 pad_maximum_fusion.2.meta
  11.6 0.9 %pad_maximum_fusion.1 = bf16[2,256,256]{2,1,0:T(8,128)(2,1)S(1)} fusion(bf16[1,256,256]{2,1,0:T(8,128)(2,1)S(1)} %bitcast.23, bf16[1,256,256]{2,1,0:T(8,128)(2,1)} %bitcast.22), kind=kLoop, calls=%fused_computation.7 | loop fusion | flops 131072 | bytes 524288 | tf_op jit(solution)/shard_map/stack | solution.py:347
  12.6 2.5 %collective-permute-done.3.refs_0_.refs_1_ = bf16[256,256]{1,0:T(8,128)(2,1)S(1)} collective-permute-done((bf16[256,256]{1,0:T(8,128)(2,1)}, bf16[256,256]{1,0:T(8,128)(2,1)S(1)}, u32[]{:S(2)}, u32[]{:S(2)}) %collective-permute-start.3) | collective-permute-done | bytes 131104 | tf_op jit(solution)/shard_map/ppermute | solution.py:325
  15.1 0.7 collective-permute-done.4.refs_2_.refs_3_
  15.8 1.5 %collective-permute-start.6 = (bf16[2,256,256]{2,1,0:T(8,128)(2,1)S(1)}, bf16[2,256,256]{2,1,0:T(8,128)(2,1)S(1)}, u32[]{:S(2)}, u32[]{:S(2)}) collective-permute-start(bf16[2,256,256]{2,1,0:T(8,128)(2,1)S(1)} %pad_maximum_fusion.1), channel_id=1, source_target_pairs={{0,2},{1,3},{2,0},{3,1},{4,6},{5,7},{6,4},{7,5},{8,10},{9,11},{10,... | collective-permute-start | bytes 786440 | tf_op jit(solution)/shard_map/ppermute | solution.py:330
  17.3 1.2 %collective-permute-start.7 = (bf16[256,256]{1,0:T(8,128)(2,1)}, bf16[256,256]{1,0:T(8,128)(2,1)S(1)}, u32[]{:S(2)}, u32[]{:S(2)}) collective-permute-start(bf16[256,256]{1,0:T(8,128)(2,1)} %bitcast.17), channel_id=1, source_target_pairs={{0,16},{4,20},{8,24},{12,28},{16,0},{20,4},{24,8},{28,12},{1,17},{... | collective-permute-start | bytes 393224 | tf_op jit(solution)/shard_map/ppermute | solution.py:325
  18.5 0.5 collective-permute-start.8
  19.0 1.5 %collective-permute-start.9 = (bf16[256,256]{1,0:T(8,128)(2,1)S(1)}, bf16[256,256]{1,0:T(8,128)(2,1)S(1)}, u32[]{:S(2)}, u32[]{:S(2)}) collective-permute-start(bf16[256,256]{1,0:T(8,128)(2,1)S(1)} %collective-permute-done.4.refs_2_.refs_3_), channel_id=1, source_target_pairs={{0,4},{4,0},{8,12},{12,8},{16,20},{20,16},{24,28},{28,24},{1,5},{5... | collective-permute-start | bytes 393224 | tf_op jit(solution)/shard_map/ppermute | solution.py:319
  20.5 2.2 %collective-permute-done.6 = bf16[2,256,256]{2,1,0:T(8,128)(2,1)S(1)} collective-permute-done((bf16[2,256,256]{2,1,0:T(8,128)(2,1)S(1)}, bf16[2,256,256]{2,1,0:T(8,128)(2,1)S(1)}, u32[]{:S(2)}, u32[]{:S(2)}) %collective-permute-start.6) | collective-permute-done | bytes 262176 | tf_op jit(solution)/shard_map/ppermute | solution.py:330
  22.7 2.3 %collective-permute-done.7.refs_1_.refs_2_ = bf16[256,256]{1,0:T(8,128)(2,1)S(1)} collective-permute-done((bf16[256,256]{1,0:T(8,128)(2,1)}, bf16[256,256]{1,0:T(8,128)(2,1)S(1)}, u32[]{:S(2)}, u32[]{:S(2)}) %collective-permute-start.7) | collective-permute-done | bytes 131104 | tf_op jit(solution)/shard_map/ppermute | solution.py:325
  25.1 0.5 collective-permute-start.5
  25.5 0.1 pad_add_fusion.place
  25.6 0.6 collective-permute-start.10
  26.2 0.8 %collective-permute-done.5.meta_core = f32[2,4,1024]{2,1,0:T(4,128)S(1)} collective-permute-done((f32[2,4,1024]{2,1,0:T(4,128)S(1)}, f32[2,4,1024]{2,1,0:T(4,128)S(1)}, u32[]{:S(2)}, u32[]{:S(2)}) %collective-permute-start.5) | collective-permute-done | bytes 32800 | tf_op jit(solution)/shard_map/ppermute | solution.py:322
  27.0 4.8 %source_rows.1.refs_8_.xt_ref = bf16[4,256,1024]{2,1,0:T(8,128)(2,1)S(1)} custom-call(s32[4]{0:T(128)S(1)} %pad_add_fusion.place, f32[2,4,1024]{2,1,0:T(4,128)S(1)} %pad_maximum_fusion.2.meta, f32[2,4,1024]{2,1,0:T(4,128)S(1)} %collective-permute-done.5.meta_core, bf16[2,2,256,256]{3,2,1,0:T(8,128)(2,1)S(1)} %pad_maximum_fusion.feats, ...), custom_call_target="tpu_custom_call" | custom-call | flops 2147483648 | bytes 4194304 | tf_op jit(solution)/shard_map/source_rows/pallas_call | solution.py:364
  31.8 5.0 %edge_grads.1 = (bf16[256,2048]{1,0:T(8,128)(2,1)S(1)}, f32[4,32,1024]{2,1,0:T(8,128)S(1)}) custom-call(s32[4]{0:T(128)S(1)} %pad_add_fusion.place, f32[2,4,1024]{2,1,0:T(4,128)S(1)} %pad_maximum_fusion.2.meta, f32[2,4,1024]{2,1,0:T(4,128)S(1)} %collective-permute-done.5.meta_core, bf16[30,2000]{1,0:T(8,128)(2,1)S(1)} %bitcast.13, ...), custom_call_target="tpu_custom_call" | custom-call | flops 2147483648 | bytes 4194304 | tf_op jit(solution)/shard_map/edge_grads/pallas_call | solution.py:375
  36.8 0.2 collective-permute-start.15
  37.0 8.2 %backed_sums.1 = (bf16[512,256]{1,0:T(8,128)(2,1)S(1)}, bf16[512,256]{1,0:T(8,128)(2,1)S(1)}, f32[128,256]{1,0:T(8,128)S(1)}, f32[128,256]{1,0:T(8,128)S(1)}) custom-call(s32[4]{0:T(128)S(1)} %pad_add_fusion.place, f32[2,4,1024]{2,1,0:T(4,128)S(1)} %pad_maximum_fusion.2.meta, bf16[256,2048]{1,0:T(8,128)(2,1)S(1)} %get-tuple-element.41.gt_ref, ...), custom_call_target="tpu_custom_call" | custom-call | flops 4026531840 | bytes 4194304 | tf_op jit(solution)/shard_map/backed_sums/pallas_call | solution.py:394
  45.2 0.4 collective-permute-start.13
  45.6 0.1 collective-permute-start.12
  45.8 0.8 %collective-permute-done.13 = f32[128,256]{1,0:T(8,128)S(1)} collective-permute-done((f32[128,256]{1,0:T(8,128)S(1)}, f32[128,256]{1,0:T(8,128)S(1)}, u32[]{:S(2)}, u32[]{:S(2)}) %collective-permute-start.13) | collective-permute-done | bytes 131104 | tf_op jit(solution)/shard_map/ppermute | solution.py:322
  46.7 0.8 collective-permute-start.14
  47.4 3.6 %basis_terms.2 = (f32[480,256]{1,0:T(8,128)S(1)}, bf16[480,256]{1,0:T(8,128)(2,1)S(1)}) custom-call(s32[4]{0:T(128)S(1)} %pad_add_fusion.place, bf16[256,2048]{1,0:T(8,128)(2,1)S(1)} %get-tuple-element.41.gt_ref, bf16[256,2048]{1,0:T(8,128)(2,1)S(1)} %collective-permute-done.15.gt_core, bf16[4,256,1024]{2,1,0:T(8,128)(2,1)S(1)} %source_rows.1.refs_8_.xt_ref, ...), custom_call_target="tpu_custom_call" | custom-call | flops 2013265920 | bytes 4194304 | tf_op jit(solution)/shard_map/basis_terms/pallas_call | solution.py:414
  51.0 1.5 %collective-permute-done.14 = f32[128,256]{1,0:T(8,128)S(1)} collective-permute-done((f32[128,256]{1,0:T(8,128)S(1)}, f32[128,256]{1,0:T(8,128)S(1)}, u32[]{:S(2)}, u32[]{:S(2)}) %collective-permute-start.14) | collective-permute-done | bytes 131104 | tf_op jit(solution)/shard_map/ppermute | solution.py:319
  52.5 1.6 %collective-permute-start.20 = (bf16[128,256]{1,0:T(8,128)(2,1)S(1)}, bf16[128,256]{1,0:T(8,128)(2,1)S(1)}, u32[]{:S(2)}, u32[]{:S(2)}) collective-permute-start(bf16[128,256]{1,0:T(8,128)(2,1)S(1)} %add_convert_fusion.2), channel_id=1, source_target_pairs={{0,16},{4,20},{8,24},{12,28},{16,0},{20,4},{24,8},{28,12},{1,17},{... | collective-permute-start | bytes 196616 | tf_op jit(solution)/shard_map/ppermute | solution.py:325
  54.2 1.6 %collective-permute-start.21 = (bf16[128,256]{1,0:T(8,128)(2,1)S(1)}, bf16[128,256]{1,0:T(8,128)(2,1)S(1)}, u32[]{:S(2)}, u32[]{:S(2)}) collective-permute-start(bf16[128,256]{1,0:T(8,128)(2,1)S(1)} %add_convert_fusion.2), channel_id=1, source_target_pairs={{0,8},{4,12},{8,16},{12,20},{16,24},{20,28},{24,0},{28,4},{1,9},{5... | collective-permute-start | bytes 196616 | tf_op jit(solution)/shard_map/ppermute | solution.py:325
  55.8 2.2 %collective-permute-start.22 = (bf16[128,256]{1,0:T(8,128)(2,1)S(1)}, bf16[128,256]{1,0:T(8,128)(2,1)S(1)}, u32[]{:S(2)}, u32[]{:S(2)}) collective-permute-start(bf16[128,256]{1,0:T(8,128)(2,1)S(1)} %add_convert_fusion.2), channel_id=1, source_target_pairs={{0,24},{4,28},{8,0},{12,4},{16,8},{20,12},{24,16},{28,20},{1,25},{... | collective-permute-start | bytes 196616 | tf_op jit(solution)/shard_map/ppermute | solution.py:325
  58.0 0.5 collective-permute-start.18
  58.5 3.6 %basis_terms.3 = (f32[480,256]{1,0:T(8,128)S(1)}, bf16[480,256]{1,0:T(8,128)(2,1)S(1)}) custom-call(s32[4]{0:T(128)S(1)} %pad_add_fusion.place, bf16[256,2048]{1,0:T(8,128)(2,1)S(1)} %get-tuple-element.41.gt_ref, bf16[256,2048]{1,0:T(8,128)(2,1)S(1)} %collective-permute-done.15.gt_core, bf16[4,256,1024]{2,1,0:T(8,128)(2,1)S(1)} %source_rows.1.refs_8_.xt_ref, ...), custom_call_target="tpu_custom_call" | custom-call | flops 2013265920 | bytes 4194304 | tf_op jit(solution)/shard_map/basis_terms/pallas_call | solution.py:414
  62.1 1.6 %collective-permute-start.16 = (bf16[480,256]{1,0:T(8,128)(2,1)S(1)}, bf16[480,256]{1,0:T(8,128)(2,1)S(1)}, u32[]{:S(2)}, u32[]{:S(2)}) collective-permute-start(bf16[480,256]{1,0:T(8,128)(2,1)S(1)} %get-tuple-element.54), channel_id=1, source_target_pairs={{0,2},{1,3},{2,0},{3,1},{4,6},{5,7},{6,4},{7,5},{8,10},{9,11},{10,... | collective-permute-start | bytes 737288 | tf_op jit(solution)/shard_map/ppermute | solution.py:330
  63.7 0.1 convert_add_fusion
  63.8 2.0 %collective-permute-done.18 = bf16[480,256]{1,0:T(8,128)(2,1)S(1)} collective-permute-done((bf16[480,256]{1,0:T(8,128)(2,1)S(1)}, bf16[480,256]{1,0:T(8,128)(2,1)S(1)}, u32[]{:S(2)}, u32[]{:S(2)}) %collective-permute-start.18) | collective-permute-done | bytes 245792 | tf_op jit(solution)/shard_map/ppermute | solution.py:330
  66.0 0.1 collective-permute-start.19
  66.0 0.1 collective-permute-start.23
  66.1 1.5 %collective-permute-start.25 = (bf16[240,256]{1,0:T(8,128)(2,1)S(1)}, bf16[240,256]{1,0:T(8,128)(2,1)S(1)}, u32[]{:S(2)}, u32[]{:S(2)}) collective-permute-start(bf16[240,256]{1,0:T(8,128)(2,1)S(1)} %get-tuple-element.62), channel_id=1, source_target_pairs={{0,16},{4,20},{8,24},{12,28},{16,0},{20,4},{24,8},{28,12},{1,17},{... | collective-permute-start | bytes 368648 | tf_op jit(solution)/shard_map/ppermute | solution.py:325
  67.6 2.9 %collective-permute-done.16 = bf16[480,256]{1,0:T(8,128)(2,1)S(1)} collective-permute-done((bf16[480,256]{1,0:T(8,128)(2,1)S(1)}, bf16[480,256]{1,0:T(8,128)(2,1)S(1)}, u32[]{:S(2)}, u32[]{:S(2)}) %collective-permute-start.16) | collective-permute-done | bytes 245792 | tf_op jit(solution)/shard_map/ppermute | solution.py:330
  70.6 1.0 %collective-permute-start.26 = (bf16[240,256]{1,0:T(8,128)(2,1)S(1)}, bf16[240,256]{1,0:T(8,128)(2,1)S(1)}, u32[]{:S(2)}, u32[]{:S(2)}) collective-permute-start(bf16[240,256]{1,0:T(8,128)(2,1)S(1)} %slice.47), channel_id=1, source_target_pairs={{0,24},{4,28},{8,0},{12,4},{16,8},{20,12},{24,16},{28,20},{1,25},{... | collective-permute-start | bytes 368648 | tf_op jit(solution)/shard_map/ppermute | solution.py:325
  71.6 0.5 collective-permute-start.17
  72.2 0.1 collective-permute-start.24
  72.2 4.4 %collective-permute-done.17 = bf16[256,256]{1,0:T(8,128)(2,1)S(1)} collective-permute-done((bf16[256,256]{1,0:T(8,128)(2,1)S(1)}, bf16[256,256]{1,0:T(8,128)(2,1)S(1)}, u32[]{:S(2)}, u32[]{:S(2)}) %collective-permute-start.17) | collective-permute-done | bytes 131104 | tf_op jit(solution)/shard_map/ppermute | solution.py:330
  76.6 0.7 fusion
  77.3 1.3 %coef_rows.1 = f32[30,2000]{1,0:T(8,128)} custom-call(s32[4]{0:T(128)S(1)} %pad_add_fusion.place, f32[128,256]{1,0:T(8,128)S(1)} %convert_add_fusion.2.own, f32[128,256]{1,0:T(8,128)S(1)} %collective-permute-done.24.other), custom_call_target="tpu_custom_call" | custom-call | flops 1048576 | bytes 4194304 | tf_op jit(solution)/shard_map/coef_rows/pallas_call | solution.py:466
  78.6 0.8 fusion.3
  (35 shorter events, 0.4 us)
Async XLA Ops:
  0.6 11.0 %collective-permute-start = (bf16[256,256]{1,0:T(8,128)(2,1)}, bf16[256,256]{1,0:T(8,128)(2,1)S(1)}, u32[]{:S(2)}, u32[]{:S(2)}) collective-permute-start(bf16[256,256]{1,0:T(8,128)(2,1)} %param.9), channel_id=1, source_target_pairs={{0,4},{4,0},{8,12},{12,8},{16,20},{20,16},{24,28},{28,24},{1,5},{5... | collective-permute-start | bytes 393224 | tf_op jit(solution)/shard_map/ppermute | solution.py:319
  5.1 5.9 %collective-permute-start.1 = (f32[4,1024]{1,0:T(4,128)}, f32[4,1024]{1,0:T(4,128)S(1)}, u32[]{:S(2)}, u32[]{:S(2)}) collective-permute-start(f32[4,1024]{1,0:T(4,128)} %edge_table.1), channel_id=1, source_target_pairs={{0,4},{4,0},{8,12},{12,8},{16,20},{20,16},{24,28},{28,24},{1,5},{5... | collective-permute-start | bytes 49160 | tf_op jit(solution)/shard_map/ppermute | solution.py:319
  5.1 7.5 %collective-permute-start.2 = (bf16[256,256]{1,0:T(8,128)(2,1)}, bf16[256,256]{1,0:T(8,128)(2,1)S(1)}, u32[]{:S(2)}, u32[]{:S(2)}) collective-permute-start(bf16[256,256]{1,0:T(8,128)(2,1)} %bitcast.14), channel_id=1, source_target_pairs={{0,4},{4,0},{8,12},{12,8},{16,20},{20,16},{24,28},{28,24},{1,5},{5... | collective-permute-start | bytes 393224 | tf_op jit(solution)/shard_map/ppermute | solution.py:319
  7.1 8.0 %collective-permute-start.3 = (bf16[256,256]{1,0:T(8,128)(2,1)}, bf16[256,256]{1,0:T(8,128)(2,1)S(1)}, u32[]{:S(2)}, u32[]{:S(2)}) collective-permute-start(bf16[256,256]{1,0:T(8,128)(2,1)} %bitcast.15), channel_id=1, source_target_pairs={{0,8},{4,12},{8,16},{12,20},{16,24},{20,28},{24,0},{28,4},{1,9},{5... | collective-permute-start | bytes 393224 | tf_op jit(solution)/shard_map/ppermute | solution.py:325
  8.7 7.1 %collective-permute-start.4 = (bf16[256,256]{1,0:T(8,128)(2,1)}, bf16[256,256]{1,0:T(8,128)(2,1)S(1)}, u32[]{:S(2)}, u32[]{:S(2)}) collective-permute-start(bf16[256,256]{1,0:T(8,128)(2,1)} %bitcast.16), channel_id=1, source_target_pairs={{0,24},{4,28},{8,0},{12,4},{16,8},{20,12},{24,16},{28,20},{1,25},{... | collective-permute-start | bytes 393224 | tf_op jit(solution)/shard_map/ppermute | solution.py:325
  15.8 6.9 %collective-permute-start.6 = (bf16[2,256,256]{2,1,0:T(8,128)(2,1)S(1)}, bf16[2,256,256]{2,1,0:T(8,128)(2,1)S(1)}, u32[]{:S(2)}, u32[]{:S(2)}) collective-permute-start(bf16[2,256,256]{2,1,0:T(8,128)(2,1)S(1)} %pad_maximum_fusion.1), channel_id=1, source_target_pairs={{0,2},{1,3},{2,0},{3,1},{4,6},{5,7},{6,4},{7,5},{8,10},{9,11},{10,... | collective-permute-start | bytes 786440 | tf_op jit(solution)/shard_map/ppermute | solution.py:330
  17.3 7.7 %collective-permute-start.7 = (bf16[256,256]{1,0:T(8,128)(2,1)}, bf16[256,256]{1,0:T(8,128)(2,1)S(1)}, u32[]{:S(2)}, u32[]{:S(2)}) collective-permute-start(bf16[256,256]{1,0:T(8,128)(2,1)} %bitcast.17), channel_id=1, source_target_pairs={{0,16},{4,20},{8,24},{12,28},{16,0},{20,4},{24,8},{28,12},{1,17},{... | collective-permute-start | bytes 393224 | tf_op jit(solution)/shard_map/ppermute | solution.py:325
  18.5 6.5 %collective-permute-start.8 = (bf16[256,256]{1,0:T(8,128)(2,1)S(1)}, bf16[256,256]{1,0:T(8,128)(2,1)S(1)}, u32[]{:S(2)}, u32[]{:S(2)}) collective-permute-start(bf16[256,256]{1,0:T(8,128)(2,1)S(1)} %collective-permute-done.3.refs_0_.refs_1_), channel_id=1, source_target_pairs={{0,4},{4,0},{8,12},{12,8},{16,20},{20,16},{24,28},{28,24},{1,5},{5... | collective-permute-start | bytes 393224 | tf_op jit(solution)/shard_map/ppermute | solution.py:319
  19.0 6.0 %collective-permute-start.9 = (bf16[256,256]{1,0:T(8,128)(2,1)S(1)}, bf16[256,256]{1,0:T(8,128)(2,1)S(1)}, u32[]{:S(2)}, u32[]{:S(2)}) collective-permute-start(bf16[256,256]{1,0:T(8,128)(2,1)S(1)} %collective-permute-done.4.refs_2_.refs_3_), channel_id=1, source_target_pairs={{0,4},{4,0},{8,12},{12,8},{16,20},{20,16},{24,28},{28,24},{1,5},{5... | collective-permute-start | bytes 393224 | tf_op jit(solution)/shard_map/ppermute | solution.py:319
  25.0 2.0 %collective-permute-start.11 = (bf16[2,2,256,256]{3,2,1,0:T(8,128)(2,1)S(1)}, bf16[2,2,256,256]{3,2,1,0:T(8,128)(2,1)S(1)}, u32[]{:S(2)}, u32[]{:S(2)}) collective-permute-start(bf16[2,2,256,256]{3,2,1,0:T(8,128)(2,1)S(1)} %pad_maximum_fusion.feats), channel_id=1, source_target_pairs={{0,1},{1,0},{2,3},{3,2},{4,5},{5,4},{6,7},{7,6},{8,9},{9,8},{10,11... | collective-permute-start | bytes 1572872 | tf_op jit(solution)/shard_map/ppermute | solution.py:322
  25.1 1.9 %collective-permute-start.5 = (f32[2,4,1024]{2,1,0:T(4,128)S(1)}, f32[2,4,1024]{2,1,0:T(4,128)S(1)}, u32[]{:S(2)}, u32[]{:S(2)}) collective-permute-start(f32[2,4,1024]{2,1,0:T(4,128)S(1)} %pad_maximum_fusion.2.meta), channel_id=1, source_target_pairs={{0,1},{1,0},{2,3},{3,2},{4,5},{5,4},{6,7},{7,6},{8,9},{9,8},{10,11... | collective-permute-start | bytes 98312 | tf_op jit(solution)/shard_map/ppermute | solution.py:322
  25.6 6.2 %copy-start.1 = (bf16[2000,30]{0,1:T(8,128)(2,1)S(1)}, bf16[2000,30]{0,1:T(8,128)(2,1)}, u32[]{:S(2)}) copy-start(bf16[2000,30]{0,1:T(8,128)(2,1)} %param.12) | copy-start | bytes 360004
  25.6 6.2 %copy-start.2 = (bf16[1,256,256]{2,1,0:T(8,128)(2,1)S(1)}, bf16[1,256,256]{2,1,0:T(8,128)(2,1)}, u32[]{:S(2)}) copy-start(bf16[1,256,256]{2,1,0:T(8,128)(2,1)} %param.10) | copy-start | bytes 393220
  25.6 6.2 %collective-permute-start.10 = (bf16[256,256]{1,0:T(8,128)(2,1)S(1)}, bf16[256,256]{1,0:T(8,128)(2,1)S(1)}, u32[]{:S(2)}, u32[]{:S(2)}) collective-permute-start(bf16[256,256]{1,0:T(8,128)(2,1)S(1)} %collective-permute-done.7.refs_1_.refs_2_), channel_id=1, source_target_pairs={{0,4},{4,0},{8,12},{12,8},{16,20},{20,16},{24,28},{28,24},{1,5},{5... | collective-permute-start | bytes 393224 | tf_op jit(solution)/shard_map/ppermute | solution.py:319
  31.8 5.2 %copy-start = (bf16[30,256,256]{2,1,0:T(8,128)(2,1)S(1)}, bf16[30,256,256]{2,1,0:T(8,128)(2,1)}, u32[]{:S(2)}) copy-start(bf16[30,256,256]{2,1,0:T(8,128)(2,1)} %bases_ref.1) | copy-start | bytes 11796484
  36.8 10.6 %collective-permute-start.15 = (bf16[256,2048]{1,0:T(8,128)(2,1)S(1)}, bf16[256,2048]{1,0:T(8,128)(2,1)S(1)}, u32[]{:S(2)}, u32[]{:S(2)}) collective-permute-start(bf16[256,2048]{1,0:T(8,128)(2,1)S(1)} %get-tuple-element.41.gt_ref), channel_id=1, source_target_pairs={{0,1},{1,0},{2,3},{3,2},{4,5},{5,4},{6,7},{7,6},{8,9},{9,8},{10,11... | collective-permute-start | bytes 3145736 | tf_op jit(solution)/shard_map/ppermute | solution.py:322
  45.2 1.4 %collective-permute-start.13 = (f32[128,256]{1,0:T(8,128)S(1)}, f32[128,256]{1,0:T(8,128)S(1)}, u32[]{:S(2)}, u32[]{:S(2)}) collective-permute-start(f32[128,256]{1,0:T(8,128)S(1)} %get-tuple-element.46), channel_id=1, source_target_pairs={{0,1},{1,0},{2,3},{3,2},{4,5},{5,4},{6,7},{7,6},{8,9},{9,8},{10,11... | collective-permute-start | bytes 393224 | tf_op jit(solution)/shard_map/ppermute | solution.py:322
  45.6 16.4 %collective-permute-start.12 = (bf16[512,256]{1,0:T(8,128)(2,1)S(1)}, bf16[512,256]{1,0:T(8,128)(2,1)S(1)}, u32[]{:S(2)}, u32[]{:S(2)}) collective-permute-start(bf16[512,256]{1,0:T(8,128)(2,1)S(1)} %get-tuple-element.44), channel_id=1, source_target_pairs={{0,1},{1,0},{2,3},{3,2},{4,5},{5,4},{6,7},{7,6},{8,9},{9,8},{10,11... | collective-permute-start | bytes 786440 | tf_op jit(solution)/shard_map/ppermute | solution.py:322
  46.7 5.8 %collective-permute-start.14 = (f32[128,256]{1,0:T(8,128)S(1)}, f32[128,256]{1,0:T(8,128)S(1)}, u32[]{:S(2)}, u32[]{:S(2)}) collective-permute-start(f32[128,256]{1,0:T(8,128)S(1)} %add.50), channel_id=1, source_target_pairs={{0,4},{4,0},{8,12},{12,8},{16,20},{20,16},{24,28},{28,24},{1,5},{5... | collective-permute-start | bytes 393224 | tf_op jit(solution)/shard_map/ppermute | solution.py:319
  52.5 11.2 %collective-permute-start.20 = (bf16[128,256]{1,0:T(8,128)(2,1)S(1)}, bf16[128,256]{1,0:T(8,128)(2,1)S(1)}, u32[]{:S(2)}, u32[]{:S(2)}) collective-permute-start(bf16[128,256]{1,0:T(8,128)(2,1)S(1)} %add_convert_fusion.2), channel_id=1, source_target_pairs={{0,16},{4,20},{8,24},{12,28},{16,0},{20,4},{24,8},{28,12},{1,17},{... | collective-permute-start | bytes 196616 | tf_op jit(solution)/shard_map/ppermute | solution.py:325
  54.2 9.6 %collective-permute-start.21 = (bf16[128,256]{1,0:T(8,128)(2,1)S(1)}, bf16[128,256]{1,0:T(8,128)(2,1)S(1)}, u32[]{:S(2)}, u32[]{:S(2)}) collective-permute-start(bf16[128,256]{1,0:T(8,128)(2,1)S(1)} %add_convert_fusion.2), channel_id=1, source_target_pairs={{0,8},{4,12},{8,16},{12,20},{16,24},{20,28},{24,0},{28,4},{1,9},{5... | collective-permute-start | bytes 196616 | tf_op jit(solution)/shard_map/ppermute | solution.py:325
  55.8 8.0 %collective-permute-start.22 = (bf16[128,256]{1,0:T(8,128)(2,1)S(1)}, bf16[128,256]{1,0:T(8,128)(2,1)S(1)}, u32[]{:S(2)}, u32[]{:S(2)}) collective-permute-start(bf16[128,256]{1,0:T(8,128)(2,1)S(1)} %add_convert_fusion.2), channel_id=1, source_target_pairs={{0,24},{4,28},{8,0},{12,4},{16,8},{20,12},{24,16},{28,20},{1,25},{... | collective-permute-start | bytes 196616 | tf_op jit(solution)/shard_map/ppermute | solution.py:325
  58.0 7.9 %collective-permute-start.18 = (bf16[480,256]{1,0:T(8,128)(2,1)S(1)}, bf16[480,256]{1,0:T(8,128)(2,1)S(1)}, u32[]{:S(2)}, u32[]{:S(2)}) collective-permute-start(bf16[480,256]{1,0:T(8,128)(2,1)S(1)} %get-tuple-element.56), channel_id=1, source_target_pairs={{0,2},{1,3},{2,0},{3,1},{4,6},{5,7},{6,4},{7,5},{8,10},{9,11},{10,... | collective-permute-start | bytes 737288 | tf_op jit(solution)/shard_map/ppermute | solution.py:330
  62.1 8.4 %collective-permute-start.16 = (bf16[480,256]{1,0:T(8,128)(2,1)S(1)}, bf16[480,256]{1,0:T(8,128)(2,1)S(1)}, u32[]{:S(2)}, u32[]{:S(2)}) collective-permute-start(bf16[480,256]{1,0:T(8,128)(2,1)S(1)} %get-tuple-element.54), channel_id=1, source_target_pairs={{0,2},{1,3},{2,0},{3,1},{4,6},{5,7},{6,4},{7,5},{8,10},{9,11},{10,... | collective-permute-start | bytes 737288 | tf_op jit(solution)/shard_map/ppermute | solution.py:330
  66.0 12.6 %collective-permute-start.19 = (bf16[240,256]{1,0:T(8,128)(2,1)S(1)}, bf16[240,256]{1,0:T(8,128)(2,1)S(1)}, u32[]{:S(2)}, u32[]{:S(2)}) collective-permute-start(bf16[240,256]{1,0:T(8,128)(2,1)S(1)} %get-tuple-element.61), channel_id=1, source_target_pairs={{0,8},{4,12},{8,16},{12,20},{16,24},{20,28},{24,0},{28,4},{1,9},{5... | collective-permute-start | bytes 368648 | tf_op jit(solution)/shard_map/ppermute | solution.py:325
  66.0 6.1 %collective-permute-start.23 = (bf16[128,256]{1,0:T(8,128)(2,1)S(1)}, bf16[128,256]{1,0:T(8,128)(2,1)S(1)}, u32[]{:S(2)}, u32[]{:S(2)}) collective-permute-start(bf16[128,256]{1,0:T(8,128)(2,1)S(1)} %add_convert_fusion.1), channel_id=1, source_target_pairs={{0,2},{1,3},{2,0},{3,1},{4,6},{5,7},{6,4},{7,5},{8,10},{9,11},{10,... | collective-permute-start | bytes 196616 | tf_op jit(solution)/shard_map/ppermute | solution.py:330
  66.1 12.5 %collective-permute-start.25 = (bf16[240,256]{1,0:T(8,128)(2,1)S(1)}, bf16[240,256]{1,0:T(8,128)(2,1)S(1)}, u32[]{:S(2)}, u32[]{:S(2)}) collective-permute-start(bf16[240,256]{1,0:T(8,128)(2,1)S(1)} %get-tuple-element.62), channel_id=1, source_target_pairs={{0,16},{4,20},{8,24},{12,28},{16,0},{20,4},{24,8},{28,12},{1,17},{... | collective-permute-start | bytes 368648 | tf_op jit(solution)/shard_map/ppermute | solution.py:325
  70.6 8.0 %collective-permute-start.26 = (bf16[240,256]{1,0:T(8,128)(2,1)S(1)}, bf16[240,256]{1,0:T(8,128)(2,1)S(1)}, u32[]{:S(2)}, u32[]{:S(2)}) collective-permute-start(bf16[240,256]{1,0:T(8,128)(2,1)S(1)} %slice.47), channel_id=1, source_target_pairs={{0,24},{4,28},{8,0},{12,4},{16,8},{20,12},{24,16},{28,20},{1,25},{... | collective-permute-start | bytes 368648 | tf_op jit(solution)/shard_map/ppermute | solution.py:325
  71.6 5.0 %collective-permute-start.17 = (bf16[256,256]{1,0:T(8,128)(2,1)S(1)}, bf16[256,256]{1,0:T(8,128)(2,1)S(1)}, u32[]{:S(2)}, u32[]{:S(2)}) collective-permute-start(bf16[256,256]{1,0:T(8,128)(2,1)S(1)} %slice.46), channel_id=1, source_target_pairs={{0,2},{1,3},{2,0},{3,1},{4,6},{5,7},{6,4},{7,5},{8,10},{9,11},{10,... | collective-permute-start | bytes 393224 | tf_op jit(solution)/shard_map/ppermute | solution.py:330
  72.2 5.1 %collective-permute-start.24 = (f32[128,256]{1,0:T(8,128)S(1)}, f32[128,256]{1,0:T(8,128)S(1)}, u32[]{:S(2)}, u32[]{:S(2)}) collective-permute-start(f32[128,256]{1,0:T(8,128)S(1)} %convert_add_fusion.2.own), channel_id=1, source_target_pairs={{0,1},{1,0},{2,3},{3,2},{4,5},{5,4},{6,7},{7,6},{8,9},{9,8},{10,11... | collective-permute-start | bytes 393224 | tf_op jit(solution)/shard_map/ppermute | solution.py:322

commit v11 on v10

--- a/solution.py
+++ b/solution.py
@@ -456,11 +456,10 @@
     coef_part = tree_sum([low.astype(F32)] + [turn_z(low, s).astype(F32) for s in range(1, a_count)])
     add_blocks(after(after(place, low), marks[0]), order[half:])
     joined = packed[0].astype(F32) + after(flip_core(packed[1]), marks[-1]).astype(F32)
-    node_sum = joined[:shard]
-    for sy in range(1, y_count):
-        value = joined[sy * shard : (sy + 1) * shard].astype(BF16)
-        node_sum = node_sum + turn_y(after(value, landed[-1]), sy).astype(F32)
-    node_grad = node_sum.astype(BF16)
+    halved = [joined[:shard]] + [
+        turn_y(after(joined[sy * shard : (sy + 1) * shard].astype(BF16), landed[-1]), sy)
+        for sy in range(1, y_count)
+    ]
     low = after(coef_part.astype(BF16), landed[0])
     coef_part = tree_sum([low.astype(F32)] + [turn_y(low, s).astype(F32) for s in range(1, y_count)])
     coef_grad = call(
@@ -478,6 +477,10 @@
         owner = i * cols + j
         basis_sum = lax.dynamic_slice_in_dim(basis_sum, owner * block % TILE, block, axis=0)
     basis_grad = basis_sum / cols
+    node_sum = halved[0]
+    for value in halved[1:]:
+        node_sum = node_sum + after(value, basis_grad).astype(F32)
+    node_grad = node_sum.astype(BF16)
     return (node_grad, basis_grad, coef_grad.T)
 
 

time: 79.6 us -> 78.7 us (0.989)
  waiting for transfers between devices: 20.2 us -> 19.3 us
    ppermute x5, waiting for transfers between devices: 11.5 us -> 8.05 us  [turn_y(): lax.ppermute(value, 'col', [(c, (c + by * PAIR) % cols) for c in range(co...]
    ppermute x9, waiting for transfers between devices: 5.52 us -> 7.39 us  [turn_z(): lax.ppermute(value, 'row', [(r, (r + by * PAIR) % rows_total) for r in ra...]
  transfers between devices with their start and end apart: 27 -> 27, of which waited for: 10 -> 13; matrix products, arithmetic and copies ran while one was open for 4% -> 4% of each run, Pallas kernels for 29% -> 29%
where the time goes in v11:
time: 78.7 us; the launch traced here: 78.5 us
  Pallas kernels  27.8 us (35%)
  starting transfers between devices  27 us (34%)
  waiting for transfers between devices  19.3 us (25%)
  other arithmetic  3.5 us (4%)
  between operations  0.86 us (1%)
    ppermute x9, starting transfers between devices, turn_z(): lax.ppermute(value, 'row', [(r, (r + by * PAIR) % rows_total) for r in ra...  13 us
    ppermute x7, starting transfers between devices, flip_x(): return lax.ppermute(value, 'row', [(r, r ^ 1) for r in range(rows_total)])  8.38 us
    pallas_call x1, Pallas kernels, on_device(): call(functools.partial(forward_kernel, (cols, shard, span, heads, padded,...  8.2 us
    ppermute x5, waiting for transfers between devices, turn_y(): lax.ppermute(value, 'col', [(c, (c + by * PAIR) % cols) for c in range(co...  8.05 us
    ppermute x9, waiting for transfers between devices, turn_z(): lax.ppermute(value, 'row', [(r, (r + by * PAIR) % rows_total) for r in ra...  7.39 us
    pallas_call x2, Pallas kernels, basis_blocks(): call(functools.partial(basis_kernel, (rows_total, cols, block, cover // T...  7.14 us
    pallas_call x1, Pallas kernels, on_device(): call(functools.partial(grad_kernel, (rows_total, dest_shard, span, heads,...  4.96 us
    pallas_call x1, Pallas kernels, on_device(): call(functools.partial(source_kernel, (cols, shard, span, a_count - 1)),...  4.79 us
  transfers between devices with their start and end apart: 27, of which 13 were waited for; matrix products, arithmetic and copies ran while one was open for 4% of the time, Pallas kernels for 29%

profile of v11, /device:TPU:0, one launch (start us, length us, event | category | flops | bytes accessed | tf_op | source)
XLA Modules:
  0.0 78.5 jit_solution(14932256739761157647)
XLA Ops:
  0.6 3.0 %collective-permute-start = (bf16[256,256]{1,0:T(8,128)(2,1)}, bf16[256,256]{1,0:T(8,128)(2,1)S(1)}, u32[]{:S(2)}, u32[]{:S(2)}) collective-permute-start(bf16[256,256]{1,0:T(8,128)(2,1)} %param.9), channel_id=1, source_target_pairs={{0,4},{4,0},{8,12},{12,8},{16,20},{20,16},{24,28},{28,24},{1,5},{5... | collective-permute-start | bytes 393224 | tf_op jit(solution)/shard_map/ppermute | solution.py:319
  3.6 1.4 %edge_table.1 = f32[4,1024]{1,0:T(4,128)} custom-call(s32[1,1,8]{2,1,0:T(1,128)} %fills.1, s32[1,1,1024]{2,1,0:T(1,128)} %src.1, s32[1,1,1024]{2,1,0:T(1,128)} %dst.1, s32[1,1,1024]{2,1,0:T(1,128)} %rel.1, f32[1,1,1024]{2,1,0:T(1,128)} %norm.1), custom_call_target="tpu_custom_call" | custom-call | tf_op jit(solution)/shard_map/edge_table/pallas_call | solution.py:336
  5.1 2.0 %collective-permute-start.2 = (bf16[256,256]{1,0:T(8,128)(2,1)}, bf16[256,256]{1,0:T(8,128)(2,1)S(1)}, u32[]{:S(2)}, u32[]{:S(2)}) collective-permute-start(bf16[256,256]{1,0:T(8,128)(2,1)} %bitcast.14), channel_id=1, source_target_pairs={{0,4},{4,0},{8,12},{12,8},{16,20},{20,16},{24,28},{28,24},{1,5},{5... | collective-permute-start | bytes 393224 | tf_op jit(solution)/shard_map/ppermute | solution.py:319
  7.1 1.6 %collective-permute-start.3 = (bf16[256,256]{1,0:T(8,128)(2,1)}, bf16[256,256]{1,0:T(8,128)(2,1)S(1)}, u32[]{:S(2)}, u32[]{:S(2)}) collective-permute-start(bf16[256,256]{1,0:T(8,128)(2,1)} %bitcast.15), channel_id=1, source_target_pairs={{0,8},{4,12},{8,16},{12,20},{16,24},{20,28},{24,0},{28,4},{1,9},{5... | collective-permute-start | bytes 393224 | tf_op jit(solution)/shard_map/ppermute | solution.py:325
  8.7 2.2 %collective-permute-start.4 = (bf16[256,256]{1,0:T(8,128)(2,1)}, bf16[256,256]{1,0:T(8,128)(2,1)S(1)}, u32[]{:S(2)}, u32[]{:S(2)}) collective-permute-start(bf16[256,256]{1,0:T(8,128)(2,1)} %bitcast.16), channel_id=1, source_target_pairs={{0,24},{4,28},{8,0},{12,4},{16,8},{20,12},{24,16},{28,20},{1,25},{... | collective-permute-start | bytes 393224 | tf_op jit(solution)/shard_map/ppermute | solution.py:325
  10.9 0.7 pad_maximum_fusion.2.meta
  11.6 0.9 %pad_maximum_fusion.1 = bf16[2,256,256]{2,1,0:T(8,128)(2,1)S(1)} fusion(bf16[1,256,256]{2,1,0:T(8,128)(2,1)S(1)} %bitcast.23, bf16[1,256,256]{2,1,0:T(8,128)(2,1)} %bitcast.22), kind=kLoop, calls=%fused_computation.7 | loop fusion | flops 131072 | bytes 524288 | tf_op jit(solution)/shard_map/stack | solution.py:347
  12.6 2.5 %collective-permute-done.3.refs_0_.refs_1_ = bf16[256,256]{1,0:T(8,128)(2,1)S(1)} collective-permute-done((bf16[256,256]{1,0:T(8,128)(2,1)}, bf16[256,256]{1,0:T(8,128)(2,1)S(1)}, u32[]{:S(2)}, u32[]{:S(2)}) %collective-permute-start.3) | collective-permute-done | bytes 131104 | tf_op jit(solution)/shard_map/ppermute | solution.py:325
  15.1 0.7 collective-permute-done.4.refs_2_.refs_3_
  15.8 1.5 %collective-permute-start.6 = (bf16[2,256,256]{2,1,0:T(8,128)(2,1)S(1)}, bf16[2,256,256]{2,1,0:T(8,128)(2,1)S(1)}, u32[]{:S(2)}, u32[]{:S(2)}) collective-permute-start(bf16[2,256,256]{2,1,0:T(8,128)(2,1)S(1)} %pad_maximum_fusion.1), channel_id=1, source_target_pairs={{0,2},{1,3},{2,0},{3,1},{4,6},{5,7},{6,4},{7,5},{8,10},{9,11},{10,... | collective-permute-start | bytes 786440 | tf_op jit(solution)/shard_map/ppermute | solution.py:330
  17.3 1.2 %collective-permute-start.7 = (bf16[256,256]{1,0:T(8,128)(2,1)}, bf16[256,256]{1,0:T(8,128)(2,1)S(1)}, u32[]{:S(2)}, u32[]{:S(2)}) collective-permute-start(bf16[256,256]{1,0:T(8,128)(2,1)} %bitcast.17), channel_id=1, source_target_pairs={{0,16},{4,20},{8,24},{12,28},{16,0},{20,4},{24,8},{28,12},{1,17},{... | collective-permute-start | bytes 393224 | tf_op jit(solution)/shard_map/ppermute | solution.py:325
  18.5 0.5 collective-permute-start.8
  19.0 1.5 %collective-permute-start.9 = (bf16[256,256]{1,0:T(8,128)(2,1)S(1)}, bf16[256,256]{1,0:T(8,128)(2,1)S(1)}, u32[]{:S(2)}, u32[]{:S(2)}) collective-permute-start(bf16[256,256]{1,0:T(8,128)(2,1)S(1)} %collective-permute-done.4.refs_2_.refs_3_), channel_id=1, source_target_pairs={{0,4},{4,0},{8,12},{12,8},{16,20},{20,16},{24,28},{28,24},{1,5},{5... | collective-permute-start | bytes 393224 | tf_op jit(solution)/shard_map/ppermute | solution.py:319
  20.5 2.2 %collective-permute-done.6 = bf16[2,256,256]{2,1,0:T(8,128)(2,1)S(1)} collective-permute-done((bf16[2,256,256]{2,1,0:T(8,128)(2,1)S(1)}, bf16[2,256,256]{2,1,0:T(8,128)(2,1)S(1)}, u32[]{:S(2)}, u32[]{:S(2)}) %collective-permute-start.6) | collective-permute-done | bytes 262176 | tf_op jit(solution)/shard_map/ppermute | solution.py:330
  22.7 2.3 %collective-permute-done.7.refs_1_.refs_2_ = bf16[256,256]{1,0:T(8,128)(2,1)S(1)} collective-permute-done((bf16[256,256]{1,0:T(8,128)(2,1)}, bf16[256,256]{1,0:T(8,128)(2,1)S(1)}, u32[]{:S(2)}, u32[]{:S(2)}) %collective-permute-start.7) | collective-permute-done | bytes 131104 | tf_op jit(solution)/shard_map/ppermute | solution.py:325
  25.1 0.5 collective-permute-start.5
  25.5 0.1 pad_add_fusion.place
  25.6 0.6 collective-permute-start.10
  26.2 0.8 %collective-permute-done.5.meta_core = f32[2,4,1024]{2,1,0:T(4,128)S(1)} collective-permute-done((f32[2,4,1024]{2,1,0:T(4,128)S(1)}, f32[2,4,1024]{2,1,0:T(4,128)S(1)}, u32[]{:S(2)}, u32[]{:S(2)}) %collective-permute-start.5) | collective-permute-done | bytes 32800 | tf_op jit(solution)/shard_map/ppermute | solution.py:322
  27.0 4.8 %source_rows.1.refs_8_.xt_ref = bf16[4,256,1024]{2,1,0:T(8,128)(2,1)S(1)} custom-call(s32[4]{0:T(128)S(1)} %pad_add_fusion.place, f32[2,4,1024]{2,1,0:T(4,128)S(1)} %pad_maximum_fusion.2.meta, f32[2,4,1024]{2,1,0:T(4,128)S(1)} %collective-permute-done.5.meta_core, bf16[2,2,256,256]{3,2,1,0:T(8,128)(2,1)S(1)} %pad_maximum_fusion.feats, ...), custom_call_target="tpu_custom_call" | custom-call | flops 2147483648 | bytes 4194304 | tf_op jit(solution)/shard_map/source_rows/pallas_call | solution.py:364
  31.8 5.0 %edge_grads.1 = (bf16[256,2048]{1,0:T(8,128)(2,1)S(1)}, f32[4,32,1024]{2,1,0:T(8,128)S(1)}) custom-call(s32[4]{0:T(128)S(1)} %pad_add_fusion.place, f32[2,4,1024]{2,1,0:T(4,128)S(1)} %pad_maximum_fusion.2.meta, f32[2,4,1024]{2,1,0:T(4,128)S(1)} %collective-permute-done.5.meta_core, bf16[30,2000]{1,0:T(8,128)(2,1)S(1)} %bitcast.13, ...), custom_call_target="tpu_custom_call" | custom-call | flops 2147483648 | bytes 4194304 | tf_op jit(solution)/shard_map/edge_grads/pallas_call | solution.py:375
  36.8 0.2 collective-permute-start.15
  37.0 8.2 %backed_sums.1 = (bf16[512,256]{1,0:T(8,128)(2,1)S(1)}, bf16[512,256]{1,0:T(8,128)(2,1)S(1)}, f32[128,256]{1,0:T(8,128)S(1)}, f32[128,256]{1,0:T(8,128)S(1)}) custom-call(s32[4]{0:T(128)S(1)} %pad_add_fusion.place, f32[2,4,1024]{2,1,0:T(4,128)S(1)} %pad_maximum_fusion.2.meta, bf16[256,2048]{1,0:T(8,128)(2,1)S(1)} %get-tuple-element.42.gt_ref, ...), custom_call_target="tpu_custom_call" | custom-call | flops 4026531840 | bytes 4194304 | tf_op jit(solution)/shard_map/backed_sums/pallas_call | solution.py:394
  45.2 0.4 collective-permute-start.13
  45.6 0.1 collective-permute-start.12
  45.8 0.8 %collective-permute-done.13 = f32[128,256]{1,0:T(8,128)S(1)} collective-permute-done((f32[128,256]{1,0:T(8,128)S(1)}, f32[128,256]{1,0:T(8,128)S(1)}, u32[]{:S(2)}, u32[]{:S(2)}) %collective-permute-start.13) | collective-permute-done | bytes 131104 | tf_op jit(solution)/shard_map/ppermute | solution.py:322
  46.7 0.8 collective-permute-start.14
  47.4 3.6 %basis_terms.2 = (f32[480,256]{1,0:T(8,128)S(1)}, bf16[480,256]{1,0:T(8,128)(2,1)S(1)}) custom-call(s32[4]{0:T(128)S(1)} %pad_add_fusion.place, bf16[256,2048]{1,0:T(8,128)(2,1)S(1)} %get-tuple-element.42.gt_ref, bf16[256,2048]{1,0:T(8,128)(2,1)S(1)} %collective-permute-done.15.gt_core, bf16[4,256,1024]{2,1,0:T(8,128)(2,1)S(1)} %source_rows.1.refs_8_.xt_ref, ...), custom_call_target="tpu_custom_call" | custom-call | flops 2013265920 | bytes 4194304 | tf_op jit(solution)/shard_map/basis_terms/pallas_call | solution.py:414
  51.0 1.5 %collective-permute-done.14 = f32[128,256]{1,0:T(8,128)S(1)} collective-permute-done((f32[128,256]{1,0:T(8,128)S(1)}, f32[128,256]{1,0:T(8,128)S(1)}, u32[]{:S(2)}, u32[]{:S(2)}) %collective-permute-start.14) | collective-permute-done | bytes 131104 | tf_op jit(solution)/shard_map/ppermute | solution.py:319
  52.5 1.6 %collective-permute-start.20 = (bf16[128,256]{1,0:T(8,128)(2,1)S(1)}, bf16[128,256]{1,0:T(8,128)(2,1)S(1)}, u32[]{:S(2)}, u32[]{:S(2)}) collective-permute-start(bf16[128,256]{1,0:T(8,128)(2,1)S(1)} %add_convert_fusion.2), channel_id=1, source_target_pairs={{0,16},{4,20},{8,24},{12,28},{16,0},{20,4},{24,8},{28,12},{1,17},{... | collective-permute-start | bytes 196616 | tf_op jit(solution)/shard_map/ppermute | solution.py:325
  54.2 1.6 %collective-permute-start.21 = (bf16[128,256]{1,0:T(8,128)(2,1)S(1)}, bf16[128,256]{1,0:T(8,128)(2,1)S(1)}, u32[]{:S(2)}, u32[]{:S(2)}) collective-permute-start(bf16[128,256]{1,0:T(8,128)(2,1)S(1)} %add_convert_fusion.2), channel_id=1, source_target_pairs={{0,8},{4,12},{8,16},{12,20},{16,24},{20,28},{24,0},{28,4},{1,9},{5... | collective-permute-start | bytes 196616 | tf_op jit(solution)/shard_map/ppermute | solution.py:325
  55.8 2.2 %collective-permute-start.22 = (bf16[128,256]{1,0:T(8,128)(2,1)S(1)}, bf16[128,256]{1,0:T(8,128)(2,1)S(1)}, u32[]{:S(2)}, u32[]{:S(2)}) collective-permute-start(bf16[128,256]{1,0:T(8,128)(2,1)S(1)} %add_convert_fusion.2), channel_id=1, source_target_pairs={{0,24},{4,28},{8,0},{12,4},{16,8},{20,12},{24,16},{28,20},{1,25},{... | collective-permute-start | bytes 196616 | tf_op jit(solution)/shard_map/ppermute | solution.py:325
  58.0 0.5 collective-permute-start.18
  58.5 3.6 %basis_terms.3 = (f32[480,256]{1,0:T(8,128)S(1)}, bf16[480,256]{1,0:T(8,128)(2,1)S(1)}) custom-call(s32[4]{0:T(128)S(1)} %pad_add_fusion.place, bf16[256,2048]{1,0:T(8,128)(2,1)S(1)} %get-tuple-element.42.gt_ref, bf16[256,2048]{1,0:T(8,128)(2,1)S(1)} %collective-permute-done.15.gt_core, bf16[4,256,1024]{2,1,0:T(8,128)(2,1)S(1)} %source_rows.1.refs_8_.xt_ref, ...), custom_call_target="tpu_custom_call" | custom-call | flops 2013265920 | bytes 4194304 | tf_op jit(solution)/shard_map/basis_terms/pallas_call | solution.py:414
  62.1 1.6 %collective-permute-start.16 = (bf16[480,256]{1,0:T(8,128)(2,1)S(1)}, bf16[480,256]{1,0:T(8,128)(2,1)S(1)}, u32[]{:S(2)}, u32[]{:S(2)}) collective-permute-start(bf16[480,256]{1,0:T(8,128)(2,1)S(1)} %get-tuple-element.55), channel_id=1, source_target_pairs={{0,2},{1,3},{2,0},{3,1},{4,6},{5,7},{6,4},{7,5},{8,10},{9,11},{10,... | collective-permute-start | bytes 737288 | tf_op jit(solution)/shard_map/ppermute | solution.py:330
  63.7 2.2 %collective-permute-done.18 = bf16[480,256]{1,0:T(8,128)(2,1)S(1)} collective-permute-done((bf16[480,256]{1,0:T(8,128)(2,1)S(1)}, bf16[480,256]{1,0:T(8,128)(2,1)S(1)}, u32[]{:S(2)}, u32[]{:S(2)}) %collective-permute-start.18) | collective-permute-done | bytes 245792 | tf_op jit(solution)/shard_map/ppermute | solution.py:330
  66.0 0.1 collective-permute-start.23
  66.1 1.5 %collective-permute-start.25 = (bf16[240,256]{1,0:T(8,128)(2,1)S(1)}, bf16[240,256]{1,0:T(8,128)(2,1)S(1)}, u32[]{:S(2)}, u32[]{:S(2)}) collective-permute-start(bf16[240,256]{1,0:T(8,128)(2,1)S(1)} %get-tuple-element.64), channel_id=1, source_target_pairs={{0,16},{4,20},{8,24},{12,28},{16,0},{20,4},{24,8},{28,12},{1,17},{... | collective-permute-start | bytes 368648 | tf_op jit(solution)/shard_map/ppermute | solution.py:325
  67.6 2.9 %collective-permute-done.16 = bf16[480,256]{1,0:T(8,128)(2,1)S(1)} collective-permute-done((bf16[480,256]{1,0:T(8,128)(2,1)S(1)}, bf16[480,256]{1,0:T(8,128)(2,1)S(1)}, u32[]{:S(2)}, u32[]{:S(2)}) %collective-permute-start.16) | collective-permute-done | bytes 245792 | tf_op jit(solution)/shard_map/ppermute | solution.py:330
  70.6 1.0 %collective-permute-start.26 = (bf16[240,256]{1,0:T(8,128)(2,1)S(1)}, bf16[240,256]{1,0:T(8,128)(2,1)S(1)}, u32[]{:S(2)}, u32[]{:S(2)}) collective-permute-start(bf16[240,256]{1,0:T(8,128)(2,1)S(1)} %slice.47), channel_id=1, source_target_pairs={{0,24},{4,28},{8,0},{12,4},{16,8},{20,12},{24,16},{28,20},{1,25},{... | collective-permute-start | bytes 368648 | tf_op jit(solution)/shard_map/ppermute | solution.py:325
  71.8 0.6 collective-permute-start.17
  72.4 0.7 collective-permute-done.24.other
  73.1 1.3 %coef_rows.1 = f32[30,2000]{1,0:T(8,128)} custom-call(s32[4]{0:T(128)S(1)} %pad_add_fusion.place, f32[128,256]{1,0:T(8,128)S(1)} %convert_add_fusion.2.own, f32[128,256]{1,0:T(8,128)S(1)} %collective-permute-done.24.other), custom_call_target="tpu_custom_call" | custom-call | flops 1048576 | bytes 4194304 | tf_op jit(solution)/shard_map/coef_rows/pallas_call | solution.py:465
  74.4 1.6 %collective-permute-done.25 = bf16[240,256]{1,0:T(8,128)(2,1)S(1)} collective-permute-done((bf16[240,256]{1,0:T(8,128)(2,1)S(1)}, bf16[240,256]{1,0:T(8,128)(2,1)S(1)}, u32[]{:S(2)}, u32[]{:S(2)}) %collective-permute-start.25) | collective-permute-done | bytes 122912 | tf_op jit(solution)/shard_map/ppermute | solution.py:325
  76.0 0.3 collective-permute-done.26
  76.2 0.8 fusion.3
  77.0 0.8 %collective-permute-done.17 = bf16[256,256]{1,0:T(8,128)(2,1)S(1)} collective-permute-done((bf16[256,256]{1,0:T(8,128)(2,1)S(1)}, bf16[256,256]{1,0:T(8,128)(2,1)S(1)}, u32[]{:S(2)}, u32[]{:S(2)}) %collective-permute-start.17) | collective-permute-done | bytes 131104 | tf_op jit(solution)/shard_map/ppermute | solution.py:330
  77.8 0.7 fusion
  (35 shorter events, 0.6 us)
Async XLA Ops:
  0.6 11.0 %collective-permute-start = (bf16[256,256]{1,0:T(8,128)(2,1)}, bf16[256,256]{1,0:T(8,128)(2,1)S(1)}, u32[]{:S(2)}, u32[]{:S(2)}) collective-permute-start(bf16[256,256]{1,0:T(8,128)(2,1)} %param.9), channel_id=1, source_target_pairs={{0,4},{4,0},{8,12},{12,8},{16,20},{20,16},{24,28},{28,24},{1,5},{5... | collective-permute-start | bytes 393224 | tf_op jit(solution)/shard_map/ppermute | solution.py:319
  5.1 5.9 %collective-permute-start.1 = (f32[4,1024]{1,0:T(4,128)}, f32[4,1024]{1,0:T(4,128)S(1)}, u32[]{:S(2)}, u32[]{:S(2)}) collective-permute-start(f32[4,1024]{1,0:T(4,128)} %edge_table.1), channel_id=1, source_target_pairs={{0,4},{4,0},{8,12},{12,8},{16,20},{20,16},{24,28},{28,24},{1,5},{5... | collective-permute-start | bytes 49160 | tf_op jit(solution)/shard_map/ppermute | solution.py:319
  5.1 7.5 %collective-permute-start.2 = (bf16[256,256]{1,0:T(8,128)(2,1)}, bf16[256,256]{1,0:T(8,128)(2,1)S(1)}, u32[]{:S(2)}, u32[]{:S(2)}) collective-permute-start(bf16[256,256]{1,0:T(8,128)(2,1)} %bitcast.14), channel_id=1, source_target_pairs={{0,4},{4,0},{8,12},{12,8},{16,20},{20,16},{24,28},{28,24},{1,5},{5... | collective-permute-start | bytes 393224 | tf_op jit(solution)/shard_map/ppermute | solution.py:319
  7.1 8.0 %collective-permute-start.3 = (bf16[256,256]{1,0:T(8,128)(2,1)}, bf16[256,256]{1,0:T(8,128)(2,1)S(1)}, u32[]{:S(2)}, u32[]{:S(2)}) collective-permute-start(bf16[256,256]{1,0:T(8,128)(2,1)} %bitcast.15), channel_id=1, source_target_pairs={{0,8},{4,12},{8,16},{12,20},{16,24},{20,28},{24,0},{28,4},{1,9},{5... | collective-permute-start | bytes 393224 | tf_op jit(solution)/shard_map/ppermute | solution.py:325
  8.7 7.1 %collective-permute-start.4 = (bf16[256,256]{1,0:T(8,128)(2,1)}, bf16[256,256]{1,0:T(8,128)(2,1)S(1)}, u32[]{:S(2)}, u32[]{:S(2)}) collective-permute-start(bf16[256,256]{1,0:T(8,128)(2,1)} %bitcast.16), channel_id=1, source_target_pairs={{0,24},{4,28},{8,0},{12,4},{16,8},{20,12},{24,16},{28,20},{1,25},{... | collective-permute-start | bytes 393224 | tf_op jit(solution)/shard_map/ppermute | solution.py:325
  15.8 6.9 %collective-permute-start.6 = (bf16[2,256,256]{2,1,0:T(8,128)(2,1)S(1)}, bf16[2,256,256]{2,1,0:T(8,128)(2,1)S(1)}, u32[]{:S(2)}, u32[]{:S(2)}) collective-permute-start(bf16[2,256,256]{2,1,0:T(8,128)(2,1)S(1)} %pad_maximum_fusion.1), channel_id=1, source_target_pairs={{0,2},{1,3},{2,0},{3,1},{4,6},{5,7},{6,4},{7,5},{8,10},{9,11},{10,... | collective-permute-start | bytes 786440 | tf_op jit(solution)/shard_map/ppermute | solution.py:330
  17.3 7.7 %collective-permute-start.7 = (bf16[256,256]{1,0:T(8,128)(2,1)}, bf16[256,256]{1,0:T(8,128)(2,1)S(1)}, u32[]{:S(2)}, u32[]{:S(2)}) collective-permute-start(bf16[256,256]{1,0:T(8,128)(2,1)} %bitcast.17), channel_id=1, source_target_pairs={{0,16},{4,20},{8,24},{12,28},{16,0},{20,4},{24,8},{28,12},{1,17},{... | collective-permute-start | bytes 393224 | tf_op jit(solution)/shard_map/ppermute | solution.py:325
  18.5 6.5 %collective-permute-start.8 = (bf16[256,256]{1,0:T(8,128)(2,1)S(1)}, bf16[256,256]{1,0:T(8,128)(2,1)S(1)}, u32[]{:S(2)}, u32[]{:S(2)}) collective-permute-start(bf16[256,256]{1,0:T(8,128)(2,1)S(1)} %collective-permute-done.3.refs_0_.refs_1_), channel_id=1, source_target_pairs={{0,4},{4,0},{8,12},{12,8},{16,20},{20,16},{24,28},{28,24},{1,5},{5... | collective-permute-start | bytes 393224 | tf_op jit(solution)/shard_map/ppermute | solution.py:319
  19.0 6.0 %collective-permute-start.9 = (bf16[256,256]{1,0:T(8,128)(2,1)S(1)}, bf16[256,256]{1,0:T(8,128)(2,1)S(1)}, u32[]{:S(2)}, u32[]{:S(2)}) collective-permute-start(bf16[256,256]{1,0:T(8,128)(2,1)S(1)} %collective-permute-done.4.refs_2_.refs_3_), channel_id=1, source_target_pairs={{0,4},{4,0},{8,12},{12,8},{16,20},{20,16},{24,28},{28,24},{1,5},{5... | collective-permute-start | bytes 393224 | tf_op jit(solution)/shard_map/ppermute | solution.py:319
  25.0 2.0 %collective-permute-start.11 = (bf16[2,2,256,256]{3,2,1,0:T(8,128)(2,1)S(1)}, bf16[2,2,256,256]{3,2,1,0:T(8,128)(2,1)S(1)}, u32[]{:S(2)}, u32[]{:S(2)}) collective-permute-start(bf16[2,2,256,256]{3,2,1,0:T(8,128)(2,1)S(1)} %pad_maximum_fusion.feats), channel_id=1, source_target_pairs={{0,1},{1,0},{2,3},{3,2},{4,5},{5,4},{6,7},{7,6},{8,9},{9,8},{10,11... | collective-permute-start | bytes 1572872 | tf_op jit(solution)/shard_map/ppermute | solution.py:322
  25.1 1.9 %collective-permute-start.5 = (f32[2,4,1024]{2,1,0:T(4,128)S(1)}, f32[2,4,1024]{2,1,0:T(4,128)S(1)}, u32[]{:S(2)}, u32[]{:S(2)}) collective-permute-start(f32[2,4,1024]{2,1,0:T(4,128)S(1)} %pad_maximum_fusion.2.meta), channel_id=1, source_target_pairs={{0,1},{1,0},{2,3},{3,2},{4,5},{5,4},{6,7},{7,6},{8,9},{9,8},{10,11... | collective-permute-start | bytes 98312 | tf_op jit(solution)/shard_map/ppermute | solution.py:322
  25.6 6.2 %copy-start.1 = (bf16[2000,30]{0,1:T(8,128)(2,1)S(1)}, bf16[2000,30]{0,1:T(8,128)(2,1)}, u32[]{:S(2)}) copy-start(bf16[2000,30]{0,1:T(8,128)(2,1)} %param.12) | copy-start | bytes 360004
  25.6 6.2 %copy-start.2 = (bf16[1,256,256]{2,1,0:T(8,128)(2,1)S(1)}, bf16[1,256,256]{2,1,0:T(8,128)(2,1)}, u32[]{:S(2)}) copy-start(bf16[1,256,256]{2,1,0:T(8,128)(2,1)} %param.10) | copy-start | bytes 393220
  25.6 6.2 %collective-permute-start.10 = (bf16[256,256]{1,0:T(8,128)(2,1)S(1)}, bf16[256,256]{1,0:T(8,128)(2,1)S(1)}, u32[]{:S(2)}, u32[]{:S(2)}) collective-permute-start(bf16[256,256]{1,0:T(8,128)(2,1)S(1)} %collective-permute-done.7.refs_1_.refs_2_), channel_id=1, source_target_pairs={{0,4},{4,0},{8,12},{12,8},{16,20},{20,16},{24,28},{28,24},{1,5},{5... | collective-permute-start | bytes 393224 | tf_op jit(solution)/shard_map/ppermute | solution.py:319
  31.8 5.2 %copy-start = (bf16[30,256,256]{2,1,0:T(8,128)(2,1)S(1)}, bf16[30,256,256]{2,1,0:T(8,128)(2,1)}, u32[]{:S(2)}) copy-start(bf16[30,256,256]{2,1,0:T(8,128)(2,1)} %bases_ref.1) | copy-start | bytes 11796484
  36.8 10.6 %collective-permute-start.15 = (bf16[256,2048]{1,0:T(8,128)(2,1)S(1)}, bf16[256,2048]{1,0:T(8,128)(2,1)S(1)}, u32[]{:S(2)}, u32[]{:S(2)}) collective-permute-start(bf16[256,2048]{1,0:T(8,128)(2,1)S(1)} %get-tuple-element.42.gt_ref), channel_id=1, source_target_pairs={{0,1},{1,0},{2,3},{3,2},{4,5},{5,4},{6,7},{7,6},{8,9},{9,8},{10,11... | collective-permute-start | bytes 3145736 | tf_op jit(solution)/shard_map/ppermute | solution.py:322
  45.2 1.4 %collective-permute-start.13 = (f32[128,256]{1,0:T(8,128)S(1)}, f32[128,256]{1,0:T(8,128)S(1)}, u32[]{:S(2)}, u32[]{:S(2)}) collective-permute-start(f32[128,256]{1,0:T(8,128)S(1)} %get-tuple-element.47), channel_id=1, source_target_pairs={{0,1},{1,0},{2,3},{3,2},{4,5},{5,4},{6,7},{7,6},{8,9},{9,8},{10,11... | collective-permute-start | bytes 393224 | tf_op jit(solution)/shard_map/ppermute | solution.py:322
  45.6 16.4 %collective-permute-start.12 = (bf16[512,256]{1,0:T(8,128)(2,1)S(1)}, bf16[512,256]{1,0:T(8,128)(2,1)S(1)}, u32[]{:S(2)}, u32[]{:S(2)}) collective-permute-start(bf16[512,256]{1,0:T(8,128)(2,1)S(1)} %get-tuple-element.45), channel_id=1, source_target_pairs={{0,1},{1,0},{2,3},{3,2},{4,5},{5,4},{6,7},{7,6},{8,9},{9,8},{10,11... | collective-permute-start | bytes 786440 | tf_op jit(solution)/shard_map/ppermute | solution.py:322
  46.7 5.8 %collective-permute-start.14 = (f32[128,256]{1,0:T(8,128)S(1)}, f32[128,256]{1,0:T(8,128)S(1)}, u32[]{:S(2)}, u32[]{:S(2)}) collective-permute-start(f32[128,256]{1,0:T(8,128)S(1)} %add.50), channel_id=1, source_target_pairs={{0,4},{4,0},{8,12},{12,8},{16,20},{20,16},{24,28},{28,24},{1,5},{5... | collective-permute-start | bytes 393224 | tf_op jit(solution)/shard_map/ppermute | solution.py:319
  52.5 11.1 %collective-permute-start.20 = (bf16[128,256]{1,0:T(8,128)(2,1)S(1)}, bf16[128,256]{1,0:T(8,128)(2,1)S(1)}, u32[]{:S(2)}, u32[]{:S(2)}) collective-permute-start(bf16[128,256]{1,0:T(8,128)(2,1)S(1)} %add_convert_fusion.2), channel_id=1, source_target_pairs={{0,16},{4,20},{8,24},{12,28},{16,0},{20,4},{24,8},{28,12},{1,17},{... | collective-permute-start | bytes 196616 | tf_op jit(solution)/shard_map/ppermute | solution.py:325
  54.2 9.5 %collective-permute-start.21 = (bf16[128,256]{1,0:T(8,128)(2,1)S(1)}, bf16[128,256]{1,0:T(8,128)(2,1)S(1)}, u32[]{:S(2)}, u32[]{:S(2)}) collective-permute-start(bf16[128,256]{1,0:T(8,128)(2,1)S(1)} %add_convert_fusion.2), channel_id=1, source_target_pairs={{0,8},{4,12},{8,16},{12,20},{16,24},{20,28},{24,0},{28,4},{1,9},{5... | collective-permute-start | bytes 196616 | tf_op jit(solution)/shard_map/ppermute | solution.py:325
  55.8 7.9 %collective-permute-start.22 = (bf16[128,256]{1,0:T(8,128)(2,1)S(1)}, bf16[128,256]{1,0:T(8,128)(2,1)S(1)}, u32[]{:S(2)}, u32[]{:S(2)}) collective-permute-start(bf16[128,256]{1,0:T(8,128)(2,1)S(1)} %add_convert_fusion.2), channel_id=1, source_target_pairs={{0,24},{4,28},{8,0},{12,4},{16,8},{20,12},{24,16},{28,20},{1,25},{... | collective-permute-start | bytes 196616 | tf_op jit(solution)/shard_map/ppermute | solution.py:325
  58.0 7.9 %collective-permute-start.18 = (bf16[480,256]{1,0:T(8,128)(2,1)S(1)}, bf16[480,256]{1,0:T(8,128)(2,1)S(1)}, u32[]{:S(2)}, u32[]{:S(2)}) collective-permute-start(bf16[480,256]{1,0:T(8,128)(2,1)S(1)} %get-tuple-element.57), channel_id=1, source_target_pairs={{0,2},{1,3},{2,0},{3,1},{4,6},{5,7},{6,4},{7,5},{8,10},{9,11},{10,... | collective-permute-start | bytes 737288 | tf_op jit(solution)/shard_map/ppermute | solution.py:330
  62.1 8.4 %collective-permute-start.16 = (bf16[480,256]{1,0:T(8,128)(2,1)S(1)}, bf16[480,256]{1,0:T(8,128)(2,1)S(1)}, u32[]{:S(2)}, u32[]{:S(2)}) collective-permute-start(bf16[480,256]{1,0:T(8,128)(2,1)S(1)} %get-tuple-element.55), channel_id=1, source_target_pairs={{0,2},{1,3},{2,0},{3,1},{4,6},{5,7},{6,4},{7,5},{8,10},{9,11},{10,... | collective-permute-start | bytes 737288 | tf_op jit(solution)/shard_map/ppermute | solution.py:330
  66.0 8.4 %collective-permute-start.19 = (bf16[240,256]{1,0:T(8,128)(2,1)S(1)}, bf16[240,256]{1,0:T(8,128)(2,1)S(1)}, u32[]{:S(2)}, u32[]{:S(2)}) collective-permute-start(bf16[240,256]{1,0:T(8,128)(2,1)S(1)} %get-tuple-element.63), channel_id=1, source_target_pairs={{0,8},{4,12},{8,16},{12,20},{16,24},{20,28},{24,0},{28,4},{1,9},{5... | collective-permute-start | bytes 368648 | tf_op jit(solution)/shard_map/ppermute | solution.py:325
  66.0 5.6 %collective-permute-start.23 = (bf16[128,256]{1,0:T(8,128)(2,1)S(1)}, bf16[128,256]{1,0:T(8,128)(2,1)S(1)}, u32[]{:S(2)}, u32[]{:S(2)}) collective-permute-start(bf16[128,256]{1,0:T(8,128)(2,1)S(1)} %add_convert_fusion.1), channel_id=1, source_target_pairs={{0,2},{1,3},{2,0},{3,1},{4,6},{5,7},{6,4},{7,5},{8,10},{9,11},{10,... | collective-permute-start | bytes 196616 | tf_op jit(solution)/shard_map/ppermute | solution.py:330
  66.1 9.9 %collective-permute-start.25 = (bf16[240,256]{1,0:T(8,128)(2,1)S(1)}, bf16[240,256]{1,0:T(8,128)(2,1)S(1)}, u32[]{:S(2)}, u32[]{:S(2)}) collective-permute-start(bf16[240,256]{1,0:T(8,128)(2,1)S(1)} %get-tuple-element.64), channel_id=1, source_target_pairs={{0,16},{4,20},{8,24},{12,28},{16,0},{20,4},{24,8},{28,12},{1,17},{... | collective-permute-start | bytes 368648 | tf_op jit(solution)/shard_map/ppermute | solution.py:325
  70.6 5.6 %collective-permute-start.26 = (bf16[240,256]{1,0:T(8,128)(2,1)S(1)}, bf16[240,256]{1,0:T(8,128)(2,1)S(1)}, u32[]{:S(2)}, u32[]{:S(2)}) collective-permute-start(bf16[240,256]{1,0:T(8,128)(2,1)S(1)} %slice.47), channel_id=1, source_target_pairs={{0,24},{4,28},{8,0},{12,4},{16,8},{20,12},{24,16},{28,20},{1,25},{... | collective-permute-start | bytes 368648 | tf_op jit(solution)/shard_map/ppermute | solution.py:325
  71.7 1.4 %collective-permute-start.24 = (f32[128,256]{1,0:T(8,128)S(1)}, f32[128,256]{1,0:T(8,128)S(1)}, u32[]{:S(2)}, u32[]{:S(2)}) collective-permute-start(f32[128,256]{1,0:T(8,128)S(1)} %convert_add_fusion.2.own), channel_id=1, source_target_pairs={{0,1},{1,0},{2,3},{3,2},{4,5},{5,4},{6,7},{7,6},{8,9},{9,8},{10,11... | collective-permute-start | bytes 393224 | tf_op jit(solution)/shard_map/ppermute | solution.py:322
  71.8 6.0 %collective-permute-start.17 = (bf16[256,256]{1,0:T(8,128)(2,1)S(1)}, bf16[256,256]{1,0:T(8,128)(2,1)S(1)}, u32[]{:S(2)}, u32[]{:S(2)}) collective-permute-start(bf16[256,256]{1,0:T(8,128)(2,1)S(1)} %slice.46), channel_id=1, source_target_pairs={{0,2},{1,3},{2,0},{3,1},{4,6},{5,7},{6,4},{7,5},{8,10},{9,11},{10,... | collective-permute-start | bytes 393224 | tf_op jit(solution)/shard_map/ppermute | solution.py:330

commit v12 on v11

--- a/solution.py
+++ b/solution.py
@@ -351,7 +351,7 @@
     feats = jnp.stack([feats] + [turn_y(feats, s) for s in range(1, y_count)])
     across = [None if s == middle else flip_x(turned[s]) for s in range(a_count - 1)]
     feats, turned[middle], *early = lax.optimization_barrier(
-        (feats, turned[middle], *[across[s] for s in sides])
+        (feats, turned[middle], *[across[s] for s in sides[:1]])
     )
     for s, value in zip(sides, early):
         across[s] = value

time: 78.7 us -> 79.4 us (level)
  waiting for transfers between devices: 19.3 us -> 21.8 us
  starting transfers between devices: 27 us -> 25.2 us
    ppermute x5, waiting for transfers between devices: 8.05 us -> 9.77 us  [turn_y(): lax.ppermute(value, 'col', [(c, (c + by * PAIR) % cols) for c in range(co...]
    ppermute x9, starting transfers between devices: 13 us -> 11.4 us  [turn_z(): lax.ppermute(value, 'row', [(r, (r + by * PAIR) % rows_total) for r in ra...]
    ppermute x7, waiting for transfers between devices: 1.5 us -> 3.01 us  [flip_x(): return lax.ppermute(value, 'row', [(r, r ^ 1) for r in range(rows_total)])]
where the time goes in v12:
time: 79.4 us; the launch traced here: 79.1 us
  Pallas kernels  27.8 us (35%)
  starting transfers between devices  25.2 us (32%)
  waiting for transfers between devices  21.8 us (27%)
  other arithmetic  3.5 us (4%)
  between operations  0.8 us (1%)
    ppermute x9, starting transfers between devices, turn_z(): lax.ppermute(value, 'row', [(r, (r + by * PAIR) % rows_total) for r in ra...  11.4 us
    ppermute x5, waiting for transfers between devices, turn_y(): lax.ppermute(value, 'col', [(c, (c + by * PAIR) % cols) for c in range(co...  9.77 us
    ppermute x7, starting transfers between devices, flip_x(): return lax.ppermute(value, 'row', [(r, r ^ 1) for r in range(rows_total)])  8.24 us
    pallas_call x1, Pallas kernels, on_device(): call(functools.partial(forward_kernel, (cols, shard, span, heads, padded,...  8.2 us
    ppermute x9, waiting for transfers between devices, turn_z(): lax.ppermute(value, 'row', [(r, (r + by * PAIR) % rows_total) for r in ra...  7.46 us
    pallas_call x2, Pallas kernels, basis_blocks(): call(functools.partial(basis_kernel, (rows_total, cols, block, cover // T...  7.14 us
    pallas_call x1, Pallas kernels, on_device(): call(functools.partial(grad_kernel, (rows_total, dest_shard, span, heads,...  4.95 us
    pallas_call x1, Pallas kernels, on_device(): call(functools.partial(source_kernel, (cols, shard, span, a_count - 1)),...  4.79 us
  transfers between devices with their start and end apart: 27, of which 13 were waited for; matrix products, arithmetic and copies ran while one was open for 4% of the time, Pallas kernels for 29%

profile of v12, /device:TPU:0, one launch (start us, length us, event | category | flops | bytes accessed | tf_op | source)
XLA Modules:
  0.0 79.1 jit_solution(3258601608343616452)
XLA Ops:
  0.6 3.0 %collective-permute-start = (bf16[256,256]{1,0:T(8,128)(2,1)}, bf16[256,256]{1,0:T(8,128)(2,1)S(1)}, u32[]{:S(2)}, u32[]{:S(2)}) collective-permute-start(bf16[256,256]{1,0:T(8,128)(2,1)} %param.9), channel_id=1, source_target_pairs={{0,4},{4,0},{8,12},{12,8},{16,20},{20,16},{24,28},{28,24},{1,5},{5... | collective-permute-start | bytes 393224 | tf_op jit(solution)/shard_map/ppermute | solution.py:319
  3.6 1.4 %edge_table.1 = f32[4,1024]{1,0:T(4,128)} custom-call(s32[1,1,8]{2,1,0:T(1,128)} %fills.1, s32[1,1,1024]{2,1,0:T(1,128)} %src.1, s32[1,1,1024]{2,1,0:T(1,128)} %dst.1, s32[1,1,1024]{2,1,0:T(1,128)} %rel.1, f32[1,1,1024]{2,1,0:T(1,128)} %norm.1), custom_call_target="tpu_custom_call" | custom-call | tf_op jit(solution)/shard_map/edge_table/pallas_call | solution.py:336
  5.1 2.0 %collective-permute-start.2 = (bf16[256,256]{1,0:T(8,128)(2,1)}, bf16[256,256]{1,0:T(8,128)(2,1)S(1)}, u32[]{:S(2)}, u32[]{:S(2)}) collective-permute-start(bf16[256,256]{1,0:T(8,128)(2,1)} %bitcast.14), channel_id=1, source_target_pairs={{0,4},{4,0},{8,12},{12,8},{16,20},{20,16},{24,28},{28,24},{1,5},{5... | collective-permute-start | bytes 393224 | tf_op jit(solution)/shard_map/ppermute | solution.py:319
  7.1 1.6 %collective-permute-start.3 = (bf16[256,256]{1,0:T(8,128)(2,1)}, bf16[256,256]{1,0:T(8,128)(2,1)S(1)}, u32[]{:S(2)}, u32[]{:S(2)}) collective-permute-start(bf16[256,256]{1,0:T(8,128)(2,1)} %bitcast.15), channel_id=1, source_target_pairs={{0,8},{4,12},{8,16},{12,20},{16,24},{20,28},{24,0},{28,4},{1,9},{5... | collective-permute-start | bytes 393224 | tf_op jit(solution)/shard_map/ppermute | solution.py:325
  8.7 2.2 %collective-permute-start.4 = (bf16[256,256]{1,0:T(8,128)(2,1)}, bf16[256,256]{1,0:T(8,128)(2,1)S(1)}, u32[]{:S(2)}, u32[]{:S(2)}) collective-permute-start(bf16[256,256]{1,0:T(8,128)(2,1)} %bitcast.16), channel_id=1, source_target_pairs={{0,24},{4,28},{8,0},{12,4},{16,8},{20,12},{24,16},{28,20},{1,25},{... | collective-permute-start | bytes 393224 | tf_op jit(solution)/shard_map/ppermute | solution.py:325
  10.9 0.7 pad_maximum_fusion.2.meta
  11.6 0.9 %pad_maximum_fusion.1 = bf16[2,256,256]{2,1,0:T(8,128)(2,1)S(1)} fusion(bf16[1,256,256]{2,1,0:T(8,128)(2,1)S(1)} %bitcast.23, bf16[1,256,256]{2,1,0:T(8,128)(2,1)} %bitcast.22), kind=kLoop, calls=%fused_computation.7 | loop fusion | flops 131072 | bytes 524288 | tf_op jit(solution)/shard_map/stack | solution.py:347
  12.6 2.5 %collective-permute-done.3.refs_0_.refs_1_ = bf16[256,256]{1,0:T(8,128)(2,1)S(1)} collective-permute-done((bf16[256,256]{1,0:T(8,128)(2,1)}, bf16[256,256]{1,0:T(8,128)(2,1)S(1)}, u32[]{:S(2)}, u32[]{:S(2)}) %collective-permute-start.3) | collective-permute-done | bytes 131104 | tf_op jit(solution)/shard_map/ppermute | solution.py:325
  15.1 0.7 collective-permute-done.4.refs_2_.refs_3_
  15.8 1.5 %collective-permute-start.6 = (bf16[2,256,256]{2,1,0:T(8,128)(2,1)S(1)}, bf16[2,256,256]{2,1,0:T(8,128)(2,1)S(1)}, u32[]{:S(2)}, u32[]{:S(2)}) collective-permute-start(bf16[2,256,256]{2,1,0:T(8,128)(2,1)S(1)} %pad_maximum_fusion.1), channel_id=1, source_target_pairs={{0,2},{1,3},{2,0},{3,1},{4,6},{5,7},{6,4},{7,5},{8,10},{9,11},{10,... | collective-permute-start | bytes 786440 | tf_op jit(solution)/shard_map/ppermute | solution.py:330
  17.3 1.2 %collective-permute-start.7 = (bf16[256,256]{1,0:T(8,128)(2,1)}, bf16[256,256]{1,0:T(8,128)(2,1)S(1)}, u32[]{:S(2)}, u32[]{:S(2)}) collective-permute-start(bf16[256,256]{1,0:T(8,128)(2,1)} %bitcast.17), channel_id=1, source_target_pairs={{0,16},{4,20},{8,24},{12,28},{16,0},{20,4},{24,8},{28,12},{1,17},{... | collective-permute-start | bytes 393224 | tf_op jit(solution)/shard_map/ppermute | solution.py:325
  18.5 0.5 collective-permute-start.8
  19.0 3.6 %collective-permute-done.6 = bf16[2,256,256]{2,1,0:T(8,128)(2,1)S(1)} collective-permute-done((bf16[2,256,256]{2,1,0:T(8,128)(2,1)S(1)}, bf16[2,256,256]{2,1,0:T(8,128)(2,1)S(1)}, u32[]{:S(2)}, u32[]{:S(2)}) %collective-permute-start.6) | collective-permute-done | bytes 262176 | tf_op jit(solution)/shard_map/ppermute | solution.py:330
  22.7 2.3 %collective-permute-done.7.refs_1_.refs_2_ = bf16[256,256]{1,0:T(8,128)(2,1)S(1)} collective-permute-done((bf16[256,256]{1,0:T(8,128)(2,1)}, bf16[256,256]{1,0:T(8,128)(2,1)S(1)}, u32[]{:S(2)}, u32[]{:S(2)}) %collective-permute-start.7) | collective-permute-done | bytes 131104 | tf_op jit(solution)/shard_map/ppermute | solution.py:325
  25.0 0.5 collective-permute-start.5
  25.5 0.1 pad_add_fusion.place
  25.6 0.6 collective-permute-start.10
  26.2 1.5 %collective-permute-start.9 = (bf16[256,256]{1,0:T(8,128)(2,1)S(1)}, bf16[256,256]{1,0:T(8,128)(2,1)S(1)}, u32[]{:S(2)}, u32[]{:S(2)}) collective-permute-start(bf16[256,256]{1,0:T(8,128)(2,1)S(1)} %collective-permute-done.7.refs_1_.refs_2_), channel_id=1, source_target_pairs={{0,4},{4,0},{8,12},{12,8},{16,20},{20,16},{24,28},{28,24},{1,5},{5... | collective-permute-start | bytes 393224 | tf_op jit(solution)/shard_map/ppermute | solution.py:319
  27.7 4.8 %source_rows.1.refs_8_.xt_ref = bf16[4,256,1024]{2,1,0:T(8,128)(2,1)S(1)} custom-call(s32[4]{0:T(128)S(1)} %pad_add_fusion.place, f32[2,4,1024]{2,1,0:T(4,128)S(1)} %pad_maximum_fusion.2.meta, f32[2,4,1024]{2,1,0:T(4,128)S(1)} %collective-permute-done.5.meta_core, bf16[2,2,256,256]{3,2,1,0:T(8,128)(2,1)S(1)} %pad_maximum_fusion.feats, ...), custom_call_target="tpu_custom_call" | custom-call | flops 2147483648 | bytes 4194304 | tf_op jit(solution)/shard_map/source_rows/pallas_call | solution.py:364
  32.5 1.4 %collective-permute-done.9.refs_6_ = bf16[256,256]{1,0:T(8,128)(2,1)S(1)} collective-permute-done((bf16[256,256]{1,0:T(8,128)(2,1)S(1)}, bf16[256,256]{1,0:T(8,128)(2,1)S(1)}, u32[]{:S(2)}, u32[]{:S(2)}) %collective-permute-start.9) | collective-permute-done | bytes 131104 | tf_op jit(solution)/shard_map/ppermute | solution.py:319
  33.9 5.0 %edge_grads.1 = (bf16[256,2048]{1,0:T(8,128)(2,1)S(1)}, f32[4,32,1024]{2,1,0:T(8,128)S(1)}) custom-call(s32[4]{0:T(128)S(1)} %pad_add_fusion.place, f32[2,4,1024]{2,1,0:T(4,128)S(1)} %pad_maximum_fusion.2.meta, f32[2,4,1024]{2,1,0:T(4,128)S(1)} %collective-permute-done.5.meta_core, bf16[30,2000]{1,0:T(8,128)(2,1)S(1)} %bitcast.13, ...), custom_call_target="tpu_custom_call" | custom-call | flops 2147483648 | bytes 4194304 | tf_op jit(solution)/shard_map/edge_grads/pallas_call | solution.py:375
  38.8 0.1 collective-permute-start.15
  38.9 8.2 %backed_sums.1 = (bf16[512,256]{1,0:T(8,128)(2,1)S(1)}, bf16[512,256]{1,0:T(8,128)(2,1)S(1)}, f32[128,256]{1,0:T(8,128)S(1)}, f32[128,256]{1,0:T(8,128)S(1)}) custom-call(s32[4]{0:T(128)S(1)} %pad_add_fusion.place, f32[2,4,1024]{2,1,0:T(4,128)S(1)} %pad_maximum_fusion.2.meta, bf16[256,2048]{1,0:T(8,128)(2,1)S(1)} %get-tuple-element.40.gt_ref, ...), custom_call_target="tpu_custom_call" | custom-call | flops 4026531840 | bytes 4194304 | tf_op jit(solution)/shard_map/backed_sums/pallas_call | solution.py:394
  47.1 0.5 collective-permute-start.13
  47.7 0.1 collective-permute-start.12
  47.7 0.9 %collective-permute-done.13 = f32[128,256]{1,0:T(8,128)S(1)} collective-permute-done((f32[128,256]{1,0:T(8,128)S(1)}, f32[128,256]{1,0:T(8,128)S(1)}, u32[]{:S(2)}, u32[]{:S(2)}) %collective-permute-start.13) | collective-permute-done | bytes 131104 | tf_op jit(solution)/shard_map/ppermute | solution.py:322
  48.7 0.6 collective-permute-start.14
  49.3 3.6 %basis_terms.2 = (f32[480,256]{1,0:T(8,128)S(1)}, bf16[480,256]{1,0:T(8,128)(2,1)S(1)}) custom-call(s32[4]{0:T(128)S(1)} %pad_add_fusion.place, bf16[256,2048]{1,0:T(8,128)(2,1)S(1)} %get-tuple-element.40.gt_ref, bf16[256,2048]{1,0:T(8,128)(2,1)S(1)} %collective-permute-done.15.gt_core, bf16[4,256,1024]{2,1,0:T(8,128)(2,1)S(1)} %source_rows.1.refs_8_.xt_ref, ...), custom_call_target="tpu_custom_call" | custom-call | flops 2013265920 | bytes 4194304 | tf_op jit(solution)/shard_map/basis_terms/pallas_call | solution.py:414
  52.9 1.6 %collective-permute-done.14 = f32[128,256]{1,0:T(8,128)S(1)} collective-permute-done((f32[128,256]{1,0:T(8,128)S(1)}, f32[128,256]{1,0:T(8,128)S(1)}, u32[]{:S(2)}, u32[]{:S(2)}) %collective-permute-start.14) | collective-permute-done | bytes 131104 | tf_op jit(solution)/shard_map/ppermute | solution.py:319
  54.5 0.3 collective-permute-start.20
  54.8 2.2 %collective-permute-start.21 = (bf16[128,256]{1,0:T(8,128)(2,1)S(1)}, bf16[128,256]{1,0:T(8,128)(2,1)S(1)}, u32[]{:S(2)}, u32[]{:S(2)}) collective-permute-start(bf16[128,256]{1,0:T(8,128)(2,1)S(1)} %add_convert_fusion.2), channel_id=1, source_target_pairs={{0,8},{4,12},{8,16},{12,20},{16,24},{20,28},{24,0},{28,4},{1,9},{5... | collective-permute-start | bytes 196616 | tf_op jit(solution)/shard_map/ppermute | solution.py:325
  57.0 1.6 %collective-permute-start.22 = (bf16[128,256]{1,0:T(8,128)(2,1)S(1)}, bf16[128,256]{1,0:T(8,128)(2,1)S(1)}, u32[]{:S(2)}, u32[]{:S(2)}) collective-permute-start(bf16[128,256]{1,0:T(8,128)(2,1)S(1)} %add_convert_fusion.2), channel_id=1, source_target_pairs={{0,24},{4,28},{8,0},{12,4},{16,8},{20,12},{24,16},{28,20},{1,25},{... | collective-permute-start | bytes 196616 | tf_op jit(solution)/shard_map/ppermute | solution.py:325
  58.6 0.5 collective-permute-start.18
  59.1 3.6 %basis_terms.3 = (f32[480,256]{1,0:T(8,128)S(1)}, bf16[480,256]{1,0:T(8,128)(2,1)S(1)}) custom-call(s32[4]{0:T(128)S(1)} %pad_add_fusion.place, bf16[256,2048]{1,0:T(8,128)(2,1)S(1)} %get-tuple-element.40.gt_ref, bf16[256,2048]{1,0:T(8,128)(2,1)S(1)} %collective-permute-done.15.gt_core, bf16[4,256,1024]{2,1,0:T(8,128)(2,1)S(1)} %source_rows.1.refs_8_.xt_ref, ...), custom_call_target="tpu_custom_call" | custom-call | flops 2013265920 | bytes 4194304 | tf_op jit(solution)/shard_map/basis_terms/pallas_call | solution.py:414
  62.7 1.6 %collective-permute-start.16 = (bf16[480,256]{1,0:T(8,128)(2,1)S(1)}, bf16[480,256]{1,0:T(8,128)(2,1)S(1)}, u32[]{:S(2)}, u32[]{:S(2)}) collective-permute-start(bf16[480,256]{1,0:T(8,128)(2,1)S(1)} %get-tuple-element.53), channel_id=1, source_target_pairs={{0,2},{1,3},{2,0},{3,1},{4,6},{5,7},{6,4},{7,5},{8,10},{9,11},{10,... | collective-permute-start | bytes 737288 | tf_op jit(solution)/shard_map/ppermute | solution.py:330
  64.3 2.3 %collective-permute-done.18 = bf16[480,256]{1,0:T(8,128)(2,1)S(1)} collective-permute-done((bf16[480,256]{1,0:T(8,128)(2,1)S(1)}, bf16[480,256]{1,0:T(8,128)(2,1)S(1)}, u32[]{:S(2)}, u32[]{:S(2)}) %collective-permute-start.18) | collective-permute-done | bytes 245792 | tf_op jit(solution)/shard_map/ppermute | solution.py:330
  66.7 0.4 collective-permute-start.19
  67.1 1.1 %collective-permute-start.25 = (bf16[240,256]{1,0:T(8,128)(2,1)S(1)}, bf16[240,256]{1,0:T(8,128)(2,1)S(1)}, u32[]{:S(2)}, u32[]{:S(2)}) collective-permute-start(bf16[240,256]{1,0:T(8,128)(2,1)S(1)} %get-tuple-element.62), channel_id=1, source_target_pairs={{0,16},{4,20},{8,24},{12,28},{16,0},{20,4},{24,8},{28,12},{1,17},{... | collective-permute-start | bytes 368648 | tf_op jit(solution)/shard_map/ppermute | solution.py:325
  68.2 3.1 %collective-permute-done.16 = bf16[480,256]{1,0:T(8,128)(2,1)S(1)} collective-permute-done((bf16[480,256]{1,0:T(8,128)(2,1)S(1)}, bf16[480,256]{1,0:T(8,128)(2,1)S(1)}, u32[]{:S(2)}, u32[]{:S(2)}) %collective-permute-start.16) | collective-permute-done | bytes 245792 | tf_op jit(solution)/shard_map/ppermute | solution.py:330
  71.4 0.9 %collective-permute-start.26 = (bf16[240,256]{1,0:T(8,128)(2,1)S(1)}, bf16[240,256]{1,0:T(8,128)(2,1)S(1)}, u32[]{:S(2)}, u32[]{:S(2)}) collective-permute-start(bf16[240,256]{1,0:T(8,128)(2,1)S(1)} %slice.47), channel_id=1, source_target_pairs={{0,24},{4,28},{8,0},{12,4},{16,8},{20,12},{24,16},{28,20},{1,25},{... | collective-permute-start | bytes 368648 | tf_op jit(solution)/shard_map/ppermute | solution.py:325
  72.5 0.6 collective-permute-start.17
  73.0 0.7 collective-permute-done.24.other
  73.7 1.3 %coef_rows.1 = f32[30,2000]{1,0:T(8,128)} custom-call(s32[4]{0:T(128)S(1)} %pad_add_fusion.place, f32[128,256]{1,0:T(8,128)S(1)} %convert_add_fusion.2.own, f32[128,256]{1,0:T(8,128)S(1)} %collective-permute-done.24.other), custom_call_target="tpu_custom_call" | custom-call | flops 1048576 | bytes 4194304 | tf_op jit(solution)/shard_map/coef_rows/pallas_call | solution.py:465
  75.0 1.5 %collective-permute-done.25 = bf16[240,256]{1,0:T(8,128)(2,1)S(1)} collective-permute-done((bf16[240,256]{1,0:T(8,128)(2,1)S(1)}, bf16[240,256]{1,0:T(8,128)(2,1)S(1)}, u32[]{:S(2)}, u32[]{:S(2)}) %collective-permute-start.25) | collective-permute-done | bytes 122912 | tf_op jit(solution)/shard_map/ppermute | solution.py:325
  76.5 0.5 collective-permute-done.26
  76.9 0.8 fusion.3
  77.7 0.7 collective-permute-done.17
  78.4 0.7 fusion
  (35 shorter events, 0.5 us)
Async XLA Ops:
  0.6 11.0 %collective-permute-start = (bf16[256,256]{1,0:T(8,128)(2,1)}, bf16[256,256]{1,0:T(8,128)(2,1)S(1)}, u32[]{:S(2)}, u32[]{:S(2)}) collective-permute-start(bf16[256,256]{1,0:T(8,128)(2,1)} %param.9), channel_id=1, source_target_pairs={{0,4},{4,0},{8,12},{12,8},{16,20},{20,16},{24,28},{28,24},{1,5},{5... | collective-permute-start | bytes 393224 | tf_op jit(solution)/shard_map/ppermute | solution.py:319
  5.1 5.9 %collective-permute-start.1 = (f32[4,1024]{1,0:T(4,128)}, f32[4,1024]{1,0:T(4,128)S(1)}, u32[]{:S(2)}, u32[]{:S(2)}) collective-permute-start(f32[4,1024]{1,0:T(4,128)} %edge_table.1), channel_id=1, source_target_pairs={{0,4},{4,0},{8,12},{12,8},{16,20},{20,16},{24,28},{28,24},{1,5},{5... | collective-permute-start | bytes 49160 | tf_op jit(solution)/shard_map/ppermute | solution.py:319
  5.1 7.5 %collective-permute-start.2 = (bf16[256,256]{1,0:T(8,128)(2,1)}, bf16[256,256]{1,0:T(8,128)(2,1)S(1)}, u32[]{:S(2)}, u32[]{:S(2)}) collective-permute-start(bf16[256,256]{1,0:T(8,128)(2,1)} %bitcast.14), channel_id=1, source_target_pairs={{0,4},{4,0},{8,12},{12,8},{16,20},{20,16},{24,28},{28,24},{1,5},{5... | collective-permute-start | bytes 393224 | tf_op jit(solution)/shard_map/ppermute | solution.py:319
  7.1 8.0 %collective-permute-start.3 = (bf16[256,256]{1,0:T(8,128)(2,1)}, bf16[256,256]{1,0:T(8,128)(2,1)S(1)}, u32[]{:S(2)}, u32[]{:S(2)}) collective-permute-start(bf16[256,256]{1,0:T(8,128)(2,1)} %bitcast.15), channel_id=1, source_target_pairs={{0,8},{4,12},{8,16},{12,20},{16,24},{20,28},{24,0},{28,4},{1,9},{5... | collective-permute-start | bytes 393224 | tf_op jit(solution)/shard_map/ppermute | solution.py:325
  8.7 7.1 %collective-permute-start.4 = (bf16[256,256]{1,0:T(8,128)(2,1)}, bf16[256,256]{1,0:T(8,128)(2,1)S(1)}, u32[]{:S(2)}, u32[]{:S(2)}) collective-permute-start(bf16[256,256]{1,0:T(8,128)(2,1)} %bitcast.16), channel_id=1, source_target_pairs={{0,24},{4,28},{8,0},{12,4},{16,8},{20,12},{24,16},{28,20},{1,25},{... | collective-permute-start | bytes 393224 | tf_op jit(solution)/shard_map/ppermute | solution.py:325
  15.8 6.9 %collective-permute-start.6 = (bf16[2,256,256]{2,1,0:T(8,128)(2,1)S(1)}, bf16[2,256,256]{2,1,0:T(8,128)(2,1)S(1)}, u32[]{:S(2)}, u32[]{:S(2)}) collective-permute-start(bf16[2,256,256]{2,1,0:T(8,128)(2,1)S(1)} %pad_maximum_fusion.1), channel_id=1, source_target_pairs={{0,2},{1,3},{2,0},{3,1},{4,6},{5,7},{6,4},{7,5},{8,10},{9,11},{10,... | collective-permute-start | bytes 786440 | tf_op jit(solution)/shard_map/ppermute | solution.py:330
  17.3 7.7 %collective-permute-start.7 = (bf16[256,256]{1,0:T(8,128)(2,1)}, bf16[256,256]{1,0:T(8,128)(2,1)S(1)}, u32[]{:S(2)}, u32[]{:S(2)}) collective-permute-start(bf16[256,256]{1,0:T(8,128)(2,1)} %bitcast.17), channel_id=1, source_target_pairs={{0,16},{4,20},{8,24},{12,28},{16,0},{20,4},{24,8},{28,12},{1,17},{... | collective-permute-start | bytes 393224 | tf_op jit(solution)/shard_map/ppermute | solution.py:325
  18.5 6.5 %collective-permute-start.8 = (bf16[256,256]{1,0:T(8,128)(2,1)S(1)}, bf16[256,256]{1,0:T(8,128)(2,1)S(1)}, u32[]{:S(2)}, u32[]{:S(2)}) collective-permute-start(bf16[256,256]{1,0:T(8,128)(2,1)S(1)} %collective-permute-done.3.refs_0_.refs_1_), channel_id=1, source_target_pairs={{0,4},{4,0},{8,12},{12,8},{16,20},{20,16},{24,28},{28,24},{1,5},{5... | collective-permute-start | bytes 393224 | tf_op jit(solution)/shard_map/ppermute | solution.py:319
  25.0 2.6 %collective-permute-start.11 = (bf16[2,2,256,256]{3,2,1,0:T(8,128)(2,1)S(1)}, bf16[2,2,256,256]{3,2,1,0:T(8,128)(2,1)S(1)}, u32[]{:S(2)}, u32[]{:S(2)}) collective-permute-start(bf16[2,2,256,256]{3,2,1,0:T(8,128)(2,1)S(1)} %pad_maximum_fusion.feats), channel_id=1, source_target_pairs={{0,1},{1,0},{2,3},{3,2},{4,5},{5,4},{6,7},{7,6},{8,9},{9,8},{10,11... | collective-permute-start | bytes 1572872 | tf_op jit(solution)/shard_map/ppermute | solution.py:322
  25.0 2.6 %collective-permute-start.5 = (f32[2,4,1024]{2,1,0:T(4,128)S(1)}, f32[2,4,1024]{2,1,0:T(4,128)S(1)}, u32[]{:S(2)}, u32[]{:S(2)}) collective-permute-start(f32[2,4,1024]{2,1,0:T(4,128)S(1)} %pad_maximum_fusion.2.meta), channel_id=1, source_target_pairs={{0,1},{1,0},{2,3},{3,2},{4,5},{5,4},{6,7},{7,6},{8,9},{9,8},{10,11... | collective-permute-start | bytes 98312 | tf_op jit(solution)/shard_map/ppermute | solution.py:322
  25.6 8.2 %copy-start.1 = (bf16[2000,30]{0,1:T(8,128)(2,1)S(1)}, bf16[2000,30]{0,1:T(8,128)(2,1)}, u32[]{:S(2)}) copy-start(bf16[2000,30]{0,1:T(8,128)(2,1)} %param.12) | copy-start | bytes 360004
  25.6 8.2 %copy-start.2 = (bf16[1,256,256]{2,1,0:T(8,128)(2,1)S(1)}, bf16[1,256,256]{2,1,0:T(8,128)(2,1)}, u32[]{:S(2)}) copy-start(bf16[1,256,256]{2,1,0:T(8,128)(2,1)} %param.10) | copy-start | bytes 393220
  25.6 6.9 %collective-permute-start.10 = (bf16[256,256]{1,0:T(8,128)(2,1)S(1)}, bf16[256,256]{1,0:T(8,128)(2,1)S(1)}, u32[]{:S(2)}, u32[]{:S(2)}) collective-permute-start(bf16[256,256]{1,0:T(8,128)(2,1)S(1)} %collective-permute-done.4.refs_2_.refs_3_), channel_id=1, source_target_pairs={{0,4},{4,0},{8,12},{12,8},{16,20},{20,16},{24,28},{28,24},{1,5},{5... | collective-permute-start | bytes 393224 | tf_op jit(solution)/shard_map/ppermute | solution.py:319
  26.2 7.7 %collective-permute-start.9 = (bf16[256,256]{1,0:T(8,128)(2,1)S(1)}, bf16[256,256]{1,0:T(8,128)(2,1)S(1)}, u32[]{:S(2)}, u32[]{:S(2)}) collective-permute-start(bf16[256,256]{1,0:T(8,128)(2,1)S(1)} %collective-permute-done.7.refs_1_.refs_2_), channel_id=1, source_target_pairs={{0,4},{4,0},{8,12},{12,8},{16,20},{20,16},{24,28},{28,24},{1,5},{5... | collective-permute-start | bytes 393224 | tf_op jit(solution)/shard_map/ppermute | solution.py:319
  33.9 5.0 %copy-start = (bf16[30,256,256]{2,1,0:T(8,128)(2,1)S(1)}, bf16[30,256,256]{2,1,0:T(8,128)(2,1)}, u32[]{:S(2)}) copy-start(bf16[30,256,256]{2,1,0:T(8,128)(2,1)} %bases_ref.1) | copy-start | bytes 11796484
  38.8 10.5 %collective-permute-start.15 = (bf16[256,2048]{1,0:T(8,128)(2,1)S(1)}, bf16[256,2048]{1,0:T(8,128)(2,1)S(1)}, u32[]{:S(2)}, u32[]{:S(2)}) collective-permute-start(bf16[256,2048]{1,0:T(8,128)(2,1)S(1)} %get-tuple-element.40.gt_ref), channel_id=1, source_target_pairs={{0,1},{1,0},{2,3},{3,2},{4,5},{5,4},{6,7},{7,6},{8,9},{9,8},{10,11... | collective-permute-start | bytes 3145736 | tf_op jit(solution)/shard_map/ppermute | solution.py:322
  47.1 1.5 %collective-permute-start.13 = (f32[128,256]{1,0:T(8,128)S(1)}, f32[128,256]{1,0:T(8,128)S(1)}, u32[]{:S(2)}, u32[]{:S(2)}) collective-permute-start(f32[128,256]{1,0:T(8,128)S(1)} %get-tuple-element.45), channel_id=1, source_target_pairs={{0,1},{1,0},{2,3},{3,2},{4,5},{5,4},{6,7},{7,6},{8,9},{9,8},{10,11... | collective-permute-start | bytes 393224 | tf_op jit(solution)/shard_map/ppermute | solution.py:322
  47.7 15.0 %collective-permute-start.12 = (bf16[512,256]{1,0:T(8,128)(2,1)S(1)}, bf16[512,256]{1,0:T(8,128)(2,1)S(1)}, u32[]{:S(2)}, u32[]{:S(2)}) collective-permute-start(bf16[512,256]{1,0:T(8,128)(2,1)S(1)} %get-tuple-element.43), channel_id=1, source_target_pairs={{0,1},{1,0},{2,3},{3,2},{4,5},{5,4},{6,7},{7,6},{8,9},{9,8},{10,11... | collective-permute-start | bytes 786440 | tf_op jit(solution)/shard_map/ppermute | solution.py:322
  48.7 5.8 %collective-permute-start.14 = (f32[128,256]{1,0:T(8,128)S(1)}, f32[128,256]{1,0:T(8,128)S(1)}, u32[]{:S(2)}, u32[]{:S(2)}) collective-permute-start(f32[128,256]{1,0:T(8,128)S(1)} %add.50), channel_id=1, source_target_pairs={{0,4},{4,0},{8,12},{12,8},{16,20},{20,16},{24,28},{28,24},{1,5},{5... | collective-permute-start | bytes 393224 | tf_op jit(solution)/shard_map/ppermute | solution.py:319
  54.5 9.8 %collective-permute-start.20 = (bf16[128,256]{1,0:T(8,128)(2,1)S(1)}, bf16[128,256]{1,0:T(8,128)(2,1)S(1)}, u32[]{:S(2)}, u32[]{:S(2)}) collective-permute-start(bf16[128,256]{1,0:T(8,128)(2,1)S(1)} %add_convert_fusion.2), channel_id=1, source_target_pairs={{0,16},{4,20},{8,24},{12,28},{16,0},{20,4},{24,8},{28,12},{1,17},{... | collective-permute-start | bytes 196616 | tf_op jit(solution)/shard_map/ppermute | solution.py:325
  54.8 9.5 %collective-permute-start.21 = (bf16[128,256]{1,0:T(8,128)(2,1)S(1)}, bf16[128,256]{1,0:T(8,128)(2,1)S(1)}, u32[]{:S(2)}, u32[]{:S(2)}) collective-permute-start(bf16[128,256]{1,0:T(8,128)(2,1)S(1)} %add_convert_fusion.2), channel_id=1, source_target_pairs={{0,8},{4,12},{8,16},{12,20},{16,24},{20,28},{24,0},{28,4},{1,9},{5... | collective-permute-start | bytes 196616 | tf_op jit(solution)/shard_map/ppermute | solution.py:325
  57.0 7.3 %collective-permute-start.22 = (bf16[128,256]{1,0:T(8,128)(2,1)S(1)}, bf16[128,256]{1,0:T(8,128)(2,1)S(1)}, u32[]{:S(2)}, u32[]{:S(2)}) collective-permute-start(bf16[128,256]{1,0:T(8,128)(2,1)S(1)} %add_convert_fusion.2), channel_id=1, source_target_pairs={{0,24},{4,28},{8,0},{12,4},{16,8},{20,12},{24,16},{28,20},{1,25},{... | collective-permute-start | bytes 196616 | tf_op jit(solution)/shard_map/ppermute | solution.py:325
  58.6 8.0 %collective-permute-start.18 = (bf16[480,256]{1,0:T(8,128)(2,1)S(1)}, bf16[480,256]{1,0:T(8,128)(2,1)S(1)}, u32[]{:S(2)}, u32[]{:S(2)}) collective-permute-start(bf16[480,256]{1,0:T(8,128)(2,1)S(1)} %get-tuple-element.55), channel_id=1, source_target_pairs={{0,2},{1,3},{2,0},{3,1},{4,6},{5,7},{6,4},{7,5},{8,10},{9,11},{10,... | collective-permute-start | bytes 737288 | tf_op jit(solution)/shard_map/ppermute | solution.py:330
  62.7 8.6 %collective-permute-start.16 = (bf16[480,256]{1,0:T(8,128)(2,1)S(1)}, bf16[480,256]{1,0:T(8,128)(2,1)S(1)}, u32[]{:S(2)}, u32[]{:S(2)}) collective-permute-start(bf16[480,256]{1,0:T(8,128)(2,1)S(1)} %get-tuple-element.53), channel_id=1, source_target_pairs={{0,2},{1,3},{2,0},{3,1},{4,6},{5,7},{6,4},{7,5},{8,10},{9,11},{10,... | collective-permute-start | bytes 737288 | tf_op jit(solution)/shard_map/ppermute | solution.py:330
  66.7 8.3 %collective-permute-start.19 = (bf16[240,256]{1,0:T(8,128)(2,1)S(1)}, bf16[240,256]{1,0:T(8,128)(2,1)S(1)}, u32[]{:S(2)}, u32[]{:S(2)}) collective-permute-start(bf16[240,256]{1,0:T(8,128)(2,1)S(1)} %get-tuple-element.61), channel_id=1, source_target_pairs={{0,8},{4,12},{8,16},{12,20},{16,24},{20,28},{24,0},{28,4},{1,9},{5... | collective-permute-start | bytes 368648 | tf_op jit(solution)/shard_map/ppermute | solution.py:325
  67.1 5.2 %collective-permute-start.23 = (bf16[128,256]{1,0:T(8,128)(2,1)S(1)}, bf16[128,256]{1,0:T(8,128)(2,1)S(1)}, u32[]{:S(2)}, u32[]{:S(2)}) collective-permute-start(bf16[128,256]{1,0:T(8,128)(2,1)S(1)} %add_convert_fusion.1), channel_id=1, source_target_pairs={{0,2},{1,3},{2,0},{3,1},{4,6},{5,7},{6,4},{7,5},{8,10},{9,11},{10,... | collective-permute-start | bytes 196616 | tf_op jit(solution)/shard_map/ppermute | solution.py:330
  67.1 9.4 %collective-permute-start.25 = (bf16[240,256]{1,0:T(8,128)(2,1)S(1)}, bf16[240,256]{1,0:T(8,128)(2,1)S(1)}, u32[]{:S(2)}, u32[]{:S(2)}) collective-permute-start(bf16[240,256]{1,0:T(8,128)(2,1)S(1)} %get-tuple-element.62), channel_id=1, source_target_pairs={{0,16},{4,20},{8,24},{12,28},{16,0},{20,4},{24,8},{28,12},{1,17},{... | collective-permute-start | bytes 368648 | tf_op jit(solution)/shard_map/ppermute | solution.py:325
  71.4 5.6 %collective-permute-start.26 = (bf16[240,256]{1,0:T(8,128)(2,1)S(1)}, bf16[240,256]{1,0:T(8,128)(2,1)S(1)}, u32[]{:S(2)}, u32[]{:S(2)}) collective-permute-start(bf16[240,256]{1,0:T(8,128)(2,1)S(1)} %slice.47), channel_id=1, source_target_pairs={{0,24},{4,28},{8,0},{12,4},{16,8},{20,12},{24,16},{28,20},{1,25},{... | collective-permute-start | bytes 368648 | tf_op jit(solution)/shard_map/ppermute | solution.py:325
  72.3 1.4 %collective-permute-start.24 = (f32[128,256]{1,0:T(8,128)S(1)}, f32[128,256]{1,0:T(8,128)S(1)}, u32[]{:S(2)}, u32[]{:S(2)}) collective-permute-start(f32[128,256]{1,0:T(8,128)S(1)} %convert_add_fusion.2.own), channel_id=1, source_target_pairs={{0,1},{1,0},{2,3},{3,2},{4,5},{5,4},{6,7},{7,6},{8,9},{9,8},{10,11... | collective-permute-start | bytes 393224 | tf_op jit(solution)/shard_map/ppermute | solution.py:322
  72.5 6.0 %collective-permute-start.17 = (bf16[256,256]{1,0:T(8,128)(2,1)S(1)}, bf16[256,256]{1,0:T(8,128)(2,1)S(1)}, u32[]{:S(2)}, u32[]{:S(2)}) collective-permute-start(bf16[256,256]{1,0:T(8,128)(2,1)S(1)} %slice.46), channel_id=1, source_target_pairs={{0,2},{1,3},{2,0},{3,1},{4,6},{5,7},{6,4},{7,5},{8,10},{9,11},{10,... | collective-permute-start | bytes 393224 | tf_op jit(solution)/shard_map/ppermute | solution.py:330
